TPU v7x, 32 devices: a whole 2x2x4 slice. The times are simulated.
32 devices in a mesh: dp: 4 (over x, core), fsdp: 8 (over z, y).
Axes of the slice: x: 2, y: 2, z: 4, core: 2. Of those that a mesh axis runs over, the one named last changes fastest.
Arguments:
- frames_in: bfloat16 [64, 256, 512], P(('dp', 'fsdp')), may hold values from -6 to 6
- frame_lengths: int32 [64], P(('dp', 'fsdp')), may hold values from 128 to 256, as said below
- label_ids: int32 [64, 24], P(('dp', 'fsdp')), may hold values from 1 to 1023
- label_lengths: int32 [64], P(('dp', 'fsdp')), may hold values from 12 to 24, as said below
- pred_states: bfloat16 [64, 25, 640], P(('dp', 'fsdp')), may hold values from -6 to 6
- norm_gains: bfloat16 [2, 5, 512], P(None, None, 'fsdp'), may hold values from 0.5 to 1.5
- first_in: bfloat16 [2, 512, 2048], P(None, 'fsdp'), may hold values from -0.25 to 0.25
- first_out: bfloat16 [2, 2048, 512], P(None, 'fsdp'), may hold values from -0.125 to 0.125
- attend_joint: bfloat16 [2, 512, 1536], P(None, 'fsdp'), may hold values from -0.25 to 0.25
- attend_out: bfloat16 [2, 512, 512], P(None, 'fsdp'), may hold values from -1 to 1
- point_in: bfloat16 [2, 512, 1024], P(None, 'fsdp'), may hold values from -0.25 to 0.25
- depth_taps: bfloat16 [2, 9, 512], P(None, None, 'fsdp'), may hold values from -2 to 2
- batch_gain: bfloat16 [2, 512], P(None, 'fsdp'), may hold values from 0.5 to 1.5
- batch_bias: bfloat16 [2, 512], P(None, 'fsdp'), may hold values from -3 to 3
- point_out: bfloat16 [2, 512, 512], P(None, 'fsdp'), may hold values from -0.25 to 0.25
- second_in: bfloat16 [2, 512, 2048], P(None, 'fsdp'), may hold values from -0.25 to 0.25
- second_out: bfloat16 [2, 2048, 512], P(None, 'fsdp'), may hold values from -0.125 to 0.125
- enc_weight: bfloat16 [512, 640], P('fsdp'), may hold values from -0.25 to 0.25
- pred_weight: bfloat16 [640, 640], P('fsdp'), may hold values from -0.25 to 0.25
- token_weight: bfloat16 [640, 1024], P('fsdp'), may hold values from -0.5 to 0.5
- duration_weight: bfloat16 [640, 5], P('fsdp'), may hold values from -0.5 to 0.5
Outputs:
- utt_loss: float32 [64], P(('dp', 'fsdp'))
- grad_frames: float32 [64, 256, 512], P(('dp', 'fsdp'))
- grad_norm_gains: float32 [2, 5, 512], P(None, None, 'fsdp')
- grad_first_in: float32 [2, 512, 2048], P(None, 'fsdp')
- grad_first_out: float32 [2, 2048, 512], P(None, 'fsdp')
- grad_attend_joint: float32 [2, 512, 1536], P(None, 'fsdp')
- grad_attend_out: float32 [2, 512, 512], P(None, 'fsdp')
- grad_point_in: float32 [2, 512, 1024], P(None, 'fsdp')
- grad_depth_taps: float32 [2, 9, 512], P(None, None, 'fsdp')
- grad_batch_gain: float32 [2, 512], P(None, 'fsdp')
- grad_batch_bias: float32 [2, 512], P(None, 'fsdp')
- grad_point_out: float32 [2, 512, 512], P(None, 'fsdp')
- grad_second_in: float32 [2, 512, 2048], P(None, 'fsdp')
- grad_second_out: float32 [2, 2048, 512], P(None, 'fsdp')
- grad_enc_weight: float32 [512, 640], P('fsdp')
- grad_pred_weight: float32 [640, 640], P('fsdp')
- grad_token_weight: float32 [640, 1024], P('fsdp')
- grad_duration_weight: float32 [640, 5], P('fsdp')
Inputs may be any that keep to these rules, and one draw needn't show every extreme that they name: `frame_lengths`: every utterance has at least half of its 256 frames valid; the first utterance of every draw has all 256. `label_lengths`: every utterance has at least half of its 24 targets; the first utterance of every draw has all 24.
All inputs are finite; a program needn't handle non-finite values.
Results may differ from a plain program's by a relative error of at most 0.028.
Values may be sent and summed in bfloat16 or wider, within the bound.
A program may use at most 256 MiB of HBM per device.

v0:
```python
from functools import partial

import jax
import jax.numpy as jnp
from jax import lax
from jax.sharding import PartitionSpec as P

HEADS = 8


EPS = 1e-05
MASKED = -1000000000.0
NEG = -1e30


def log_total(value, axis):
    top = jnp.max(value, axis, keepdims=True)
    return jnp.squeeze(top, axis) + jnp.log(jnp.sum(jnp.exp(value - top), axis))


def lattice(blank, label, dur, t_len, u_len):
    utts, frames, slots = blank.shape
    reach = dur.shape[-1] - 1
    lower = lax.broadcasted_iota(jnp.int32, (slots, slots), 1) <= lax.broadcasted_iota(
        jnp.int32, (slots, slots), 0
    )
    start_row = jnp.where(
        lax.broadcasted_iota(jnp.int32, (utts, 1, slots), 2) == 0, 0.0, NEG
    ).astype(jnp.float32)
    pending = jnp.concatenate([start_row, jnp.full((utts, reach - 1, slots), NEG, jnp.float32)], 1)
    edge = jnp.full((utts, 1), NEG, jnp.float32)

    def advance(waiting, inputs):
        blank_t, label_t, dur_t = inputs
        arrive = waiting[:, 0]
        emit = label_t + dur_t[:, :, 0]
        climb = jnp.cumsum(emit, -1) - emit
        table = jnp.where(lower[None], (arrive - climb)[:, None, :], NEG)
        alpha = climb + log_total(table, -1)
        moves = []
        for skip in range(1, reach + 1):
            stay = alpha + blank_t + dur_t[:, :, skip]
            rise = jnp.concatenate([edge, (alpha + label_t + dur_t[:, :, skip])[:, :-1]], 1)
            moves.append(jnp.logaddexp(stay, rise))
        later = [jnp.logaddexp(waiting[:, skip], moves[skip - 1]) for skip in range(1, reach)] + [
            moves[reach - 1]
        ]
        return (jnp.stack(later, 1), alpha)

    inputs = (jnp.swapaxes(blank, 0, 1), jnp.swapaxes(label, 0, 1), jnp.swapaxes(dur, 0, 1))
    unused, alphas = lax.scan(advance, pending, inputs)
    alphas = jnp.swapaxes(alphas, 0, 1)
    times = lax.broadcasted_iota(jnp.int32, (utts, frames, slots), 1)
    places = lax.broadcasted_iota(jnp.int32, (utts, frames, slots), 2)
    at_end = places == u_len[:, None, None]
    ends = []
    for skip in range(1, reach + 1):
        hit = at_end & (times + skip == t_len[:, None, None])
        ends.append(jnp.where(hit, alphas + blank + dur[..., skip], NEG))
    return log_total(jnp.stack(ends, -1).reshape(utts, -1), -1)


def norm_rows(value, gain):
    centre = jnp.mean(value, -1, keepdims=True)
    centred = value - centre
    spread = jnp.mean(centred * centred, -1, keepdims=True)
    return centred * lax.rsqrt(spread + EPS) * gain


def norm_back(value, gain, grad):
    result, pullback = jax.vjp(norm_rows, value, gain)
    return pullback(grad)


def matmul(left, right):
    return jnp.dot(left, right, preferred_element_type=jnp.float32)


def contract_rows(left, right):
    return lax.dot_general(
        left, right, (((0,), (0,)), ((), ())), preferred_element_type=jnp.float32
    )


def contract_cols(left, right):
    return lax.dot_general(
        left, right, (((1,), (1,)), ((), ())), preferred_element_type=jnp.float32
    )


def swish_slope(value):
    sigmoid_value = jax.nn.sigmoid(value)
    return sigmoid_value * (1.0 + value * (1.0 - sigmoid_value))


def ffn_forward(resid, gain, w_in, w_out):
    normed_low = norm_rows(resid, gain).astype(jnp.bfloat16)
    hidden = matmul(normed_low, w_in)
    active_low = jax.nn.silu(hidden).astype(jnp.bfloat16)
    return (resid + 0.5 * matmul(active_low, w_out), (normed_low, hidden, active_low))


def ffn_backward(resid, gain, w_in, w_out, saved, grad_out):
    normed_low, hidden, active_low = saved
    grad_branch = (0.5 * grad_out).astype(jnp.bfloat16)
    grad_w_out = contract_rows(active_low, grad_branch)
    grad_hidden = (contract_cols(grad_branch, w_out) * swish_slope(hidden)).astype(jnp.bfloat16)
    grad_w_in = contract_rows(normed_low, grad_hidden)
    grad_normed = contract_cols(grad_hidden, w_in)
    grad_resid, grad_gain = norm_back(resid, gain, grad_normed)
    return (grad_out + grad_resid, grad_gain, grad_w_in, grad_w_out)


def attend_forward(resid, gain, w_joint, w_proj, key_bias):
    rows, width = resid.shape
    utts = key_bias.shape[0]
    head_dim = width // HEADS
    normed_low = norm_rows(resid, gain).astype(jnp.bfloat16)
    joint_low = (
        matmul(normed_low, w_joint)
        .astype(jnp.bfloat16)
        .reshape(utts, rows // utts, 3, HEADS, head_dim)
    )
    scores = (
        jnp.einsum(
            "uqhe,ukhe->uhqk",
            joint_low[:, :, 0],
            joint_low[:, :, 1],
            preferred_element_type=jnp.float32,
        )
        * head_dim ** (-0.5)
        + key_bias
    )
    weights = jax.nn.softmax(scores, axis=-1)
    weights_low = weights.astype(jnp.bfloat16)
    context = jnp.einsum(
        "uhqk,ukhe->uqhe", weights_low, joint_low[:, :, 2], preferred_element_type=jnp.float32
    )
    context_low = context.reshape(rows, width).astype(jnp.bfloat16)
    return (
        resid + matmul(context_low, w_proj),
        (normed_low, joint_low, weights, weights_low, context_low),
    )


def attend_backward(resid, gain, w_joint, w_proj, saved, grad_out):
    normed_low, joint_low, weights, weights_low, context_low = saved
    rows, width = resid.shape
    utts, frames, three, heads, head_dim = joint_low.shape
    scale = head_dim ** (-0.5)
    query, key, value = (joint_low[:, :, 0], joint_low[:, :, 1], joint_low[:, :, 2])
    grad_branch = grad_out.astype(jnp.bfloat16)
    grad_proj = contract_rows(context_low, grad_branch)
    grad_context = (
        contract_cols(grad_branch, w_proj)
        .astype(jnp.bfloat16)
        .reshape(utts, frames, heads, head_dim)
    )
    grad_weights = jnp.einsum(
        "uqhe,ukhe->uhqk", grad_context, value, preferred_element_type=jnp.float32
    )
    grad_value = jnp.einsum(
        "uhqk,uqhe->ukhe", weights_low, grad_context, preferred_element_type=jnp.float32
    )
    grad_scores = (
        weights * (grad_weights - jnp.sum(grad_weights * weights, -1, keepdims=True))
    ).astype(jnp.bfloat16)
    grad_query = (
        jnp.einsum("uhqk,ukhe->uqhe", grad_scores, key, preferred_element_type=jnp.float32) * scale
    )
    grad_key = (
        jnp.einsum("uhqk,uqhe->ukhe", grad_scores, query, preferred_element_type=jnp.float32)
        * scale
    )
    grad_joint = (
        jnp.stack([grad_query, grad_key, grad_value], 2)
        .reshape(rows, 3 * width)
        .astype(jnp.bfloat16)
    )
    grad_w_joint = contract_rows(normed_low, grad_joint)
    grad_normed = contract_cols(grad_joint, w_joint)
    grad_resid, grad_gain = norm_back(resid, gain, grad_normed)
    return (grad_out + grad_resid, grad_gain, grad_w_joint, grad_proj)


def conv_inner(projected, depth, valid_rows, utts):
    rows, double = projected.shape
    width = double // 2
    frames = rows // utts
    taps = depth.shape[0]
    gated = projected[:, :width] * jax.nn.sigmoid(projected[:, width:]) * valid_rows
    padded = jnp.pad(gated.reshape(utts, frames, width), ((0, 0), (taps // 2, taps // 2), (0, 0)))
    total = padded[:, 0:frames] * depth[0]
    for tap in range(1, taps):
        total = total + padded[:, tap : tap + frames] * depth[tap]
    return total.reshape(rows, width)


def batch_stats(depthwise, valid_rows):
    total, count = lax.psum(
        (jnp.sum(depthwise * valid_rows, 0), jnp.sum(valid_rows)), ("dp", "fsdp")
    )
    centre = total / count
    centred = depthwise - centre
    spread = lax.psum(jnp.sum(valid_rows * centred * centred, 0), ("dp", "fsdp")) / count
    return (centre, lax.rsqrt(spread + EPS), count)


def run_layer(resid, weights, valid_rows, key_bias):
    gains, f_in, f_out, w_joint, w_proj, p_in, depth, bn_gain, bn_bias, p_out, s_in, s_out = weights
    gains = gains.astype(jnp.float32)
    utts = key_bias.shape[0]
    first, saved_first = ffn_forward(resid, gains[0], f_in, f_out)
    second, saved_attend = attend_forward(first, gains[1], w_joint, w_proj, key_bias)
    normed_low = norm_rows(second, gains[2]).astype(jnp.bfloat16)
    projected = matmul(normed_low, p_in)
    depthwise = conv_inner(projected, depth.astype(jnp.float32), valid_rows, utts)
    centre, inv_std, count = batch_stats(depthwise, valid_rows)
    normalized = (depthwise - centre) * inv_std
    shifted = normalized * bn_gain.astype(jnp.float32) + bn_bias.astype(jnp.float32)
    active_low = jax.nn.silu(shifted).astype(jnp.bfloat16)
    third = second + matmul(active_low, p_out)
    fourth, saved_fourth = ffn_forward(third, gains[3], s_in, s_out)
    output = norm_rows(fourth, gains[4])
    record = (
        resid,
        first,
        second,
        third,
        fourth,
        saved_first,
        saved_attend,
        saved_fourth,
        normed_low,
        projected,
        normalized,
        shifted,
        active_low,
        inv_std,
        count,
    )
    return (output, record)


def layer_backward(weights, record, grad_out, valid_rows, key_bias):
    gains, f_in, f_out, w_joint, w_proj, p_in, depth, bn_gain, bn_bias, p_out, s_in, s_out = weights
    gains = gains.astype(jnp.float32)
    utts = key_bias.shape[0]
    (
        resid,
        first,
        second,
        third,
        fourth,
        saved_first,
        saved_attend,
        saved_fourth,
        normed_low,
        projected,
        normalized,
        shifted,
        active_low,
        inv_std,
        count,
    ) = record
    grad_fourth, grad_gain_four = norm_back(fourth, gains[4], grad_out)
    grad_third, grad_gain_three, grad_s_in, grad_s_out = ffn_backward(
        third, gains[3], s_in, s_out, saved_fourth, grad_fourth
    )
    grad_branch = grad_third.astype(jnp.bfloat16)
    grad_p_out = contract_rows(active_low, grad_branch)
    grad_shifted = contract_cols(grad_branch, p_out) * swish_slope(shifted)
    bias_sum, gain_sum = lax.psum(
        (jnp.sum(grad_shifted, 0), jnp.sum(grad_shifted * normalized, 0)), ("dp", "fsdp")
    )
    grad_depthwise = (
        bn_gain.astype(jnp.float32)
        * inv_std
        * (grad_shifted - valid_rows * (bias_sum + normalized * gain_sum) / count)
    )
    conv_local = partial(conv_inner, valid_rows=valid_rows, utts=utts)
    result, pullback = jax.vjp(conv_local, projected, depth.astype(jnp.float32))
    grad_projected, grad_depth = pullback(grad_depthwise)
    grad_projected_low = grad_projected.astype(jnp.bfloat16)
    grad_p_in = contract_rows(normed_low, grad_projected_low)
    grad_normed = contract_cols(grad_projected_low, p_in)
    grad_conv_resid, grad_gain_two = norm_back(second, gains[2], grad_normed)
    grad_second = grad_third + grad_conv_resid
    grad_first, grad_gain_one, grad_joint, grad_proj = attend_backward(
        first, gains[1], w_joint, w_proj, saved_attend, grad_second
    )
    grad_resid, grad_gain_zero, grad_f_in, grad_f_out = ffn_backward(
        resid, gains[0], f_in, f_out, saved_first, grad_first
    )
    grad_gains = jnp.stack(
        [grad_gain_zero, grad_gain_one, grad_gain_two, grad_gain_three, grad_gain_four]
    )
    return (
        grad_resid,
        (
            grad_gains,
            grad_f_in,
            grad_f_out,
            grad_joint,
            grad_proj,
            grad_p_in,
            grad_depth,
            gain_sum,
            bias_sum,
            grad_p_out,
            grad_s_in,
            grad_s_out,
        ),
    )


def reduce_grads(stacked, joint_grads):
    shares = (
        lax.psum_scatter(
            stacked[0].astype(jnp.bfloat16), "fsdp", scatter_dimension=1, tiled=True
        ).astype(jnp.float32),
        lax.psum_scatter(
            stacked[1].astype(jnp.bfloat16), "fsdp", scatter_dimension=1, tiled=True
        ).astype(jnp.float32),
        lax.psum_scatter(
            stacked[2].astype(jnp.bfloat16), "fsdp", scatter_dimension=1, tiled=True
        ).astype(jnp.float32),
        lax.psum_scatter(
            stacked[3].astype(jnp.bfloat16), "fsdp", scatter_dimension=1, tiled=True
        ).astype(jnp.float32),
        lax.psum_scatter(
            stacked[4].astype(jnp.bfloat16), "fsdp", scatter_dimension=1, tiled=True
        ).astype(jnp.float32),
        lax.psum_scatter(
            stacked[5].astype(jnp.bfloat16), "fsdp", scatter_dimension=1, tiled=True
        ).astype(jnp.float32),
        lax.psum_scatter(
            stacked[6].astype(jnp.bfloat16), "fsdp", scatter_dimension=1, tiled=True
        ).astype(jnp.float32),
        lax.psum_scatter(
            stacked[7].astype(jnp.bfloat16), "fsdp", scatter_dimension=1, tiled=True
        ).astype(jnp.float32),
        lax.psum_scatter(
            stacked[8].astype(jnp.bfloat16), "fsdp", scatter_dimension=1, tiled=True
        ).astype(jnp.float32),
        lax.psum_scatter(
            stacked[9].astype(jnp.bfloat16), "fsdp", scatter_dimension=1, tiled=True
        ).astype(jnp.float32),
        lax.psum_scatter(
            joint_grads[0].astype(jnp.bfloat16), "fsdp", scatter_dimension=0, tiled=True
        ).astype(jnp.float32),
        lax.psum_scatter(
            joint_grads[1].astype(jnp.bfloat16), "fsdp", scatter_dimension=0, tiled=True
        ).astype(jnp.float32),
        lax.psum_scatter(
            joint_grads[2].astype(jnp.bfloat16), "fsdp", scatter_dimension=0, tiled=True
        ).astype(jnp.float32),
        lax.psum_scatter(
            joint_grads[3].astype(jnp.bfloat16), "fsdp", scatter_dimension=0, tiled=True
        ).astype(jnp.float32),
    )
    return (
        lax.psum(shares[0].astype(jnp.bfloat16), "dp").astype(jnp.float32),
        lax.psum(shares[1].astype(jnp.bfloat16), "dp").astype(jnp.float32),
        lax.psum(shares[2].astype(jnp.bfloat16), "dp").astype(jnp.float32),
        lax.psum(shares[3].astype(jnp.bfloat16), "dp").astype(jnp.float32),
        lax.psum(shares[4].astype(jnp.bfloat16), "dp").astype(jnp.float32),
        lax.psum(shares[5].astype(jnp.bfloat16), "dp").astype(jnp.float32),
        lax.psum(shares[6].astype(jnp.bfloat16), "dp").astype(jnp.float32),
        lax.psum(shares[7].astype(jnp.bfloat16), "dp").astype(jnp.float32),
        lax.psum(shares[8].astype(jnp.bfloat16), "dp").astype(jnp.float32),
        lax.psum(shares[9].astype(jnp.bfloat16), "dp").astype(jnp.float32),
        lax.psum(shares[10].astype(jnp.bfloat16), "dp").astype(jnp.float32),
        lax.psum(shares[11].astype(jnp.bfloat16), "dp").astype(jnp.float32),
        lax.psum(shares[12].astype(jnp.bfloat16), "dp").astype(jnp.float32),
        lax.psum(shares[13].astype(jnp.bfloat16), "dp").astype(jnp.float32),
    )


def local(
    frames_in,
    frame_lengths,
    label_ids,
    label_lengths,
    pred_states,
    norm_gains,
    first_in,
    first_out,
    attend_joint,
    attend_out,
    point_in,
    depth_taps,
    batch_gain,
    batch_bias,
    point_out,
    second_in,
    second_out,
    enc_weight,
    pred_weight,
    token_weight,
    duration_weight,
):
    utts, frames, width = frames_in.shape
    slots = pred_states.shape[1]
    rows = utts * frames
    positions = lax.broadcasted_iota(jnp.int32, (utts, frames), 1)
    valid = (positions < frame_lengths[:, None]).astype(jnp.float32)
    valid_rows = valid.reshape(rows, 1)
    key_bias = ((1.0 - valid) * MASKED)[:, None, None, :]
    layers = norm_gains.shape[0]
    resid = frames_in.reshape(rows, width).astype(jnp.float32)
    records = []
    for layer in range(layers):
        weights = (
            lax.all_gather(norm_gains[layer], "fsdp", axis=1, tiled=True),
            lax.all_gather(first_in[layer], "fsdp", axis=0, tiled=True),
            lax.all_gather(first_out[layer], "fsdp", axis=0, tiled=True),
            lax.all_gather(attend_joint[layer], "fsdp", axis=0, tiled=True),
            lax.all_gather(attend_out[layer], "fsdp", axis=0, tiled=True),
            lax.all_gather(point_in[layer], "fsdp", axis=0, tiled=True),
            lax.all_gather(depth_taps[layer], "fsdp", axis=1, tiled=True),
            lax.all_gather(batch_gain[layer], "fsdp", axis=0, tiled=True),
            lax.all_gather(batch_bias[layer], "fsdp", axis=0, tiled=True),
            lax.all_gather(point_out[layer], "fsdp", axis=0, tiled=True),
            lax.all_gather(second_in[layer], "fsdp", axis=0, tiled=True),
            lax.all_gather(second_out[layer], "fsdp", axis=0, tiled=True),
        )
        resid, record = run_layer(resid, weights, valid_rows, key_bias)
        kept = None
        records.append((kept, record))
    w_enc, w_pred, w_tok, w_dur = (
        lax.all_gather(enc_weight, "fsdp", axis=0, tiled=True),
        lax.all_gather(pred_weight, "fsdp", axis=0, tiled=True),
        lax.all_gather(token_weight, "fsdp", axis=0, tiled=True),
        lax.all_gather(duration_weight, "fsdp", axis=0, tiled=True),
    )
    joint = w_enc.shape[1]
    vocab = w_tok.shape[1]
    out_low = resid.astype(jnp.bfloat16)
    enc = matmul(out_low, w_enc)
    pred_low = pred_states.reshape(utts * slots, joint)
    pred = matmul(pred_low, w_pred).reshape(utts, slots, joint)
    labels_ext = jnp.concatenate([label_ids, jnp.zeros((utts, 1), jnp.int32)], 1)
    span = min(frames, 32)
    blocks = frames // span
    enc_blocks = enc.reshape(utts * blocks, span, joint)
    indices = lax.iota(jnp.int32, utts * blocks)

    def scores_of(index):
        owner = index // blocks
        enc_block = lax.dynamic_index_in_dim(enc_blocks, index, 0, keepdims=False)
        pred_rows = lax.dynamic_index_in_dim(pred, owner, 0, keepdims=False)
        lab_row = lax.dynamic_index_in_dim(labels_ext, owner, 0, keepdims=False)
        squashed = jnp.tanh(enc_block[:, None, :] + pred_rows[None, :, :])
        hidden_low = squashed.astype(jnp.bfloat16).reshape(span * slots, joint)
        tok = matmul(hidden_low, w_tok).reshape(span, slots, vocab)
        durl = matmul(hidden_low, w_dur).reshape(span, slots, -1)
        total = log_total(tok, -1)
        picked = lax.broadcasted_iota(jnp.int32, tok.shape, 2) == lab_row[None, :, None]
        return (squashed, hidden_low, tok, durl, total, picked)

    def forward_block(index):
        squashed, hidden_low, tok, durl, total, picked = scores_of(index)
        blank = tok[..., 0] - total
        label = jnp.sum(jnp.where(picked, tok, 0.0), -1) - total
        dur = durl - log_total(durl, -1)[..., None]
        return (blank, label, dur)

    blank, label, dur = lax.map(forward_block, indices)
    blank = blank.reshape(utts, frames, slots)
    label = label.reshape(utts, frames, slots)
    dur = dur.reshape(utts, frames, slots, -1)
    lattice_local = partial(lattice, t_len=frame_lengths, u_len=label_lengths)
    log_prob, pullback = jax.vjp(lattice_local, blank, label, dur)
    utt_loss = -log_prob / frame_lengths.astype(jnp.float32)
    grad_blank, grad_label, grad_dur = pullback(-jnp.ones_like(log_prob))
    grad_blank = grad_blank.reshape(utts * blocks, span, slots)
    grad_label = grad_label.reshape(utts * blocks, span, slots)
    grad_dur = grad_dur.reshape(utts * blocks, span, slots, -1)

    def backward_block(carry, index):
        acc_tok, acc_dur, acc_pred = carry
        squashed, hidden_low, tok, durl, total, picked = scores_of(index)
        g_blank = lax.dynamic_index_in_dim(grad_blank, index, 0, keepdims=False)
        g_label = lax.dynamic_index_in_dim(grad_label, index, 0, keepdims=False)
        g_dur = lax.dynamic_index_in_dim(grad_dur, index, 0, keepdims=False)
        prob = jnp.exp(tok - total[..., None])
        first_col = lax.broadcasted_iota(jnp.int32, tok.shape, 2) == 0
        d_tok = (
            jnp.where(first_col, g_blank[..., None], 0.0)
            + jnp.where(picked, g_label[..., None], 0.0)
            - (g_blank + g_label)[..., None] * prob
        )
        d_tok_low = d_tok.astype(jnp.bfloat16).reshape(span * slots, vocab)
        dur_prob = jnp.exp(durl - log_total(durl, -1)[..., None])
        d_dur_low = (
            (g_dur - jnp.sum(g_dur, -1, keepdims=True) * dur_prob)
            .astype(jnp.bfloat16)
            .reshape(span * slots, -1)
        )
        acc_tok = acc_tok + contract_rows(hidden_low, d_tok_low)
        acc_dur = acc_dur + contract_rows(hidden_low, d_dur_low)
        d_hidden = contract_cols(d_tok_low, w_tok) + contract_cols(d_dur_low, w_dur)
        d_pre = d_hidden.reshape(span, slots, joint) * (1.0 - squashed * squashed)
        owner = index // blocks
        pred_row = lax.dynamic_index_in_dim(acc_pred, owner, 0, keepdims=False) + jnp.sum(d_pre, 0)
        acc_pred = lax.dynamic_update_index_in_dim(acc_pred, pred_row, owner, 0)
        return ((acc_tok, acc_dur, acc_pred), jnp.sum(d_pre, 1))

    start_carry = (
        jnp.zeros((joint, vocab), jnp.float32),
        jnp.zeros((joint, w_dur.shape[1]), jnp.float32),
        jnp.zeros((utts, slots, joint), jnp.float32),
    )
    carried, grad_enc_blocks = lax.scan(backward_block, start_carry, indices)
    grad_tok, grad_dur_w, grad_pred_rows = carried
    grad_enc_low = grad_enc_blocks.reshape(rows, joint).astype(jnp.bfloat16)
    grad_w_enc = contract_rows(out_low, grad_enc_low)
    grad = contract_cols(grad_enc_low, w_enc)
    grad_w_pred = contract_rows(
        pred_low, grad_pred_rows.reshape(utts * slots, joint).astype(jnp.bfloat16)
    )
    shard = width // lax.axis_size("fsdp")
    offset = lax.axis_index("fsdp") * shard
    collected = [None] * layers
    for layer in reversed(range(layers)):
        kept, record = records[layer]
        weights = (
            lax.all_gather(norm_gains[layer], "fsdp", axis=1, tiled=True),
            lax.all_gather(first_in[layer], "fsdp", axis=0, tiled=True),
            lax.all_gather(first_out[layer], "fsdp", axis=0, tiled=True),
            lax.all_gather(attend_joint[layer], "fsdp", axis=0, tiled=True),
            lax.all_gather(attend_out[layer], "fsdp", axis=0, tiled=True),
            lax.all_gather(point_in[layer], "fsdp", axis=0, tiled=True),
            lax.all_gather(depth_taps[layer], "fsdp", axis=1, tiled=True),
            lax.all_gather(batch_gain[layer], "fsdp", axis=0, tiled=True),
            lax.all_gather(batch_bias[layer], "fsdp", axis=0, tiled=True),
            lax.all_gather(point_out[layer], "fsdp", axis=0, tiled=True),
            lax.all_gather(second_in[layer], "fsdp", axis=0, tiled=True),
            lax.all_gather(second_out[layer], "fsdp", axis=0, tiled=True),
        )
        grad, grads = layer_backward(weights, record, grad, valid_rows, key_bias)
        collected[layer] = grads

    def stack_member(member):
        return jnp.stack([collected[layer][member] for layer in range(layers)])

    stacked = (
        jnp.swapaxes(stack_member(0), 1, 2),
        stack_member(1),
        stack_member(2),
        stack_member(3),
        stack_member(4),
        stack_member(5),
        jnp.swapaxes(stack_member(6), 1, 2),
        stack_member(9),
        stack_member(10),
        stack_member(11),
    )
    summed = reduce_grads(stacked, (grad_w_enc, grad_w_pred, grad_tok, grad_dur_w))
    gain_piece = lax.dynamic_slice_in_dim(stack_member(7), offset, shard, 1)
    bias_piece = lax.dynamic_slice_in_dim(stack_member(8), offset, shard, 1)
    grad_frames = grad.reshape(utts, frames, width)
    return (
        utt_loss,
        grad_frames,
        jnp.swapaxes(summed[0], 1, 2),
        summed[1],
        summed[2],
        summed[3],
        summed[4],
        summed[5],
        jnp.swapaxes(summed[6], 1, 2),
        gain_piece,
        bias_piece,
        summed[7],
        summed[8],
        summed[9],
        summed[10],
        summed[11],
        summed[12],
        summed[13],
    )


def solution(mesh):
    placed = (
        P(("dp", "fsdp"), None, None),
        P(("dp", "fsdp")),
        P(("dp", "fsdp"), None),
        P(("dp", "fsdp")),
        P(("dp", "fsdp"), None, None),
        P(None, None, "fsdp"),
        P(None, "fsdp", None),
        P(None, "fsdp", None),
        P(None, "fsdp", None),
        P(None, "fsdp", None),
        P(None, "fsdp", None),
        P(None, None, "fsdp"),
        P(None, "fsdp"),
        P(None, "fsdp"),
        P(None, "fsdp", None),
        P(None, "fsdp", None),
        P(None, "fsdp", None),
        P("fsdp", None),
        P("fsdp", None),
        P("fsdp", None),
        P("fsdp", None),
    )
    return jax.shard_map(
        local,
        mesh=mesh,
        in_specs=placed,
        out_specs=(
            P(("dp", "fsdp")),
            P(("dp", "fsdp"), None, None),
            P(None, None, "fsdp"),
            P(None, "fsdp", None),
            P(None, "fsdp", None),
            P(None, "fsdp", None),
            P(None, "fsdp", None),
            P(None, "fsdp", None),
            P(None, None, "fsdp"),
            P(None, "fsdp"),
            P(None, "fsdp"),
            P(None, "fsdp", None),
            P(None, "fsdp", None),
            P(None, "fsdp", None),
            P("fsdp", None),
            P("fsdp", None),
            P("fsdp", None),
            P("fsdp", None),
        ),
        check_vma=False,
    )
```

profile of v0, /device:TPU:0, one launch (start us, length us, event | category | flops | bytes accessed | tf_op | source)
XLA Modules:
  0.0 6848.4 jit_solution(3205326821295859300)
XLA Ops:
  21.2 33.4 all-gather
  54.8 9.6 slice_reduce_fusion.15
  65.0 33.8 all-gather.4
  99.0 31.9 all-gather.6
  131.2 15.7 slice_reduce_fusion.25
  149.2 21.6 all-reduce.76
  171.9 33.6 all-gather.9
  205.7 31.2 all-gather.12
  237.2 9.7 slice_reduce_fusion.1
  246.9 34.4 all-gather.16
  281.4 31.7 all-gather.18
  313.5 16.4 slice_reduce_fusion.11
  331.0 34.9 all-gather.21
  365.9 34.6 all_gather.130
  400.5 33.3 all_gather.131
  433.7 26.1 all-gather.24
  460.6 5.1 fusion.164
  474.5 4.4 reshape.1323
  497.4 38.7 all-reduce.75
  537.0 41.9 psum.166
  582.7 6.0 multiply_convert_fusion.8
  593.8 5.1 fusion.150
  633.0 40.5 psum.167
  674.4 40.3 psum.168
  718.4 5.3 multiply_convert_fusion.6
  730.5 232.6 %while.107 = (s32[]{:T(128)}, f32[16,32,25]{1,0,2:T(8,128)S(1)}, f32[16,32,25]{1,0,2:T(8,128)}, f32[16,32,25,5]{1,0,3,2:T(8,128)S(1)}, s32[16]{0:T(128)S(1)}, /*...) while((s32[]{:T(128)}, f32[16,32,25]{1,0,2:T(8,128)S(1)}, ...), condition=%wide.region_40.41_spmd, body=%wide.region_34.40_spmd.sunk | while | flops 1060674432 | bytes 8663102 | solution.py:469
  981.7 2186.8 %while.108 = (s32[]{:T(128)}, f32[2,4,25]{2,0,1:T(2,128)S(1)}, f32[256,2,25]{2,1,0:T(2,128)}, f32[256,2,25,25]{3,1,2,0:T(2,128)}, f32[256,2,25]{2,1,0:T(2,128)},...) while((s32[]{:T(128)}, f32[2,4,25]{2,0,1:T(2,128)S(1)}, ...), condition=%wide.region_46.47_spmd.clone.clone, body=%wide.region_41.46_spmd.clone.clone.sunk | while | flops 25252 | bytes 116941 | solution.py:51
  3177.0 1927.9 %while.109 = (s32[]{:T(128)}, f32[2,4,25]{2,0,1:T(2,128)S(1)}, f32[256,2,25]{2,1,0:T(2,128)S(1)}, f32[256,2,25]{2,1,0:T(2,128)}, f32[256,2,25,5]{2,1,3,0:T(2,128...) while((s32[]{:T(128)}, f32[2,4,25]{2,0,1:T(2,128)S(1)}, ...), condition=%wide.region_58.59_spmd.clone, body=%wide.region_54.58_spmd.clone.sunk | while | flops 15454 | bytes 61272 | solution.py:51
  5111.5 515.0 %while.110 = (s32[]{:T(128)}, f32[640,1024]{1,0:T(8,128)}, f32[640,5]{0,1:T(8,128)S(1)}, f32[2,25,640]{2,1,0:T(8,128)S(1)}, bf16[16,32,640]{2,1,0:T(8,128)(2,1)}...) while((s32[]{:T(128)}, f32[640,1024]{1,0:T(8,128)}, ...), condition=%wide.region_67.68_spmd.clone, body=%wide.region_59.67_spmd.clone.sunk | while | flops 3179107328 | bytes 62266752 | solution.py:515
  5137.7 4.8 bitcast_add_fusion.17
  5169.1 5.6 bitcast_add_fusion.17
  5201.4 5.6 bitcast_add_fusion.17
  5233.6 5.6 bitcast_add_fusion.17
  5265.8 5.6 bitcast_add_fusion.17
  5298.1 5.6 bitcast_add_fusion.17
  5330.3 5.6 bitcast_add_fusion.17
  5362.5 5.6 bitcast_add_fusion.17
  5394.8 5.6 bitcast_add_fusion.17
  5427.0 5.6 bitcast_add_fusion.17
  5459.2 5.6 bitcast_add_fusion.17
  5491.5 5.6 bitcast_add_fusion.17
  5523.7 5.6 bitcast_add_fusion.17
  5555.9 5.6 bitcast_add_fusion.17
  5588.2 5.6 bitcast_add_fusion.17
  5620.4 5.6 bitcast_add_fusion.17
  5631.2 4.4 multiply_convert_fusion.5
  5643.6 40.2 all-reduce.74
  5737.6 40.2 all-reduce.73
  5867.9 4.7 multiply_convert_fusion
  5886.3 5.7 multiply_reduce_fusion.19
  5897.3 22.8 reduce-scatter.33.cloned.1.call-done
  5920.1 66.7 reduce-scatter.29.cloned.1.call-done
  5986.8 66.6 reduce-scatter.41.cloned.1.call-done
  6053.4 70.0 %reduce-scatter.31.cloned.1.call-done = bf16[2,64,1024]{2,1,0:T(8,128)(2,1)} async-done(((bf16[2,512,1024]{2,1,0:T(8,128)(2,1)}), bf16[2,64,1024]{2,1,0:T(8,128)(2,1)}) %reduce-scatter.31.cloned.1.call-update) | async-done | bytes 262160 | tf_op jit(solution)/shard_map/reduce_scatter | solution.py:334
  6123.4 77.0 %reduce-scatter.27.cloned.1.call-done = bf16[2,64,1536]{2,1,0:T(8,128)(2,1)} async-done(((bf16[2,512,1536]{2,1,0:T(8,128)(2,1)}), bf16[2,64,1536]{2,1,0:T(8,128)(2,1)}) %reduce-scatter.27.cloned.1.call-update) | async-done | bytes 393232 | tf_op jit(solution)/shard_map/reduce_scatter | solution.py:328
  6200.4 90.9 %reduce-scatter.37.cloned.1.call-done = bf16[2,256,512]{2,1,0:T(8,128)(2,1)} async-done(((bf16[2,2048,512]{2,1,0:T(8,128)(2,1)}), bf16[2,256,512]{2,1,0:T(8,128)(2,1)}) %reduce-scatter.37.cloned.1.call-update) | async-done | bytes 524304 | tf_op jit(solution)/shard_map/reduce_scatter | solution.py:346
  6291.3 91.9 %reduce-scatter.35.cloned.1.call-done = bf16[2,64,2048]{2,1,0:T(8,128)(2,1)} async-done(((bf16[2,512,2048]{2,1,0:T(8,128)(2,1)}), bf16[2,64,2048]{2,1,0:T(8,128)(2,1)}) %reduce-scatter.35.cloned.1.call-update) | async-done | bytes 524304 | tf_op jit(solution)/shard_map/reduce_scatter | solution.py:343
  6383.2 91.3 %reduce-scatter.25.cloned.1.call-done = bf16[2,256,512]{2,1,0:T(8,128)(2,1)} async-done(((bf16[2,2048,512]{2,1,0:T(8,128)(2,1)}), bf16[2,256,512]{2,1,0:T(8,128)(2,1)}) %reduce-scatter.25.cloned.1.call-update) | async-done | bytes 524304 | tf_op jit(solution)/shard_map/reduce_scatter | solution.py:325
  6474.6 91.6 %reduce-scatter.23.cloned.1.call-done = bf16[2,64,2048]{2,1,0:T(8,128)(2,1)} async-done(((bf16[2,512,2048]{2,1,0:T(8,128)(2,1)}), bf16[2,64,2048]{2,1,0:T(8,128)(2,1)}) %reduce-scatter.23.cloned.1.call-update) | async-done | bytes 524304 | tf_op jit(solution)/shard_map/reduce_scatter | solution.py:322
  6568.9 55.1 reduce-scatter.49.cloned.1.call-done
  6624.8 62.9 reduce-scatter.43.cloned.1.call-done
  6688.6 62.8 reduce-scatter.45.cloned.1.call-done
  6752.3 10.2 all-reduce.77
  6764.2 64.9 all-reduce.81.cloned.1.call-done
  (12311 shorter events, 4955.3 us)
Async XLA Ops:
  7.2 453.3 %all-gather.41.cloned.1.call-start = ((), (), s32[]{:S(2)}) async-start(), calls=%async_computation.25 | async-start | bytes 2359296 | tf_op jit(solution)/shard_map/all_gather | solution.py:416
  9.3 456.4 %all-gather.43.cloned.1.call-start = ((), (), s32[]{:S(2)}) async-start(), calls=%async_computation.26 | async-start | bytes 2359296 | tf_op jit(solution)/shard_map/all_gather | solution.py:417
  11.2 459.0 %all-gather.45.cloned.1.call-start = ((), (), s32[]{:S(2)}) async-start(), calls=%async_computation.27 | async-start | bytes 1769472 | tf_op jit(solution)/shard_map/all_gather | solution.py:418
  12.1 479.5 %all-gather.47.cloned.1.call-start = ((), (), s32[]{:S(2)}) async-start(), calls=%async_computation.28 | async-start | bytes 1179648 | tf_op jit(solution)/shard_map/all_gather | solution.py:420
  12.9 569.8 %all-gather.49.cloned.1.call-start = ((), (), s32[]{:S(2)}) async-start(), calls=%async_computation.29 | async-start | bytes 2359296 | tf_op jit(solution)/shard_map/all_gather | solution.py:425
  13.8 575.0 %all-gather.51.cloned.1.call-start = ((), (), s32[]{:S(2)}) async-start(), calls=%async_computation.30 | async-start | bytes 2359296 | tf_op jit(solution)/shard_map/all_gather | solution.py:426
  14.7 579.0 %all-gather.53.cloned.1.call-start = ((), (), s32[]{:S(2)}) async-start(), calls=%async_computation.31 | async-start | bytes 2359296 | tf_op jit(solution)/shard_map/all_gather | solution.py:416
  15.5 583.4 %all-gather.55.cloned.1.call-start = ((), (), s32[]{:S(2)}) async-start(), calls=%async_computation.32 | async-start | bytes 2359296 | tf_op jit(solution)/shard_map/all_gather | solution.py:417
  16.2 587.3 %all-gather.57.cloned.1.call-start = ((), (), s32[]{:S(2)}) async-start(), calls=%async_computation.33 | async-start | bytes 1769472 | tf_op jit(solution)/shard_map/all_gather | solution.py:418
  17.0 609.4 %all-gather.59.cloned.1.call-start = ((), (), s32[]{:S(2)}) async-start(), calls=%async_computation.34 | async-start | bytes 1179648 | tf_op jit(solution)/shard_map/all_gather | solution.py:420
  17.6 700.9 %all-gather.61.cloned.1.call-start = ((), (), s32[]{:S(2)}) async-start(), calls=%async_computation.35 | async-start | bytes 2359296 | tf_op jit(solution)/shard_map/all_gather | solution.py:425
  18.3 705.5 %all-gather.63.cloned.1.call-start = ((), (), s32[]{:S(2)}) async-start(), calls=%async_computation.36 | async-start | bytes 2359296 | tf_op jit(solution)/shard_map/all_gather | solution.py:426
  18.9 711.6 %all-gather.39.cloned.1.call-start = ((), (), s32[]{:S(2)}) async-start(), calls=%async_computation.14 | async-start | bytes 1474560 | tf_op jit(solution)/shard_map/all_gather | solution.py:434
  19.6 5876.0 %reduce-scatter.47.cloned.1.call-start = ((), (), s32[]{:S(2)}) async-start(), calls=%async_computation.39 | async-start | bytes 921600
  64.4 395.9 %copy-start.157 = (f32[512]{0:T(512)}, f32[512]{0:T(512)S(1)}, u32[]{:S(2)}) copy-start(f32[512]{0:T(512)S(1)} %get-tuple-element.1680) | copy-start | bytes 6148
  64.4 405.9 %copy-start.246 = (f32[512]{0:T(512)}, f32[512]{0:T(512)S(1)}, u32[]{:S(2)}) copy-start(f32[512]{0:T(512)S(1)} %get-tuple-element.1679) | copy-start | bytes 6148
  64.4 427.2 %copy-start.198 = (f32[512]{0:T(512)}, f32[512]{0:T(512)S(1)}, u32[]{:S(2)}) copy-start(f32[512]{0:T(512)S(1)} %get-tuple-element.1678) | copy-start | bytes 6148
  64.4 534.5 %copy-start.140 = (f32[512]{0:T(512)}, f32[512]{0:T(512)S(1)}, u32[]{:S(2)}) copy-start(f32[512]{0:T(512)S(1)} %get-tuple-element.1676) | copy-start | bytes 6148
  64.9 82.2 %copy-start.271 = (u32[32]{0:T(128)S(1)}, u32[32]{0:T(128)}, u32[]{:S(2)}) copy-start(u32[32]{0:T(128)} %constant.551) | copy-start | bytes 388
  64.9 107.0 %copy-start.139 = (bf16[2,64,512]{2,1,0:T(8,128)(2,1)S(1)}, bf16[2,64,512]{2,1,0:T(8,128)(2,1)}, u32[]{:S(2)}) copy-start(bf16[2,64,512]{2,1,0:T(8,128)(2,1)} %param.43) | copy-start | bytes 393220
  64.9 107.0 %copy-start.195 = (f32[1,2,2,128]{3,1,2,0:T(2,128)}, f32[1,2,2,128]{3,1,2,0:T(2,128)S(1)}, u32[]{:S(2)}) copy-start(f32[1,2,2,128]{3,1,2,0:T(2,128)S(1)} %copy.436) | copy-start | bytes 6148
  65.0 395.3 %copy-start.159 = (f32[512]{0:T(512)}, f32[512]{0:T(512)S(1)}, u32[]{:S(2)}) copy-start(f32[512]{0:T(512)S(1)} %rsqrt.116) | copy-start | bytes 6148
  65.0 395.3 %copy-start.161 = (f32[1,2,2,128]{3,1,2,0:T(2,128)}, f32[1,2,2,128]{3,1,2,0:T(2,128)S(1)}, u32[]{:S(2)}) copy-start(f32[1,2,2,128]{3,1,2,0:T(2,128)S(1)} %copy.435) | copy-start | bytes 6148
  98.8 529.6 %copy-start.145 = (f32[1,2,2,128]{3,1,2,0:T(2,128)}, f32[1,2,2,128]{3,1,2,0:T(2,128)S(1)}, u32[]{:S(2)}) copy-start(f32[1,2,2,128]{3,1,2,0:T(2,128)S(1)} %copy.438) | copy-start | bytes 6148
  146.9 348.4 %copy-start.218 = (f32[512]{0:T(512)}, f32[512]{0:T(512)S(1)}, u32[]{:S(2)}) copy-start(f32[512]{0:T(512)S(1)} %get-tuple-element.1681) | copy-start | bytes 6148
  146.9 348.4 %copy-start.220 = (f32[512]{0:T(512)}, f32[512]{0:T(512)S(1)}, u32[]{:S(2)}) copy-start(f32[512]{0:T(512)S(1)} %get-tuple-element.1682) | copy-start | bytes 6148
  146.9 348.4 %copy-start.222 = (f32[512]{0:T(512)}, f32[512]{0:T(512)S(1)}, u32[]{:S(2)}) copy-start(f32[512]{0:T(512)S(1)} %get-tuple-element.1683) | copy-start | bytes 6148
  147.0 348.4 %copy-start.224 = (f32[512]{0:T(512)}, f32[512]{0:T(512)S(1)}, u32[]{:S(2)}) copy-start(f32[512]{0:T(512)S(1)} %get-tuple-element.1684) | copy-start | bytes 6148
  147.0 348.4 %copy-start.226 = (f32[512]{0:T(512)}, f32[512]{0:T(512)S(1)}, u32[]{:S(2)}) copy-start(f32[512]{0:T(512)S(1)} %get-tuple-element.1685) | copy-start | bytes 6148
  147.0 348.4 %copy-start.228 = (f32[512]{0:T(512)}, f32[512]{0:T(512)S(1)}, u32[]{:S(2)}) copy-start(f32[512]{0:T(512)S(1)} %get-tuple-element.1686) | copy-start | bytes 6148
  147.0 348.4 %copy-start.230 = (f32[512]{0:T(512)}, f32[512]{0:T(512)S(1)}, u32[]{:S(2)}) copy-start(f32[512]{0:T(512)S(1)} %get-tuple-element.1687) | copy-start | bytes 6148
  147.0 348.4 %copy-start.232 = (f32[512]{0:T(512)}, f32[512]{0:T(512)S(1)}, u32[]{:S(2)}) copy-start(f32[512]{0:T(512)S(1)} %get-tuple-element.1688) | copy-start | bytes 6148
  147.0 348.4 %copy-start.234 = (f32[512]{0:T(512)}, f32[512]{0:T(512)S(1)}, u32[]{:S(2)}) copy-start(f32[512]{0:T(512)S(1)} %get-tuple-element.1689) | copy-start | bytes 6148
  246.9 346.9 %copy-start.155 = (f32[512]{0:T(512)}, f32[512]{0:T(512)S(1)}, u32[]{:S(2)}) copy-start(f32[512]{0:T(512)S(1)} %get-tuple-element.1666) | copy-start | bytes 6148
  246.9 119.0 %copy-start.150 = (bf16[64,640]{1,0:T(8,128)(2,1)S(1)}, bf16[64,640]{1,0:T(8,128)(2,1)}, u32[]{:S(2)}) copy-start(bf16[64,640]{1,0:T(8,128)(2,1)} %param.46) | copy-start | bytes 245764
  313.1 87.3 %copy-start.144 = (bf16[80,640]{1,0:T(8,128)(2,1)S(1)}, bf16[80,640]{1,0:T(8,128)(2,1)}, u32[]{:S(2)}) copy-start(bf16[80,640]{1,0:T(8,128)(2,1)} %param.47) | copy-start | bytes 307204
  313.4 120.3 %copy-start.256 = (bf16[80,5]{0,1:T(8,128)(2,1)S(1)}, bf16[80,5]{0,1:T(8,128)(2,1)}, u32[]{:S(2)}) copy-start(bf16[80,5]{0,1:T(8,128)(2,1)} %param.49) | copy-start | bytes 2404
  313.4 146.5 %copy-start.262 = (s32[2,24]{1,0:T(2,128)S(1)}, s32[2,24]{1,0:T(2,128)}, u32[]{:S(2)}) copy-start(s32[2,24]{1,0:T(2,128)} %param.31) | copy-start | bytes 580
  313.4 146.5 %copy-start.122 = (bf16[2,25,640]{2,0,1:T(2,128)(2,1)S(1)}, bf16[2,25,640]{2,0,1:T(2,128)(2,1)}, u32[]{:S(2)}) copy-start(bf16[2,25,640]{2,0,1:T(2,128)(2,1)} %param.33) | copy-start | bytes 192004
  491.3 89.0 %copy-start.13 = (f32[512,512]{1,0:T(8,128)}, f32[512,512]{1,0:T(8,128)S(1)}, u32[]{:S(2)}) copy-start(f32[512,512]{1,0:T(8,128)S(1)} %get-tuple-element.2036) | copy-start | bytes 3145732
  497.4 84.9 %copy-start.10 = (f32[2,256,512]{2,1,0:T(8,128)}, f32[2,256,512]{2,1,0:T(8,128)S(1)}, u32[]{:S(2)}) copy-start(f32[2,256,512]{2,1,0:T(8,128)S(1)} %get-tuple-element.1913) | copy-start | bytes 3145732
  626.0 90.0 %copy-start.16 = (f32[512,512]{1,0:T(8,128)}, f32[512,512]{1,0:T(8,128)S(1)}, u32[]{:S(2)}) copy-start(f32[512,512]{1,0:T(8,128)S(1)} %get-tuple-element.2048) | copy-start | bytes 3145732
  633.0 85.1 %copy-start.11 = (f32[2,256,512]{2,1,0:T(8,128)}, f32[2,256,512]{2,1,0:T(8,128)S(1)}, u32[]{:S(2)}) copy-start(f32[2,256,512]{2,1,0:T(8,128)S(1)} %get-tuple-element.1911) | copy-start | bytes 3145732
  977.1 2192.5 %copy-start.236 = (s32[2]{0:T(128)S(1)}, s32[2]{0:T(128)}, u32[]{:S(2)}) copy-start(s32[2]{0:T(128)} %param.32) | copy-start | bytes 28
  5111.5 515.0 %copy-start.171 = (f32[512]{0:T(512)S(1)}, f32[512]{0:T(512)}, u32[]{:S(2)}) copy-start(f32[512]{0:T(512)} %copy-done.170) | copy-start | bytes 6148
  5111.5 515.0 %copy-start.213 = (f32[512]{0:T(512)S(1)}, f32[512]{0:T(512)}, u32[]{:S(2)}) copy-start(f32[512]{0:T(512)} %copy-done.212) | copy-start | bytes 6148
  5732.0 165.3 %reduce-scatter.39.cloned.1.call-start = ((), (), s32[]{:S(2)}) async-start(), calls=%async_computation.23 | async-start | bytes 737280 | tf_op jit(solution)/shard_map/reduce_scatter | solution.py:349
  5783.2 136.9 %reduce-scatter.33.cloned.1.call-start = ((), (), s32[]{:S(2)}) async-start(), calls=%async_computation.20 | async-start | bytes 1179648 | tf_op jit(solution)/shard_map/reduce_scatter | solution.py:340
  5794.7 192.0 %reduce-scatter.29.cloned.1.call-start = ((), (), s32[]{:S(2)}) async-start(), calls=%async_computation.18 | async-start | bytes 1179648 | tf_op jit(solution)/shard_map/reduce_scatter | solution.py:331
  5808.0 245.4 %reduce-scatter.41.cloned.1.call-start = ((), (), s32[]{:S(2)}) async-start(), calls=%async_computation.24 | async-start | bytes 1474560 | tf_op jit(solution)/shard_map/reduce_scatter | solution.py:355
  5811.2 312.2 %reduce-scatter.31.cloned.1.call-start = ((), (), s32[]{:S(2)}) async-start(), calls=%async_computation.19 | async-start | bytes 2359296 | tf_op jit(solution)/shard_map/reduce_scatter | solution.py:334
  5817.1 383.4 %reduce-scatter.27.cloned.1.call-start = ((), (), s32[]{:S(2)}) async-start(), calls=%async_computation.17 | async-start | bytes 3538944 | tf_op jit(solution)/shard_map/reduce_scatter | solution.py:328
  5839.7 451.6 %reduce-scatter.37.cloned.1.call-start = ((), (), s32[]{:S(2)}) async-start(), calls=%async_computation.22 | async-start | bytes 4718592 | tf_op jit(solution)/shard_map/reduce_scatter | solution.py:346
  5846.9 536.3 %reduce-scatter.35.cloned.1.call-start = ((), (), s32[]{:S(2)}) async-start(), calls=%async_computation.21 | async-start | bytes 4718592 | tf_op jit(solution)/shard_map/reduce_scatter | solution.py:343
  5855.3 619.3 %reduce-scatter.25.cloned.1.call-start = ((), (), s32[]{:S(2)}) async-start(), calls=%async_computation.16 | async-start | bytes 4718592 | tf_op jit(solution)/shard_map/reduce_scatter | solution.py:325
  5867.6 698.6 %reduce-scatter.23.cloned.1.call-start = ((), (), s32[]{:S(2)}) async-start(), calls=%async_computation.15 | async-start | bytes 4718592 | tf_op jit(solution)/shard_map/reduce_scatter | solution.py:322
  5879.0 745.0 %reduce-scatter.49.cloned.1.call-start = ((), (), s32[]{:S(2)}) async-start(), calls=%async_computation.40 | async-start | bytes 184320
  5893.1 794.6 %reduce-scatter.43.cloned.1.call-start = ((), (), s32[]{:S(2)}) async-start(), calls=%async_computation.37 | async-start | bytes 147456
  5894.3 857.1 %reduce-scatter.45.cloned.1.call-start = ((), (), s32[]{:S(2)}) async-start(), calls=%async_computation.38 | async-start | bytes 147456
  5894.7 671.5 %copy-start.245 = (f32[512]{0:T(512)S(1)}, f32[512]{0:T(512)}, u32[]{:S(2)}) copy-start(f32[512]{0:T(512)} %copy-done.244) | copy-start | bytes 6148
  5894.7 672.2 %copy-start.243 = (f32[512]{0:T(512)S(1)}, f32[512]{0:T(512)}, u32[]{:S(2)}) copy-start(f32[512]{0:T(512)} %copy-done.242) | copy-start | bytes 6148
  5894.7 672.8 %copy-start.59 = (f32[512,512]{1,0:T(8,128)S(1)}, f32[512,512]{1,0:T(8,128)}, u32[]{:S(2)}) copy-start(f32[512,512]{1,0:T(8,128)} %copy-done.58) | copy-start | bytes 3145732
  5894.7 672.8 %copy-start.63 = (f32[512,512]{1,0:T(8,128)S(1)}, f32[512,512]{1,0:T(8,128)}, u32[]{:S(2)}) copy-start(f32[512,512]{1,0:T(8,128)} %copy-done.62) | copy-start | bytes 3145732
  5895.5 933.6 %all-reduce.81.cloned.1.call-start = ((), (), s32[]{:S(2)}) async-start(), calls=%async_computation.41 | async-start | bytes 6848512 | tf_op jit(solution)/shard_map/psum | solution.py:374
  (290 other events, 1716.8 us)
Sparse Core Ops, SparseCore 0:
  10.8 53.4 all-gather.40
  66.9 52.9 all-gather.42
  122.6 45.6 all-gather.44
  170.3 40.3 all-gather.46
  213.3 53.9 all-gather.48
  269.3 52.0 all-gather.50
  324.1 57.2 all-gather.52
  384.1 52.8 all-gather.54
  439.1 44.6 all-gather.56
  486.3 38.8 all-gather.58
  527.4 48.2 all-gather.60
  577.7 47.8 all-gather.62
  627.8 40.4 all-gather.38
  5732.1 57.5 reduce-scatter.46
  5793.2 61.1 reduce-scatter.38
  5857.7 62.3 reduce-scatter.32
  5924.3 62.3 reduce-scatter.28
  5990.0 63.3 reduce-scatter.40
  6056.9 66.4 reduce-scatter.30
  6126.8 73.5 reduce-scatter.26
  6204.1 87.2 reduce-scatter.36
  6295.4 87.8 reduce-scatter.34
  6386.9 87.6 reduce-scatter.24
  6478.5 87.6 reduce-scatter.22
  6569.9 54.0 reduce-scatter.48
  6627.7 59.8 reduce-scatter.42
  6691.4 59.8 reduce-scatter.44
  6755.1 73.9 all-reduce.80
where the time goes:
time: 6940 us; the launch traced here: 6850 us
  other arithmetic  3980 us (57%)
  waiting for transfers between devices  920 us (13%)
  local copies, waits for them, and re-layouts  701 us (10%)
  blocking collectives  632 us (9%)
  matrix products  448 us (6%)
  loops' own time  145 us (2%)
    dynamic_update_slice x2304, other arithmetic, lattice(): unused, alphas = lax.scan(advance, pending, inputs)  1680 us
    mul x768, other arithmetic, advance(): moves.append(jnp.logaddexp(stay, rise))  543 us
    reduce_sum x305, other arithmetic, log_total(): return jnp.squeeze(top, axis) + jnp.log(jnp.sum(jnp.exp(value - top), axis))  246 us
    reduce_sum x256, other arithmetic, advance(): table = jnp.where(lower[None], (arrive - climb)[:, None, :], NEG)  227 us
    div x257, other arithmetic, log_total(): return jnp.squeeze(top, axis) + jnp.log(jnp.sum(jnp.exp(value - top), axis))  191 us
    unnamed x32, waiting for transfers between devices  186 us
    dot_general x82, matrix products, matmul(): return jnp.dot(left, right, preferred_element_type=jnp.float32)  179 us
    div x257, other arithmetic, log_total(): top = jnp.max(value, axis, keepdims=True)  175 us

commit v1 on v0

--- a/solution.py
+++ b/solution.py
@@ -1,8 +1,11 @@
+import functools
 from functools import partial
 
 import jax
 import jax.numpy as jnp
 from jax import lax
+from jax.experimental import pallas as pl
+from jax.experimental.pallas import tpu as pltpu
 from jax.sharding import PartitionSpec as P
 
 HEADS = 8
@@ -13,51 +16,294 @@
 NEG = -1e30
 
 
-def log_total(value, axis):
-    top = jnp.max(value, axis, keepdims=True)
-    return jnp.squeeze(top, axis) + jnp.log(jnp.sum(jnp.exp(value - top), axis))
-
-
-def lattice(blank, label, dur, t_len, u_len):
-    utts, frames, slots = blank.shape
-    reach = dur.shape[-1] - 1
-    lower = lax.broadcasted_iota(jnp.int32, (slots, slots), 1) <= lax.broadcasted_iota(
-        jnp.int32, (slots, slots), 0
-    )
-    start_row = jnp.where(
-        lax.broadcasted_iota(jnp.int32, (utts, 1, slots), 2) == 0, 0.0, NEG
-    ).astype(jnp.float32)
-    pending = jnp.concatenate([start_row, jnp.full((utts, reach - 1, slots), NEG, jnp.float32)], 1)
-    edge = jnp.full((utts, 1), NEG, jnp.float32)
-
-    def advance(waiting, inputs):
-        blank_t, label_t, dur_t = inputs
-        arrive = waiting[:, 0]
-        emit = label_t + dur_t[:, :, 0]
-        climb = jnp.cumsum(emit, -1) - emit
-        table = jnp.where(lower[None], (arrive - climb)[:, None, :], NEG)
-        alpha = climb + log_total(table, -1)
-        moves = []
-        for skip in range(1, reach + 1):
-            stay = alpha + blank_t + dur_t[:, :, skip]
-            rise = jnp.concatenate([edge, (alpha + label_t + dur_t[:, :, skip])[:, :-1]], 1)
-            moves.append(jnp.logaddexp(stay, rise))
-        later = [jnp.logaddexp(waiting[:, skip], moves[skip - 1]) for skip in range(1, reach)] + [
-            moves[reach - 1]
-        ]
-        return (jnp.stack(later, 1), alpha)
-
-    inputs = (jnp.swapaxes(blank, 0, 1), jnp.swapaxes(label, 0, 1), jnp.swapaxes(dur, 0, 1))
-    unused, alphas = lax.scan(advance, pending, inputs)
-    alphas = jnp.swapaxes(alphas, 0, 1)
-    times = lax.broadcasted_iota(jnp.int32, (utts, frames, slots), 1)
-    places = lax.broadcasted_iota(jnp.int32, (utts, frames, slots), 2)
-    at_end = places == u_len[:, None, None]
-    ends = []
-    for skip in range(1, reach + 1):
-        hit = at_end & (times + skip == t_len[:, None, None])
-        ends.append(jnp.where(hit, alphas + blank + dur[..., skip], NEG))
-    return log_total(jnp.stack(ends, -1).reshape(utts, -1), -1)
+def lattice_kernel(slots, feats_ref, tlen_ref, ulen_ref, grads_ref, prob_ref, s_ref, l_ref, ls_ref, a_ref, b_ref, init_ref):
+    utts = tlen_ref.shape[0]
+    frames = feats_ref.shape[2]
+    rows = feats_ref.shape[1]
+    wide = frames + 128
+    reach = feats_ref.shape[0] - 3
+    diags = frames + slots
+    pad = 8
+    total = a_ref.shape[0]
+    body = wide
+
+    def skew(x, sign):
+        k = lax.broadcasted_iota(jnp.int32, x.shape, 0) % 32
+        for bit in range(5):
+            step = 1 << bit
+            x = jnp.where((k // step) % 2 == 1, pltpu.roll(x, step if sign > 0 else wide - step, 1), x)
+        return x
+
+    def to_diag(x):
+        x = jnp.concatenate([x, jnp.zeros((rows, 128), jnp.float32)], 1)
+        x = skew(x, 1)
+        x = jnp.concatenate([x, jnp.zeros((128 - rows, wide), jnp.float32)], 0)
+        return x.T
+
+    lane = lax.broadcasted_iota(jnp.int32, (wide, 128), 1)
+    diag = lax.broadcasted_iota(jnp.int32, (wide, 128), 0)
+    k_of = lane % 32
+    t_of = diag - k_of
+    t_len = jnp.full((wide, 128), -1, jnp.int32)
+    u_len = jnp.full((wide, 128), -1, jnp.int32)
+    for u in range(utts):
+        mine = (lane // 32) == u
+        t_len = jnp.where(mine, tlen_ref[u], t_len)
+        u_len = jnp.where(mine, ulen_ref[u], u_len)
+    blank = to_diag(feats_ref[0])
+    label = to_diag(feats_ref[1])
+    edge = jnp.full((pad, 128), NEG, jnp.float32)
+    real = (t_of >= 0)
+    for ref in (s_ref, l_ref, ls_ref):
+        for e in range(ref.shape[0]):
+            ref[e, 0:pad, :] = edge
+            ref[e, pad + wide:, :] = jnp.full((ref.shape[1] - pad - wide, 128), NEG, jnp.float32)
+    for e in range(reach + 1):
+        dur = to_diag(feats_ref[2 + e])
+        if e > 0:
+            keep = real & (k_of <= u_len) & ((t_of + e < t_len) | ((t_of + e == t_len) & (k_of == u_len)))
+            s_ref[e - 1, pad:pad + wide, :] = jnp.where(keep, blank + dur, NEG)
+        keep = real & (k_of < u_len) & (t_of + e < t_len)
+        lab = jnp.where(keep, label + dur, NEG)
+        l_ref[e, pad:pad + wide, :] = lab
+        ls_ref[e, pad:pad + wide, :] = pltpu.roll(lab, 1, 1)
+    init_ref[pad:pad + wide, :] = jnp.where((t_of == t_len) & (k_of == u_len), 0.0, NEG)
+    a_ref[...] = jnp.full(a_ref.shape, NEG, jnp.float32)
+    b_ref[...] = jnp.full(b_ref.shape, NEG, jnp.float32)
+
+    first = jnp.where((lax.broadcasted_iota(jnp.int32, (1, 128), 1) % 32 == 0)
+                      & (lax.broadcasted_iota(jnp.int32, (1, 128), 1) < 32 * utts), 0.0, NEG)
+
+    def lse(terms):
+        tops = list(terms)
+        while len(tops) > 1:
+            tops = [jnp.maximum(tops[i], tops[i + 1]) if i + 1 < len(tops) else tops[i] for i in range(0, len(tops), 2)]
+        top = tops[0]
+        parts = [jnp.exp(x - top) for x in terms]
+        while len(parts) > 1:
+            parts = [parts[i] + parts[i + 1] if i + 1 < len(parts) else parts[i] for i in range(0, len(parts), 2)]
+        return jnp.maximum(top + jnp.log(parts[0]), NEG)
+
+    a_ref[pl.ds(pad, 1), :] = first
+    last = diags
+
+    def step(i, carry):
+        ha, hra, hb, hrb = carry
+        row = pad + i
+        terms = [ha[e - 1] + s_ref[e - 1, pl.ds(row - e, 1), :] for e in range(1, reach + 1)]
+        terms += [hra[e] + ls_ref[e, pl.ds(row - e - 1, 1), :] for e in range(reach + 1)]
+        a = lse(terms[::-1])
+        a_ref[pl.ds(row, 1), :] = a
+        ra = pltpu.roll(a, 1, 1)
+        rowb = pad + last - i
+        terms = [hb[e - 1] + s_ref[e - 1, pl.ds(rowb, 1), :] for e in range(1, reach + 1)]
+        terms += [hrb[e] + l_ref[e, pl.ds(rowb, 1), :] for e in range(reach + 1)]
+        b = jnp.maximum(lse(terms[::-1]), init_ref[pl.ds(rowb, 1), :])
+        b_ref[pl.ds(rowb, 1), :] = b
+        rb = pltpu.roll(b, 127, 1)
+        return ((a,) + ha[:-1], (ra,) + hra[:-1], (b,) + hb[:-1], (rb,) + hrb[:-1])
+
+    b0 = init_ref[pl.ds(pad + last, 1), :]
+    b_ref[pl.ds(pad + last, 1), :] = b0
+    none = a_ref[pl.ds(0, 1), :]
+    first = a_ref[pl.ds(pad, 1), :]
+    ha = (first,) + (none,) * (reach - 1)
+    hra = (pltpu.roll(first, 1, 1),) + (none,) * reach
+    hb = (b0,) + (none,) * (reach - 1)
+    hrb = (pltpu.roll(b0, 127, 1),) + (none,) * reach
+    lax.fori_loop(1, last + 1, step, (ha, hra, hb, hrb))
+
+    zrow = b_ref[pl.ds(pad, 1), :]
+    lane1 = lax.broadcasted_iota(jnp.int32, (1, 128), 1)
+    z = jnp.zeros((1, 128), jnp.float32)
+    for u in range(utts):
+        zu = jnp.max(jnp.where(lane1 == 32 * u, zrow, 2 * NEG), axis=1, keepdims=True)
+        z = jnp.where(lane1 // 32 == u, zu, z)
+        prob_ref[pl.ds(u, 1), :] = jnp.broadcast_to(zu, (1, 128))
+
+    def from_diag(x):
+        x = x.T[:rows]
+        return skew(x, -1)[:, :frames]
+
+    a = a_ref[pad:pad + wide, :] - z
+    g_blank = jnp.zeros((wide, 128), jnp.float32)
+    g_label = jnp.zeros((wide, 128), jnp.float32)
+    for e in range(reach + 1):
+        bb = b_ref[pad + e + 1: pad + e + 1 + wide, :]
+        pl_ = jnp.exp(a + l_ref[e, pad:pad + wide, :] + pltpu.roll(bb, 127, 1))
+        g_label = g_label - pl_
+        g = -pl_
+        if e > 0:
+            ps = jnp.exp(a + s_ref[e - 1, pad:pad + wide, :] + b_ref[pad + e: pad + e + wide, :])
+            g_blank = g_blank - ps
+            g = g - ps
+        grads_ref[2 + e] = from_diag(g)
+    grads_ref[0] = from_diag(g_blank)
+    grads_ref[1] = from_diag(g_label)
+
+
+def lattice(feats, t_len, u_len, slots):
+    _, rows, frames = feats.shape
+    wide = frames + 128
+    total = wide + 16
+    reach = feats.shape[0] - 3
+    return pl.pallas_call(
+        functools.partial(lattice_kernel, slots),
+        out_shape=(jax.ShapeDtypeStruct(feats.shape, jnp.float32), jax.ShapeDtypeStruct((8, 128), jnp.float32)),
+        in_specs=[pl.BlockSpec(memory_space=pltpu.VMEM), pl.BlockSpec(memory_space=pltpu.SMEM), pl.BlockSpec(memory_space=pltpu.SMEM)],
+        out_specs=(pl.BlockSpec(memory_space=pltpu.VMEM),) * 2,
+        scratch_shapes=[pltpu.VMEM((reach, total, 128), jnp.float32), pltpu.VMEM((reach + 1, total, 128), jnp.float32),
+                        pltpu.VMEM((reach + 1, total, 128), jnp.float32), pltpu.VMEM((total, 128), jnp.float32),
+                        pltpu.VMEM((total, 128), jnp.float32), pltpu.VMEM((total, 128), jnp.float32)],
+        compiler_params=pltpu.CompilerParams(vmem_limit_bytes=48 << 20),
+        name="lattice",
+    )(feats, t_len, u_len)
+
+
+GROUP=5
+CHUNK=256
+
+def nn(a,b): return jnp.dot(a,b,preferred_element_type=jnp.float32)
+def nt(a,b): return lax.dot_general(a,b,(((1,),(1,)),((),())),preferred_element_type=jnp.float32)
+
+def fold8(x, op):
+    parts=[x[i:i+8] for i in range(0,x.shape[0],8)]
+    while len(parts)>1:
+        parts=[op(parts[i],parts[i+1]) if i+1<len(parts) else parts[i] for i in range(0,len(parts),2)]
+    return parts[0]
+
+def joint_fwd_kernel(groups, durs, labels_ref, enc_ref, pred_ref, wt_ref, feats_ref, p_ref, tok_ref):
+    step=pl.program_id(0)
+    vocab=p_ref.shape[2]
+    u=step//groups
+    g=step%groups
+    for j in range(GROUP):
+        k=g*GROUP+j
+        hid=jnp.tanh(enc_ref[...]+pred_ref[0,:,j:j+1]).astype(jnp.bfloat16)
+        tops=[]
+        for c in range(0,vocab,CHUNK):
+            t=nn(wt_ref[c:c+CHUNK,:],hid)
+            tok_ref[j%2,c:c+CHUNK,:]=t
+            tops.append(fold8(t,jnp.maximum))
+        dl=nn(wt_ref[vocab:,:],hid)[:8]
+        top=jnp.max(functools.reduce(jnp.maximum,tops),0,keepdims=True)
+        sums=[]
+        for c in range(0,vocab,CHUNK):
+            e=jnp.exp(tok_ref[j%2,c:c+CHUNK,:]-top)
+            p_ref[0,j,c:c+CHUNK,:]=e.astype(jnp.bfloat16)
+            sums.append(fold8(e,jnp.add))
+        total=jnp.sum(functools.reduce(jnp.add,sums),0,keepdims=True)
+        lse=top+jnp.log(total)
+        row=u*32+k
+        feats_ref[0,pl.ds(row,1),:]=tok_ref[j%2,0:1,:]-lse
+        feats_ref[1,pl.ds(row,1),:]=tok_ref[j%2,pl.ds(labels_ref[u,k],1),:]-lse
+        real=lax.broadcasted_iota(jnp.int32,dl.shape,0)<durs
+        dtop=jnp.max(jnp.where(real,dl,-1e30),0,keepdims=True)
+        dlse=dtop+jnp.log(jnp.sum(jnp.where(real,jnp.exp(dl-dtop),0.0),0,keepdims=True))
+        dlp=dl-dlse
+        for e in range(durs):
+            feats_ref[2+e,pl.ds(row,1),:]=dlp[e:e+1]
+        feats_ref[2+durs,pl.ds(row,1),:]=1.0/total
+
+def joint_forward(enc_t, pred_t, labels, w_t, vocab, durs, frames):
+    joint, rows=enc_t.shape
+    utts,slots=labels.shape
+    groups=slots//GROUP
+    return pl.pallas_call(
+        partial(joint_fwd_kernel,groups,durs),
+        grid=(utts*groups,),
+        in_specs=[pl.BlockSpec(memory_space=pltpu.SMEM),
+            pl.BlockSpec((joint,frames),lambda s:(0,s//groups)),
+            pl.BlockSpec((1,joint,8),lambda s:(s,0,0)),
+            pl.BlockSpec(w_t.shape,lambda s:(0,0))],
+        out_specs=[pl.BlockSpec((3+durs,utts*32,frames),lambda s:(0,0,0)),
+            pl.BlockSpec((1,GROUP,vocab,frames),lambda s:(s,0,0,0))],
+        out_shape=[jax.ShapeDtypeStruct((3+durs,utts*32,frames),jnp.float32),
+            jax.ShapeDtypeStruct((utts*groups,GROUP,vocab,frames),jnp.bfloat16)],
+        scratch_shapes=[pltpu.VMEM((2,vocab,frames),jnp.float32)],
+        compiler_params=pltpu.CompilerParams(vmem_limit_bytes=50<<20),
+        name="joint_forward",
+    )(labels,enc_t,pred_t,w_t)
+
+def joint_bwd_kernel(groups, durs, labels_ref, enc_ref, pred_ref, w_ref, feats_ref, grads_ref, p_ref, genc_ref, gpred_ref, gtok_ref, gdur_ref, h_ref, d_ref, acc_ref):
+    step=pl.program_id(0)
+    vocab=p_ref.shape[2]
+    frames=p_ref.shape[3]
+    u=step//groups
+    g=step%groups
+
+    @pl.when(step==0)
+    def _():
+        acc_ref[...]=jnp.zeros_like(acc_ref)
+    @pl.when(g==0)
+    def _():
+        genc_ref[...]=jnp.zeros_like(genc_ref)
+    for j in range(GROUP):
+        k=g*GROUP+j
+        row=u*32+k
+        cols=slice(j*frames,(j+1)*frames)
+        th=jnp.tanh(enc_ref[...]+pred_ref[0,:,j:j+1])
+        h_ref[:,cols]=th.astype(jnp.bfloat16)
+        gb=grads_ref[0,pl.ds(row,1),:]
+        gl=grads_ref[1,pl.ds(row,1),:]
+        scale=-(gb+gl)*feats_ref[2+durs,pl.ds(row,1),:]
+        for c in range(0,vocab,CHUNK):
+            d_ref[c:c+CHUNK,cols]=(p_ref[0,j,c:c+CHUNK,:].astype(jnp.float32)*scale).astype(jnp.bfloat16)
+        label=labels_ref[u,k]
+        def fix(base):
+            v=p_ref[0,j,pl.ds(base,16),:].astype(jnp.float32)*scale
+            at=lax.broadcasted_iota(jnp.int32,v.shape,0)+base
+            v=v+jnp.where(at==0,gb,0.0)+jnp.where(at==label,gl,0.0)
+            d_ref[pl.ds(base,16),cols]=v.astype(jnp.bfloat16)
+        fix(0)
+        fix(pl.multiple_of((label//16)*16,16))
+        gd=[grads_ref[2+e,pl.ds(row,1),:] for e in range(durs)]
+        gsum=functools.reduce(jnp.add,gd)
+        at=lax.broadcasted_iota(jnp.int32,(16,frames),0)
+        dd=jnp.zeros((16,frames),jnp.float32)
+        for e in range(durs):
+            dd=jnp.where(at==e,gd[e]-gsum*jnp.exp(feats_ref[2+e,pl.ds(row,1),:]),dd)
+        d_ref[vocab:vocab+16,cols]=dd.astype(jnp.bfloat16)
+        d_ref[vocab+16:,cols]=jnp.zeros((d_ref.shape[0]-vocab-16,frames),jnp.bfloat16)
+        dh=nn(w_ref[...],d_ref[:,cols])
+        th=jnp.tanh(enc_ref[...]+pred_ref[0,:,j:j+1])
+        dp=dh*(1.0-th*th)
+        genc_ref[...]+=dp
+        gpred_ref[0,:,j:j+1]=jnp.sum(dp,1,keepdims=True)
+    for c in range(0,d_ref.shape[0],384):
+        acc_ref[:,c:c+384]+=nt(h_ref[...],d_ref[c:c+384,:])
+    @pl.when(step==pl.num_programs(0)-1)
+    def _():
+        gtok_ref[...]=acc_ref[:,:vocab].astype(jnp.bfloat16)
+        gdur_ref[...]=acc_ref[:,vocab:].astype(jnp.bfloat16)
+
+def joint_backward(enc_t, pred_t, labels, w, feats, grads, p, vocab, durs, frames):
+    joint, rows=enc_t.shape
+    utts,slots=labels.shape
+    groups=slots//GROUP
+    full=lambda a: pl.BlockSpec(a.shape,lambda s:(0,)*a.ndim)
+    return pl.pallas_call(
+        partial(joint_bwd_kernel,groups,durs),
+        grid=(utts*groups,),
+        in_specs=[pl.BlockSpec(memory_space=pltpu.SMEM),
+            pl.BlockSpec((joint,frames),lambda s:(0,s//groups)),
+            pl.BlockSpec((1,joint,8),lambda s:(s,0,0)),
+            full(w),full(feats),full(grads),
+            pl.BlockSpec((1,GROUP,vocab,frames),lambda s:(s,0,0,0))],
+        out_specs=[pl.BlockSpec((joint,frames),lambda s:(0,s//groups)),
+            pl.BlockSpec((1,joint,8),lambda s:(s,0,0)),
+            pl.BlockSpec((joint,vocab),lambda s:(0,0)),
+            pl.BlockSpec((joint,128),lambda s:(0,0))],
+        out_shape=[jax.ShapeDtypeStruct((joint,rows),jnp.float32),
+            jax.ShapeDtypeStruct((utts*groups,joint,8),jnp.float32),
+            jax.ShapeDtypeStruct((joint,vocab),jnp.bfloat16),
+            jax.ShapeDtypeStruct((joint,128),jnp.bfloat16)],
+        scratch_shapes=[pltpu.VMEM((joint,GROUP*frames),jnp.bfloat16),
+            pltpu.VMEM((vocab+128,GROUP*frames),jnp.bfloat16),
+            pltpu.VMEM((joint,vocab+128),jnp.float32)],
+        compiler_params=pltpu.CompilerParams(vmem_limit_bytes=56<<20),
+        name="joint_backward",
+    )(labels,enc_t,pred_t,w,feats,grads,p)
 
 
 def norm_rows(value, gain):
@@ -440,81 +686,25 @@
     enc = matmul(out_low, w_enc)
     pred_low = pred_states.reshape(utts * slots, joint)
     pred = matmul(pred_low, w_pred).reshape(utts, slots, joint)
+    groups = slots // GROUP
+    durs = w_dur.shape[1]
+    pred_t = jnp.pad(
+        jnp.swapaxes(pred.reshape(utts * groups, GROUP, joint), 1, 2),
+        ((0, 0), (0, 0), (0, 8 - GROUP)),
+    )
+    w_cat = jnp.concatenate([w_tok, jnp.pad(w_dur, ((0, 0), (0, 128 - durs)))], 1)
+    enc_t = enc.T
     labels_ext = jnp.concatenate([label_ids, jnp.zeros((utts, 1), jnp.int32)], 1)
-    span = min(frames, 32)
-    blocks = frames // span
-    enc_blocks = enc.reshape(utts * blocks, span, joint)
-    indices = lax.iota(jnp.int32, utts * blocks)
-
-    def scores_of(index):
-        owner = index // blocks
-        enc_block = lax.dynamic_index_in_dim(enc_blocks, index, 0, keepdims=False)
-        pred_rows = lax.dynamic_index_in_dim(pred, owner, 0, keepdims=False)
-        lab_row = lax.dynamic_index_in_dim(labels_ext, owner, 0, keepdims=False)
-        squashed = jnp.tanh(enc_block[:, None, :] + pred_rows[None, :, :])
-        hidden_low = squashed.astype(jnp.bfloat16).reshape(span * slots, joint)
-        tok = matmul(hidden_low, w_tok).reshape(span, slots, vocab)
-        durl = matmul(hidden_low, w_dur).reshape(span, slots, -1)
-        total = log_total(tok, -1)
-        picked = lax.broadcasted_iota(jnp.int32, tok.shape, 2) == lab_row[None, :, None]
-        return (squashed, hidden_low, tok, durl, total, picked)
-
-    def forward_block(index):
-        squashed, hidden_low, tok, durl, total, picked = scores_of(index)
-        blank = tok[..., 0] - total
-        label = jnp.sum(jnp.where(picked, tok, 0.0), -1) - total
-        dur = durl - log_total(durl, -1)[..., None]
-        return (blank, label, dur)
-
-    blank, label, dur = lax.map(forward_block, indices)
-    blank = blank.reshape(utts, frames, slots)
-    label = label.reshape(utts, frames, slots)
-    dur = dur.reshape(utts, frames, slots, -1)
-    lattice_local = partial(lattice, t_len=frame_lengths, u_len=label_lengths)
-    log_prob, pullback = jax.vjp(lattice_local, blank, label, dur)
+    feats, expd = joint_forward(enc_t, pred_t, labels_ext, w_cat.T, vocab, durs, frames)
+    lat_grads, scores = lattice(feats[: 2 + durs], frame_lengths, label_lengths, slots)
+    log_prob = scores[:utts, 0]
     utt_loss = -log_prob / frame_lengths.astype(jnp.float32)
-    grad_blank, grad_label, grad_dur = pullback(-jnp.ones_like(log_prob))
-    grad_blank = grad_blank.reshape(utts * blocks, span, slots)
-    grad_label = grad_label.reshape(utts * blocks, span, slots)
-    grad_dur = grad_dur.reshape(utts * blocks, span, slots, -1)
-
-    def backward_block(carry, index):
-        acc_tok, acc_dur, acc_pred = carry
-        squashed, hidden_low, tok, durl, total, picked = scores_of(index)
-        g_blank = lax.dynamic_index_in_dim(grad_blank, index, 0, keepdims=False)
-        g_label = lax.dynamic_index_in_dim(grad_label, index, 0, keepdims=False)
-        g_dur = lax.dynamic_index_in_dim(grad_dur, index, 0, keepdims=False)
-        prob = jnp.exp(tok - total[..., None])
-        first_col = lax.broadcasted_iota(jnp.int32, tok.shape, 2) == 0
-        d_tok = (
-            jnp.where(first_col, g_blank[..., None], 0.0)
-            + jnp.where(picked, g_label[..., None], 0.0)
-            - (g_blank + g_label)[..., None] * prob
-        )
-        d_tok_low = d_tok.astype(jnp.bfloat16).reshape(span * slots, vocab)
-        dur_prob = jnp.exp(durl - log_total(durl, -1)[..., None])
-        d_dur_low = (
-            (g_dur - jnp.sum(g_dur, -1, keepdims=True) * dur_prob)
-            .astype(jnp.bfloat16)
-            .reshape(span * slots, -1)
-        )
-        acc_tok = acc_tok + contract_rows(hidden_low, d_tok_low)
-        acc_dur = acc_dur + contract_rows(hidden_low, d_dur_low)
-        d_hidden = contract_cols(d_tok_low, w_tok) + contract_cols(d_dur_low, w_dur)
-        d_pre = d_hidden.reshape(span, slots, joint) * (1.0 - squashed * squashed)
-        owner = index // blocks
-        pred_row = lax.dynamic_index_in_dim(acc_pred, owner, 0, keepdims=False) + jnp.sum(d_pre, 0)
-        acc_pred = lax.dynamic_update_index_in_dim(acc_pred, pred_row, owner, 0)
-        return ((acc_tok, acc_dur, acc_pred), jnp.sum(d_pre, 1))
-
-    start_carry = (
-        jnp.zeros((joint, vocab), jnp.float32),
-        jnp.zeros((joint, w_dur.shape[1]), jnp.float32),
-        jnp.zeros((utts, slots, joint), jnp.float32),
-    )
-    carried, grad_enc_blocks = lax.scan(backward_block, start_carry, indices)
-    grad_tok, grad_dur_w, grad_pred_rows = carried
-    grad_enc_low = grad_enc_blocks.reshape(rows, joint).astype(jnp.bfloat16)
+    grad_enc_t, grad_pred_t, grad_tok, grad_dur_w = joint_backward(
+        enc_t, pred_t, labels_ext, w_cat, feats, lat_grads, expd, vocab, durs, frames
+    )
+    grad_dur_w = grad_dur_w[:, :durs]
+    grad_pred_rows = jnp.swapaxes(grad_pred_t[:, :, :GROUP], 1, 2)
+    grad_enc_low = grad_enc_t.T.astype(jnp.bfloat16)
     grad_w_enc = contract_rows(out_low, grad_enc_low)
     grad = contract_cols(grad_enc_low, w_enc)
     grad_w_pred = contract_rows(

time: 6940 us -> 2100 us (0.30); the launches traced: 6850 us -> 2090 us
  other arithmetic: 3980 us -> 94.1 us
  local copies, waits for them, and re-layouts: 701 us -> 171 us
  matrix products: 448 us -> 136 us
  loops' own time: 145 us -> 0 us
  Pallas kernels: 0 us -> 132 us
    dynamic_update_slice x2320 -> x0, other arithmetic: 1680 us -> none  [the longest x2304 1680 us: lattice(): unused, alphas = lax.scan(advance, pending, inputs)]
    reduce_sum x866 -> x0, other arithmetic: 559 us -> none  [the longest x305 246 us: log_total(): return jnp.squeeze(top, axis) + jnp.log(jnp.sum(jnp.exp(value - top), axis))]
    mul x768 -> x0, other arithmetic: 543 us -> none  [advance(): moves.append(jnp.logaddexp(stay, rise))]
    div x514 -> x1, other arithmetic: 367 us -> 0.52 us  [local(): utt_loss = -log_prob / frame_lengths.astype(jnp.float32)]
    add x850 -> x0, other arithmetic: 339 us -> none  [the longest x512 171 us: advance(): alpha + label_t + dur_t[:, :, skip]]
    dynamic_update_slice x336 -> x0, local copies, waits for them, and re-layouts: 260 us -> none  [the longest x256 171 us: lattice(): unused, alphas = lax.scan(advance, pending, inputs)]
    broadcast_in_dim x530 -> x0, other arithmetic: 169 us -> none  [the longest x256 167 us: advance(): table = jnp.where(lower[None], (arrive - climb)[:, None, :], NEG)]
    another operation x4 -> x0, loops' own time: 145 us -> none  [the longest x1 65.3 us: local(): carried, grad_enc_blocks = lax.scan(backward_block, start_carry, indices)]
where the time goes in v1:
time: 2100 us; the launch traced here: 2090 us
  waiting for transfers between devices  903 us (43%)
  blocking collectives  630 us (30%)
  local copies, waits for them, and re-layouts  171 us (8%)
  matrix products  136 us (6%)
  Pallas kernels  132 us (6%)
  other arithmetic  94.1 us (4%)
    unnamed x31, waiting for transfers between devices  130 us
    reduce_scatter x1, waiting for transfers between devices, reduce_grads(): lax.psum_scatter(stacked[1].astype(jnp.bfloat16), 'fsdp', scatter_dimensi...  91.8 us
    reduce_scatter x1, waiting for transfers between devices, reduce_grads(): lax.psum_scatter(stacked[8].astype(jnp.bfloat16), 'fsdp', scatter_dimensi...  91.8 us
    reduce_scatter x1, waiting for transfers between devices, reduce_grads(): lax.psum_scatter(stacked[2].astype(jnp.bfloat16), 'fsdp', scatter_dimensi...  91.3 us
    reduce_scatter x1, waiting for transfers between devices, reduce_grads(): lax.psum_scatter(stacked[9].astype(jnp.bfloat16), 'fsdp', scatter_dimensi...  90.6 us
    psum x2, blocking collectives, batch_stats(): lax.psum(jnp.sum(valid_rows * centred * centred, 0), ('dp', 'fsdp')) / count  83.3 us
    psum x2, blocking collectives, layer_backward(): lax.psum((jnp.sum(grad_shifted, 0), jnp.sum(grad_shifted * normalized, 0)...  80.3 us
    reduce_scatter x1, waiting for transfers between devices, reduce_grads(): lax.psum_scatter(stacked[3].astype(jnp.bfloat16), 'fsdp', scatter_dimensi...  77.1 us
  transfers between devices with their start and end apart: 28, of which 13 were waited for; matrix products, arithmetic and copies ran while one was open for 14% of the time, Pallas kernels for 0%

profile of v1, /device:TPU:0, one launch (start us, length us, event | category | flops | bytes accessed | tf_op | source)
XLA Modules:
  0.0 2087.8 jit_solution(16232055406991332063)
XLA Ops:
  23.4 23.4 %all-reduce.52 = (bf16[512]{0:T(512)(128)(2,1)S(1)}, bf16[512]{0:T(512)(128)(2,1)S(1)}, bf16[512]{0:T(512)(128)(2,1)S(1)}, bf16[512]{0:T(512)(128)(2,1)S(1)}) all-reduce(bf16[512]{0:T(512)(128)(2,1)S(1)} %dynamic-update-slice.1, bf16[512]{0:T(512)(128)(2,1)S(1)} %dynamic-update-slice, ...), channel_id=10, replica_groups=mesh['dp'=4,'fsdp'=8] {'fsdp'}, use_global_device_ids=true, to_apply=%add.46 | all-reduce | flops 2048 | bytes 8192
  49.7 26.2 %all-gather.24 = bf16[8,80,5]{1,2,0:T(8,128)(2,1)S(1)} all-gather(bf16[1,80,5]{1,2,0:T(8,128)(2,1)S(1)} %bitcast.484), channel_id=1, replica_groups=mesh['dp'=4,'fsdp'=8] {'fsdp'}, dimensions={0}, use_global_device_ids=true | all-gather | bytes 7200 | tf_op jit(solution)/shard_map/all_gather | solution.py:681
  76.6 31.6 %all-gather = bf16[1,5,512]{1,0,2:T(2,128)(2,1)S(1)} all-gather(bf16[1,5,64]{1,0,2:T(2,128)(2,1)S(1)} %copy.206), channel_id=2, replica_groups=mesh['dp'=4,'fsdp'=8] {'fsdp'}, dimensions={2}, use_global_device_ids=true | all-gather | bytes 5760 | tf_op jit(solution)/shard_map/all_gather | solution.py:661
  108.5 9.5 slice_reduce_fusion.14
  118.0 31.8 %all-gather.6 = bf16[1,9,512]{1,0,2:T(2,128)(2,1)S(1)} all-gather(bf16[1,9,64]{1,0,2:T(2,128)(2,1)S(1)} %copy.210), channel_id=8, replica_groups=mesh['dp'=4,'fsdp'=8] {'fsdp'}, dimensions={2}, use_global_device_ids=true | all-gather | bytes 10368 | tf_op jit(solution)/shard_map/all_gather | solution.py:667
  150.1 15.7 slice_reduce_fusion.24
  165.9 31.4 %all-gather.12 = bf16[1,5,512]{1,0,2:T(2,128)(2,1)S(1)} all-gather(bf16[1,5,64]{1,0,2:T(2,128)(2,1)S(1)} %copy.211), channel_id=14, replica_groups=mesh['dp'=4,'fsdp'=8] {'fsdp'}, dimensions={2}, use_global_device_ids=true | all-gather | bytes 5760 | tf_op jit(solution)/shard_map/all_gather | solution.py:661
  197.6 9.7 slice_reduce_fusion
  207.3 31.4 %all-gather.18 = bf16[1,9,512]{1,0,2:T(2,128)(2,1)S(1)} all-gather(bf16[1,9,64]{1,0,2:T(2,128)(2,1)S(1)} %copy.215), channel_id=20, replica_groups=mesh['dp'=4,'fsdp'=8] {'fsdp'}, dimensions={2}, use_global_device_ids=true | all-gather | bytes 10368 | tf_op jit(solution)/shard_map/all_gather | solution.py:667
  239.0 16.3 slice_reduce_fusion.10
  255.4 34.6 %all-gather.21 = bf16[1,512,512]{2,1,0:T(8,128)(2,1)} all-gather(bf16[1,64,512]{2,1,0:T(8,128)(2,1)S(1)} %get-tuple-element.269), channel_id=23, replica_groups=mesh['dp'=4,'fsdp'=8] {'fsdp'}, dimensions={1}, use_global_device_ids=true | all-gather | bytes 589824 | tf_op jit(solution)/shard_map/all_gather | solution.py:670
  289.9 34.2 %all-gather.16 = bf16[1,512,512]{2,1,0:T(8,128)(2,1)} all-gather(bf16[1,64,512]{2,1,0:T(8,128)(2,1)S(1)} %get-tuple-element.271), channel_id=18, replica_groups=mesh['dp'=4,'fsdp'=8] {'fsdp'}, dimensions={1}, use_global_device_ids=true | all-gather | bytes 589824 | tf_op jit(solution)/shard_map/all_gather | solution.py:665
  324.1 34.9 %all-gather.9 = bf16[1,512,512]{2,1,0:T(8,128)(2,1)} all-gather(bf16[1,64,512]{2,1,0:T(8,128)(2,1)S(1)} %get-tuple-element.270), channel_id=11, replica_groups=mesh['dp'=4,'fsdp'=8] {'fsdp'}, dimensions={1}, use_global_device_ids=true | all-gather | bytes 589824 | tf_op jit(solution)/shard_map/all_gather | solution.py:670
  359.0 34.0 %all-gather.4 = bf16[1,512,512]{2,1,0:T(8,128)(2,1)} all-gather(bf16[1,64,512]{2,1,0:T(8,128)(2,1)S(1)} %get-tuple-element.272), channel_id=6, replica_groups=mesh['dp'=4,'fsdp'=8] {'fsdp'}, dimensions={1}, use_global_device_ids=true | all-gather | bytes 589824 | tf_op jit(solution)/shard_map/all_gather | solution.py:665
  393.0 33.0 %all_gather.130 = bf16[512,640]{1,0:T(8,128)(2,1)S(1)} all-gather(bf16[64,640]{1,0:T(8,128)(2,1)S(1)} %copy-done.130), channel_id=1, replica_groups=mesh['dp'=4,'fsdp'=8] {'fsdp'}, dimensions={0}, use_global_device_ids=true | all-gather | bytes 737280 | tf_op jit(solution)/shard_map/all_gather | solution.py:678
  426.0 32.8 %all_gather.131 = bf16[640,640]{1,0:T(8,128)(2,1)S(1)} all-gather(bf16[80,640]{1,0:T(8,128)(2,1)S(1)} %copy-done.129), channel_id=1, replica_groups=mesh['dp'=4,'fsdp'=8] {'fsdp'}, dimensions={0}, use_global_device_ids=true | all-gather | bytes 921600 | tf_op jit(solution)/shard_map/all_gather | solution.py:679
  462.6 3.3 fusion.54
  468.7 5.0 fusion.41
  473.7 4.2 fusion.215
  479.2 4.0 convolution_convert_fusion.3
  483.2 5.0 reshape.730
  488.2 3.7 fusion.204
  510.4 37.4 %all-reduce.51 = (f32[512]{0:T(512)S(1)}, f32[]{:T(128)}) all-reduce(f32[512]{0:T(512)S(1)} %get-tuple-element.225, f32[]{:T(128)} %get-tuple-element.279), channel_id=1, replica_groups=mesh['dp'=4,'fsdp'=8] {'dp','fsdp'}, use_global_device_ids=true, to_apply=%region_9.10 | all-reduce | flops 513 | bytes 4104 | tf_op jit(solution)/shard_map/psum | solution.py:446
  548.7 42.6 %psum.166 = f32[512]{0:T(512)S(1)} all-reduce(f32[512]{0:T(512)S(1)} %fusion.98), channel_id=1, replica_groups=mesh['dp'=4,'fsdp'=8] {'dp','fsdp'}, use_global_device_ids=true, to_apply=%region_13.14 | all-reduce | flops 512 | bytes 4096 | tf_op jit(solution)/shard_map/psum | solution.py:451
  595.1 6.5 multiply_convert_fusion.8
  601.6 3.8 fusion.219
  607.0 5.0 fusion.27
  612.0 4.3 fusion.220
  617.7 3.9 convolution_convert_fusion.2
  621.6 5.1 reshape.731
  626.6 3.7 fusion.203
  653.9 39.0 %psum.167 = f32[512]{0:T(512)S(1)} all-reduce(f32[512]{0:T(512)S(1)} %get-tuple-element.223), channel_id=1, replica_groups=mesh['dp'=4,'fsdp'=8] {'dp','fsdp'}, use_global_device_ids=true, to_apply=%region_27.28 | all-reduce | flops 512 | bytes 4096 | tf_op jit(solution)/shard_map/psum | solution.py:446
  695.0 40.7 %psum.168 = f32[512]{0:T(512)S(1)} all-reduce(f32[512]{0:T(512)S(1)} %fusion.99), channel_id=1, replica_groups=mesh['dp'=4,'fsdp'=8] {'dp','fsdp'}, use_global_device_ids=true, to_apply=%region_29.30 | all-reduce | flops 512 | bytes 4096 | tf_op jit(solution)/shard_map/psum | solution.py:451
  740.2 6.2 multiply_convert_fusion.6
  746.3 3.8 fusion.224
  751.2 34.8 %joint_forward.1 = (f32[8,64,256]{2,1,0:T(8,128)S(1)}, bf16[10,5,1024,256]{3,2,1,0:T(8,128)(2,1)}) custom-call(s32[2,25]{1,0:T(2,128)S(1)} %concatenate.6.labels_ref, f32[640,512]{1,0:T(8,128)S(1)} %convolution_bitcast_fusion.1.enc_ref, f32[10,640,8]{2,1,0:T(8,128)} %pad.150.pred_ref, bf16[1152,640]{1,0:T(8,128)(2,1)S(1)} %copy.161.wt_ref), custom_call_target="tpu_custom_call" | custom-call | tf_op jit(solution)/shard_map/joint_forward/pallas_call | solution.py:212
  786.1 37.7 %lattice.1 = (f32[7,64,256]{2,1,0:T(8,128)S(1)}, f32[8,128]{1,0:T(8,128)S(1)}) custom-call(f32[7,64,256]{2,1,0:T(8,128)S(1)} %slice.407.feats_ref, s32[2]{0:T(128)S(1)} %copy-done.4, s32[2]{0:T(128)S(1)} %copy-done.5), custom_call_target="tpu_custom_call" | custom-call | tf_op jit(solution)/shard_map/lattice/pallas_call | solution.py:150
  824.6 59.6 %joint_backward.1 = (f32[640,512]{1,0:T(8,128)}, f32[10,640,8]{2,1,0:T(8,128)}, bf16[640,1024]{1,0:T(8,128)(2,1)}, bf16[640,128]{1,0:T(8,128)(2,1)}) custom-call(s32[2,25]{1,0:T(2,128)} %copy-done.3, f32[640,512]{1,0:T(8,128)} %copy-done, f32[10,640,8]{2,1,0:T(8,128)} %pad.150.pred_ref, bf16[640,1152]{1,0:T(8,128)(2,1)} %get-tuple-element.237.w_ref, ...), custom_call_target="tpu_custom_call" | custom-call | tf_op jit(solution)/shard_map/joint_backward/pallas_call | solution.py:285
  896.8 39.5 %all-reduce.50 = (f32[512]{0:T(512)S(1)}, f32[512]{0:T(512)S(1)}) all-reduce(f32[512]{0:T(512)S(1)} %get-tuple-element.145, f32[512]{0:T(512)S(1)} %get-tuple-element.144), channel_id=1, replica_groups=mesh['dp'=4,'fsdp'=8] {'dp','fsdp'}, use_global_device_ids=true, to_apply=%region_41.42 | all-reduce | flops 1024 | bytes 8192 | tf_op jit(solution)/shard_map/psum | solution.py:519
  936.4 3.4 multiply_reduce_fusion.6
  953.8 4.1 fusion.92
  999.9 40.7 %all-reduce.49 = (f32[512]{0:T(512)S(1)}, f32[512]{0:T(512)S(1)}) all-reduce(f32[512]{0:T(512)S(1)} %get-tuple-element.143, f32[512]{0:T(512)S(1)} %get-tuple-element.142), channel_id=1, replica_groups=mesh['dp'=4,'fsdp'=8] {'dp','fsdp'}, use_global_device_ids=true, to_apply=%region_56.57 | all-reduce | flops 1024 | bytes 8192 | tf_op jit(solution)/shard_map/psum | solution.py:519
  1048.4 3.8 broadcast_multiply_fusion.9
  1077.1 3.5 multiply_reduce_fusion
  1094.1 3.4 fusion.12
  1101.8 3.5 fusion.10
  1109.2 3.2 multiply_reduce_fusion.28
  1121.8 4.8 multiply_convert_fusion
  1134.6 3.1 multiply_reduce_fusion.30
  1140.4 5.6 multiply_reduce_fusion.10
  1150.7 6.2 reduce-scatter.31.cloned.1.call-done
  1156.9 66.0 %reduce-scatter.27.cloned.1.call-done = bf16[2,64,512]{2,1,0:T(8,128)(2,1)} async-done(((bf16[2,512,512]{2,1,0:T(8,128)(2,1)}), bf16[2,64,512]{2,1,0:T(8,128)(2,1)}) %reduce-scatter.27.cloned.1.call-update) | async-done | bytes 131088 | tf_op jit(solution)/shard_map/reduce_scatter | solution.py:577
  1222.9 66.6 %reduce-scatter.39.cloned.1.call-done = bf16[80,1024]{1,0:T(8,128)(2,1)} async-done(((bf16[640,1024]{1,0:T(8,128)(2,1)}), bf16[80,1024]{1,0:T(8,128)(2,1)}) %reduce-scatter.39.cloned.1.call-update) | async-done | bytes 163856 | tf_op jit(solution)/shard_map/reduce_scatter | solution.py:601
  1289.5 70.2 %reduce-scatter.29.cloned.1.call-done = bf16[2,64,1024]{2,1,0:T(8,128)(2,1)} async-done(((bf16[2,512,1024]{2,1,0:T(8,128)(2,1)}), bf16[2,64,1024]{2,1,0:T(8,128)(2,1)}) %reduce-scatter.29.cloned.1.call-update) | async-done | bytes 262160 | tf_op jit(solution)/shard_map/reduce_scatter | solution.py:580
  1359.7 77.1 %reduce-scatter.25.cloned.1.call-done = bf16[2,64,1536]{2,1,0:T(8,128)(2,1)} async-done(((bf16[2,512,1536]{2,1,0:T(8,128)(2,1)}), bf16[2,64,1536]{2,1,0:T(8,128)(2,1)}) %reduce-scatter.25.cloned.1.call-update) | async-done | bytes 393232 | tf_op jit(solution)/shard_map/reduce_scatter | solution.py:574
  1436.7 90.6 %reduce-scatter.35.cloned.1.call-done = bf16[2,256,512]{2,1,0:T(8,128)(2,1)} async-done(((bf16[2,2048,512]{2,1,0:T(8,128)(2,1)}), bf16[2,256,512]{2,1,0:T(8,128)(2,1)}) %reduce-scatter.35.cloned.1.call-update) | async-done | bytes 524304 | tf_op jit(solution)/shard_map/reduce_scatter | solution.py:592
  1527.4 91.8 %reduce-scatter.33.cloned.1.call-done = bf16[2,64,2048]{2,1,0:T(8,128)(2,1)} async-done(((bf16[2,512,2048]{2,1,0:T(8,128)(2,1)}), bf16[2,64,2048]{2,1,0:T(8,128)(2,1)}) %reduce-scatter.33.cloned.1.call-update) | async-done | bytes 524304 | tf_op jit(solution)/shard_map/reduce_scatter | solution.py:589
  1619.1 91.3 %reduce-scatter.23.cloned.1.call-done = bf16[2,256,512]{2,1,0:T(8,128)(2,1)} async-done(((bf16[2,2048,512]{2,1,0:T(8,128)(2,1)}), bf16[2,256,512]{2,1,0:T(8,128)(2,1)}) %reduce-scatter.23.cloned.1.call-update) | async-done | bytes 524304 | tf_op jit(solution)/shard_map/reduce_scatter | solution.py:571
  1710.4 91.8 %reduce-scatter.21.cloned.1.call-done = bf16[2,64,2048]{2,1,0:T(8,128)(2,1)} async-done(((bf16[2,512,2048]{2,1,0:T(8,128)(2,1)}), bf16[2,64,2048]{2,1,0:T(8,128)(2,1)}) %reduce-scatter.21.cloned.1.call-update) | async-done | bytes 524304 | tf_op jit(solution)/shard_map/reduce_scatter | solution.py:568
  1804.9 61.8 %reduce-scatter.43.cloned.1.call-done = bf16[64,10]{1,0:T(8,128)(2,1)} async-done(((bf16[512,10]{1,0:T(8,128)(2,1)}), bf16[64,10]{1,0:T(8,128)(2,1)}) %reduce-scatter.43.cloned.1.call-update) | async-done | bytes 1296
  1867.6 62.8 %reduce-scatter.45.cloned.1.call-done = bf16[64,18]{1,0:T(8,128)(2,1)} async-done(((bf16[512,18]{1,0:T(8,128)(2,1)}), bf16[64,18]{1,0:T(8,128)(2,1)}) %reduce-scatter.45.cloned.1.call-update) | async-done | bytes 2320
  1931.3 56.0 %reduce-scatter.41.cloned.1.call-done = bf16[80,5]{1,0:T(8,128)(2,1)} async-done(((bf16[640,5]{1,0:T(8,128)(2,1)}), bf16[80,5]{1,0:T(8,128)(2,1)}) %reduce-scatter.41.cloned.1.call-update) | async-done | bytes 816 | tf_op jit(solution)/shard_map/reduce_scatter | solution.py:604
  1987.3 10.8 all-reduce.53
  2000.0 65.1 %all-reduce.57.cloned.1.call-done = (bf16[80,640]{0,1:T(8,128)(2,1)}, bf16[2,64,2048]{2,1,0:T(8,128)(2,1)}, bf16[2,256,512]{2,1,0:T(8,128)(2,1)}, bf16[2,64,1536...) async-done(((bf16[80,640]{0,1:T(8,128)(2,1)}, ...) | async-done | bytes 3362832 | tf_op jit(solution)/shard_map/psum | solution.py:620
  (871 shorter events, 252.6 us)
Async XLA Ops:
  7.2 455.4 %all-gather.39.cloned.1.call-start = ((), (), s32[]{:S(2)}) async-start(), calls=%async_computation.14 | async-start | bytes 1474560 | tf_op jit(solution)/shard_map/all_gather | solution.py:680
  8.0 460.8 %all-gather.41.cloned.1.call-start = ((), (), s32[]{:S(2)}) async-start(), calls=%async_computation.26 | async-start | bytes 2359296 | tf_op jit(solution)/shard_map/all_gather | solution.py:662
  10.0 463.7 %all-gather.43.cloned.1.call-start = ((), (), s32[]{:S(2)}) async-start(), calls=%async_computation.27 | async-start | bytes 2359296 | tf_op jit(solution)/shard_map/all_gather | solution.py:663
  11.9 467.3 %all-gather.45.cloned.1.call-start = ((), (), s32[]{:S(2)}) async-start(), calls=%async_computation.28 | async-start | bytes 1769472 | tf_op jit(solution)/shard_map/all_gather | solution.py:664
  12.8 491.8 %all-gather.47.cloned.1.call-start = ((), (), s32[]{:S(2)}) async-start(), calls=%async_computation.29 | async-start | bytes 1179648 | tf_op jit(solution)/shard_map/all_gather | solution.py:666
  13.6 581.4 %all-gather.49.cloned.1.call-start = ((), (), s32[]{:S(2)}) async-start(), calls=%async_computation.30 | async-start | bytes 2359296 | tf_op jit(solution)/shard_map/all_gather | solution.py:671
  14.6 587.0 %all-gather.51.cloned.1.call-start = ((), (), s32[]{:S(2)}) async-start(), calls=%async_computation.31 | async-start | bytes 2359296 | tf_op jit(solution)/shard_map/all_gather | solution.py:672
  15.5 591.5 %all-gather.53.cloned.1.call-start = ((), (), s32[]{:S(2)}) async-start(), calls=%async_computation.32 | async-start | bytes 2359296 | tf_op jit(solution)/shard_map/all_gather | solution.py:662
  16.3 595.8 %all-gather.55.cloned.1.call-start = ((), (), s32[]{:S(2)}) async-start(), calls=%async_computation.33 | async-start | bytes 2359296 | tf_op jit(solution)/shard_map/all_gather | solution.py:663
  17.0 600.7 %all-gather.57.cloned.1.call-start = ((), (), s32[]{:S(2)}) async-start(), calls=%async_computation.34 | async-start | bytes 1769472 | tf_op jit(solution)/shard_map/all_gather | solution.py:664
  17.6 629.2 %all-gather.59.cloned.1.call-start = ((), (), s32[]{:S(2)}) async-start(), calls=%async_computation.35 | async-start | bytes 1179648 | tf_op jit(solution)/shard_map/all_gather | solution.py:666
  18.3 721.8 %all-gather.61.cloned.1.call-start = ((), (), s32[]{:S(2)}) async-start(), calls=%async_computation.36 | async-start | bytes 2359296 | tf_op jit(solution)/shard_map/all_gather | solution.py:671
  18.9 727.5 %all-gather.63.cloned.1.call-start = ((), (), s32[]{:S(2)}) async-start(), calls=%async_computation.37 | async-start | bytes 2359296 | tf_op jit(solution)/shard_map/all_gather | solution.py:672
  19.6 1129.4 %reduce-scatter.47.cloned.1.call-start = ((), (), s32[]{:S(2)}) async-start(), calls=%async_computation.40 | async-start | bytes 921600
  49.3 413.1 %copy-start.140 = (f32[1,2,2,128]{3,1,2,0:T(2,128)}, f32[1,2,2,128]{3,1,2,0:T(2,128)S(1)}, u32[]{:S(2)}) copy-start(f32[1,2,2,128]{3,1,2,0:T(2,128)S(1)} %copy.216) | copy-start | bytes 6148
  49.6 116.2 %copy-start.162 = (f32[1,2,2,128]{3,1,2,0:T(2,128)}, f32[1,2,2,128]{3,1,2,0:T(2,128)S(1)}, u32[]{:S(2)}) copy-start(f32[1,2,2,128]{3,1,2,0:T(2,128)S(1)} %copy.217) | copy-start | bytes 6148
  49.6 412.7 %copy-start.142 = (f32[512]{0:T(512)}, f32[512]{0:T(512)S(1)}, u32[]{:S(2)}) copy-start(f32[512]{0:T(512)S(1)} %rsqrt.116) | copy-start | bytes 6148
  118.0 344.3 %copy-start.138 = (f32[512]{0:T(512)}, f32[512]{0:T(512)S(1)}, u32[]{:S(2)}) copy-start(f32[512]{0:T(512)S(1)} %get-tuple-element.164) | copy-start | bytes 6148
  118.0 361.2 %copy-start.217 = (f32[512]{0:T(512)}, f32[512]{0:T(512)S(1)}, u32[]{:S(2)}) copy-start(f32[512]{0:T(512)S(1)} %get-tuple-element.163) | copy-start | bytes 6148
  118.0 386.5 %copy-start.165 = (f32[512]{0:T(512)}, f32[512]{0:T(512)S(1)}, u32[]{:S(2)}) copy-start(f32[512]{0:T(512)S(1)} %get-tuple-element.162) | copy-start | bytes 6148
  165.8 342.5 %copy-start.181 = (f32[512]{0:T(512)}, f32[512]{0:T(512)S(1)}, u32[]{:S(2)}) copy-start(f32[512]{0:T(512)S(1)} %get-tuple-element.165) | copy-start | bytes 6148
  165.8 342.5 %copy-start.183 = (f32[512]{0:T(512)}, f32[512]{0:T(512)S(1)}, u32[]{:S(2)}) copy-start(f32[512]{0:T(512)S(1)} %get-tuple-element.166) | copy-start | bytes 6148
  165.8 342.5 %copy-start.185 = (f32[512]{0:T(512)}, f32[512]{0:T(512)S(1)}, u32[]{:S(2)}) copy-start(f32[512]{0:T(512)S(1)} %get-tuple-element.167) | copy-start | bytes 6148
  165.8 342.5 %copy-start.187 = (f32[512]{0:T(512)}, f32[512]{0:T(512)S(1)}, u32[]{:S(2)}) copy-start(f32[512]{0:T(512)S(1)} %get-tuple-element.168) | copy-start | bytes 6148
  165.8 342.5 %copy-start.189 = (f32[512]{0:T(512)}, f32[512]{0:T(512)S(1)}, u32[]{:S(2)}) copy-start(f32[512]{0:T(512)S(1)} %get-tuple-element.169) | copy-start | bytes 6148
  165.8 342.5 %copy-start.191 = (f32[512]{0:T(512)}, f32[512]{0:T(512)S(1)}, u32[]{:S(2)}) copy-start(f32[512]{0:T(512)S(1)} %get-tuple-element.170) | copy-start | bytes 6148
  165.9 342.5 %copy-start.193 = (f32[512]{0:T(512)}, f32[512]{0:T(512)S(1)}, u32[]{:S(2)}) copy-start(f32[512]{0:T(512)S(1)} %get-tuple-element.171) | copy-start | bytes 6148
  165.9 342.5 %copy-start.195 = (f32[512]{0:T(512)}, f32[512]{0:T(512)S(1)}, u32[]{:S(2)}) copy-start(f32[512]{0:T(512)S(1)} %get-tuple-element.172) | copy-start | bytes 6148
  165.9 342.5 %copy-start.197 = (f32[512]{0:T(512)}, f32[512]{0:T(512)S(1)}, u32[]{:S(2)}) copy-start(f32[512]{0:T(512)S(1)} %get-tuple-element.173) | copy-start | bytes 6148
  207.3 679.8 %copy-start.134 = (f32[512]{0:T(512)}, f32[512]{0:T(512)S(1)}, u32[]{:S(2)}) copy-start(f32[512]{0:T(512)S(1)} %get-tuple-element.146) | copy-start | bytes 6148
  239.0 154.0 %copy-start.130 = (bf16[64,640]{1,0:T(8,128)(2,1)S(1)}, bf16[64,640]{1,0:T(8,128)(2,1)}, u32[]{:S(2)}) copy-start(bf16[64,640]{1,0:T(8,128)(2,1)} %param.38) | copy-start | bytes 245764
  255.4 170.6 %copy-start.129 = (bf16[80,640]{1,0:T(8,128)(2,1)S(1)}, bf16[80,640]{1,0:T(8,128)(2,1)}, u32[]{:S(2)}) copy-start(bf16[80,640]{1,0:T(8,128)(2,1)} %param.39) | copy-start | bytes 307204
  255.4 203.4 %copy-start.251 = (s32[2,24]{1,0:T(2,128)S(1)}, s32[2,24]{1,0:T(2,128)}, u32[]{:S(2)}) copy-start(s32[2,24]{1,0:T(2,128)} %param.23) | copy-start | bytes 580
  458.8 292.4 %copy-start.3 = (s32[2,25]{1,0:T(2,128)}, s32[2,25]{1,0:T(2,128)S(1)}, u32[]{:S(2)}) copy-start(s32[2,25]{1,0:T(2,128)S(1)} %concatenate.6.labels_ref) | copy-start | bytes 604
  508.3 83.0 %copy-start.237 = (bf16[512]{0:T(512)(128)(2,1)S(1)}, bf16[512]{0:T(512)(128)(2,1)}, u32[]{:S(2)}) copy-start(bf16[512]{0:T(512)(128)(2,1)} %copy-done.236) | copy-start | bytes 3076
  510.4 83.0 %copy-start.16 = (f32[2,256,512]{2,1,0:T(8,128)}, f32[2,256,512]{2,1,0:T(8,128)S(1)}, u32[]{:S(2)}) copy-start(f32[2,256,512]{2,1,0:T(8,128)S(1)} %get-tuple-element.226) | copy-start | bytes 3145732
  510.4 82.4 %copy-start.239 = (f32[512]{0:T(512)S(1)}, f32[512]{0:T(512)}, u32[]{:S(2)}) copy-start(f32[512]{0:T(512)} %convert_element_type.401) | copy-start | bytes 6148
  645.5 301.6 %copy-start.146 = (f32[512]{0:T(512)}, f32[512]{0:T(512)S(1)}, u32[]{:S(2)}) copy-start(f32[512]{0:T(512)S(1)} %broadcast_multiply_fusion.20) | copy-start | bytes 6148
  646.7 300.3 %copy-start.177 = (f32[512]{0:T(512)}, f32[512]{0:T(512)S(1)}, u32[]{:S(2)}) copy-start(f32[512]{0:T(512)S(1)} %fusion.172) | copy-start | bytes 6148
  650.8 84.9 %copy-start.235 = (bf16[512]{0:T(512)(128)(2,1)S(1)}, bf16[512]{0:T(512)(128)(2,1)}, u32[]{:S(2)}) copy-start(bf16[512]{0:T(512)(128)(2,1)} %copy-done.234) | copy-start | bytes 3076
  653.9 84.0 %copy-start.243 = (f32[512]{0:T(512)S(1)}, f32[512]{0:T(512)}, u32[]{:S(2)}) copy-start(f32[512]{0:T(512)} %convert_element_type.403) | copy-start | bytes 6148
  653.9 84.0 %copy-start.245 = (f32[512]{0:T(512)S(1)}, f32[512]{0:T(512)}, u32[]{:S(2)}) copy-start(f32[512]{0:T(512)} %convert_element_type.402) | copy-start | bytes 6148
  738.9 154.4 %copy-start.175 = (f32[512]{0:T(512)}, f32[512]{0:T(512)S(1)}, u32[]{:S(2)}) copy-start(f32[512]{0:T(512)S(1)} %broadcast_multiply_fusion.19) | copy-start | bytes 6148
  740.1 153.1 %copy-start.231 = (f32[512]{0:T(512)}, f32[512]{0:T(512)S(1)}, u32[]{:S(2)}) copy-start(f32[512]{0:T(512)S(1)} %fusion.173) | copy-start | bytes 6148
  750.2 136.9 %copy-start.10 = (f32[512,512]{1,0:T(8,128)}, f32[512,512]{1,0:T(8,128)S(1)}, u32[]{:S(2)}) copy-start(f32[512,512]{1,0:T(8,128)S(1)} %get-tuple-element.310) | copy-start | bytes 3145732
  750.5 136.6 %copy-start.136 = (f32[512]{0:T(512)}, f32[512]{0:T(512)S(1)}, u32[]{:S(2)}) copy-start(f32[512]{0:T(512)S(1)} %fusion.174) | copy-start | bytes 6148
  968.7 182.1 %reduce-scatter.37.cloned.1.call-start = ((), (), s32[]{:S(2)}) async-start(), calls=%async_computation.23 | async-start | bytes 737280 | tf_op jit(solution)/shard_map/reduce_scatter | solution.py:595
  999.8 157.1 %reduce-scatter.31.cloned.1.call-start = ((), (), s32[]{:S(2)}) async-start(), calls=%async_computation.20 | async-start | bytes 1179648 | tf_op jit(solution)/shard_map/reduce_scatter | solution.py:586
  1052.2 170.8 %reduce-scatter.27.cloned.1.call-start = ((), (), s32[]{:S(2)}) async-start(), calls=%async_computation.18 | async-start | bytes 1179648 | tf_op jit(solution)/shard_map/reduce_scatter | solution.py:577
  1065.5 224.0 %reduce-scatter.39.cloned.1.call-start = ((), (), s32[]{:S(2)}) async-start(), calls=%async_computation.24 | async-start | bytes 1474560 | tf_op jit(solution)/shard_map/reduce_scatter | solution.py:601
  1066.1 293.6 %reduce-scatter.29.cloned.1.call-start = ((), (), s32[]{:S(2)}) async-start(), calls=%async_computation.19 | async-start | bytes 2359296 | tf_op jit(solution)/shard_map/reduce_scatter | solution.py:580
  1071.5 365.2 %reduce-scatter.25.cloned.1.call-start = ((), (), s32[]{:S(2)}) async-start(), calls=%async_computation.17 | async-start | bytes 3538944 | tf_op jit(solution)/shard_map/reduce_scatter | solution.py:574
  1093.4 434.0 %reduce-scatter.35.cloned.1.call-start = ((), (), s32[]{:S(2)}) async-start(), calls=%async_computation.22 | async-start | bytes 4718592 | tf_op jit(solution)/shard_map/reduce_scatter | solution.py:592
  1101.1 518.0 %reduce-scatter.33.cloned.1.call-start = ((), (), s32[]{:S(2)}) async-start(), calls=%async_computation.21 | async-start | bytes 4718592 | tf_op jit(solution)/shard_map/reduce_scatter | solution.py:589
  1109.2 601.3 %reduce-scatter.23.cloned.1.call-start = ((), (), s32[]{:S(2)}) async-start(), calls=%async_computation.16 | async-start | bytes 4718592 | tf_op jit(solution)/shard_map/reduce_scatter | solution.py:571
  1121.5 680.7 %reduce-scatter.21.cloned.1.call-start = ((), (), s32[]{:S(2)}) async-start(), calls=%async_computation.15 | async-start | bytes 4718592 | tf_op jit(solution)/shard_map/reduce_scatter | solution.py:568
  1132.9 733.8 %reduce-scatter.43.cloned.1.call-start = ((), (), s32[]{:S(2)}) async-start(), calls=%async_computation.38 | async-start | bytes 147456
  1147.1 783.2 %reduce-scatter.45.cloned.1.call-start = ((), (), s32[]{:S(2)}) async-start(), calls=%async_computation.39 | async-start | bytes 147456
  1148.3 653.9 %copy-start.213 = (f32[512]{0:T(512)S(1)}, f32[512]{0:T(512)}, u32[]{:S(2)}) copy-start(f32[512]{0:T(512)} %copy-done.212) | copy-start | bytes 6148
  1148.3 653.9 %copy-start.215 = (f32[512]{0:T(512)S(1)}, f32[512]{0:T(512)}, u32[]{:S(2)}) copy-start(f32[512]{0:T(512)} %copy-done.214) | copy-start | bytes 6148
  1148.3 655.2 %copy-start.61 = (f32[512,512]{1,0:T(8,128)S(1)}, f32[512,512]{1,0:T(8,128)}, u32[]{:S(2)}) copy-start(f32[512,512]{1,0:T(8,128)} %copy-done.60) | copy-start | bytes 3145732
  1148.3 655.2 %copy-start.65 = (f32[512,512]{1,0:T(8,128)S(1)}, f32[512,512]{1,0:T(8,128)}, u32[]{:S(2)}) copy-start(f32[512,512]{1,0:T(8,128)} %copy-done.64) | copy-start | bytes 3145732
  1148.3 839.0 %reduce-scatter.41.cloned.1.call-start = ((), (), s32[]{:S(2)}) async-start(), calls=%async_computation.25 | async-start | bytes 184320 | tf_op jit(solution)/shard_map/reduce_scatter | solution.py:604
  1148.9 916.2 %all-reduce.57.cloned.1.call-start = ((), (), s32[]{:S(2)}) async-start(), calls=%async_computation.41 | async-start | bytes 6848512 | tf_op jit(solution)/shard_map/psum | solution.py:620
  (232 other events, 1151.1 us)
Sparse Core Ops, SparseCore 0:
  10.2 44.5 all-gather.38
  57.5 50.6 all-gather.40
  110.9 50.0 all-gather.42
  163.6 44.2 all-gather.44
  209.9 41.0 all-gather.46
  253.6 56.3 all-gather.48
  312.7 57.1 all-gather.50
  372.6 54.8 all-gather.52
  430.2 50.0 all-gather.54
  482.9 43.6 all-gather.56
  529.3 39.1 all-gather.58
  570.5 47.9 all-gather.60
  620.7 47.1 all-gather.62
  968.8 57.0 reduce-scatter.46
  1029.9 61.1 reduce-scatter.36
  1094.4 62.4 reduce-scatter.30
  1160.5 62.3 reduce-scatter.26
  1226.2 63.2 reduce-scatter.38
  1293.0 66.5 reduce-scatter.28
  1363.1 73.5 reduce-scatter.24
  1440.4 86.9 reduce-scatter.34
  1531.4 87.6 reduce-scatter.32
  1622.8 87.6 reduce-scatter.22
  1714.4 87.8 reduce-scatter.20
  1806.1 60.5 reduce-scatter.42
  1870.5 59.8 reduce-scatter.44
  1934.0 53.3 reduce-scatter.40
  1991.1 73.9 all-reduce.56

commit v2 on v1

--- a/solution.py
+++ b/solution.py
@@ -1,5 +1,4 @@
-import functools
-from functools import partial
+from functools import partial, reduce
 
 import jax
 import jax.numpy as jnp
@@ -148,7 +147,7 @@
     total = wide + 16
     reach = feats.shape[0] - 3
     return pl.pallas_call(
-        functools.partial(lattice_kernel, slots),
+        partial(lattice_kernel, slots),
         out_shape=(jax.ShapeDtypeStruct(feats.shape, jnp.float32), jax.ShapeDtypeStruct((8, 128), jnp.float32)),
         in_specs=[pl.BlockSpec(memory_space=pltpu.VMEM), pl.BlockSpec(memory_space=pltpu.SMEM), pl.BlockSpec(memory_space=pltpu.SMEM)],
         out_specs=(pl.BlockSpec(memory_space=pltpu.VMEM),) * 2,
@@ -186,13 +185,13 @@
             tok_ref[j%2,c:c+CHUNK,:]=t
             tops.append(fold8(t,jnp.maximum))
         dl=nn(wt_ref[vocab:,:],hid)[:8]
-        top=jnp.max(functools.reduce(jnp.maximum,tops),0,keepdims=True)
+        top=jnp.max(reduce(jnp.maximum,tops),0,keepdims=True)
         sums=[]
         for c in range(0,vocab,CHUNK):
             e=jnp.exp(tok_ref[j%2,c:c+CHUNK,:]-top)
             p_ref[0,j,c:c+CHUNK,:]=e.astype(jnp.bfloat16)
             sums.append(fold8(e,jnp.add))
-        total=jnp.sum(functools.reduce(jnp.add,sums),0,keepdims=True)
+        total=jnp.sum(reduce(jnp.add,sums),0,keepdims=True)
         lse=top+jnp.log(total)
         row=u*32+k
         feats_ref[0,pl.ds(row,1),:]=tok_ref[j%2,0:1,:]-lse
@@ -258,7 +257,7 @@
         fix(0)
         fix(pl.multiple_of((label//16)*16,16))
         gd=[grads_ref[2+e,pl.ds(row,1),:] for e in range(durs)]
-        gsum=functools.reduce(jnp.add,gd)
+        gsum=reduce(jnp.add,gd)
         at=lax.broadcasted_iota(jnp.int32,(16,frames),0)
         dd=jnp.zeros((16,frames),jnp.float32)
         for e in range(durs):
@@ -306,6 +305,436 @@
     )(labels,enc_t,pred_t,w,feats,grads,p)
 
 
+MESH=pl.DeviceIdType.MESH
+QA=64
+QB=64
+HALF=2*QA+QB
+TILE=2*HALF
+
+def place():
+    dp=lax.axis_index("dp"); fs=lax.axis_index("fsdp")
+    return dp, fs, dp//2, dp%2, fs//2, fs%2
+
+def greet(n1, dp, fs, a, c, i1, i2):
+    barrier=pltpu.get_barrier_semaphore()
+    for d in range(1,n1):
+        pl.semaphore_signal(barrier,inc=1,device_id=(dp,lax.rem(i1+d,n1)*2+i2),device_id_type=MESH)
+    pl.semaphore_signal(barrier,inc=1,device_id=(dp,i1*2+1-i2),device_id_type=MESH)
+    pl.semaphore_signal(barrier,inc=1,device_id=((1-a)*2+c,fs),device_id_type=MESH)
+    pl.semaphore_signal(barrier,inc=1,device_id=(a*2+1-c,fs),device_id_type=MESH)
+    pl.semaphore_wait(barrier,n1+2)
+
+def remote(s, d, ss, rs, dev):
+    return pltpu.make_async_remote_copy(src_ref=s,dst_ref=d,send_sem=ss,recv_sem=rs,device_id=dev,device_id_type=MESH)
+
+def rows(base, size):
+    return pl.ds(pl.multiple_of(base,16),size)
+
+def gather_kernel(n1, tiles, lag, src, out, own_sem, sz, rz, sy, ry, sx, rx, sc, rc):
+    dp,fs,a,c,i1,i2=place()
+    greet(n1,dp,fs,a,c,i1,i2)
+    ypeer=(dp,i1*2+1-i2); xpeer=((1-a)*2+c,fs); cpeer=(a*2+1-c,fs)
+    items=n1*tiles
+    def main(t): return rows(t*TILE+c*HALF+a*QA,QA+QB)
+    def quarter(t,aa): return rows(t*TILE+c*HALF+aa*(QA+QB),QA)
+    def half(t,cc): return rows(t*TILE+cc*HALF,HALF)
+    def of(m): return m//n1, m%n1, lax.rem(i1+n1-m%n1,n1)
+    def zcopy(t,d):
+        j=lax.rem(i1+d,n1)
+        return remote(src.at[main(t),:],out.at[fs,main(t),:],sz.at[t,d],rz.at[t,i1],(dp,j*2+i2))
+    def zin(t,j):
+        return remote(src.at[main(t),:],out.at[j*2+i2,main(t),:],sz.at[t,0],rz.at[t,j],ypeer)
+    def ycopy(t,j):
+        s=j*2+i2
+        return remote(out.at[s,main(t),:],out.at[s,main(t),:],sy.at[t,j],ry.at[t,j],ypeer)
+    def ycopy_own(t):
+        return remote(src.at[main(t),:],out.at[fs,main(t),:],sy.at[t,i1],ry.at[t,i1],ypeer)
+    def yin(t,j):
+        s=j*2+1-i2
+        return remote(src.at[main(t),:],out.at[s,main(t),:],sy.at[t,j],ry.at[t,j],ypeer)
+    def xcopy(t,s):
+        return remote(out.at[s,quarter(t,a),:],out.at[s,quarter(t,a),:],sx.at[t,s],rx.at[t,s],xpeer)
+    def xin(t,s):
+        return remote(src.at[quarter(t,a),:],out.at[s,quarter(t,1-a),:],sx.at[t,s],rx.at[t,s],xpeer)
+    def ccopy(t,s):
+        return remote(out.at[s,half(t,c),:],out.at[s,half(t,c),:],sc.at[t,s],rc.at[t,s],cpeer)
+    def cin(t,s):
+        return remote(src.at[half(t,c),:],out.at[s,half(t,1-c),:],sc.at[t,s],rc.at[t,s],cpeer)
+    local=pltpu.make_async_copy(src,out.at[fs],own_sem)
+    local.start()
+
+    def tick(tau,carry):
+        @pl.when(tau<items)
+        def _():
+            t,d,j=of(tau)
+            @pl.when(d>0)
+            def _(): zcopy(t,d).start()
+            @pl.when(d==0)
+            def _(): ycopy_own(t).start()
+        m1=tau-lag
+        @pl.when((m1>=0)&(m1<items))
+        def _():
+            t,d,j=of(m1)
+            @pl.when(d>0)
+            def _():
+                zin(t,j).wait_recv()
+                ycopy(t,j).start()
+                xcopy(t,j*2+i2).start()
+        m2=tau-2*lag
+        @pl.when((m2>=0)&(m2<items))
+        def _():
+            t,d,j=of(m2)
+            yin(t,j).wait_recv()
+            xcopy(t,j*2+1-i2).start()
+        m3=tau-3*lag
+        @pl.when((m3>=0)&(m3<items))
+        def _():
+            t,d,j=of(m3)
+            @pl.when(d>0)
+            def _():
+                xin(t,j*2+i2).wait_recv()
+                ccopy(t,j*2+i2).start()
+            xin(t,j*2+1-i2).wait_recv()
+            ccopy(t,j*2+1-i2).start()
+        return carry
+    lax.fori_loop(0,items+3*lag,tick,0)
+    local.wait()
+    def finish(m,carry):
+        t,d,j=of(m)
+        @pl.when(d>0)
+        def _():
+            cin(t,j*2+i2).wait_recv()
+            zcopy(t,d).wait_send()
+            xcopy(t,j*2+i2).wait_send()
+            ccopy(t,j*2+i2).wait_send()
+        cin(t,j*2+1-i2).wait_recv()
+        ycopy(t,j).wait_send()
+        xcopy(t,j*2+1-i2).wait_send()
+        ccopy(t,j*2+1-i2).wait_send()
+        return carry
+    lax.fori_loop(0,items,finish,0)
+
+def gather(packed, collective_id, lag=1):
+    n=lax.axis_size("fsdp"); n1=n//2
+    tiles=packed.shape[0]//TILE
+    dma=pltpu.SemaphoreType.DMA
+    return pl.pallas_call(
+        partial(gather_kernel,n1,tiles,lag),
+        out_shape=jax.ShapeDtypeStruct((n,)+packed.shape,packed.dtype),
+        in_specs=[pl.BlockSpec(memory_space=pl.ANY)],
+        out_specs=pl.BlockSpec(memory_space=pl.ANY),
+        scratch_shapes=[dma]+[dma((tiles,n1))]*4+[dma((tiles,n))]*4,
+        compiler_params=pltpu.CompilerParams(collective_id=collective_id,has_side_effects=True),
+        name="gather_weights",
+    )(packed)
+
+def scatter_kernel(n1, tiles, lag, src, out, own, gc, gx, gy, gz, gf, fin,
+                   lo, sc, rc, sx, rx, sy, ry, sz, rz, sf, rf, se, re, wo):
+    dp,fs,a,c,i1,i2=place()
+    greet(n1,dp,fs,a,c,i1,i2)
+    ypeer=(dp,i1*2+1-i2); xpeer=((1-a)*2+c,fs); cpeer=(a*2+1-c,fs)
+    items=n1*tiles
+    main=rows(a*QA,QA+QB)
+    def quarter(aa): return rows(aa*(QA+QB),QA)
+    middle=pl.ds(QA,QB)
+    def of(m): return m//n1, lax.rem(i1+1+m%n1,n1)
+    def load(t,s): return pltpu.make_async_copy(src.at[s,rows(t*TILE+c*HALF,HALF),:],own.at[t,s],lo.at[t,s])
+    def ccopy(t,s): return remote(src.at[s,rows(t*TILE+(1-c)*HALF,HALF),:],gc.at[t,s],sc.at[t,s],rc.at[t,s],cpeer)
+    def xcopy(t,s): return remote(own.at[t,s,quarter(1-a),:],gx.at[t,s],sx.at[t,s],rx.at[t,s],xpeer)
+    def ycopy(t,j): return remote(own.at[t,j*2+1-i2,main,:],gy.at[t,j],sy.at[t,j],ry.at[t,j],ypeer)
+    def zcopy(t,j): return remote(own.at[t,j*2+i2,main,:],gz.at[t,i1],sz.at[t,j],rz.at[t,i1],(dp,j*2+i2))
+    def zin(t,j): return remote(own.at[t,fs,main,:],gz.at[t,j],sz.at[t,j],rz.at[t,j],ypeer)
+    def fcopy(t): return remote(own.at[t,fs,main,:],gf.at[t],sf.at[t],rf.at[t],xpeer)
+    def ecopy(t): return remote(fin.at[t,c],fin.at[t,c],se.at[t],re.at[t],cpeer)
+    def ein(t): return remote(fin.at[t,1-c],fin.at[t,1-c],se.at[t],re.at[t],cpeer)
+    def store(t): return pltpu.make_async_copy(fin.at[t],out.at[t],wo.at[t])
+
+    def tick(tau,carry):
+        def at(shift,body):
+            m=tau-shift
+            @pl.when((m>=0)&(m<items))
+            def _(): body(*of(m))
+        def at_tile(shift,body):
+            m=tau-shift
+            @pl.when((m>=0)&(m<items)&(lax.rem(m+n1,n1)==n1-1))
+            def _(): body(m//n1)
+        def stage_c(t,j):
+            for i in range(2):
+                load(t,j*2+i).start(); ccopy(t,j*2+i).start()
+        def stage_x(t,j):
+            for i in range(2):
+                s=j*2+i
+                load(t,s).wait(); ccopy(t,s).wait_recv()
+                own[t,s]=own[t,s]+gc[t,s]
+                xcopy(t,s).start()
+        def stage_y(t,j):
+            for i in range(2):
+                s=j*2+(1-i2 if i==0 else i2)
+                xcopy(t,s).wait_recv()
+                own[t,s,quarter(a),:]=own[t,s,quarter(a),:]+gx[t,s]
+                if i==0: ycopy(t,j).start()
+        def stage_z(t,j):
+            s=j*2+i2
+            ycopy(t,j).wait_recv()
+            own[t,s,main,:]=own[t,s,main,:]+gy[t,j]
+            @pl.when(j!=i1)
+            def _(): zcopy(t,j).start()
+        def stage_f(t):
+            total=own[t,fs,main,:].astype(jnp.float32)
+            for d in range(1,n1):
+                j=lax.rem(i1+n1-d,n1)
+                zin(t,j).wait_recv()
+                total=total+gz[t,j].astype(jnp.float32)
+            own[t,fs,main,:]=total.astype(jnp.bfloat16)
+            fcopy(t).start()
+        def stage_e(t):
+            fcopy(t).wait_recv()
+            fin[t,c,quarter(a),:]=own[t,fs,quarter(a),:]
+            fin[t,c,quarter(1-a),:]=gf[t,rows((1-a)*QB,QA),:]
+            fin[t,c,middle,:]=own[t,fs,middle,:]+gf[t,rows(a*QA,QB),:]
+            ecopy(t).start()
+        def stage_o(t):
+            ein(t).wait_recv()
+            ecopy(t).wait_send()
+            store(t).start()
+        at(0,stage_c); at(lag,stage_x); at(2*lag,stage_y); at(3*lag,stage_z)
+        at_tile(3*lag+1,stage_f); at_tile(4*lag+1,stage_e); at_tile(5*lag+1,stage_o)
+        return carry
+    lax.fori_loop(0,items+5*lag+1,tick,0)
+    def finish(m,carry):
+        t,j=of(m)
+        for i in range(2):
+            ccopy(t,j*2+i).wait_send(); xcopy(t,j*2+i).wait_send()
+        ycopy(t,j).wait_send()
+        @pl.when(j!=i1)
+        def _(): zcopy(t,j).wait_send()
+        return carry
+    lax.fori_loop(0,items,finish,0)
+    def finish_tile(t,carry):
+        fcopy(t).wait_send(); store(t).wait()
+        return carry
+    lax.fori_loop(0,tiles,finish_tile,0)
+
+def scatter(grads, collective_id, lag=2):
+    n=lax.axis_size("fsdp"); n1=n//2
+    tiles=grads.shape[1]//TILE; w=grads.shape[2]
+    dma=pltpu.SemaphoreType.DMA
+    bf=jnp.bfloat16
+    out=pl.pallas_call(
+        partial(scatter_kernel,n1,tiles,lag),
+        out_shape=jax.ShapeDtypeStruct((tiles,2,HALF,w),bf),
+        in_specs=[pl.BlockSpec(memory_space=pl.ANY)],
+        out_specs=pl.BlockSpec(memory_space=pl.ANY),
+        scratch_shapes=[pltpu.VMEM((tiles,n,HALF,w),bf),pltpu.VMEM((tiles,n,HALF,w),bf),pltpu.VMEM((tiles,n,QA,w),bf),
+            pltpu.VMEM((tiles,n1,QA+QB,w),bf),pltpu.VMEM((tiles,n1,QA+QB,w),bf),pltpu.VMEM((tiles,QA+QB,w),bf),pltpu.VMEM((tiles,2,HALF,w),bf)]
+            +[dma((tiles,n))]*5+[dma((tiles,n1))]*4+[dma((tiles,))]*5,
+        compiler_params=pltpu.CompilerParams(collective_id=collective_id,has_side_effects=True,vmem_limit_bytes=56<<20),
+        name="scatter_grads",
+    )(grads)
+    return out.reshape(tiles*TILE,w)
+
+
+def pooled(parts):
+    counts = [x[8:9] for x in parts]
+    count = sum(counts[1:], counts[0])
+    mean = sum((x[0:4] * n for x, n in zip(parts[1:], counts[1:])), parts[0][0:4] * counts[0]) / count
+    dev = jnp.zeros_like(mean)
+    for x, n in zip(parts, counts):
+        gap = x[0:4] - mean
+        dev = dev + (x[4:8] + gap * gap * n)
+    return mean, dev, count
+
+
+def exchange_kernel(kind, groups, n, x_ref, out_ref, near, far, s1, r1, s2, r2):
+    dp = lax.axis_index("dp")
+    fs = lax.axis_index("fsdp")
+    barrier = pltpu.get_barrier_semaphore()
+    for d in range(1, groups):
+        pl.semaphore_signal(barrier, inc=1, device_id=(lax.rem(dp + d, groups), fs), device_id_type=MESH)
+    for d in range(1, n):
+        pl.semaphore_signal(barrier, inc=1, device_id=(dp, lax.rem(fs + d, n)), device_id_type=MESH)
+    pl.semaphore_wait(barrier, groups + n - 2)
+
+    def merge(ref, members):
+        if kind == "sum":
+            total = ref[0]
+            for i in range(1, members):
+                total = total + ref[i]
+            return total
+        mean, dev, count = pooled([ref[i] for i in range(members)])
+        return jnp.concatenate([mean, dev, jnp.broadcast_to(count, (8, 128))], 0)
+
+    near[dp] = x_ref[...]
+    first = []
+    for d in range(1, groups):
+        cp = remote(near.at[dp], near.at[dp], s1.at[d], r1.at[dp], (lax.rem(dp + d, groups), fs))
+        cp.start()
+        first.append(cp)
+    for d in range(1, groups):
+        other = lax.rem(dp + d, groups)
+        remote(near.at[dp], near.at[other], s1.at[d], r1.at[other], (other, fs)).wait_recv()
+    far[fs] = merge(near, groups)
+    for d in range(1, n):
+        cp = remote(far.at[fs], far.at[fs], s2.at[d], r2.at[fs], (dp, lax.rem(fs + d, n)))
+        cp.start()
+        first.append(cp)
+    for d in range(1, n):
+        other = lax.rem(fs + d, n)
+        remote(far.at[fs], far.at[other], s2.at[d], r2.at[other], (dp, other)).wait_recv()
+    out_ref[...] = merge(far, n)
+    for cp in first:
+        cp.wait_send()
+
+
+def exchange(x, kind, collective_id):
+    n = lax.axis_size("fsdp")
+    groups = lax.axis_size("dp")
+    dma = pltpu.SemaphoreType.DMA
+    return pl.pallas_call(
+        partial(exchange_kernel, kind, groups, n),
+        out_shape=jax.ShapeDtypeStruct(x.shape, x.dtype),
+        in_specs=[pl.BlockSpec(memory_space=pltpu.VMEM)],
+        out_specs=pl.BlockSpec(memory_space=pltpu.VMEM),
+        scratch_shapes=[
+            pltpu.VMEM((groups,) + x.shape, x.dtype),
+            pltpu.VMEM((n,) + x.shape, x.dtype),
+            dma((groups,)), dma((groups,)), dma((n,)), dma((n,)),
+        ],
+        compiler_params=pltpu.CompilerParams(collective_id=collective_id, has_side_effects=True),
+        name="exchange_" + kind,
+    )(x)
+
+
+def global_stats(depthwise, valid_rows, collective_id):
+    width = depthwise.shape[1]
+    count = jnp.sum(valid_rows)
+    mean = jnp.sum(depthwise * valid_rows, 0) / count
+    gap = (depthwise - mean) * valid_rows
+    dev = jnp.sum(gap * gap, 0)
+    x = jnp.concatenate([mean.reshape(-1, 128), dev.reshape(-1, 128), jnp.full((8, 128), count)], 0)
+    x = exchange(x, "pool", collective_id)
+    count = x[8, 0]
+    return x[0:4].reshape(width), lax.rsqrt(x[4:8].reshape(width) / count + EPS), count
+
+
+def global_sums(one, two, collective_id):
+    width = one.shape[0]
+    x = jnp.concatenate([one.reshape(-1, 128), two.reshape(-1, 128), jnp.zeros((8, 128))], 0)
+    x = exchange(x, "sum", collective_id)
+    return x[0:4].reshape(width), x[4:8].reshape(width)
+
+
+WIDE = 512
+
+
+def to_blocks(w):
+    rows, cols = w.shape
+    return jnp.swapaxes(w.reshape(rows, cols // WIDE, WIDE), 0, 1).reshape(-1, WIDE)
+
+
+def from_blocks(part, cols):
+    n, height, _ = part.shape
+    blocks = cols // WIDE
+    return jnp.swapaxes(part.reshape(n, blocks, height // blocks, WIDE), 1, 2).reshape(-1, cols)
+
+
+def padded(parts):
+    rows = sum(p.shape[-2] for p in parts)
+    short = -rows % TILE
+    shape = parts[0].shape[:-2] + (short, WIDE)
+    return jnp.concatenate(parts + [jnp.zeros(shape, jnp.bfloat16)], -2)
+
+
+def pack_layer(mats, smalls):
+    f_in, f_out, w_joint, w_proj, p_in, p_out, s_in, s_out = mats
+    small = jnp.concatenate(smalls, 0)
+    small = jnp.pad(small, ((0, 16 - small.shape[0]), (0, WIDE - small.shape[1])))
+    return [to_blocks(f_in), f_out, to_blocks(w_joint), w_proj, to_blocks(p_in), p_out, to_blocks(s_in), s_out, small]
+
+
+def pack_joint(w_enc, w_pred, w_tok, w_dur):
+    tall = w_pred.shape[0]
+    rest = jnp.concatenate(
+        [
+            jnp.pad(w_enc[:, WIDE:], ((0, tall - w_enc.shape[0]), (0, 0))),
+            w_pred[:, WIDE:],
+            jnp.pad(w_dur, ((0, 0), (0, 256 - w_dur.shape[1]))),
+        ],
+        1,
+    )
+    return [w_enc[:, :WIDE], w_pred[:, :WIDE], to_blocks(w_tok), rest]
+
+
+def cut(whole, sizes, offset=0):
+    parts = []
+    for size in sizes:
+        parts.append(whole[..., offset : offset + size, :])
+        offset += size
+    return parts
+
+
+def layer_sizes(n, mats):
+    return [m.shape[1] * m.shape[2] // WIDE for m in mats] + [16]
+
+
+def unpack_layer(whole, sizes, mats, width):
+    parts = cut(whole, sizes)
+    full = [
+        from_blocks(p, m.shape[2]) if m.shape[2] != WIDE else p.reshape(-1, WIDE)
+        for p, m in zip(parts, mats)
+    ]
+    shard = width // whole.shape[0]
+    small = jnp.swapaxes(parts[-1][:, :, :shard], 0, 1).reshape(16, width)
+    return full, small
+
+
+def unpack_joint(whole, sizes, w_enc, w_dur):
+    enc, pred, tok, rest = cut(whole, sizes[1:], sizes[0])
+    joint = w_enc.shape[1]
+    low = w_enc.shape[0]
+    w_enc = jnp.concatenate([enc, rest[:, :low, : joint - WIDE]], 2).reshape(-1, joint)
+    w_pred = jnp.concatenate([pred, rest[:, :, 128 : 128 + joint - WIDE]], 2).reshape(-1, joint)
+    return w_enc, w_pred, from_blocks(tok, 1024), rest[:, :, 256:384].reshape(-1, 128)
+
+
+def split_rows(grad, n):
+    rows, cols = grad.shape
+    blocks = cols // WIDE
+    grad = grad.astype(jnp.bfloat16).reshape(n, rows // n, blocks, WIDE)
+    return jnp.swapaxes(grad, 1, 2).reshape(n, -1, WIDE)
+
+
+def pack_layer_grads(mats, gains, depth, n):
+    width = gains.shape[1]
+    small = jnp.concatenate([gains, depth], 0).astype(jnp.bfloat16)
+    small = jnp.swapaxes(small.reshape(-1, n, width // n), 0, 1)
+    small = jnp.pad(small, ((0, 0), (0, 16 - small.shape[1]), (0, WIDE - small.shape[2])))
+    return [split_rows(m, n) for m in mats] + [small]
+
+
+def pack_joint_grads(g_enc, g_pred, g_tok, g_dur, n):
+    def shards(grad):
+        return grad.astype(jnp.bfloat16).reshape(n, -1, grad.shape[1])
+    g_enc, g_pred, g_dur = shards(g_enc), shards(g_pred), shards(g_dur)
+    tall = g_pred.shape[1]
+    rest = jnp.concatenate(
+        [
+            jnp.pad(g_enc[:, :, WIDE:], ((0, 0), (0, tall - g_enc.shape[1]), (0, 0))),
+            g_pred[:, :, WIDE:],
+            g_dur,
+            jnp.zeros((n, tall, 128), jnp.bfloat16),
+        ],
+        2,
+    )
+    return [g_enc[:, :, :WIDE], g_pred[:, :, :WIDE], split_rows(g_tok, n), rest]
+
+
+def shard_from_blocks(part, cols):
+    blocks = cols // WIDE
+    height = part.shape[0] // blocks
+    return jnp.swapaxes(part.reshape(blocks, height, WIDE), 0, 1).reshape(height, cols).astype(jnp.float32)
+
+
 def norm_rows(value, gain):
     centre = jnp.mean(value, -1, keepdims=True)
     centred = value - centre
@@ -442,17 +871,7 @@
     return total.reshape(rows, width)
 
 
-def batch_stats(depthwise, valid_rows):
-    total, count = lax.psum(
-        (jnp.sum(depthwise * valid_rows, 0), jnp.sum(valid_rows)), ("dp", "fsdp")
-    )
-    centre = total / count
-    centred = depthwise - centre
-    spread = lax.psum(jnp.sum(valid_rows * centred * centred, 0), ("dp", "fsdp")) / count
-    return (centre, lax.rsqrt(spread + EPS), count)
-
-
-def run_layer(resid, weights, valid_rows, key_bias):
+def run_layer(resid, weights, valid_rows, key_bias, layer):
     gains, f_in, f_out, w_joint, w_proj, p_in, depth, bn_gain, bn_bias, p_out, s_in, s_out = weights
     gains = gains.astype(jnp.float32)
     utts = key_bias.shape[0]
@@ -461,7 +880,7 @@
     normed_low = norm_rows(second, gains[2]).astype(jnp.bfloat16)
     projected = matmul(normed_low, p_in)
     depthwise = conv_inner(projected, depth.astype(jnp.float32), valid_rows, utts)
-    centre, inv_std, count = batch_stats(depthwise, valid_rows)
+    centre, inv_std, count = global_stats(depthwise, valid_rows, 8 + layer)
     normalized = (depthwise - centre) * inv_std
     shifted = normalized * bn_gain.astype(jnp.float32) + bn_bias.astype(jnp.float32)
     active_low = jax.nn.silu(shifted).astype(jnp.bfloat16)
@@ -488,7 +907,7 @@
     return (output, record)
 
 
-def layer_backward(weights, record, grad_out, valid_rows, key_bias):
+def layer_backward(weights, record, grad_out, valid_rows, key_bias, layer):
     gains, f_in, f_out, w_joint, w_proj, p_in, depth, bn_gain, bn_bias, p_out, s_in, s_out = weights
     gains = gains.astype(jnp.float32)
     utts = key_bias.shape[0]
@@ -516,8 +935,8 @@
     grad_branch = grad_third.astype(jnp.bfloat16)
     grad_p_out = contract_rows(active_low, grad_branch)
     grad_shifted = contract_cols(grad_branch, p_out) * swish_slope(shifted)
-    bias_sum, gain_sum = lax.psum(
-        (jnp.sum(grad_shifted, 0), jnp.sum(grad_shifted * normalized, 0)), ("dp", "fsdp")
+    bias_sum, gain_sum = global_sums(
+        jnp.sum(grad_shifted, 0), jnp.sum(grad_shifted * normalized, 0), 12 + layer
     )
     grad_depthwise = (
         bn_gain.astype(jnp.float32)
@@ -557,69 +976,6 @@
             grad_s_in,
             grad_s_out,
         ),
-    )
-
-
-def reduce_grads(stacked, joint_grads):
-    shares = (
-        lax.psum_scatter(
-            stacked[0].astype(jnp.bfloat16), "fsdp", scatter_dimension=1, tiled=True
-        ).astype(jnp.float32),
-        lax.psum_scatter(
-            stacked[1].astype(jnp.bfloat16), "fsdp", scatter_dimension=1, tiled=True
-        ).astype(jnp.float32),
-        lax.psum_scatter(
-            stacked[2].astype(jnp.bfloat16), "fsdp", scatter_dimension=1, tiled=True
-        ).astype(jnp.float32),
-        lax.psum_scatter(
-            stacked[3].astype(jnp.bfloat16), "fsdp", scatter_dimension=1, tiled=True
-        ).astype(jnp.float32),
-        lax.psum_scatter(
-            stacked[4].astype(jnp.bfloat16), "fsdp", scatter_dimension=1, tiled=True
-        ).astype(jnp.float32),
-        lax.psum_scatter(
-            stacked[5].astype(jnp.bfloat16), "fsdp", scatter_dimension=1, tiled=True
-        ).astype(jnp.float32),
-        lax.psum_scatter(
-            stacked[6].astype(jnp.bfloat16), "fsdp", scatter_dimension=1, tiled=True
-        ).astype(jnp.float32),
-        lax.psum_scatter(
-            stacked[7].astype(jnp.bfloat16), "fsdp", scatter_dimension=1, tiled=True
-        ).astype(jnp.float32),
-        lax.psum_scatter(
-            stacked[8].astype(jnp.bfloat16), "fsdp", scatter_dimension=1, tiled=True
-        ).astype(jnp.float32),
-        lax.psum_scatter(
-            stacked[9].astype(jnp.bfloat16), "fsdp", scatter_dimension=1, tiled=True
-        ).astype(jnp.float32),
-        lax.psum_scatter(
-            joint_grads[0].astype(jnp.bfloat16), "fsdp", scatter_dimension=0, tiled=True
-        ).astype(jnp.float32),
-        lax.psum_scatter(
-            joint_grads[1].astype(jnp.bfloat16), "fsdp", scatter_dimension=0, tiled=True
-        ).astype(jnp.float32),
-        lax.psum_scatter(
-            joint_grads[2].astype(jnp.bfloat16), "fsdp", scatter_dimension=0, tiled=True
-        ).astype(jnp.float32),
-        lax.psum_scatter(
-            joint_grads[3].astype(jnp.bfloat16), "fsdp", scatter_dimension=0, tiled=True
-        ).astype(jnp.float32),
-    )
-    return (
-        lax.psum(shares[0].astype(jnp.bfloat16), "dp").astype(jnp.float32),
-        lax.psum(shares[1].astype(jnp.bfloat16), "dp").astype(jnp.float32),
-        lax.psum(shares[2].astype(jnp.bfloat16), "dp").astype(jnp.float32),
-        lax.psum(shares[3].astype(jnp.bfloat16), "dp").astype(jnp.float32),
-        lax.psum(shares[4].astype(jnp.bfloat16), "dp").astype(jnp.float32),
-        lax.psum(shares[5].astype(jnp.bfloat16), "dp").astype(jnp.float32),
-        lax.psum(shares[6].astype(jnp.bfloat16), "dp").astype(jnp.float32),
-        lax.psum(shares[7].astype(jnp.bfloat16), "dp").astype(jnp.float32),
-        lax.psum(shares[8].astype(jnp.bfloat16), "dp").astype(jnp.float32),
-        lax.psum(shares[9].astype(jnp.bfloat16), "dp").astype(jnp.float32),
-        lax.psum(shares[10].astype(jnp.bfloat16), "dp").astype(jnp.float32),
-        lax.psum(shares[11].astype(jnp.bfloat16), "dp").astype(jnp.float32),
-        lax.psum(shares[12].astype(jnp.bfloat16), "dp").astype(jnp.float32),
-        lax.psum(shares[13].astype(jnp.bfloat16), "dp").astype(jnp.float32),
     )
 
 
@@ -654,32 +1010,33 @@
     valid_rows = valid.reshape(rows, 1)
     key_bias = ((1.0 - valid) * MASKED)[:, None, None, :]
     layers = norm_gains.shape[0]
+    n = lax.axis_size("fsdp")
+    mats = (first_in, first_out, attend_joint, attend_out, point_in, point_out, second_in, second_out)
+    sizes = layer_sizes(n, mats)
+    joint_pack = pack_joint(enc_weight, pred_weight, token_weight, duration_weight)
+    tail = [sum(sizes)] + [p.shape[0] for p in joint_pack]
+    wholes = []
+    for layer in range(layers):
+        parts = pack_layer(
+            [m[layer] for m in mats],
+            [norm_gains[layer], depth_taps[layer], batch_gain[layer : layer + 1], batch_bias[layer : layer + 1]],
+        )
+        if layer == layers - 1:
+            parts = parts + joint_pack
+        wholes.append(gather(padded(parts), 1 + layer))
+    weights_of = []
+    for layer in range(layers):
+        full, small = unpack_layer(wholes[layer], sizes, mats, width)
+        f_in, f_out, w_joint, w_proj, p_in, p_out, s_in, s_out = full
+        weights_of.append(
+            (small[:5], f_in, f_out, w_joint, w_proj, p_in, small[5:14], small[14], small[15], p_out, s_in, s_out)
+        )
     resid = frames_in.reshape(rows, width).astype(jnp.float32)
     records = []
     for layer in range(layers):
-        weights = (
-            lax.all_gather(norm_gains[layer], "fsdp", axis=1, tiled=True),
-            lax.all_gather(first_in[layer], "fsdp", axis=0, tiled=True),
-            lax.all_gather(first_out[layer], "fsdp", axis=0, tiled=True),
-            lax.all_gather(attend_joint[layer], "fsdp", axis=0, tiled=True),
-            lax.all_gather(attend_out[layer], "fsdp", axis=0, tiled=True),
-            lax.all_gather(point_in[layer], "fsdp", axis=0, tiled=True),
-            lax.all_gather(depth_taps[layer], "fsdp", axis=1, tiled=True),
-            lax.all_gather(batch_gain[layer], "fsdp", axis=0, tiled=True),
-            lax.all_gather(batch_bias[layer], "fsdp", axis=0, tiled=True),
-            lax.all_gather(point_out[layer], "fsdp", axis=0, tiled=True),
-            lax.all_gather(second_in[layer], "fsdp", axis=0, tiled=True),
-            lax.all_gather(second_out[layer], "fsdp", axis=0, tiled=True),
-        )
-        resid, record = run_layer(resid, weights, valid_rows, key_bias)
-        kept = None
-        records.append((kept, record))
-    w_enc, w_pred, w_tok, w_dur = (
-        lax.all_gather(enc_weight, "fsdp", axis=0, tiled=True),
-        lax.all_gather(pred_weight, "fsdp", axis=0, tiled=True),
-        lax.all_gather(token_weight, "fsdp", axis=0, tiled=True),
-        lax.all_gather(duration_weight, "fsdp", axis=0, tiled=True),
-    )
+        resid, record = run_layer(resid, weights_of[layer], valid_rows, key_bias, layer)
+        records.append((None, record))
+    w_enc, w_pred, w_tok, w_dur = unpack_joint(wholes[-1], tail, enc_weight, duration_weight)
     joint = w_enc.shape[1]
     vocab = w_tok.shape[1]
     out_low = resid.astype(jnp.bfloat16)
@@ -687,12 +1044,12 @@
     pred_low = pred_states.reshape(utts * slots, joint)
     pred = matmul(pred_low, w_pred).reshape(utts, slots, joint)
     groups = slots // GROUP
-    durs = w_dur.shape[1]
+    durs = duration_weight.shape[1]
     pred_t = jnp.pad(
         jnp.swapaxes(pred.reshape(utts * groups, GROUP, joint), 1, 2),
         ((0, 0), (0, 0), (0, 8 - GROUP)),
     )
-    w_cat = jnp.concatenate([w_tok, jnp.pad(w_dur, ((0, 0), (0, 128 - durs)))], 1)
+    w_cat = jnp.concatenate([w_tok, w_dur], 1)
     enc_t = enc.T
     labels_ext = jnp.concatenate([label_ids, jnp.zeros((utts, 1), jnp.int32)], 1)
     feats, expd = joint_forward(enc_t, pred_t, labels_ext, w_cat.T, vocab, durs, frames)
@@ -702,7 +1059,6 @@
     grad_enc_t, grad_pred_t, grad_tok, grad_dur_w = joint_backward(
         enc_t, pred_t, labels_ext, w_cat, feats, lat_grads, expd, vocab, durs, frames
     )
-    grad_dur_w = grad_dur_w[:, :durs]
     grad_pred_rows = jnp.swapaxes(grad_pred_t[:, :, :GROUP], 1, 2)
     grad_enc_low = grad_enc_t.T.astype(jnp.bfloat16)
     grad_w_enc = contract_rows(out_low, grad_enc_low)
@@ -715,61 +1071,53 @@
     collected = [None] * layers
     for layer in reversed(range(layers)):
         kept, record = records[layer]
-        weights = (
-            lax.all_gather(norm_gains[layer], "fsdp", axis=1, tiled=True),
-            lax.all_gather(first_in[layer], "fsdp", axis=0, tiled=True),
-            lax.all_gather(first_out[layer], "fsdp", axis=0, tiled=True),
-            lax.all_gather(attend_joint[layer], "fsdp", axis=0, tiled=True),
-            lax.all_gather(attend_out[layer], "fsdp", axis=0, tiled=True),
-            lax.all_gather(point_in[layer], "fsdp", axis=0, tiled=True),
-            lax.all_gather(depth_taps[layer], "fsdp", axis=1, tiled=True),
-            lax.all_gather(batch_gain[layer], "fsdp", axis=0, tiled=True),
-            lax.all_gather(batch_bias[layer], "fsdp", axis=0, tiled=True),
-            lax.all_gather(point_out[layer], "fsdp", axis=0, tiled=True),
-            lax.all_gather(second_in[layer], "fsdp", axis=0, tiled=True),
-            lax.all_gather(second_out[layer], "fsdp", axis=0, tiled=True),
-        )
-        grad, grads = layer_backward(weights, record, grad, valid_rows, key_bias)
+        weights = weights_of[layer]
+        grad, grads = layer_backward(weights, record, grad, valid_rows, key_bias, layer)
         collected[layer] = grads
 
-    def stack_member(member):
-        return jnp.stack([collected[layer][member] for layer in range(layers)])
-
-    stacked = (
-        jnp.swapaxes(stack_member(0), 1, 2),
-        stack_member(1),
-        stack_member(2),
-        stack_member(3),
-        stack_member(4),
-        stack_member(5),
-        jnp.swapaxes(stack_member(6), 1, 2),
-        stack_member(9),
-        stack_member(10),
-        stack_member(11),
-    )
-    summed = reduce_grads(stacked, (grad_w_enc, grad_w_pred, grad_tok, grad_dur_w))
-    gain_piece = lax.dynamic_slice_in_dim(stack_member(7), offset, shard, 1)
-    bias_piece = lax.dynamic_slice_in_dim(stack_member(8), offset, shard, 1)
+    shares = []
+    for layer in range(layers):
+        g = collected[layer]
+        parts = pack_layer_grads([g[1], g[2], g[3], g[4], g[5], g[9], g[10], g[11]], g[0], g[6], n)
+        if layer == layers - 1:
+            parts = parts + pack_joint_grads(grad_w_enc, grad_w_pred, grad_tok, grad_dur_w, n)
+        shares.append(scatter(padded(parts), 4 + layer))
+
+    def stack(values):
+        return jnp.stack(values)
+
+    pieces = [cut(share, sizes) for share in shares]
+    out = []
+    for i, m in enumerate(mats):
+        out.append(stack([shard_from_blocks(p[i], m.shape[2]) for p in pieces]))
+    small = stack([p[-1][:, : norm_gains.shape[2]].astype(jnp.float32) for p in pieces])
+    g_enc, g_pred, g_tok, rest = cut(shares[-1], tail[1:], tail[0])
+    low = enc_weight.shape[0]
+    g_enc = jnp.concatenate([g_enc, rest[:low, : joint - WIDE]], 1).astype(jnp.float32)
+    g_pred = jnp.concatenate([g_pred, rest[:, 128 : 128 + joint - WIDE]], 1).astype(jnp.float32)
+    g_dur = rest[:, 256 : 256 + durs].astype(jnp.float32)
+    gain_piece = lax.dynamic_slice_in_dim(stack([c[7] for c in collected]), offset, shard, 1)
+    bias_piece = lax.dynamic_slice_in_dim(stack([c[8] for c in collected]), offset, shard, 1)
     grad_frames = grad.reshape(utts, frames, width)
     return (
         utt_loss,
         grad_frames,
-        jnp.swapaxes(summed[0], 1, 2),
-        summed[1],
-        summed[2],
-        summed[3],
-        summed[4],
-        summed[5],
-        jnp.swapaxes(summed[6], 1, 2),
+        small[:, :5],
+        out[0],
+        out[1],
+        out[2],
+        out[3],
+        out[4],
+        small[:, 5:14],
         gain_piece,
         bias_piece,
-        summed[7],
-        summed[8],
-        summed[9],
-        summed[10],
-        summed[11],
-        summed[12],
-        summed[13],
+        out[5],
+        out[6],
+        out[7],
+        g_enc,
+        g_pred,
+        shard_from_blocks(g_tok, vocab),
+        g_dur,
     )
 
 

time: 2100 us -> 989 us (0.47)
  waiting for transfers between devices: 903 us -> 0 us
  blocking collectives: 630 us -> 0 us
  Pallas kernels: 132 us -> 510 us
  local copies, waits for them, and re-layouts: 171 us -> 284 us
  matrix products: 136 us -> 105 us
    reduce_scatter x11 -> x0, waiting for transfers between devices: 708 us -> none  [the longest x1 91.8 us: reduce_grads(): lax.psum_scatter(stacked[1].astype(jnp.bfloat16), 'fsdp', scatter_dimensi...]
    pallas_call x1 -> x9, Pallas kernels: 37.7 us -> 416 us  [the longest x2 169 us: gather(): pl.pallas_call(partial(gather_kernel, n1, tiles, lag), out_shape=jax.Shap...]
    all_gather x11 -> x0, blocking collectives: 356 us -> none  [the longest x2 69.5 us: local(): lax.all_gather(point_out[layer], 'fsdp', axis=0, tiled=True)]
    psum x7 -> x0, blocking collectives: 251 us -> none  [the longest x2 83.3 us: batch_stats(): lax.psum(jnp.sum(valid_rows * centred * centred, 0), ('dp', 'fsdp')) / count]
    unnamed x31 -> x0, waiting for transfers between devices: 130 us -> none
    psum x1 -> x0, waiting for transfers between devices: 65.1 us -> none  [reduce_grads(): lax.psum(shares[11].astype(jnp.bfloat16), 'dp').astype(jnp.float32)]
    reshape x10 -> x26, local copies, waits for them, and re-layouts: 0.05 us -> 54.1 us  [the longest x16 41.3 us: split_rows(): grad = grad.astype(jnp.bfloat16).reshape(n, rows // n, blocks, WIDE)]
    slice x8 -> x43, local copies, waits for them, and re-layouts: 6.97 us -> 38.6 us  [the longest x23 20.8 us: cut(): parts.append(whole[..., offset:offset + size, :])]
  transfers between devices with their start and end apart: 28 -> 0, of which waited for: 13 -> 0; matrix products, arithmetic and copies ran while one was open for 14% -> 0% of each run, Pallas kernels for 0% -> 0%
where the time goes in v2:
time: 989 us; the launch traced here: 978 us
  Pallas kernels  510 us (52%)
  local copies, waits for them, and re-layouts  284 us (29%)
  matrix products  105 us (11%)
  other arithmetic  74.1 us (7%)
    pallas_call x2, Pallas kernels, gather(): pl.pallas_call(partial(gather_kernel, n1, tiles, lag), out_shape=jax.Shap...  169 us
    pallas_call x2, Pallas kernels, scatter(): pl.pallas_call(partial(scatter_kernel, n1, tiles, lag), out_shape=jax.Sha...  163 us
    unnamed x627, local copies, waits for them, and re-layouts  106 us
    pallas_call x1, Pallas kernels, joint_backward(): pl.pallas_call(partial(joint_bwd_kernel, groups, durs), grid=(utts * grou...  59.6 us
    pallas_call x4, Pallas kernels, exchange(): pl.pallas_call(partial(exchange_kernel, kind, groups, n), out_shape=jax.S...  46.3 us
    reshape x16, local copies, waits for them, and re-layouts, split_rows(): grad = grad.astype(jnp.bfloat16).reshape(n, rows // n, blocks, WIDE)  41.3 us
    pallas_call x1, Pallas kernels, lattice(): pl.pallas_call(partial(lattice_kernel, slots), out_shape=(jax.ShapeDtypeS...  37.7 us
    dot_general x18, matrix products, matmul(): return jnp.dot(left, right, preferred_element_type=jnp.float32)  34.8 us

profile of v2, /device:TPU:0, one launch (start us, length us, event | category | flops | bytes accessed | tf_op | source)
XLA Modules:
  0.0 978.0 jit_solution(15164035931446881208)
XLA Ops:
  37.8 92.0 %gather_weights.2 = bf16[8,1920,512]{2,1,0:T(8,128)(2,1)} custom-call(bf16[1920,512]{1,0:T(8,128)(2,1)} %copy-done.107), custom_call_target="tpu_custom_call" | custom-call | tf_op jit(solution)/shard_map/gather_weights/pallas_call | solution.py:421
  130.7 2.6 fusion.152
  134.2 5.9 fusion.151
  141.8 2.0 copy.214
  146.1 77.2 %gather_weights.3 = bf16[8,1536,512]{2,1,0:T(8,128)(2,1)} custom-call(bf16[1536,512]{1,0:T(8,128)(2,1)} %copy-done.108), custom_call_target="tpu_custom_call" | custom-call | tf_op jit(solution)/shard_map/gather_weights/pallas_call | solution.py:421
  223.3 6.0 fusion.153
  229.3 3.3 copy-done.8
  245.5 2.2 convolution_convert_fusion.3
  247.7 4.0 reshape.1245
  277.1 13.4 %exchange_pool.2 = f32[16,128]{1,0:T(8,128)} custom-call(f32[16,128]{1,0:T(8,128)} %maximum_maximum_fusion.x_ref), custom_call_target="tpu_custom_call" | custom-call | tf_op jit(solution)/shard_map/exchange_pool/pallas_call | solution.py:593
  291.7 2.0 fusion.142
  298.2 2.0 copy.213
  300.6 5.3 multiply_convert_fusion.8
  310.9 2.3 fusion.173
  317.7 2.3 convolution_convert_fusion.2
  320.0 4.0 reshape.1246
  346.3 11.0 %exchange_pool.3 = f32[16,128]{1,0:T(8,128)} custom-call(f32[16,128]{1,0:T(8,128)} %maximum_maximum_fusion.1.x_ref), custom_call_target="tpu_custom_call" | custom-call | tf_op jit(solution)/shard_map/exchange_pool/pallas_call | solution.py:593
  358.6 2.0 fusion.147
  365.0 1.9 copy.218
  367.3 5.4 multiply_convert_fusion.6
  372.8 3.3 fusion.177
  376.5 2.0 fusion.134.enc_ref
  380.5 2.3 copy.129
  382.8 3.9 pad.176.pred_ref
  391.5 2.6 copy.131.wt_ref
  394.1 34.5 %joint_forward.1 = (f32[8,64,256]{2,1,0:T(8,128)S(1)}, bf16[10,5,1024,256]{3,2,1,0:T(8,128)(2,1)}) custom-call(s32[2,25]{1,0:T(2,128)S(1)} %concatenate.88.labels_ref, f32[640,512]{1,0:T(8,128)S(1)} %fusion.134.enc_ref, f32[10,640,8]{2,1,0:T(8,128)} %pad.176.pred_ref, bf16[1152,640]{1,0:T(8,128)(2,1)S(1)} %copy.131.wt_ref), custom_call_target="tpu_custom_call" | custom-call | tf_op jit(solution)/shard_map/joint_forward/pallas_call | solution.py:211
  428.7 37.7 %lattice.1 = (f32[7,64,256]{2,1,0:T(8,128)S(1)}, f32[8,128]{1,0:T(8,128)S(1)}) custom-call(f32[7,64,256]{2,1,0:T(8,128)S(1)} %slice.704.feats_ref, s32[2]{0:T(128)S(1)} %copy-done.4, s32[2]{0:T(128)S(1)} %copy-done.5), custom_call_target="tpu_custom_call" | custom-call | tf_op jit(solution)/shard_map/lattice/pallas_call | solution.py:149
  467.9 59.6 %joint_backward.1 = (f32[640,512]{1,0:T(8,128)}, f32[10,640,8]{2,1,0:T(8,128)}, bf16[640,1024]{1,0:T(8,128)(2,1)}, bf16[640,128]{1,0:T(8,128)(2,1)}) custom-call(s32[2,25]{1,0:T(2,128)} %copy-done.3, f32[640,512]{1,0:T(8,128)} %copy-done, f32[10,640,8]{2,1,0:T(8,128)} %pad.176.pred_ref, bf16[640,1152]{1,0:T(8,128)(2,1)} %get-tuple-element.209.w_ref, ...), custom_call_target="tpu_custom_call" | custom-call | tf_op jit(solution)/shard_map/joint_backward/pallas_call | solution.py:284
  527.4 2.8 multiply_reduce_fusion.11
  532.2 2.3 multiply_convert_fusion.5
  534.6 2.0 multiply_reduce_fusion.12
  540.9 11.0 %exchange_sum.2 = f32[16,128]{1,0:T(8,128)} custom-call(f32[16,128]{1,0:T(8,128)} %maximum_maximum_fusion.2.x_ref), custom_call_target="tpu_custom_call" | custom-call | tf_op jit(solution)/shard_map/exchange_sum/pallas_call | solution.py:593
  553.3 2.5 multiply_reduce_fusion.6
  565.2 3.1 convolution_bitcast_fusion.1
  588.7 2.6 multiply_convert_fusion.2
  591.3 2.0 multiply_reduce_fusion.26
  597.6 11.0 %exchange_sum.3 = f32[16,128]{1,0:T(8,128)} custom-call(f32[16,128]{1,0:T(8,128)} %maximum_maximum_fusion.3.x_ref), custom_call_target="tpu_custom_call" | custom-call | tf_op jit(solution)/shard_map/exchange_sum/pallas_call | solution.py:593
  610.1 2.8 multiply_reduce_fusion.20
  625.7 3.3 convolution_bitcast_fusion
  647.5 3.1 convolution_convert_fusion.7
  650.6 4.5 reshape.1223
  655.1 2.2 copy.156
  664.2 2.4 convolution_convert_fusion
  666.6 5.6 reshape.1225
  672.2 2.0 copy.157
  683.9 2.8 convolution_convert_fusion.5
  686.7 4.8 reshape.1229
  691.6 2.1 copy.159
  699.8 5.8 multiply_reduce_fusion.10
  706.7 2.5 convolution_convert_fusion.15
  715.5 3.6 reshape.1233
  723.3 88.2 %scatter_grads.3 = bf16[5,2,192,512]{3,2,1,0:T(8,128)(2,1)} custom-call(bf16[8,1920,512]{2,1,0:T(8,128)(2,1)} %broadcast_dynamic-update-slice_fusion.src), custom_call_target="tpu_custom_call" | custom-call | tf_op jit(solution)/shard_map/scatter_grads/pallas_call | solution.py:523
  812.8 2.6 convolution_convert_fusion.11
  815.4 4.7 reshape.1214
  820.0 2.2 copy.146
  829.1 2.4 convolution_convert_fusion.1
  831.5 5.6 reshape.1216
  837.1 2.0 copy.147
  848.3 2.7 convolution_convert_fusion.9
  851.0 3.3 reshape.1220
  864.4 74.9 %scatter_grads.2 = bf16[4,2,192,512]{3,2,1,0:T(8,128)(2,1)} custom-call(bf16[8,1536,512]{2,1,0:T(8,128)(2,1)} %broadcast_dynamic-update-slice_fusion.1.src), custom_call_target="tpu_custom_call" | custom-call | tf_op jit(solution)/shard_map/scatter_grads/pallas_call | solution.py:523
  948.0 2.1 maximum_convert_fusion.2
  950.1 2.1 maximum_convert_fusion.3
  957.7 2.0 maximum_convert_fusion.6
  (984 shorter events, 299.4 us)
Async XLA Ops:
  1.3 392.8 %copy-start.3 = (s32[2,25]{1,0:T(2,128)}, s32[2,25]{1,0:T(2,128)S(1)}, u32[]{:S(2)}) copy-start(s32[2,25]{1,0:T(2,128)S(1)} %concatenate.88.labels_ref) | copy-start | bytes 604
  23.4 8.1 copy-start.185
  23.4 8.7 copy-start.228
  130.7 13.1 %slice-start = ((s8[15728640]{0:T(1024)(128)(4,1)}), s8[3145728]{0:T(1024)(128)(4,1)S(1)}, s32[]{:S(2)}) async-start(s8[15728640]{0:T(1024)(128)(4,1)} %bitcast.489), calls=%async_computation | async-start | bytes 6291456
  134.2 9.6 slice-start.1
  134.2 9.6 slice-start.2
  223.2 9.3 copy-start.8
  223.3 9.5 copy-start.32
  255.4 5.7 copy-start.147
  259.4 5.0 slice-start.9
  267.3 27.4 %copy-start.20 = (f32[512,512]{1,0:T(8,128)}, f32[512,512]{1,0:T(8,128)S(1)}, u32[]{:S(2)}) copy-start(f32[512,512]{1,0:T(8,128)S(1)} %get-tuple-element.278) | copy-start | bytes 3145732
  272.3 22.4 %copy-start.38 = (f32[512,512]{1,0:T(8,128)}, f32[512,512]{1,0:T(8,128)S(1)}, u32[]{:S(2)}) copy-start(f32[512,512]{1,0:T(8,128)S(1)} %multiply_multiply_fusion.1) | copy-start | bytes 3145732
  272.4 22.3 %copy-start.202 = (f32[512]{0:T(512)}, f32[512]{0:T(512)S(1)}, u32[]{:S(2)}) copy-start(f32[512]{0:T(512)S(1)} %mul.1376) | copy-start | bytes 6148
  272.5 22.2 %copy-start.204 = (f32[512]{0:T(512)}, f32[512]{0:T(512)S(1)}, u32[]{:S(2)}) copy-start(f32[512]{0:T(512)S(1)} %mul.1373) | copy-start | bytes 6148
  272.6 22.2 %copy-start.206 = (f32[512]{0:T(512)}, f32[512]{0:T(512)S(1)}, u32[]{:S(2)}) copy-start(f32[512]{0:T(512)S(1)} %mul.1370) | copy-start | bytes 6148
  272.6 22.1 %copy-start.208 = (f32[512]{0:T(512)}, f32[512]{0:T(512)S(1)}, u32[]{:S(2)}) copy-start(f32[512]{0:T(512)S(1)} %mul.1367) | copy-start | bytes 6148
  272.7 22.0 %copy-start.210 = (f32[512]{0:T(512)}, f32[512]{0:T(512)S(1)}, u32[]{:S(2)}) copy-start(f32[512]{0:T(512)S(1)} %mul.1364) | copy-start | bytes 6148
  273.9 22.7 %copy-start.16 = (f32[2,256,512]{2,1,0:T(8,128)}, f32[2,256,512]{2,1,0:T(8,128)S(1)}, u32[]{:S(2)}) copy-start(f32[2,256,512]{2,1,0:T(8,128)S(1)} %get-tuple-element.170) | copy-start | bytes 3145732
  274.0 22.5 %copy-start.229 = (f32[512]{0:T(512)}, f32[512]{0:T(512)S(1)}, u32[]{:S(2)}) copy-start(f32[512]{0:T(512)S(1)} %reshape.1240) | copy-start | bytes 6148
  274.1 22.5 %copy-start.177 = (f32[512]{0:T(512)}, f32[512]{0:T(512)S(1)}, u32[]{:S(2)}) copy-start(f32[512]{0:T(512)S(1)} %reshape.1239) | copy-start | bytes 6148
  276.4 15.3 %copy-start.254 = (f32[16]{0:T(128)}, f32[16]{0:T(128)S(1)}, u32[]{:S(2)}) copy-start(f32[16]{0:T(128)S(1)} %pad.273.clone) | copy-start | bytes 196
  296.6 9.4 copy-start.45
  300.3 5.6 copy-start.240
  300.3 5.6 copy-start.192
  300.6 5.4 copy-start.183
  300.6 5.3 copy-start.247
  300.6 5.4 copy-start.117
  336.5 25.1 %copy-start.23 = (f32[512,512]{1,0:T(8,128)}, f32[512,512]{1,0:T(8,128)S(1)}, u32[]{:S(2)}) copy-start(f32[512,512]{1,0:T(8,128)S(1)} %get-tuple-element.290) | copy-start | bytes 3145732
  341.9 19.6 %copy-start.40 = (f32[512,512]{1,0:T(8,128)}, f32[512,512]{1,0:T(8,128)S(1)}, u32[]{:S(2)}) copy-start(f32[512,512]{1,0:T(8,128)S(1)} %multiply_multiply_fusion) | copy-start | bytes 3145732
  342.4 19.1 %copy-start.212 = (f32[512]{0:T(512)}, f32[512]{0:T(512)S(1)}, u32[]{:S(2)}) copy-start(f32[512]{0:T(512)S(1)} %mul.1446) | copy-start | bytes 6148
  342.5 19.1 %copy-start.214 = (f32[512]{0:T(512)}, f32[512]{0:T(512)S(1)}, u32[]{:S(2)}) copy-start(f32[512]{0:T(512)S(1)} %mul.1443) | copy-start | bytes 6148
  342.6 19.0 %copy-start.216 = (f32[512]{0:T(512)}, f32[512]{0:T(512)S(1)}, u32[]{:S(2)}) copy-start(f32[512]{0:T(512)S(1)} %mul.1440) | copy-start | bytes 6148
  342.7 18.9 %copy-start.218 = (f32[512]{0:T(512)}, f32[512]{0:T(512)S(1)}, u32[]{:S(2)}) copy-start(f32[512]{0:T(512)S(1)} %mul.1437) | copy-start | bytes 6148
  343.8 19.6 %copy-start.18 = (f32[2,256,512]{2,1,0:T(8,128)}, f32[2,256,512]{2,1,0:T(8,128)S(1)}, u32[]{:S(2)}) copy-start(f32[2,256,512]{2,1,0:T(8,128)S(1)} %get-tuple-element.168) | copy-start | bytes 3145732
  343.9 194.4 %copy-start.231 = (f32[512]{0:T(512)}, f32[512]{0:T(512)S(1)}, u32[]{:S(2)}) copy-start(f32[512]{0:T(512)S(1)} %reshape.1242) | copy-start | bytes 6148
  367.3 5.4 copy-start.119
  376.2 154.1 %copy-start.165 = (f32[512]{0:T(512)}, f32[512]{0:T(512)S(1)}, u32[]{:S(2)}) copy-start(f32[512]{0:T(512)S(1)} %mul.1483) | copy-start | bytes 6148
  376.2 154.1 %copy-start.160 = (f32[512]{0:T(512)}, f32[512]{0:T(512)S(1)}, u32[]{:S(2)}) copy-start(f32[512]{0:T(512)S(1)} %broadcast_multiply_fusion.18) | copy-start | bytes 6148
  376.5 153.9 %copy-start.167 = (f32[512]{0:T(512)}, f32[512]{0:T(512)S(1)}, u32[]{:S(2)}) copy-start(f32[512]{0:T(512)S(1)} %fusion.109) | copy-start | bytes 6148
  378.5 15.6 %copy-start = (f32[640,512]{1,0:T(8,128)}, f32[640,512]{1,0:T(8,128)S(1)}, u32[]{:S(2)}) copy-start(f32[640,512]{1,0:T(8,128)S(1)} %fusion.134.enc_ref) | copy-start | bytes 3932164
  394.1 34.6 %copy-start.5 = (s32[2]{0:T(128)S(1)}, s32[2]{0:T(128)}, u32[]{:S(2)}) copy-start(s32[2]{0:T(128)} %ulen_ref.1) | copy-start | bytes 28
  394.1 73.7 %copy-start.236 = (f32[1,2,2,128]{3,2,1,0:T(2,128)S(1)}, f32[1,2,2,128]{3,2,1,0:T(2,128)}, u32[]{:S(2)}) copy-start(f32[1,2,2,128]{3,2,1,0:T(2,128)} %get-tuple-element.263) | copy-start | bytes 6148
  428.7 39.1 %copy-start.1 = (f32[8,64,256]{2,1,0:T(8,128)}, f32[8,64,256]{2,1,0:T(8,128)S(1)}, u32[]{:S(2)}) copy-start(f32[8,64,256]{2,1,0:T(8,128)S(1)} %get-tuple-element.26.feats_ref) | copy-start | bytes 1572868
  467.8 59.6 %copy-start.14 = (f32[512,512]{1,0:T(8,128)S(1)}, f32[512,512]{1,0:T(8,128)}, u32[]{:S(2)}) copy-start(f32[512,512]{1,0:T(8,128)} %copy-done.13) | copy-start | bytes 3145732
  467.8 59.6 %copy-start.63 = (bf16[8,64,640]{2,1,0:T(8,128)(2,1)S(1)}, bf16[8,64,640]{2,1,0:T(8,128)(2,1)}, u32[]{:S(2)}) copy-start(bf16[8,64,640]{2,1,0:T(8,128)(2,1)} %pad_maximum_fusion.2) | copy-start | bytes 1966084
  530.8 6.2 copy-start.90
  538.4 14.9 %copy-start.12 = (f32[512,1024]{1,0:T(8,128)S(1)}, f32[512,1024]{1,0:T(8,128)}, u32[]{:S(2)}) copy-start(f32[512,1024]{1,0:T(8,128)} %copy-done.11) | copy-start | bytes 6291460
  538.4 14.8 %copy-start.234 = (f32[512]{0:T(512)S(1)}, f32[512]{0:T(512)}, u32[]{:S(2)}) copy-start(f32[512]{0:T(512)} %get-tuple-element.161) | copy-start | bytes 6148
  563.6 14.7 %copy-start.30 = (f32[512,512]{1,0:T(8,128)}, f32[512,512]{1,0:T(8,128)S(1)}, u32[]{:S(2)}) copy-start(f32[512,512]{1,0:T(8,128)S(1)} %add_add_fusion.16) | copy-start | bytes 3145732
  587.0 6.8 copy-start.92
  595.2 14.8 %copy-start.10 = (f32[512,1024]{1,0:T(8,128)S(1)}, f32[512,1024]{1,0:T(8,128)}, u32[]{:S(2)}) copy-start(f32[512,1024]{1,0:T(8,128)} %copy-done.9) | copy-start | bytes 6291460
  595.2 14.7 %copy-start.233 = (f32[512]{0:T(512)S(1)}, f32[512]{0:T(512)}, u32[]{:S(2)}) copy-start(f32[512]{0:T(512)} %get-tuple-element.150) | copy-start | bytes 6148
  699.4 7.3 copy-start.15
  699.4 7.3 copy-start.161
  699.4 7.3 copy-start.166
  699.4 7.3 copy-start.168
  723.3 89.5 %copy-start.152 = (bf16[512,512]{1,0:T(8,128)(2,1)S(1)}, bf16[512,512]{1,0:T(8,128)(2,1)}, u32[]{:S(2)}) copy-start(bf16[512,512]{1,0:T(8,128)(2,1)} %get-tuple-element.229) | copy-start | bytes 1572868
  723.3 89.5 %copy-start.266 = (bf16[512,2048]{1,0:T(8,128)(2,1)S(1)}, bf16[512,2048]{1,0:T(8,128)(2,1)}, u32[]{:S(2)}) copy-start(bf16[512,2048]{1,0:T(8,128)(2,1)} %copy-done.265) | copy-start | bytes 6291460
  864.4 75.8 %copy-start.227 = (bf16[1,16,64]{2,1,0:T(8,128)(2,1)S(1)}, bf16[1,16,64]{2,1,0:T(8,128)(2,1)}, u32[]{:S(2)}) copy-start(bf16[1,16,64]{2,1,0:T(8,128)(2,1)} %slice_bitcast_fusion.10) | copy-start | bytes 6148
  864.4 76.4 %copy-start.61 = (bf16[5,2,192,512]{3,2,1,0:T(8,128)(2,1)S(1)}, bf16[5,2,192,512]{3,2,1,0:T(8,128)(2,1)}, u32[]{:S(2)}) copy-start(bf16[5,2,192,512]{3,2,1,0:T(8,128)(2,1)} %scatter_grads.3) | copy-start | bytes 5898244
  939.3 5.1 copy-start.62
  964.1 8.1 copy-start.141
  966.1 7.6 copy-start.142
  966.1 7.6 copy-start.143
  (224 other events, 502.8 us)

commit v3 on v2

--- a/solution.py
+++ b/solution.py
@@ -306,10 +306,15 @@
 
 
 MESH=pl.DeviceIdType.MESH
-QA=64
-QB=64
-HALF=2*QA+QB
-TILE=2*HALF
+QA = QB = HALF = TILE = 0
+
+
+def set_tile(shards):
+    global QA, QB, HALF, TILE
+    QA = QB = max(16, 256 // shards)
+    HALF = 2 * QA + QB
+    TILE = 2 * HALF
+
 
 def place():
     dp=lax.axis_index("dp"); fs=lax.axis_index("fsdp")
@@ -414,7 +419,7 @@
         return carry
     lax.fori_loop(0,items,finish,0)
 
-def gather(packed, collective_id, lag=1):
+def gather(packed, collective_id, lag=4):
     n=lax.axis_size("fsdp"); n1=n//2
     tiles=packed.shape[0]//TILE
     dma=pltpu.SemaphoreType.DMA
@@ -428,18 +433,23 @@
         name="gather_weights",
     )(packed)
 
-def scatter_kernel(n1, tiles, lag, src, out, own, gc, gx, gy, gz, gf, fin,
+def scatter_kernel(n1, counts, lag, *refs):
+    srcs = refs[:len(counts)]
+    scatter_body(n1, counts, lag, srcs, *refs[len(counts):])
+
+def scatter_body(n1, counts, lag, srcs, out, own, gc, gx, gy, gz, gf, fin,
                    lo, sc, rc, sx, rx, sy, ry, sz, rz, sf, rf, se, re, wo):
     dp,fs,a,c,i1,i2=place()
     greet(n1,dp,fs,a,c,i1,i2)
     ypeer=(dp,i1*2+1-i2); xpeer=((1-a)*2+c,fs); cpeer=(a*2+1-c,fs)
+    tiles=sum(counts)
     items=n1*tiles
     main=rows(a*QA,QA+QB)
     def quarter(aa): return rows(aa*(QA+QB),QA)
     middle=pl.ds(QA,QB)
     def of(m): return m//n1, lax.rem(i1+1+m%n1,n1)
-    def load(t,s): return pltpu.make_async_copy(src.at[s,rows(t*TILE+c*HALF,HALF),:],own.at[t,s],lo.at[t,s])
-    def ccopy(t,s): return remote(src.at[s,rows(t*TILE+(1-c)*HALF,HALF),:],gc.at[t,s],sc.at[t,s],rc.at[t,s],cpeer)
+    def load(t,s,src=srcs[0],f=0): return pltpu.make_async_copy(src.at[s,rows((t-f)*TILE+c*HALF,HALF),:],own.at[t,s],lo.at[t,s])
+    def ccopy(t,s,src=srcs[0],f=0): return remote(src.at[s,rows((t-f)*TILE+(1-c)*HALF,HALF),:],gc.at[t,s],sc.at[t,s],rc.at[t,s],cpeer)
     def xcopy(t,s): return remote(own.at[t,s,quarter(1-a),:],gx.at[t,s],sx.at[t,s],rx.at[t,s],xpeer)
     def ycopy(t,j): return remote(own.at[t,j*2+1-i2,main,:],gy.at[t,j],sy.at[t,j],ry.at[t,j],ypeer)
     def zcopy(t,j): return remote(own.at[t,j*2+i2,main,:],gz.at[t,i1],sz.at[t,j],rz.at[t,i1],(dp,j*2+i2))
@@ -459,12 +469,17 @@
             @pl.when((m>=0)&(m<items)&(lax.rem(m+n1,n1)==n1-1))
             def _(): body(m//n1)
         def stage_c(t,j):
-            for i in range(2):
-                load(t,j*2+i).start(); ccopy(t,j*2+i).start()
+            first=0
+            for src,count in zip(srcs,counts):
+                @pl.when((t>=first)&(t<first+count))
+                def _(src=src,first=first):
+                    for i in range(2):
+                        load(t,j*2+i,src,first).start(); ccopy(t,j*2+i,src,first).start()
+                first+=count
         def stage_x(t,j):
             for i in range(2):
                 s=j*2+i
-                load(t,s).wait(); ccopy(t,s).wait_recv()
+                pltpu.make_async_copy(own.at[t,s],own.at[t,s],lo.at[t,s]).wait(); remote(own.at[t,s],gc.at[t,s],sc.at[t,s],rc.at[t,s],cpeer).wait_recv()
                 own[t,s]=own[t,s]+gc[t,s]
                 xcopy(t,s).start()
         def stage_y(t,j):
@@ -504,7 +519,7 @@
     def finish(m,carry):
         t,j=of(m)
         for i in range(2):
-            ccopy(t,j*2+i).wait_send(); xcopy(t,j*2+i).wait_send()
+            remote(own.at[t,j*2+i],gc.at[t,j*2+i],sc.at[t,j*2+i],rc.at[t,j*2+i],cpeer).wait_send(); xcopy(t,j*2+i).wait_send()
         ycopy(t,j).wait_send()
         @pl.when(j!=i1)
         def _(): zcopy(t,j).wait_send()
@@ -515,23 +530,25 @@
         return carry
     lax.fori_loop(0,tiles,finish_tile,0)
 
-def scatter(grads, collective_id, lag=2):
+def scatter(sources, collective_id, lag=3):
     n=lax.axis_size("fsdp"); n1=n//2
-    tiles=grads.shape[1]//TILE; w=grads.shape[2]
+    counts=tuple(x.shape[1]//TILE for x in sources)
+    tiles=sum(counts); w=sources[0].shape[2]
     dma=pltpu.SemaphoreType.DMA
     bf=jnp.bfloat16
     out=pl.pallas_call(
-        partial(scatter_kernel,n1,tiles,lag),
+        partial(scatter_kernel,n1,counts,lag),
         out_shape=jax.ShapeDtypeStruct((tiles,2,HALF,w),bf),
-        in_specs=[pl.BlockSpec(memory_space=pl.ANY)],
+        in_specs=[pl.BlockSpec(memory_space=pl.ANY)]*len(sources),
         out_specs=pl.BlockSpec(memory_space=pl.ANY),
         scratch_shapes=[pltpu.VMEM((tiles,n,HALF,w),bf),pltpu.VMEM((tiles,n,HALF,w),bf),pltpu.VMEM((tiles,n,QA,w),bf),
             pltpu.VMEM((tiles,n1,QA+QB,w),bf),pltpu.VMEM((tiles,n1,QA+QB,w),bf),pltpu.VMEM((tiles,QA+QB,w),bf),pltpu.VMEM((tiles,2,HALF,w),bf)]
             +[dma((tiles,n))]*5+[dma((tiles,n1))]*4+[dma((tiles,))]*5,
-        compiler_params=pltpu.CompilerParams(collective_id=collective_id,has_side_effects=True,vmem_limit_bytes=56<<20),
+        compiler_params=pltpu.CompilerParams(collective_id=collective_id,has_side_effects=True,vmem_limit_bytes=60<<20),
         name="scatter_grads",
-    )(grads)
-    return out.reshape(tiles*TILE,w)
+    )(*sources)
+    out=out.reshape(tiles*TILE,w)
+    return out
 
 
 def pooled(parts):
@@ -605,64 +622,713 @@
     )(x)
 
 
-def global_stats(depthwise, valid_rows, collective_id):
-    width = depthwise.shape[1]
-    count = jnp.sum(valid_rows)
-    mean = jnp.sum(depthwise * valid_rows, 0) / count
-    gap = (depthwise - mean) * valid_rows
-    dev = jnp.sum(gap * gap, 0)
-    x = jnp.concatenate([mean.reshape(-1, 128), dev.reshape(-1, 128), jnp.full((8, 128), count)], 0)
-    x = exchange(x, "pool", collective_id)
-    count = x[8, 0]
-    return x[0:4].reshape(width), lax.rsqrt(x[4:8].reshape(width) / count + EPS), count
-
-
-def global_sums(one, two, collective_id):
-    width = one.shape[0]
-    x = jnp.concatenate([one.reshape(-1, 128), two.reshape(-1, 128), jnp.zeros((8, 128))], 0)
-    x = exchange(x, "sum", collective_id)
-    return x[0:4].reshape(width), x[4:8].reshape(width)
-
-
+CHUNK_ROWS = 64
 WIDE = 512
-
-
-def to_blocks(w):
-    rows, cols = w.shape
-    return jnp.swapaxes(w.reshape(rows, cols // WIDE, WIDE), 0, 1).reshape(-1, WIDE)
-
-
-def from_blocks(part, cols):
-    n, height, _ = part.shape
-    blocks = cols // WIDE
-    return jnp.swapaxes(part.reshape(n, blocks, height // blocks, WIDE), 1, 2).reshape(-1, cols)
-
-
-def padded(parts):
-    rows = sum(p.shape[-2] for p in parts)
-    short = -rows % TILE
-    shape = parts[0].shape[:-2] + (short, WIDE)
-    return jnp.concatenate(parts + [jnp.zeros(shape, jnp.bfloat16)], -2)
-
-
-def pack_layer(mats, smalls):
-    f_in, f_out, w_joint, w_proj, p_in, p_out, s_in, s_out = mats
-    small = jnp.concatenate(smalls, 0)
-    small = jnp.pad(small, ((0, 16 - small.shape[0]), (0, WIDE - small.shape[1])))
-    return [to_blocks(f_in), f_out, to_blocks(w_joint), w_proj, to_blocks(p_in), p_out, to_blocks(s_in), s_out, small]
-
-
-def pack_joint(w_enc, w_pred, w_tok, w_dur):
-    tall = w_pred.shape[0]
-    rest = jnp.concatenate(
-        [
-            jnp.pad(w_enc[:, WIDE:], ((0, tall - w_enc.shape[0]), (0, 0))),
-            w_pred[:, WIDE:],
-            jnp.pad(w_dur, ((0, 0), (0, 256 - w_dur.shape[1]))),
-        ],
-        1,
-    )
-    return [w_enc[:, :WIDE], w_pred[:, :WIDE], to_blocks(w_tok), rest]
+PLACE = ("p_out", "s_in", "s_out", "p_in", "w_proj", "w_joint", "f_in", "f_out")
+
+
+def tn(a, b):
+    return lax.dot_general(a, b, (((0,), (0,)), ((), ())), preferred_element_type=jnp.float32)
+
+
+def row_loop(count, body, init=0):
+    def step(i, carry):
+        return body(pl.ds(pl.multiple_of(i * CHUNK_ROWS, CHUNK_ROWS), CHUNK_ROWS), i, carry)
+
+    return lax.fori_loop(0, count // CHUNK_ROWS, step, init)
+
+
+def ln_parts(v):
+    centred = v - jnp.mean(v, -1, keepdims=True)
+    rstd = lax.rsqrt(jnp.mean(centred * centred, -1, keepdims=True) + EPS)
+    return centred * rstd, rstd
+
+
+def ln_back(v, gain, grad):
+    hat, rstd = ln_parts(v)
+    dy = grad * gain
+    dv = rstd * (dy - jnp.mean(dy, -1, keepdims=True) - hat * jnp.mean(dy * hat, -1, keepdims=True))
+    return dv, fold8(grad * hat, jnp.add)
+
+
+def offsets(n, width, ff):
+    low = width // n
+    tall = ff // n
+    sizes = {
+        "p_out": low, "s_in": low * (ff // WIDE), "s_out": tall, "p_in": 2 * low,
+        "w_proj": low, "w_joint": 3 * low, "f_in": low * (ff // WIDE), "f_out": tall,
+    }
+    table = {}
+    at = 0
+    for name in PLACE:
+        table[name] = at
+        at += sizes[name]
+    return table, at
+
+
+class Mover:
+    def __init__(self, sems):
+        self.sems = sems
+        self.used = 0
+        self.pending = []
+
+    def take(self):
+        self.used += 1
+        return self.sems.at[self.used - 1]
+
+    def load(self, src, dst):
+        cp = pltpu.make_async_copy(src, dst, self.take())
+        cp.start()
+        return cp
+
+    def put(self, src, dst):
+        cp = pltpu.make_async_copy(src, dst, self.take())
+        cp.start()
+        self.pending.append(cp)
+
+    def load_weight(self, whole, at, dst, tall):
+        n = whole.shape[0]
+        height = dst.shape[0] // n
+        sem = self.take()
+
+        def one(s, carry):
+            for b in range(dst.shape[1] // WIDE):
+                pltpu.make_async_copy(
+                    whole.at[s, pl.ds(at + b * height, height), :],
+                    dst.at[pl.ds(pl.multiple_of(s * height, 16), height), pl.ds(b * WIDE, WIDE)],
+                    sem,
+                ).start()
+            return carry
+
+        lax.fori_loop(0, n, one, 0)
+        return pltpu.make_async_copy(dst, dst, sem)
+
+    def put_weight(self, src, grads, at):
+        n = grads.shape[0]
+        height = src.shape[0] // n
+        sem = self.take()
+
+        def one(s, carry):
+            for b in range(src.shape[1] // WIDE):
+                pltpu.make_async_copy(
+                    src.at[pl.ds(pl.multiple_of(s * height, 16), height), pl.ds(b * WIDE, WIDE)],
+                    grads.at[s, pl.ds(at + b * height, height), :],
+                    sem,
+                ).start()
+            return carry
+
+        lax.fori_loop(0, n, one, 0)
+        self.pending.append(pltpu.make_async_copy(src, src, sem))
+
+    def finish(self):
+        for cp in self.pending:
+            cp.wait()
+
+
+def valid_rows_of(t_ref, frames, i):
+    per = frames // CHUNK_ROWS
+    t_len = t_ref[i // per]
+    at = lax.broadcasted_iota(jnp.int32, (CHUNK_ROWS, 1), 0) + lax.rem(i, per) * CHUNK_ROWS
+    return jnp.where(at < t_len, 1.0, 0.0)
+
+
+def write_rows(out, base, vec):
+    for i in range(vec.shape[1] // 128):
+        out[base + i : base + i + 1, :] = vec[:, i * 128 : (i + 1) * 128]
+
+
+def read_rows(ref, base, width):
+    return jnp.concatenate([ref[base + i : base + i + 1, :] for i in range(width // 128)], 1)
+
+
+def ffn_fwd(rows, x_ref, gain, w_in, w_out, normed, h, act, y, mover, h_out):
+    def prepare(r, i, c):
+        normed[r, :] = (ln_parts(x_ref[r, :].astype(jnp.float32))[0] * gain).astype(jnp.bfloat16)
+        return c
+
+    row_loop(rows, prepare)
+    w_in[1].wait()
+    for b in range(h.shape[0]):
+        h[b] = nn(normed[...], w_in[0][:, b * WIDE : (b + 1) * WIDE])
+        mover.put(h.at[b], h_out.at[b])
+
+        def swish(r, i, c):
+            v = h[b, r, :]
+            act[r, b * WIDE : (b + 1) * WIDE] = (v * jax.nn.sigmoid(v)).astype(jnp.bfloat16)
+            return c
+
+        row_loop(rows, swish)
+    w_out[1].wait()
+    y[...] = x_ref[...].astype(jnp.float32) + 0.5 * nn(act[...], w_out[0][...])
+
+
+def part_one_kernel(utts, table, t_ref, x_ref, small, whole, y1_out, h_out, y2_out, t_out, c_out, r_out, d_out, stats,
+                    w_fin, w_fout, w_joint, w_proj, w_pin, y1, y2, normed, h, act, tq, ctx, r, gp, d, sems):
+    rows, width = y1.shape
+    frames = rows // utts
+    mover = Mover(sems)
+    gains = small[...]
+    fin = mover.load_weight(whole, table["f_in"], w_fin, False)
+    fout = mover.load_weight(whole, table["f_out"], w_fout, True)
+    wj = mover.load_weight(whole, table["w_joint"], w_joint, False)
+    wp = mover.load_weight(whole, table["w_proj"], w_proj, False)
+    wi = mover.load_weight(whole, table["p_in"], w_pin, False)
+    ffn_fwd(rows, x_ref, gains[0:1], (w_fin, fin), (w_fout, fout), normed, h, act, y1, mover, h_out)
+    mover.put(y1, y1_out)
+
+    def prepare(rr, i, c):
+        normed[rr, :] = (ln_parts(y1[rr, :])[0] * gains[1:2]).astype(jnp.bfloat16)
+        return c
+
+    row_loop(rows, prepare)
+    wj.wait()
+    for b in range(3):
+        tq[:, b * width : (b + 1) * width] = nn(normed[...], w_joint[:, b * width : (b + 1) * width]).astype(jnp.bfloat16)
+    mover.put(tq, t_out)
+    pairs = width // 128
+    side = lax.broadcasted_iota(jnp.int32, (frames, 128), 1) < 64
+    key_at = lax.broadcasted_iota(jnp.int32, (1, frames), 1)
+
+    def pair_step(m, carry):
+        u = m // pairs
+        base = lax.rem(m, pairs) * 128
+        rr = pl.ds(pl.multiple_of(u * frames, frames), frames)
+        bias = jnp.where(key_at < t_ref[u], 0.0, MASKED)
+        q = tq[rr, pl.ds(pl.multiple_of(base, 128), 128)]
+        k = tq[rr, pl.ds(pl.multiple_of(base + width, 128), 128)]
+        v = tq[rr, pl.ds(pl.multiple_of(base + 2 * width, 128), 128)]
+        got = []
+        for half in range(2):
+            mine = side if half == 0 else ~side
+            s = nt(jnp.where(mine, q, jnp.zeros_like(q)), k) * 0.125 + bias
+            p = jnp.exp(s - jnp.max(s, -1, keepdims=True))
+            p = p * (1.0 / jnp.sum(p, -1, keepdims=True))
+            got.append(nn(p.astype(jnp.bfloat16), v))
+        ctx[rr, pl.ds(pl.multiple_of(base, 128), 128)] = jnp.where(side, got[0], got[1]).astype(jnp.bfloat16)
+        return carry
+
+    lax.fori_loop(0, utts * pairs, pair_step, 0)
+    mover.put(ctx, c_out)
+    wp.wait()
+    y2[...] = y1[...] + nn(ctx[...], w_proj[...])
+    mover.put(y2, y2_out)
+
+    def prepare_conv(rr, i, c):
+        normed[rr, :] = (ln_parts(y2[rr, :])[0] * gains[2:3]).astype(jnp.bfloat16)
+        return c
+
+    row_loop(rows, prepare_conv)
+    wi.wait()
+    for b in range(2):
+        r[:, b * width : (b + 1) * width] = nn(normed[...], w_pin[:, b * width : (b + 1) * width])
+    mover.put(r, r_out)
+    fill_gated(utts, frames, t_ref, r, gp)
+    taps = gains[5:14]
+
+    def conv(rr, i, total):
+        d_chunk = spread(gp, utts, frames, i, taps)
+        d[rr, :] = d_chunk
+        return total + fold8(d_chunk * valid_rows_of(t_ref, frames, i), jnp.add)
+
+    total = row_loop(rows, conv, jnp.zeros((8, width), jnp.float32))
+    mover.put(d, d_out)
+    count = t_ref[0]
+    for u in range(1, utts):
+        count = count + t_ref[u]
+    count = count.astype(jnp.float32)
+    mean = jnp.sum(total, 0, keepdims=True) / count
+
+    def deviate(rr, i, total):
+        gap = (d[rr, :] - mean) * valid_rows_of(t_ref, frames, i)
+        return total + fold8(gap * gap, jnp.add)
+
+    dev = jnp.sum(row_loop(rows, deviate, jnp.zeros((8, width), jnp.float32)), 0, keepdims=True)
+    write_rows(stats, 0, mean)
+    write_rows(stats, 4, dev)
+    stats[8:16, :] = jnp.full((8, 128), count, jnp.float32)
+    mover.finish()
+
+
+def fill_gated(utts, frames, t_ref, r, gp):
+    width = gp.shape[1]
+    span = frames + 16
+    per = frames // CHUNK_ROWS
+    for u in range(utts):
+        gp[u * span : u * span + 8, :] = jnp.zeros((8, width), jnp.float32)
+        gp[u * span + 8 + frames : (u + 1) * span, :] = jnp.zeros((8, width), jnp.float32)
+
+    def gate(rr, i, c):
+        g = r[rr, :width] * jax.nn.sigmoid(r[rr, width:]) * valid_rows_of(t_ref, frames, i)
+        at = (i // per) * span + 8 + lax.rem(i, per) * CHUNK_ROWS
+        gp[pl.ds(pl.multiple_of(at, 8), CHUNK_ROWS), :] = g
+        return c
+
+    row_loop(utts * frames, gate)
+
+
+def window(gp, frames, i):
+    per = frames // CHUNK_ROWS
+    at = (i // per) * (frames + 16) + lax.rem(i, per) * CHUNK_ROWS
+    return gp[pl.ds(pl.multiple_of(at, 8), CHUNK_ROWS + 16), :]
+
+
+def spread(gp, utts, frames, i, taps, flip=False):
+    win = window(gp, frames, i)
+    count = taps.shape[0]
+    total = None
+    for j in range(count):
+        shift = 8 - count // 2 + (count - 1 - j if flip else j)
+        term = win[shift : shift + CHUNK_ROWS] * taps[j : j + 1]
+        total = term if total is None else total + term
+    return total
+
+
+def part_two_kernel(table, d_ref, y2_ref, pooled_ref, small, whole, y3_out, h_out, y4_out, x_out,
+                    w_pout, w_sin, w_sout, act_b, y3, normed, h, act, y4, x, sems):
+    rows, width = y3.shape
+    mover = Mover(sems)
+    gains = small[...]
+    wo = mover.load_weight(whole, table["p_out"], w_pout, False)
+    sin = mover.load_weight(whole, table["s_in"], w_sin, False)
+    sout = mover.load_weight(whole, table["s_out"], w_sout, True)
+    mean = read_rows(pooled_ref, 0, width)
+    count = pooled_ref[8:9, 0:1]
+    istd = lax.rsqrt(read_rows(pooled_ref, 4, width) / count + EPS)
+
+    def bn(rr, i, c):
+        b = (d_ref[rr, :] - mean) * istd * gains[14:15] + gains[15:16]
+        act_b[rr, :] = (b * jax.nn.sigmoid(b)).astype(jnp.bfloat16)
+        return c
+
+    row_loop(rows, bn)
+    wo.wait()
+    y3[...] = y2_ref[...] + nn(act_b[...], w_pout[...])
+    mover.put(y3, y3_out)
+    ffn_fwd(rows, y3, gains[3:4], (w_sin, sin), (w_sout, sout), normed, h, act, y4, mover, h_out)
+    mover.put(y4, y4_out)
+
+    def last(rr, i, c):
+        x[rr, :] = ln_parts(y4[rr, :])[0] * gains[4:5]
+        return c
+
+    row_loop(rows, last)
+    mover.put(x, x_out)
+    mover.finish()
+
+
+def ffn_bwd(rows, v_ref, gain, w_in, w_out, h, loads, g_ref, gb, normed, dact, act, dh, dn, dw_in, dw_out, mover, grads, at_in, at_out):
+    def prepare(rr, i, c):
+        normed[rr, :] = (ln_parts(v_ref[rr, :].astype(jnp.float32))[0] * gain).astype(jnp.bfloat16)
+        gb[rr, :] = (0.5 * g_ref[rr, :]).astype(jnp.bfloat16)
+        return c
+
+    row_loop(rows, prepare)
+    w_out[1].wait()
+    for b in range(h.shape[0]):
+        cols = slice(b * WIDE, (b + 1) * WIDE)
+        dact[...] = nt(gb[...], w_out[0][cols, :])
+        loads[b].wait()
+
+        def slope(rr, i, c):
+            v = h[b, rr, :]
+            sg = jax.nn.sigmoid(v)
+            act[rr, :] = (v * sg).astype(jnp.bfloat16)
+            dh[rr, cols] = (dact[rr, :] * (sg * (1.0 + v * (1.0 - sg)))).astype(jnp.bfloat16)
+            return c
+
+        row_loop(rows, slope)
+        dw_out[cols, :] = tn(act[...], gb[...]).astype(jnp.bfloat16)
+        dw_in[:, cols] = tn(normed[...], dh[:, cols]).astype(jnp.bfloat16)
+    mover.put_weight(dw_out, grads, at_out)
+    mover.put_weight(dw_in, grads, at_in)
+    w_in[1].wait()
+    dn[...] = nt(dh[...], w_in[0][...])
+
+    def back(rr, i, total):
+        dv, dg = ln_back(v_ref[rr, :].astype(jnp.float32), gain, dn[rr, :])
+        g_ref[rr, :] = g_ref[rr, :] + dv
+        return total + dg
+
+    return row_loop(rows, back, jnp.zeros((8, g_ref.shape[1]), jnp.float32))
+
+
+def down(folded):
+    return jnp.sum(folded, 0, keepdims=True)
+
+
+def back_one_kernel(table, grad_ref, y4_ref, y3_ref, d_ref, pooled_ref, small, whole, h_hbm, g_out, db_out, grads, sums, gain_out,
+                    w_pout, w_sin, w_sout, g, gb, normed, dact, act, dh, dn, dw_in, dw_out, dw_pout, h, db, sems):
+    rows, width = g.shape
+    mover = Mover(sems)
+    gains = small[...]
+    sout = mover.load_weight(whole, table["s_out"], w_sout, True)
+    loads = [mover.load(h_hbm.at[b], h.at[b]) for b in range(h.shape[0])]
+    sin = mover.load_weight(whole, table["s_in"], w_sin, False)
+    wo = mover.load_weight(whole, table["p_out"], w_pout, False)
+
+    def first(rr, i, total):
+        dv, dg = ln_back(y4_ref[rr, :], gains[4:5], grad_ref[rr, :])
+        g[rr, :] = dv
+        return total + dg
+
+    gain4 = down(row_loop(rows, first, jnp.zeros((8, width), jnp.float32)))
+    gain3 = down(ffn_bwd(rows, y3_ref, gains[3:4], (w_sin, sin), (w_sout, sout), h, loads, g, gb, normed, dact, act, dh, dn,
+                         dw_in, dw_out, mover, grads, table["s_in"], table["s_out"]))
+    mover.put(g, g_out)
+    gain_out[...] = jnp.concatenate([gain3, gain4, jnp.zeros((6, width), jnp.float32)], 0)
+    mean = read_rows(pooled_ref, 0, width)
+    istd = lax.rsqrt(read_rows(pooled_ref, 4, width) / pooled_ref[8:9, 0:1] + EPS)
+
+    def cast(rr, i, c):
+        gb[rr, :] = g[rr, :].astype(jnp.bfloat16)
+        return c
+
+    row_loop(rows, cast)
+    wo.wait()
+    dact[...] = nt(gb[...], w_pout[...])
+
+    def bn(rr, i, totals):
+        z = (d_ref[rr, :] - mean) * istd
+        b = z * gains[14:15] + gains[15:16]
+        sg = jax.nn.sigmoid(b)
+        act[rr, :] = (b * sg).astype(jnp.bfloat16)
+        db_chunk = dact[rr, :] * (sg * (1.0 + b * (1.0 - sg)))
+        db[rr, :] = db_chunk
+        return totals[0] + fold8(db_chunk, jnp.add), totals[1] + fold8(db_chunk * z, jnp.add)
+
+    zero = jnp.zeros((8, width), jnp.float32)
+    one, two = row_loop(rows, bn, (zero, zero))
+    mover.put(db, db_out)
+    write_rows(sums, 0, down(one))
+    write_rows(sums, 4, down(two))
+    sums[8:16, :] = jnp.zeros((8, 128), jnp.float32)
+    dw_pout[...] = tn(act[...], gb[...]).astype(jnp.bfloat16)
+    mover.put_weight(dw_pout, grads, table["p_out"])
+    mover.finish()
+
+
+def back_two_kernel(utts, table, start, end, t_ref, x_ref, y1_ref, y2_ref, r_ref, t_in, c_ref, d_ref, db_ref, g_in, pooled_ref, sums_ref, late_ref, small, whole, h_hbm,
+                    g_out, grads,
+                    w_pin, w_proj, w_joint, w_fin, w_fout, g, gb, normed, dact, act, dh, dn, dw_pin, dw_proj, dw_joint, dw_in, dw_out, h, gp, dd, dr, dt, sm, sems):
+    rows, width = g.shape
+    frames = rows // utts
+    mover = Mover(sems)
+    gains = small[...]
+    wi = mover.load_weight(whole, table["p_in"], w_pin, False)
+    wp = mover.load_weight(whole, table["w_proj"], w_proj, False)
+    wj = mover.load_weight(whole, table["w_joint"], w_joint, False)
+    fout = mover.load_weight(whole, table["f_out"], w_fout, True)
+    loads = [mover.load(h_hbm.at[b], h.at[b]) for b in range(h.shape[0])]
+    fin = mover.load_weight(whole, table["f_in"], w_fin, False)
+    mean = read_rows(pooled_ref, 0, width)
+    count = pooled_ref[8:9, 0:1]
+    istd = lax.rsqrt(read_rows(pooled_ref, 4, width) / count + EPS)
+    bias_sum = read_rows(sums_ref, 0, width)
+    gain_sum = read_rows(sums_ref, 4, width)
+    taps = gains[5:14]
+    ntaps = taps.shape[0]
+    span = frames + 16
+    per = frames // CHUNK_ROWS
+    fill_gated(utts, frames, t_ref, r_ref, gp)
+    for u in range(utts):
+        dd[u * span : u * span + 8, :] = jnp.zeros((8, width), jnp.float32)
+        dd[u * span + 8 + frames : (u + 1) * span, :] = jnp.zeros((8, width), jnp.float32)
+
+    def bn(rr, i, c):
+        z = (d_ref[rr, :] - mean) * istd
+        v = gains[14:15] * istd * (db_ref[rr, :] - valid_rows_of(t_ref, frames, i) * (bias_sum + z * gain_sum) / count)
+        at = (i // per) * span + 8 + lax.rem(i, per) * CHUNK_ROWS
+        dd[pl.ds(pl.multiple_of(at, 8), CHUNK_ROWS), :] = v
+        return c
+
+    row_loop(rows, bn)
+
+    def conv(rr, i, totals):
+        dg = spread(dd, utts, frames, i, taps, True) * valid_rows_of(t_ref, frames, i)
+        sg = jax.nn.sigmoid(r_ref[rr, width:])
+        dr[rr, :width] = (dg * sg).astype(jnp.bfloat16)
+        dr[rr, width:] = (dg * r_ref[rr, :width] * sg * (1.0 - sg)).astype(jnp.bfloat16)
+        win = window(gp, frames, i)
+        mine = window(dd, frames, i)[8 : 8 + CHUNK_ROWS]
+        normed[rr, :] = (ln_parts(y2_ref[rr, :])[0] * gains[2:3]).astype(jnp.bfloat16)
+        return tuple(
+            totals[j] + fold8(win[8 - ntaps // 2 + j : 8 - ntaps // 2 + j + CHUNK_ROWS] * mine, jnp.add) for j in range(ntaps)
+        )
+
+    zero = jnp.zeros((8, width), jnp.float32)
+    tap_grads = [down(x) for x in row_loop(rows, conv, (zero,) * ntaps)]
+    for b in range(2):
+        cols = slice(b * width, (b + 1) * width)
+        dw_pin[:, cols] = tn(normed[...], dr[:, cols]).astype(jnp.bfloat16)
+    mover.put_weight(dw_pin, grads, table["p_in"] - start)
+    wi.wait()
+    dn[...] = nt(dr[...], w_pin[...])
+
+    def back_conv(rr, i, total):
+        dv, dg = ln_back(y2_ref[rr, :], gains[2:3], dn[rr, :])
+        v = g_in[rr, :] + dv
+        g[rr, :] = v
+        gb[rr, :] = v.astype(jnp.bfloat16)
+        normed[rr, :] = (ln_parts(y1_ref[rr, :])[0] * gains[1:2]).astype(jnp.bfloat16)
+        return total + dg
+
+    gain2 = down(row_loop(rows, back_conv, zero))
+    dw_proj[...] = tn(c_ref[...], gb[...]).astype(jnp.bfloat16)
+    mover.put_weight(dw_proj, grads, table["w_proj"] - start)
+    wp.wait()
+    act[...] = nt(gb[...], w_proj[...]).astype(jnp.bfloat16)
+    pairs = width // 128
+    side = lax.broadcasted_iota(jnp.int32, (frames, 128), 1) < 64
+    key_at = lax.broadcasted_iota(jnp.int32, (frames, 1), 0)
+
+    def pair_step(m, carry):
+        u = m // pairs
+        base = lax.rem(m, pairs) * 128
+        rr = pl.ds(pl.multiple_of(u * frames, frames), frames)
+        at = [pl.ds(pl.multiple_of(base + b * width, 128), 128) for b in range(3)]
+        bias = jnp.where(key_at < t_ref[u], 0.0, MASKED)
+        q = t_in[rr, at[0]]
+        k = t_in[rr, at[1]]
+        v = t_in[rr, at[2]]
+        dc = act[rr, at[0]]
+        got = []
+        for half in range(2):
+            mine = side if half == 0 else ~side
+            nothing = jnp.zeros_like(k)
+            s = nt(jnp.where(mine, k, nothing), q) * 0.125 + bias
+            p = jnp.exp(s - jnp.max(s, 0, keepdims=True))
+            p = p * (1.0 / jnp.sum(p, 0, keepdims=True))
+            dp = nt(jnp.where(mine, v, nothing), dc)
+            ds = (p * (dp - jnp.sum(dp * p, 0, keepdims=True))).astype(jnp.bfloat16)
+            got.append((tn(ds, k) * 0.125, nn(ds, q) * 0.125, nn(p.astype(jnp.bfloat16), dc)))
+        for b in range(3):
+            dt[rr, at[b]] = jnp.where(side, got[0][b], got[1][b]).astype(jnp.bfloat16)
+        return carry
+
+    lax.fori_loop(0, utts * pairs, pair_step, 0)
+    for b in range(3):
+        cols = slice(b * width, (b + 1) * width)
+        dw_joint[:, cols] = tn(normed[...], dt[:, cols]).astype(jnp.bfloat16)
+    mover.put_weight(dw_joint, grads, table["w_joint"] - start)
+    wj.wait()
+    dn[...] = nt(dt[...], w_joint[...])
+
+    def back_attend(rr, i, total):
+        dv, dg = ln_back(y1_ref[rr, :], gains[1:2], dn[rr, :])
+        g[rr, :] = g[rr, :] + dv
+        return total + dg
+
+    gain1 = down(row_loop(rows, back_attend, zero))
+    gain0 = down(ffn_bwd(rows, x_ref, gains[0:1], (w_fin, fin), (w_fout, fout), h, loads, g, gb, normed, dact, act, dh, dn,
+                         dw_in, dw_out, mover, grads, table["f_in"] - start, table["f_out"] - start))
+    mover.put(g, g_out)
+    packed = jnp.concatenate([gain0, gain1, gain2, late_ref[0:2, :]] + tap_grads + [jnp.zeros((2, width), jnp.float32)], 0)
+    n = grads.shape[0]
+    low = width // n
+    for s in range(n):
+        sm[s] = jnp.concatenate([packed[:, s * low : (s + 1) * low], jnp.zeros((16, WIDE - low), jnp.float32)], 1).astype(jnp.bfloat16)
+    mover.put(sm, grads.at[:, pl.ds(end - start, 16), :])
+    mover.finish()
+
+
+VMEM_SPEC = pl.BlockSpec(memory_space=pltpu.VMEM)
+SMEM_SPEC = pl.BlockSpec(memory_space=pltpu.SMEM)
+ANY_SPEC = pl.BlockSpec(memory_space=pl.ANY)
+F32 = jnp.float32
+BF16 = jnp.bfloat16
+
+
+def sds(shape, dtype=jnp.float32):
+    return jax.ShapeDtypeStruct(shape, dtype)
+
+
+def part_one(t_len, x, small, whole, ff):
+    rows, width = x.shape
+    utts = t_len.shape[0]
+    table, _ = offsets(whole.shape[0], width, ff)
+    nb = ff // WIDE
+    v = pltpu.VMEM
+    return pl.pallas_call(
+        partial(part_one_kernel, utts, table),
+        in_specs=[SMEM_SPEC, VMEM_SPEC, VMEM_SPEC, ANY_SPEC],
+        out_specs=[ANY_SPEC] * 7 + [VMEM_SPEC],
+        out_shape=[sds((rows, width)), sds((nb, rows, WIDE)), sds((rows, width)), sds((rows, 3 * width), BF16),
+                   sds((rows, width), BF16), sds((rows, 2 * width)), sds((rows, width)), sds((16, 128))],
+        scratch_shapes=[v((width, ff), BF16), v((ff, width), BF16), v((width, 3 * width), BF16), v((width, width), BF16),
+                        v((width, 2 * width), BF16), v((rows, width), F32), v((rows, width), F32), v((rows, width), BF16),
+                        v((nb, rows, WIDE), F32), v((rows, ff), BF16), v((rows, 3 * width), BF16), v((rows, width), BF16),
+                        v((rows, 2 * width), F32), v((utts * (rows // utts + 16), width), F32), v((rows, width), F32),
+                        pltpu.SemaphoreType.DMA((24,))],
+        compiler_params=pltpu.CompilerParams(vmem_limit_bytes=56 << 20),
+        name="layer_part_one",
+    )(t_len, x, small, whole)
+
+
+def part_two(d, y2, pooled, small, whole, ff):
+    rows, width = d.shape
+    table, _ = offsets(whole.shape[0], width, ff)
+    nb = ff // WIDE
+    v = pltpu.VMEM
+    return pl.pallas_call(
+        partial(part_two_kernel, table),
+        in_specs=[VMEM_SPEC] * 4 + [ANY_SPEC],
+        out_specs=[ANY_SPEC] * 4,
+        out_shape=[sds((rows, width)), sds((nb, rows, WIDE)), sds((rows, width)), sds((rows, width))],
+        scratch_shapes=[v((width, width), BF16), v((width, ff), BF16), v((ff, width), BF16), v((rows, width), BF16),
+                        v((rows, width), F32), v((rows, width), BF16), v((nb, rows, WIDE), F32), v((rows, ff), BF16),
+                        v((rows, width), F32), v((rows, width), F32), pltpu.SemaphoreType.DMA((16,))],
+        compiler_params=pltpu.CompilerParams(vmem_limit_bytes=56 << 20),
+        name="layer_part_two",
+    )(d, y2, pooled, small, whole)
+
+
+def tiled(count):
+    return -(-count // TILE) * TILE
+
+
+def back_one(grad, y4, y3, d, pooled, small, whole, h, ff):
+    rows, width = grad.shape
+    n = whole.shape[0]
+    table, _ = offsets(n, width, ff)
+    nb = ff // WIDE
+    v = pltpu.VMEM
+    return pl.pallas_call(
+        partial(back_one_kernel, table),
+        in_specs=[VMEM_SPEC] * 6 + [ANY_SPEC] * 2,
+        out_specs=[ANY_SPEC] * 3 + [VMEM_SPEC] * 2,
+        out_shape=[sds((rows, width)), sds((rows, width)), sds((n, tiled(table["p_in"]), WIDE), BF16), sds((16, 128)), sds((8, width))],
+        scratch_shapes=[v((width, width), BF16), v((width, ff), BF16), v((ff, width), BF16), v((rows, width), F32),
+                        v((rows, width), BF16), v((rows, width), BF16), v((rows, width), F32), v((rows, width), BF16),
+                        v((rows, ff), BF16), v((rows, width), F32), v((width, ff), BF16), v((ff, width), BF16),
+                        v((width, width), BF16), v((nb, rows, WIDE), F32), v((rows, width), F32), pltpu.SemaphoreType.DMA((16,))],
+        compiler_params=pltpu.CompilerParams(vmem_limit_bytes=56 << 20),
+        name="back_part_one",
+    )(grad, y4, y3, d, pooled, small, whole, h)
+
+
+def back_two(t_len, x, y1, y2, r, t, c, d, db, g, pooled, sums, late, small, whole, h, ff):
+    rows, width = d.shape
+    utts = t_len.shape[0]
+    n = whole.shape[0]
+    table, end = offsets(n, width, ff)
+    start = table["p_in"]
+    nb = ff // WIDE
+    v = pltpu.VMEM
+    pad_rows = utts * (rows // utts + 16)
+    return pl.pallas_call(
+        partial(back_two_kernel, utts, table, start, end),
+        in_specs=[SMEM_SPEC] + [VMEM_SPEC] * 13 + [ANY_SPEC] * 2,
+        out_specs=[ANY_SPEC] * 2,
+        out_shape=[sds((rows, width)), sds((n, tiled(end - start + 16), WIDE), BF16)],
+        scratch_shapes=[v((width, 2 * width), BF16), v((width, width), BF16), v((width, 3 * width), BF16), v((width, ff), BF16),
+                        v((ff, width), BF16), v((rows, width), F32), v((rows, width), BF16), v((rows, width), BF16),
+                        v((rows, width), F32), v((rows, width), BF16), v((rows, ff), BF16), v((rows, width), F32),
+                        v((width, 2 * width), BF16), v((width, width), BF16), v((width, 3 * width), BF16), v((width, ff), BF16),
+                        v((ff, width), BF16), v((nb, rows, WIDE), F32), v((pad_rows, width), F32), v((pad_rows, width), F32),
+                        v((rows, 2 * width), BF16), v((rows, 3 * width), BF16), v((n, 16, WIDE), BF16), pltpu.SemaphoreType.DMA((20,))],
+        compiler_params=pltpu.CompilerParams(vmem_limit_bytes=60 << 20),
+        name="back_part_two",
+    )(t_len, x, y1, y2, r, t, c, d, db, g, pooled, sums, late, small, whole, h)
+
+
+def lift(rows):
+    return -(-rows // 16) * 16
+
+
+def joint_sizes(w_enc, w_pred, w_tok):
+    low, tall = lift(w_enc.shape[0]), lift(w_pred.shape[0])
+    return [low, tall, tall * (w_tok.shape[1] // WIDE), tall]
+
+
+def pack_kernel(layers, table, end, *refs):
+    names = PLACE + ("gains", "taps", "bn_gain", "bn_bias", "enc", "pred", "tok", "dur")
+    src = dict(zip(names, refs))
+    outs = refs[len(names) :]
+    for layer in range(layers):
+        out = outs[layer]
+        for name in PLACE:
+            ref = src[name]
+            height = ref.shape[1]
+            for b in range(ref.shape[2] // WIDE):
+                at = table[name] + b * height
+                out[at : at + height, :] = ref[layer, :, b * WIDE : (b + 1) * WIDE]
+        small = [src["gains"][layer], src["taps"][layer], src["bn_gain"][layer : layer + 1, :], src["bn_bias"][layer : layer + 1, :]]
+        small = jnp.concatenate([x.astype(jnp.float32) for x in small], 0)
+        small = jnp.concatenate([small, jnp.zeros((16, WIDE - small.shape[1]), jnp.float32)], 1)
+        out[end : end + 16, :] = small.astype(jnp.bfloat16)
+        if out.shape[0] > end + 16:
+            out[end + 16 :, :] = jnp.zeros((out.shape[0] - end - 16, WIDE), jnp.bfloat16)
+    out = outs[layers - 1]
+    enc, pred, tok, dur = src["enc"], src["pred"], src["tok"], src["dur"]
+    low, tall = enc.shape[0], pred.shape[0]
+    at = end + 16
+    out[at : at + low, :] = enc[:, :WIDE]
+    at += lift(low)
+    out[at : at + tall, :] = pred[:, :WIDE]
+    at += lift(tall)
+    for b in range(tok.shape[1] // WIDE):
+        out[at : at + tall, :] = tok[:, b * WIDE : (b + 1) * WIDE]
+        at += lift(tall)
+    out[at : at + low, 0:128] = enc[:, WIDE:]
+    out[at : at + tall, 128:256] = pred[:, WIDE:]
+    dur = dur[...].astype(jnp.float32)
+    out[at : at + tall, 256:384] = jnp.concatenate([dur, jnp.zeros((tall, 128 - dur.shape[1]), jnp.float32)], 1).astype(jnp.bfloat16)
+
+
+def pack(layers, table, end, extra, arrays):
+    shapes = []
+    for layer in range(layers):
+        count = end + 16 + (extra if layer == layers - 1 else 0)
+        shapes.append(sds((tiled(count), WIDE), BF16))
+    return pl.pallas_call(
+        partial(pack_kernel, layers, table, end),
+        in_specs=[VMEM_SPEC] * len(arrays),
+        out_specs=[VMEM_SPEC] * layers,
+        out_shape=shapes,
+        compiler_params=pltpu.CompilerParams(vmem_limit_bytes=48 << 20),
+        name="pack_weights",
+    )(*arrays)
+
+
+def unpack_kernel(layers, table, end, dims, share, gains, f_in, f_out, w_joint, w_proj, p_in, taps, p_out, s_in, s_out, enc, pred, tok, dur):
+    outs = {"f_in": f_in, "f_out": f_out, "w_joint": w_joint, "w_proj": w_proj, "p_in": p_in, "p_out": p_out, "s_in": s_in, "s_out": s_out}
+    starts, width, joint = dims
+    shard = gains.shape[2]
+    for layer in range(layers):
+        for name in PLACE:
+            out = outs[name]
+            height = out.shape[1]
+            early = table[name] < table["p_in"]
+            base = starts[layer][0] + table[name] if early else starts[layer][1] + table[name] - table["p_in"]
+            for b in range(out.shape[2] // WIDE):
+                out[layer, :, b * WIDE : (b + 1) * WIDE] = share[base + b * height : base + (b + 1) * height, :].astype(jnp.float32)
+        base = starts[layer][1] + end - table["p_in"]
+        small = share[base : base + 16, 0:128].astype(jnp.float32)
+        gains[layer] = small[0:5, :shard]
+        taps[layer] = small[5 : 5 + taps.shape[1], :shard]
+    at = starts[layers]
+    low, tall = enc.shape[0], pred.shape[0]
+    enc[:, :WIDE] = share[at : at + low, :].astype(jnp.float32)
+    at += lift(low)
+    pred[:, :WIDE] = share[at : at + tall, :].astype(jnp.float32)
+    at += lift(tall)
+    for b in range(tok.shape[1] // WIDE):
+        tok[:, b * WIDE : (b + 1) * WIDE] = share[at : at + tall, :].astype(jnp.float32)
+        at += lift(tall)
+    enc[:, WIDE:] = share[at : at + low, 0:128].astype(jnp.float32)
+    pred[:, WIDE:] = share[at : at + tall, 128:256].astype(jnp.float32)
+    dur[...] = share[at : at + tall, 256:384].astype(jnp.float32)[:, : dur.shape[1]]
+
+
+def unpack(layers, table, end, dims, share, like):
+    return pl.pallas_call(
+        partial(unpack_kernel, layers, table, end, dims),
+        in_specs=[VMEM_SPEC],
+        out_specs=[VMEM_SPEC] * len(like),
+        out_shape=[sds(x.shape) for x in like],
+        compiler_params=pltpu.CompilerParams(vmem_limit_bytes=48 << 20),
+        name="unpack_grads",
+    )(share)
 
 
 def cut(whole, sizes, offset=0):
@@ -673,49 +1339,31 @@
     return parts
 
 
-def layer_sizes(n, mats):
-    return [m.shape[1] * m.shape[2] // WIDE for m in mats] + [16]
-
-
-def unpack_layer(whole, sizes, mats, width):
-    parts = cut(whole, sizes)
-    full = [
-        from_blocks(p, m.shape[2]) if m.shape[2] != WIDE else p.reshape(-1, WIDE)
-        for p, m in zip(parts, mats)
-    ]
-    shard = width // whole.shape[0]
-    small = jnp.swapaxes(parts[-1][:, :, :shard], 0, 1).reshape(16, width)
-    return full, small
-
-
-def unpack_joint(whole, sizes, w_enc, w_dur):
-    enc, pred, tok, rest = cut(whole, sizes[1:], sizes[0])
+def from_blocks(part, cols, rows):
+    n, height, _ = part.shape
+    blocks = cols // WIDE
+    return jnp.swapaxes(part.reshape(n, blocks, height // blocks, WIDE)[:, :, :rows], 1, 2).reshape(-1, cols)
+
+
+def unpack_joint(whole, first, sizes, w_enc, w_pred, vocab):
+    enc, pred, tok, rest = cut(whole, sizes, first)
     joint = w_enc.shape[1]
     low = w_enc.shape[0]
-    w_enc = jnp.concatenate([enc, rest[:, :low, : joint - WIDE]], 2).reshape(-1, joint)
-    w_pred = jnp.concatenate([pred, rest[:, :, 128 : 128 + joint - WIDE]], 2).reshape(-1, joint)
-    return w_enc, w_pred, from_blocks(tok, 1024), rest[:, :, 256:384].reshape(-1, 128)
-
-
-def split_rows(grad, n):
-    rows, cols = grad.shape
-    blocks = cols // WIDE
-    grad = grad.astype(jnp.bfloat16).reshape(n, rows // n, blocks, WIDE)
-    return jnp.swapaxes(grad, 1, 2).reshape(n, -1, WIDE)
-
-
-def pack_layer_grads(mats, gains, depth, n):
-    width = gains.shape[1]
-    small = jnp.concatenate([gains, depth], 0).astype(jnp.bfloat16)
-    small = jnp.swapaxes(small.reshape(-1, n, width // n), 0, 1)
-    small = jnp.pad(small, ((0, 0), (0, 16 - small.shape[1]), (0, WIDE - small.shape[2])))
-    return [split_rows(m, n) for m in mats] + [small]
+    tall = w_pred.shape[0]
+    w_enc = jnp.concatenate([enc[:, :low], rest[:, :low, : joint - WIDE]], 2).reshape(-1, joint)
+    w_pred = jnp.concatenate([pred[:, :tall], rest[:, :tall, 128 : 128 + joint - WIDE]], 2).reshape(-1, joint)
+    return w_enc, w_pred, from_blocks(tok, vocab, tall), rest[:, :tall, 256:384].reshape(-1, 128)
+
+
+def grow(part):
+    short = lift(part.shape[1]) - part.shape[1]
+    return jnp.pad(part, ((0, 0), (0, short), (0, 0))) if short else part
 
 
 def pack_joint_grads(g_enc, g_pred, g_tok, g_dur, n):
     def shards(grad):
-        return grad.astype(jnp.bfloat16).reshape(n, -1, grad.shape[1])
-    g_enc, g_pred, g_dur = shards(g_enc), shards(g_pred), shards(g_dur)
+        return grow(grad.astype(jnp.bfloat16).reshape(n, -1, grad.shape[1]))
+    g_enc, g_pred, g_tok, g_dur = shards(g_enc), shards(g_pred), shards(g_tok), shards(g_dur)
     tall = g_pred.shape[1]
     rest = jnp.concatenate(
         [
@@ -726,25 +1374,10 @@
         ],
         2,
     )
-    return [g_enc[:, :, :WIDE], g_pred[:, :, :WIDE], split_rows(g_tok, n), rest]
-
-
-def shard_from_blocks(part, cols):
-    blocks = cols // WIDE
-    height = part.shape[0] // blocks
-    return jnp.swapaxes(part.reshape(blocks, height, WIDE), 0, 1).reshape(height, cols).astype(jnp.float32)
-
-
-def norm_rows(value, gain):
-    centre = jnp.mean(value, -1, keepdims=True)
-    centred = value - centre
-    spread = jnp.mean(centred * centred, -1, keepdims=True)
-    return centred * lax.rsqrt(spread + EPS) * gain
-
-
-def norm_back(value, gain, grad):
-    result, pullback = jax.vjp(norm_rows, value, gain)
-    return pullback(grad)
+    parts = [g_enc[:, :, :WIDE], g_pred[:, :, :WIDE]]
+    parts += [g_tok[:, :, b : b + WIDE] for b in range(0, g_tok.shape[2], WIDE)] + [rest]
+    rows = sum(p.shape[1] for p in parts)
+    return jnp.concatenate(parts + [jnp.zeros((n, tiled(rows) - rows, WIDE), jnp.bfloat16)], 1)
 
 
 def matmul(left, right):
@@ -760,222 +1393,6 @@
 def contract_cols(left, right):
     return lax.dot_general(
         left, right, (((1,), (1,)), ((), ())), preferred_element_type=jnp.float32
-    )
-
-
-def swish_slope(value):
-    sigmoid_value = jax.nn.sigmoid(value)
-    return sigmoid_value * (1.0 + value * (1.0 - sigmoid_value))
-
-
-def ffn_forward(resid, gain, w_in, w_out):
-    normed_low = norm_rows(resid, gain).astype(jnp.bfloat16)
-    hidden = matmul(normed_low, w_in)
-    active_low = jax.nn.silu(hidden).astype(jnp.bfloat16)
-    return (resid + 0.5 * matmul(active_low, w_out), (normed_low, hidden, active_low))
-
-
-def ffn_backward(resid, gain, w_in, w_out, saved, grad_out):
-    normed_low, hidden, active_low = saved
-    grad_branch = (0.5 * grad_out).astype(jnp.bfloat16)
-    grad_w_out = contract_rows(active_low, grad_branch)
-    grad_hidden = (contract_cols(grad_branch, w_out) * swish_slope(hidden)).astype(jnp.bfloat16)
-    grad_w_in = contract_rows(normed_low, grad_hidden)
-    grad_normed = contract_cols(grad_hidden, w_in)
-    grad_resid, grad_gain = norm_back(resid, gain, grad_normed)
-    return (grad_out + grad_resid, grad_gain, grad_w_in, grad_w_out)
-
-
-def attend_forward(resid, gain, w_joint, w_proj, key_bias):
-    rows, width = resid.shape
-    utts = key_bias.shape[0]
-    head_dim = width // HEADS
-    normed_low = norm_rows(resid, gain).astype(jnp.bfloat16)
-    joint_low = (
-        matmul(normed_low, w_joint)
-        .astype(jnp.bfloat16)
-        .reshape(utts, rows // utts, 3, HEADS, head_dim)
-    )
-    scores = (
-        jnp.einsum(
-            "uqhe,ukhe->uhqk",
-            joint_low[:, :, 0],
-            joint_low[:, :, 1],
-            preferred_element_type=jnp.float32,
-        )
-        * head_dim ** (-0.5)
-        + key_bias
-    )
-    weights = jax.nn.softmax(scores, axis=-1)
-    weights_low = weights.astype(jnp.bfloat16)
-    context = jnp.einsum(
-        "uhqk,ukhe->uqhe", weights_low, joint_low[:, :, 2], preferred_element_type=jnp.float32
-    )
-    context_low = context.reshape(rows, width).astype(jnp.bfloat16)
-    return (
-        resid + matmul(context_low, w_proj),
-        (normed_low, joint_low, weights, weights_low, context_low),
-    )
-
-
-def attend_backward(resid, gain, w_joint, w_proj, saved, grad_out):
-    normed_low, joint_low, weights, weights_low, context_low = saved
-    rows, width = resid.shape
-    utts, frames, three, heads, head_dim = joint_low.shape
-    scale = head_dim ** (-0.5)
-    query, key, value = (joint_low[:, :, 0], joint_low[:, :, 1], joint_low[:, :, 2])
-    grad_branch = grad_out.astype(jnp.bfloat16)
-    grad_proj = contract_rows(context_low, grad_branch)
-    grad_context = (
-        contract_cols(grad_branch, w_proj)
-        .astype(jnp.bfloat16)
-        .reshape(utts, frames, heads, head_dim)
-    )
-    grad_weights = jnp.einsum(
-        "uqhe,ukhe->uhqk", grad_context, value, preferred_element_type=jnp.float32
-    )
-    grad_value = jnp.einsum(
-        "uhqk,uqhe->ukhe", weights_low, grad_context, preferred_element_type=jnp.float32
-    )
-    grad_scores = (
-        weights * (grad_weights - jnp.sum(grad_weights * weights, -1, keepdims=True))
-    ).astype(jnp.bfloat16)
-    grad_query = (
-        jnp.einsum("uhqk,ukhe->uqhe", grad_scores, key, preferred_element_type=jnp.float32) * scale
-    )
-    grad_key = (
-        jnp.einsum("uhqk,uqhe->ukhe", grad_scores, query, preferred_element_type=jnp.float32)
-        * scale
-    )
-    grad_joint = (
-        jnp.stack([grad_query, grad_key, grad_value], 2)
-        .reshape(rows, 3 * width)
-        .astype(jnp.bfloat16)
-    )
-    grad_w_joint = contract_rows(normed_low, grad_joint)
-    grad_normed = contract_cols(grad_joint, w_joint)
-    grad_resid, grad_gain = norm_back(resid, gain, grad_normed)
-    return (grad_out + grad_resid, grad_gain, grad_w_joint, grad_proj)
-
-
-def conv_inner(projected, depth, valid_rows, utts):
-    rows, double = projected.shape
-    width = double // 2
-    frames = rows // utts
-    taps = depth.shape[0]
-    gated = projected[:, :width] * jax.nn.sigmoid(projected[:, width:]) * valid_rows
-    padded = jnp.pad(gated.reshape(utts, frames, width), ((0, 0), (taps // 2, taps // 2), (0, 0)))
-    total = padded[:, 0:frames] * depth[0]
-    for tap in range(1, taps):
-        total = total + padded[:, tap : tap + frames] * depth[tap]
-    return total.reshape(rows, width)
-
-
-def run_layer(resid, weights, valid_rows, key_bias, layer):
-    gains, f_in, f_out, w_joint, w_proj, p_in, depth, bn_gain, bn_bias, p_out, s_in, s_out = weights
-    gains = gains.astype(jnp.float32)
-    utts = key_bias.shape[0]
-    first, saved_first = ffn_forward(resid, gains[0], f_in, f_out)
-    second, saved_attend = attend_forward(first, gains[1], w_joint, w_proj, key_bias)
-    normed_low = norm_rows(second, gains[2]).astype(jnp.bfloat16)
-    projected = matmul(normed_low, p_in)
-    depthwise = conv_inner(projected, depth.astype(jnp.float32), valid_rows, utts)
-    centre, inv_std, count = global_stats(depthwise, valid_rows, 8 + layer)
-    normalized = (depthwise - centre) * inv_std
-    shifted = normalized * bn_gain.astype(jnp.float32) + bn_bias.astype(jnp.float32)
-    active_low = jax.nn.silu(shifted).astype(jnp.bfloat16)
-    third = second + matmul(active_low, p_out)
-    fourth, saved_fourth = ffn_forward(third, gains[3], s_in, s_out)
-    output = norm_rows(fourth, gains[4])
-    record = (
-        resid,
-        first,
-        second,
-        third,
-        fourth,
-        saved_first,
-        saved_attend,
-        saved_fourth,
-        normed_low,
-        projected,
-        normalized,
-        shifted,
-        active_low,
-        inv_std,
-        count,
-    )
-    return (output, record)
-
-
-def layer_backward(weights, record, grad_out, valid_rows, key_bias, layer):
-    gains, f_in, f_out, w_joint, w_proj, p_in, depth, bn_gain, bn_bias, p_out, s_in, s_out = weights
-    gains = gains.astype(jnp.float32)
-    utts = key_bias.shape[0]
-    (
-        resid,
-        first,
-        second,
-        third,
-        fourth,
-        saved_first,
-        saved_attend,
-        saved_fourth,
-        normed_low,
-        projected,
-        normalized,
-        shifted,
-        active_low,
-        inv_std,
-        count,
-    ) = record
-    grad_fourth, grad_gain_four = norm_back(fourth, gains[4], grad_out)
-    grad_third, grad_gain_three, grad_s_in, grad_s_out = ffn_backward(
-        third, gains[3], s_in, s_out, saved_fourth, grad_fourth
-    )
-    grad_branch = grad_third.astype(jnp.bfloat16)
-    grad_p_out = contract_rows(active_low, grad_branch)
-    grad_shifted = contract_cols(grad_branch, p_out) * swish_slope(shifted)
-    bias_sum, gain_sum = global_sums(
-        jnp.sum(grad_shifted, 0), jnp.sum(grad_shifted * normalized, 0), 12 + layer
-    )
-    grad_depthwise = (
-        bn_gain.astype(jnp.float32)
-        * inv_std
-        * (grad_shifted - valid_rows * (bias_sum + normalized * gain_sum) / count)
-    )
-    conv_local = partial(conv_inner, valid_rows=valid_rows, utts=utts)
-    result, pullback = jax.vjp(conv_local, projected, depth.astype(jnp.float32))
-    grad_projected, grad_depth = pullback(grad_depthwise)
-    grad_projected_low = grad_projected.astype(jnp.bfloat16)
-    grad_p_in = contract_rows(normed_low, grad_projected_low)
-    grad_normed = contract_cols(grad_projected_low, p_in)
-    grad_conv_resid, grad_gain_two = norm_back(second, gains[2], grad_normed)
-    grad_second = grad_third + grad_conv_resid
-    grad_first, grad_gain_one, grad_joint, grad_proj = attend_backward(
-        first, gains[1], w_joint, w_proj, saved_attend, grad_second
-    )
-    grad_resid, grad_gain_zero, grad_f_in, grad_f_out = ffn_backward(
-        resid, gains[0], f_in, f_out, saved_first, grad_first
-    )
-    grad_gains = jnp.stack(
-        [grad_gain_zero, grad_gain_one, grad_gain_two, grad_gain_three, grad_gain_four]
-    )
-    return (
-        grad_resid,
-        (
-            grad_gains,
-            grad_f_in,
-            grad_f_out,
-            grad_joint,
-            grad_proj,
-            grad_p_in,
-            grad_depth,
-            gain_sum,
-            bias_sum,
-            grad_p_out,
-            grad_s_in,
-            grad_s_out,
-        ),
     )
 
 
@@ -1005,38 +1422,41 @@
     utts, frames, width = frames_in.shape
     slots = pred_states.shape[1]
     rows = utts * frames
-    positions = lax.broadcasted_iota(jnp.int32, (utts, frames), 1)
-    valid = (positions < frame_lengths[:, None]).astype(jnp.float32)
-    valid_rows = valid.reshape(rows, 1)
-    key_bias = ((1.0 - valid) * MASKED)[:, None, None, :]
     layers = norm_gains.shape[0]
     n = lax.axis_size("fsdp")
-    mats = (first_in, first_out, attend_joint, attend_out, point_in, point_out, second_in, second_out)
-    sizes = layer_sizes(n, mats)
-    joint_pack = pack_joint(enc_weight, pred_weight, token_weight, duration_weight)
-    tail = [sum(sizes)] + [p.shape[0] for p in joint_pack]
+    ff = first_in.shape[2]
+    mats = {
+        "f_in": first_in, "f_out": first_out, "w_joint": attend_joint, "w_proj": attend_out,
+        "p_in": point_in, "p_out": point_out, "s_in": second_in, "s_out": second_out,
+    }
+    table, end = offsets(n, width, ff)
+    shard = width // n
+    sizes = joint_sizes(enc_weight, pred_weight, token_weight)
+    vocab = token_weight.shape[1]
+    packs = pack(
+        layers,
+        table,
+        end,
+        sum(sizes),
+        [mats[name] for name in PLACE]
+        + [norm_gains, depth_taps, batch_gain, batch_bias, enc_weight, pred_weight, token_weight, duration_weight],
+    )
     wholes = []
+    smalls = []
     for layer in range(layers):
-        parts = pack_layer(
-            [m[layer] for m in mats],
-            [norm_gains[layer], depth_taps[layer], batch_gain[layer : layer + 1], batch_bias[layer : layer + 1]],
-        )
-        if layer == layers - 1:
-            parts = parts + joint_pack
-        wholes.append(gather(padded(parts), 1 + layer))
-    weights_of = []
-    for layer in range(layers):
-        full, small = unpack_layer(wholes[layer], sizes, mats, width)
-        f_in, f_out, w_joint, w_proj, p_in, p_out, s_in, s_out = full
-        weights_of.append(
-            (small[:5], f_in, f_out, w_joint, w_proj, p_in, small[5:14], small[14], small[15], p_out, s_in, s_out)
-        )
-    resid = frames_in.reshape(rows, width).astype(jnp.float32)
+        whole = gather(packs[layer], 1 + layer)
+        small = whole[:, end : end + 16, :shard].astype(jnp.float32)
+        wholes.append(whole)
+        smalls.append(jnp.swapaxes(small, 0, 1).reshape(16, width))
+    resid = frames_in.reshape(rows, width)
     records = []
     for layer in range(layers):
-        resid, record = run_layer(resid, weights_of[layer], valid_rows, key_bias, layer)
-        records.append((None, record))
-    w_enc, w_pred, w_tok, w_dur = unpack_joint(wholes[-1], tail, enc_weight, duration_weight)
+        y1, h1, y2, qkv, ctx, gates, depthwise, stats = part_one(frame_lengths, resid, smalls[layer], wholes[layer], ff)
+        pooled = exchange(stats, "pool", 8 + layer)
+        y3, h2, y4, result = part_two(depthwise, y2, pooled, smalls[layer], wholes[layer], ff)
+        records.append((resid, y1, h1, y2, qkv, ctx, gates, depthwise, pooled, y3, h2, y4))
+        resid = result
+    w_enc, w_pred, w_tok, w_dur = unpack_joint(wholes[-1], end + 16, sizes, enc_weight, pred_weight, vocab)
     joint = w_enc.shape[1]
     vocab = w_tok.shape[1]
     out_low = resid.astype(jnp.bfloat16)
@@ -1066,62 +1486,48 @@
     grad_w_pred = contract_rows(
         pred_low, grad_pred_rows.reshape(utts * slots, joint).astype(jnp.bfloat16)
     )
-    shard = width // lax.axis_size("fsdp")
+    sources = [pack_joint_grads(grad_w_enc, grad_w_pred, grad_tok, grad_dur_w, n)]
+    bn_grads = [None] * layers
+    for layer in reversed(range(layers)):
+        x0, y1, h1, y2, qkv, ctx, gates, depthwise, pooled, y3, h2, y4 = records[layer]
+        g3, db, grads_one, sums, late_gains = back_one(grad, y4, y3, depthwise, pooled, smalls[layer], wholes[layer], h2, ff)
+        sums = exchange(sums, "sum", 12 + layer)
+        grad, grads_two = back_two(
+            frame_lengths, x0, y1, y2, gates, qkv, ctx, depthwise, db, g3, pooled, sums, late_gains, smalls[layer], wholes[layer], h1, ff
+        )
+        sources += [grads_one, grads_two]
+        bn_grads[layer] = (sums[4:8].reshape(width), sums[0:4].reshape(width))
+    share = scatter(sources, 4)
+    starts = [None] * layers + [0]
+    at = sources[0].shape[1]
+    for place, layer in enumerate(reversed(range(layers))):
+        one, two = sources[1 + 2 * place], sources[2 + 2 * place]
+        starts[layer] = (at, at + one.shape[1])
+        at += one.shape[1] + two.shape[1]
+    grads = unpack(
+        layers,
+        table,
+        end,
+        (starts, width, joint),
+        share,
+        [norm_gains, first_in, first_out, attend_joint, attend_out, point_in, depth_taps, point_out, second_in, second_out,
+         enc_weight, pred_weight, token_weight, duration_weight],
+    )
     offset = lax.axis_index("fsdp") * shard
-    collected = [None] * layers
-    for layer in reversed(range(layers)):
-        kept, record = records[layer]
-        weights = weights_of[layer]
-        grad, grads = layer_backward(weights, record, grad, valid_rows, key_bias, layer)
-        collected[layer] = grads
-
-    shares = []
-    for layer in range(layers):
-        g = collected[layer]
-        parts = pack_layer_grads([g[1], g[2], g[3], g[4], g[5], g[9], g[10], g[11]], g[0], g[6], n)
-        if layer == layers - 1:
-            parts = parts + pack_joint_grads(grad_w_enc, grad_w_pred, grad_tok, grad_dur_w, n)
-        shares.append(scatter(padded(parts), 4 + layer))
-
-    def stack(values):
-        return jnp.stack(values)
-
-    pieces = [cut(share, sizes) for share in shares]
-    out = []
-    for i, m in enumerate(mats):
-        out.append(stack([shard_from_blocks(p[i], m.shape[2]) for p in pieces]))
-    small = stack([p[-1][:, : norm_gains.shape[2]].astype(jnp.float32) for p in pieces])
-    g_enc, g_pred, g_tok, rest = cut(shares[-1], tail[1:], tail[0])
-    low = enc_weight.shape[0]
-    g_enc = jnp.concatenate([g_enc, rest[:low, : joint - WIDE]], 1).astype(jnp.float32)
-    g_pred = jnp.concatenate([g_pred, rest[:, 128 : 128 + joint - WIDE]], 1).astype(jnp.float32)
-    g_dur = rest[:, 256 : 256 + durs].astype(jnp.float32)
-    gain_piece = lax.dynamic_slice_in_dim(stack([c[7] for c in collected]), offset, shard, 1)
-    bias_piece = lax.dynamic_slice_in_dim(stack([c[8] for c in collected]), offset, shard, 1)
-    grad_frames = grad.reshape(utts, frames, width)
+    gain_piece = lax.dynamic_slice_in_dim(jnp.stack([g[0] for g in bn_grads]), offset, shard, 1)
+    bias_piece = lax.dynamic_slice_in_dim(jnp.stack([g[1] for g in bn_grads]), offset, shard, 1)
     return (
         utt_loss,
-        grad_frames,
-        small[:, :5],
-        out[0],
-        out[1],
-        out[2],
-        out[3],
-        out[4],
-        small[:, 5:14],
+        grad.reshape(utts, frames, width),
+        *grads[:7],
         gain_piece,
         bias_piece,
-        out[5],
-        out[6],
-        out[7],
-        g_enc,
-        g_pred,
-        shard_from_blocks(g_tok, vocab),
-        g_dur,
+        *grads[7:],
     )
 
 
 def solution(mesh):
+    set_tile(mesh.shape["fsdp"])
     placed = (
         P(("dp", "fsdp"), None, None),
         P(("dp", "fsdp")),

time: 989 us -> 728 us (0.74)
  local copies, waits for them, and re-layouts: 284 us -> 42.7 us
  Pallas kernels: 510 us -> 661 us
  matrix products: 105 us -> 6.09 us
  other arithmetic: 74.1 us -> 5.79 us
    pallas_call x2 -> x11, Pallas kernels: 163 us -> 345 us  [the longest x1 153 us: scatter(): pl.pallas_call(partial(scatter_kernel, n1, counts, lag), out_shape=jax.Sh...]
    unnamed x627 -> x74, local copies, waits for them, and re-layouts: 106 us -> 25.1 us
    reshape x32 -> x5, local copies, waits for them, and re-layouts: 66.3 us -> 2.78 us  [the longest x4 1.43 us: local(): smalls.append(jnp.swapaxes(small, 0, 1).reshape(16, width))]
    dot_general x18 -> x2, matrix products: 34.8 us -> 2.03 us  [matmul(): return jnp.dot(left, right, preferred_element_type=jnp.float32)]
    pallas_call x2, Pallas kernels: 169 us -> 139 us  [gather(): pl.pallas_call(partial(gather_kernel, n1, tiles, lag), out_shape=jax.Shap...]
    dot_general x18 -> x2, matrix products: 28.1 us -> 1.06 us  [contract_rows(): lax.dot_general(left, right, (((0,), (0,)), ((), ())), preferred_element_...]
    dot_general x17 -> x1, matrix products: 28.6 us -> 3 us  [contract_cols(): lax.dot_general(left, right, (((1,), (1,)), ((), ())), preferred_element_...]
    reduce_sum x32 -> x0, other arithmetic: 25.3 us -> none  [the longest x4 12.2 us: conv_inner(): total = total + padded[:, tap:tap + frames] * depth[tap]]
where the time goes in v3:
time: 728 us; the launch traced here: 718 us
  Pallas kernels  661 us (91%)
  local copies, waits for them, and re-layouts  42.7 us (6%)
    pallas_call x1, Pallas kernels, scatter(): pl.pallas_call(partial(scatter_kernel, n1, counts, lag), out_shape=jax.Sh...  153 us
    pallas_call x2, Pallas kernels, gather(): pl.pallas_call(partial(gather_kernel, n1, tiles, lag), out_shape=jax.Shap...  139 us
    pallas_call x2, Pallas kernels, back_two(): pl.pallas_call(partial(back_two_kernel, utts, table, start, end), in_spec...  80.6 us
    pallas_call x1, Pallas kernels, joint_backward(): pl.pallas_call(partial(joint_bwd_kernel, groups, durs), grid=(utts * grou...  59.1 us
    pallas_call x2, Pallas kernels, part_one(): pl.pallas_call(partial(part_one_kernel, utts, table), in_specs=[SMEM_SPEC...  46.8 us
    pallas_call x4, Pallas kernels, exchange(): pl.pallas_call(partial(exchange_kernel, kind, groups, n), out_shape=jax.S...  43.9 us
    pallas_call x2, Pallas kernels, back_one(): pl.pallas_call(partial(back_one_kernel, table), in_specs=[VMEM_SPEC] * 6...  38.4 us
    pallas_call x1, Pallas kernels, lattice(): pl.pallas_call(partial(lattice_kernel, slots), out_shape=(jax.ShapeDtypeS...  37.7 us

profile of v3, /device:TPU:0, one launch (start us, length us, event | category | flops | bytes accessed | tf_op | source)
XLA Modules:
  0.0 717.6 jit_solution(6004420346120819487)
XLA Ops:
  0.7 0.7 concatenate.18.labels_ref
  1.3 0.7 copy.49.refs_8_
  2.0 0.7 copy.50.refs_9_
  2.7 0.8 copy.51.refs_15_
  3.5 1.0 copy-done.4
  4.6 1.0 copy-done.5
  5.6 1.0 copy-done.6
  6.6 1.0 copy-done.7
  7.7 1.0 copy-done.9
  8.7 0.9 copy-done.10
  9.6 0.9 copy-done.11
  10.5 0.9 copy-done.12
  11.5 0.9 copy-done.13
  12.4 0.9 copy-done.14
  13.3 0.9 copy-done.15
  14.1 0.7 copy-done.18
  14.8 0.7 copy-done.19
  15.5 1.6 pack_weights.1
  17.0 1.2 copy-done.3
  18.2 76.7 %gather_weights.2.whole = bf16[8,1920,512]{2,1,0:T(8,128)(2,1)} custom-call(bf16[1920,512]{1,0:T(8,128)(2,1)} %get-tuple-element.80.src), custom_call_target="tpu_custom_call" | custom-call | tf_op jit(solution)/shard_map/gather_weights/pallas_call | solution.py:426
  94.9 1.0 slice.69
  96.1 62.5 %gather_weights.3.whole = bf16[8,1536,512]{2,1,0:T(8,128)(2,1)} custom-call(bf16[1536,512]{1,0:T(8,128)(2,1)} %copy-done.3), custom_call_target="tpu_custom_call" | custom-call | tf_op jit(solution)/shard_map/gather_weights/pallas_call | solution.py:426
  158.6 0.8 convert_bitcast_fusion.1
  159.4 0.7 reshape.106.small
  160.1 23.2 %layer_part_one.2 = (f32[512,512]{1,0:T(8,128)}, f32[4,512,512]{2,1,0:T(8,128)}, f32[512,512]{1,0:T(8,128)}, bf16[512,1536]{1,0:T(8,128)(2,1)}, bf16[512,512]{1,...) custom-call(s32[2]{0:T(128)} %t_ref.7, bf16[512,512]{1,0:T(8,128)(2,1)} %bitcast.50, ...), custom_call_target="tpu_custom_call" | custom-call | tf_op jit(solution)/shard_map/layer_part_one/pallas_call | solution.py:1151
  183.3 11.4 %exchange_pool.2.pooled_ref = f32[16,128]{1,0:T(8,128)} custom-call(f32[16,128]{1,0:T(8,128)} %get-tuple-element.84.x_ref), custom_call_target="tpu_custom_call" | custom-call | tf_op jit(solution)/shard_map/exchange_pool/pallas_call | solution.py:610
  194.7 11.1 %layer_part_two.2 = (f32[512,512]{1,0:T(8,128)}, f32[4,512,512]{2,1,0:T(8,128)}, f32[512,512]{1,0:T(8,128)}, f32[512,512]{1,0:T(8,128)}) custom-call(f32[512,512]{1,0:T(8,128)} %get-tuple-element.82.d_ref, f32[512,512]{1,0:T(8,128)} %get-tuple-element.83.y2_ref, f32[16,128]{1,0:T(8,128)} %exchange_pool.2.pooled_ref, f32[16,512]{1,0:T(8,128)} %reshape.106.small, ...), custom_call_target="tpu_custom_call" | custom-call | tf_op jit(solution)/shard_map/layer_part_two/pallas_call | solution.py:1172
  205.8 0.8 convert_bitcast_fusion
  206.6 0.7 reshape.108.small
  207.3 23.6 %layer_part_one.3 = (f32[512,512]{1,0:T(8,128)}, f32[4,512,512]{2,1,0:T(8,128)}, f32[512,512]{1,0:T(8,128)}, bf16[512,1536]{1,0:T(8,128)(2,1)}, bf16[512,512]{1,...) custom-call(s32[2]{0:T(128)} %t_ref.7, f32[512,512]{1,0:T(8,128)} %get-tuple-element.85.x_ref, ...), custom_call_target="tpu_custom_call" | custom-call | tf_op jit(solution)/shard_map/layer_part_one/pallas_call | solution.py:1151
  230.9 10.9 %exchange_pool.3.pooled_ref = f32[16,128]{1,0:T(8,128)} custom-call(f32[16,128]{1,0:T(8,128)} %get-tuple-element.88.x_ref), custom_call_target="tpu_custom_call" | custom-call | tf_op jit(solution)/shard_map/exchange_pool/pallas_call | solution.py:610
  241.8 11.1 %layer_part_two.3 = (f32[512,512]{1,0:T(8,128)}, f32[4,512,512]{2,1,0:T(8,128)}, f32[512,512]{1,0:T(8,128)}, f32[512,512]{1,0:T(8,128)}) custom-call(f32[512,512]{1,0:T(8,128)} %get-tuple-element.86.d_ref, f32[512,512]{1,0:T(8,128)} %get-tuple-element.87.y2_ref, f32[16,128]{1,0:T(8,128)} %exchange_pool.3.pooled_ref, f32[16,512]{1,0:T(8,128)} %reshape.108.small, ...), custom_call_target="tpu_custom_call" | custom-call | tf_op jit(solution)/shard_map/layer_part_two/pallas_call | solution.py:1172
  252.9 1.8 fusion.10.enc_ref
  254.7 1.5 fusion.15
  256.5 0.6 copy-done.28
  257.4 2.3 copy.55
  259.7 3.9 pad.9.pred_ref
  263.6 1.3 slice-done.2
  264.9 1.3 copy.56
  266.6 1.8 pad_maximum_fusion
  268.4 2.6 copy.57.wt_ref
  271.0 36.4 %joint_forward.1 = (f32[8,64,256]{2,1,0:T(8,128)S(1)}, bf16[10,5,1024,256]{3,2,1,0:T(8,128)(2,1)}) custom-call(s32[2,25]{1,0:T(2,128)S(1)} %concatenate.18.labels_ref, f32[640,512]{1,0:T(8,128)S(1)} %fusion.10.enc_ref, f32[10,640,8]{2,1,0:T(8,128)} %pad.9.pred_ref, bf16[1152,640]{1,0:T(8,128)(2,1)S(1)} %copy.57.wt_ref), custom_call_target="tpu_custom_call" | custom-call | tf_op jit(solution)/shard_map/joint_forward/pallas_call | solution.py:211
  307.5 37.7 %lattice.1 = (f32[7,64,256]{2,1,0:T(8,128)S(1)}, f32[8,128]{1,0:T(8,128)S(1)}) custom-call(f32[7,64,256]{2,1,0:T(8,128)S(1)} %slice.76.feats_ref, s32[2]{0:T(128)S(1)} %copy-done.16, s32[2]{0:T(128)S(1)} %copy-done.20), custom_call_target="tpu_custom_call" | custom-call | tf_op jit(solution)/shard_map/lattice/pallas_call | solution.py:149
  345.2 0.8 copy-done.8
  346.6 59.1 %joint_backward.1 = (f32[640,512]{1,0:T(8,128)}, f32[10,640,8]{2,1,0:T(8,128)}, bf16[640,1024]{1,0:T(8,128)(2,1)}, bf16[640,128]{1,0:T(8,128)(2,1)}) custom-call(s32[2,25]{1,0:T(2,128)} %copy-done.17, f32[640,512]{1,0:T(8,128)} %copy-done.1, f32[10,640,8]{2,1,0:T(8,128)} %pad.9.pred_ref, bf16[640,1152]{1,0:T(8,128)(2,1)} %get-tuple-element.180.w_ref, ...), custom_call_target="tpu_custom_call" | custom-call | tf_op jit(solution)/shard_map/joint_backward/pallas_call | solution.py:284
  405.7 3.0 fusion.7.grad_ref
  408.7 19.3 %back_part_one.2 = (f32[512,512]{1,0:T(8,128)}, f32[512,512]{1,0:T(8,128)}, bf16[8,576,512]{2,1,0:T(8,128)(2,1)}, f32[16,128]{1,0:T(8,128)}, f32[8,512]{1,0:T(8,128)}) custom-call(f32[512,512]{1,0:T(8,128)} %fusion.7.grad_ref, f32[512,512]{1,0:T(8,128)} %get-tuple-element.103.y4_ref, f32[512,512]{1,0:T(8,128)} %get-tuple-element.104.y3_ref, ...), custom_call_target="tpu_custom_call" | custom-call | tf_op jit(solution)/shard_map/back_part_one/pallas_call | solution.py:1195
  428.0 10.9 %exchange_sum.2.sums_ref = f32[16,128]{1,0:T(8,128)} custom-call(f32[16,128]{1,0:T(8,128)} %get-tuple-element.108.x_ref), custom_call_target="tpu_custom_call" | custom-call | tf_op jit(solution)/shard_map/exchange_sum/pallas_call | solution.py:610
  439.0 40.3 %back_part_two.2 = (f32[512,512]{1,0:T(8,128)}, bf16[8,960,512]{2,1,0:T(8,128)(2,1)}) custom-call(s32[2]{0:T(128)} %t_ref.7, f32[512,512]{1,0:T(8,128)} %get-tuple-element.85.x_ref, f32[512,512]{1,0:T(8,128)} %get-tuple-element.96.y1_ref, f32[512,512]{1,0:T(8,128)} %get-tuple-element.87.y2_ref, f32[512,1024]{1,0:T(8,128)} %get-tuple-element.97.r_ref, ...), custom_call_target="tpu_custom_call" | custom-call | tf_op jit(solution)/shard_map/back_part_two/pallas_call | solution.py:1218
  479.3 19.1 %back_part_one.3 = (f32[512,512]{1,0:T(8,128)}, f32[512,512]{1,0:T(8,128)}, bf16[8,576,512]{2,1,0:T(8,128)(2,1)}, f32[16,128]{1,0:T(8,128)}, f32[8,512]{1,0:T(8,128)}) custom-call(f32[512,512]{1,0:T(8,128)} %get-tuple-element.111.grad_ref, f32[512,512]{1,0:T(8,128)} %get-tuple-element.112.y4_ref, f32[512,512]{1,0:T(8,128)} %get-tuple-element.113.y3_ref, ...), custom_call_target="tpu_custom_call" | custom-call | tf_op jit(solution)/shard_map/back_part_one/pallas_call | solution.py:1195
  498.4 10.7 %exchange_sum.3.sums_ref = f32[16,128]{1,0:T(8,128)} custom-call(f32[16,128]{1,0:T(8,128)} %get-tuple-element.117.x_ref), custom_call_target="tpu_custom_call" | custom-call | tf_op jit(solution)/shard_map/exchange_sum/pallas_call | solution.py:610
  509.1 40.3 %back_part_two.3 = (f32[512,512]{1,0:T(8,128)}, bf16[8,960,512]{2,1,0:T(8,128)(2,1)}) custom-call(s32[2]{0:T(128)} %t_ref.7, bf16[512,512]{1,0:T(8,128)(2,1)} %bitcast.51, f32[512,512]{1,0:T(8,128)} %get-tuple-element.92.y1_ref, f32[512,512]{1,0:T(8,128)} %get-tuple-element.83.y2_ref, f32[512,1024]{1,0:T(8,128)} %get-tuple-element.93.r_ref, ...), custom_call_target="tpu_custom_call" | custom-call | tf_op jit(solution)/shard_map/back_part_two/pallas_call | solution.py:1218
  549.5 0.6 convolution_convert_fusion.1
  550.1 0.9 slice_dynamic-update-slice_fusion.3
  551.9 0.8 copy.58
  553.2 0.9 slice_dynamic-update-slice_fusion.2
  554.1 0.9 slice_dynamic-update-slice_fusion.1
  555.0 0.9 slice_dynamic-update-slice_fusion
  556.0 1.0 fusion.5.refs_0_
  557.0 152.5 %scatter_grads.1 = bf16[18,2,96,512]{3,2,1,0:T(8,128)(2,1)} custom-call(bf16[8,384,512]{2,1,0:T(8,128)(2,1)} %fusion.5.refs_0_, bf16[8,576,512]{2,1,0:T(8,128)(2,1)} %get-tuple-element.124.refs_1_, bf16[8,960,512]{2,1,0:T(8,128)(2,1)} %get-tuple-element.125.refs_2_, bf16[8,576,512]{2,1,0:T(8,128)(2,1)} %get-tuple-element.126.refs_3_, ...), custom_call_target="tpu_custom_call" | custom-call | tf_op jit(solution)/shard_map/scatter_grads/pallas_call | solution.py:539
  709.6 2.0 copy-done
  711.6 3.1 unpack_grads.1
  715.9 0.7 fusion.12
  716.5 0.7 copy.61
  (73 shorter events, 4.5 us)
Async XLA Ops:
  1.3 269.6 %copy-start.17 = (s32[2,25]{1,0:T(2,128)}, s32[2,25]{1,0:T(2,128)S(1)}, u32[]{:S(2)}) copy-start(s32[2,25]{1,0:T(2,128)S(1)} %concatenate.18.labels_ref) | copy-start | bytes 604
  3.5 1.0 copy-start.4
  4.6 1.0 copy-start.5
  5.6 1.0 copy-start.6
  6.6 1.0 copy-start.7
  7.7 1.0 copy-start.9
  8.7 0.9 copy-start.10
  9.6 0.9 copy-start.11
  10.5 0.9 copy-start.12
  11.5 0.9 copy-start.13
  12.4 0.9 copy-start.14
  13.3 0.9 copy-start.15
  14.1 0.7 copy-start.18
  14.8 0.7 copy-start.19
  17.0 1.2 copy-start.3
  94.9 1.1 slice-start
  96.1 156.8 %copy-start.21 = (bf16[8,64,640]{2,1,0:T(8,128)(2,1)}, bf16[8,64,640]{2,1,0:T(8,128)(2,1)S(1)}, u32[]{:S(2)}) copy-start(bf16[8,64,640]{2,1,0:T(8,128)(2,1)S(1)} %pad_maximum_fusion.2) | copy-start | bytes 1966084
  254.7 16.3 %copy-start.1 = (f32[640,512]{1,0:T(8,128)}, f32[640,512]{1,0:T(8,128)S(1)}, u32[]{:S(2)}) copy-start(f32[640,512]{1,0:T(8,128)S(1)} %fusion.10.enc_ref) | copy-start | bytes 3932164
  254.7 1.7 slice-start.1
  256.2 0.9 copy-start.28
  263.6 1.3 slice-start.2
  271.0 36.5 %copy-start.16 = (s32[2]{0:T(128)S(1)}, s32[2]{0:T(128)}, u32[]{:S(2)}) copy-start(s32[2]{0:T(128)} %t_ref.7) | copy-start | bytes 28
  271.0 36.5 %copy-start.20 = (s32[2]{0:T(128)S(1)}, s32[2]{0:T(128)}, u32[]{:S(2)}) copy-start(s32[2]{0:T(128)} %ulen_ref.1) | copy-start | bytes 28
  307.4 39.2 %copy-start.2 = (f32[8,64,256]{2,1,0:T(8,128)}, f32[8,64,256]{2,1,0:T(8,128)S(1)}, u32[]{:S(2)}) copy-start(f32[8,64,256]{2,1,0:T(8,128)S(1)} %get-tuple-element.90.feats_ref) | copy-start | bytes 1572868
  345.2 0.8 copy-start.8
  346.6 59.2 %copy-start.22 = (bf16[8,64,640]{2,1,0:T(8,128)(2,1)S(1)}, bf16[8,64,640]{2,1,0:T(8,128)(2,1)}, u32[]{:S(2)}) copy-start(bf16[8,64,640]{2,1,0:T(8,128)(2,1)} %copy-done.21) | copy-start | bytes 1966084
  509.1 40.4 %copy-start.23 = (f32[640,512]{1,0:T(8,128)S(1)}, f32[640,512]{1,0:T(8,128)}, u32[]{:S(2)}) copy-start(f32[640,512]{1,0:T(8,128)} %get-tuple-element.102) | copy-start | bytes 3932164
  509.1 40.4 %copy-start.24 = (f32[512,512]{1,0:T(8,128)S(1)}, f32[512,512]{1,0:T(8,128)}, u32[]{:S(2)}) copy-start(f32[512,512]{1,0:T(8,128)} %get-tuple-element.89) | copy-start | bytes 3145732
  549.5 2.1 copy-start.26
  552.7 1.4 copy-start.25
  554.1 1.9 copy-start.27
  709.6 2.0 copy-start
  711.6 4.3 copy-start.29
  711.6 4.3 copy-start.30

commit v4 on v3

--- a/solution.py
+++ b/solution.py
@@ -306,14 +306,9 @@
 
 
 MESH=pl.DeviceIdType.MESH
-QA = QB = HALF = TILE = 0
-
-
-def set_tile(shards):
-    global QA, QB, HALF, TILE
-    QA = QB = max(16, 256 // shards)
-    HALF = 2 * QA + QB
-    TILE = 2 * HALF
+QA = QB = 16
+HALF = 2 * QA + QB
+TILE = 2 * HALF
 
 
 def place():
@@ -335,14 +330,15 @@
 def rows(base, size):
     return pl.ds(pl.multiple_of(base,16),size)
 
-def gather_kernel(n1, tiles, lag, src, out, own_sem, sz, rz, sy, ry, sx, rx, sc, rc):
+def gather_kernel(n1, tiles, lag, part, src, out, own_sem, sz, rz, sy, ry, sx, rx, sc, rc):
     dp,fs,a,c,i1,i2=place()
     greet(n1,dp,fs,a,c,i1,i2)
     ypeer=(dp,i1*2+1-i2); xpeer=((1-a)*2+c,fs); cpeer=(a*2+1-c,fs)
     items=n1*tiles
-    def main(t): return rows(t*TILE+c*HALF+a*QA,QA+QB)
-    def quarter(t,aa): return rows(t*TILE+c*HALF+aa*(QA+QB),QA)
-    def half(t,cc): return rows(t*TILE+cc*HALF,HALF)
+    half_rows=3*part
+    def main(t): return rows((2*t+c)*half_rows+a*part,2*part)
+    def quarter(t,aa): return rows((2*t+c)*half_rows+aa*2*part,part)
+    def half(t,cc): return rows((2*t+cc)*half_rows,half_rows)
     def of(m): return m//n1, m%n1, lax.rem(i1+n1-m%n1,n1)
     def zcopy(t,d):
         j=lax.rem(i1+d,n1)
@@ -421,10 +417,11 @@
 
 def gather(packed, collective_id, lag=4):
     n=lax.axis_size("fsdp"); n1=n//2
-    tiles=packed.shape[0]//TILE
+    part=32 if packed.shape[0]%192==0 else 16
+    tiles=packed.shape[0]//(6*part)
     dma=pltpu.SemaphoreType.DMA
     return pl.pallas_call(
-        partial(gather_kernel,n1,tiles,lag),
+        partial(gather_kernel,n1,tiles,lag,part),
         out_shape=jax.ShapeDtypeStruct((n,)+packed.shape,packed.dtype),
         in_specs=[pl.BlockSpec(memory_space=pl.ANY)],
         out_specs=pl.BlockSpec(memory_space=pl.ANY),
@@ -433,122 +430,229 @@
         name="gather_weights",
     )(packed)
 
-def scatter_kernel(n1, counts, lag, *refs):
-    srcs = refs[:len(counts)]
-    scatter_body(n1, counts, lag, srcs, *refs[len(counts):])
-
-def scatter_body(n1, counts, lag, srcs, out, own, gc, gx, gy, gz, gf, fin,
-                   lo, sc, rc, sx, rx, sy, ry, sz, rz, sf, rf, se, re, wo):
-    dp,fs,a,c,i1,i2=place()
-    greet(n1,dp,fs,a,c,i1,i2)
-    ypeer=(dp,i1*2+1-i2); xpeer=((1-a)*2+c,fs); cpeer=(a*2+1-c,fs)
-    tiles=sum(counts)
-    items=n1*tiles
-    main=rows(a*QA,QA+QB)
-    def quarter(aa): return rows(aa*(QA+QB),QA)
-    middle=pl.ds(QA,QB)
-    def of(m): return m//n1, lax.rem(i1+1+m%n1,n1)
-    def load(t,s,src=srcs[0],f=0): return pltpu.make_async_copy(src.at[s,rows((t-f)*TILE+c*HALF,HALF),:],own.at[t,s],lo.at[t,s])
-    def ccopy(t,s,src=srcs[0],f=0): return remote(src.at[s,rows((t-f)*TILE+(1-c)*HALF,HALF),:],gc.at[t,s],sc.at[t,s],rc.at[t,s],cpeer)
-    def xcopy(t,s): return remote(own.at[t,s,quarter(1-a),:],gx.at[t,s],sx.at[t,s],rx.at[t,s],xpeer)
-    def ycopy(t,j): return remote(own.at[t,j*2+1-i2,main,:],gy.at[t,j],sy.at[t,j],ry.at[t,j],ypeer)
-    def zcopy(t,j): return remote(own.at[t,j*2+i2,main,:],gz.at[t,i1],sz.at[t,j],rz.at[t,i1],(dp,j*2+i2))
-    def zin(t,j): return remote(own.at[t,fs,main,:],gz.at[t,j],sz.at[t,j],rz.at[t,j],ypeer)
-    def fcopy(t): return remote(own.at[t,fs,main,:],gf.at[t],sf.at[t],rf.at[t],xpeer)
-    def ecopy(t): return remote(fin.at[t,c],fin.at[t,c],se.at[t],re.at[t],cpeer)
-    def ein(t): return remote(fin.at[t,1-c],fin.at[t,1-c],se.at[t],re.at[t],cpeer)
-    def store(t): return pltpu.make_async_copy(fin.at[t],out.at[t],wo.at[t])
-
-    def tick(tau,carry):
-        def at(shift,body):
-            m=tau-shift
-            @pl.when((m>=0)&(m<items))
-            def _(): body(*of(m))
-        def at_tile(shift,body):
-            m=tau-shift
-            @pl.when((m>=0)&(m<items)&(lax.rem(m+n1,n1)==n1-1))
-            def _(): body(m//n1)
-        def stage_c(t,j):
-            first=0
-            for src,count in zip(srcs,counts):
-                @pl.when((t>=first)&(t<first+count))
-                def _(src=src,first=first):
-                    for i in range(2):
-                        load(t,j*2+i,src,first).start(); ccopy(t,j*2+i,src,first).start()
-                first+=count
-        def stage_x(t,j):
-            for i in range(2):
-                s=j*2+i
-                pltpu.make_async_copy(own.at[t,s],own.at[t,s],lo.at[t,s]).wait(); remote(own.at[t,s],gc.at[t,s],sc.at[t,s],rc.at[t,s],cpeer).wait_recv()
-                own[t,s]=own[t,s]+gc[t,s]
-                xcopy(t,s).start()
-        def stage_y(t,j):
-            for i in range(2):
-                s=j*2+(1-i2 if i==0 else i2)
-                xcopy(t,s).wait_recv()
-                own[t,s,quarter(a),:]=own[t,s,quarter(a),:]+gx[t,s]
-                if i==0: ycopy(t,j).start()
-        def stage_z(t,j):
-            s=j*2+i2
-            ycopy(t,j).wait_recv()
-            own[t,s,main,:]=own[t,s,main,:]+gy[t,j]
-            @pl.when(j!=i1)
-            def _(): zcopy(t,j).start()
+class Beats:
+    def __init__(self, tick=None, total=0, sites=1):
+        self.tick = tick
+        self.total = total
+        self.at = 0
+        self.credit = 0.0
+        self.scale = total / sites
+
+    def grant(self, count):
+        self.credit += count * self.scale
+        steps = min(int(self.credit), self.total - self.at)
+        self.credit -= int(self.credit)
+        first = self.at
+        self.at += steps
+        return first, steps
+
+    def span(self, low, high):
+        def step(i, carry):
+            self.tick(i)
+            return carry
+
+        lax.fori_loop(low, high, step, 0)
+
+    def loop(self, count):
+        if self.tick is None:
+            return lambda i: None
+        first, steps = self.grant(count)
+        return lambda i: self.span(first + i * steps // count, first + (i + 1) * steps // count)
+
+    def run(self, count):
+        if self.tick is None:
+            return
+        first, steps = self.grant(count)
+        if steps:
+            self.span(first, first + steps)
+
+    def rest(self):
+        if self.at < self.total:
+            self.span(self.at, self.total)
+            self.at = self.total
+
+
+class ScatterEngine:
+    def __init__(self, n1, plan, lag, srcs, out, own, gc, gx, gy, gz, gf, fin, lo, sc, rc, sx, rx, sy, ry, sz, rz, sf, rf, se, re, wo):
+        dp, fs, a, c, i1, i2 = place()
+        greet(n1, dp, fs, a, c, i1, i2)
+        ypeer = (dp, i1 * 2 + 1 - i2)
+        xpeer = ((1 - a) * 2 + c, fs)
+        cpeer = (a * 2 + 1 - c, fs)
+        tiles = sum(count for _, count in plan)
+        main = rows(a * QA, QA + QB)
+        middle = pl.ds(QA, QB)
+
+        def quarter(aa):
+            return rows(aa * (QA + QB), QA)
+
+        def cwait(t):
+            return remote(own.at[t], gc.at[t], sc.at[t], rc.at[t], cpeer)
+
+        def xcopy(t):
+            return remote(own.at[t, :, :, quarter(1 - a), :], gx.at[t], sx.at[t], rx.at[t], xpeer)
+
+        def ycopy(t):
+            return remote(own.at[t, :, 1 - i2, main, :], gy.at[t], sy.at[t], ry.at[t], ypeer)
+
+        def zcopy(t, j):
+            return remote(own.at[t, j, i2, main, :], gz.at[t, i1], sz.at[t, j], rz.at[t, i1], (dp, j * 2 + i2))
+
+        def zin(t, j):
+            return remote(own.at[t, i1, i2, main, :], gz.at[t, j], sz.at[t, j], rz.at[t, j], ypeer)
+
+        def fcopy(t):
+            return remote(own.at[t, i1, i2, main, :], gf.at[t], sf.at[t], rf.at[t], xpeer)
+
+        def ecopy(t):
+            return remote(fin.at[t, c], fin.at[t, c], se.at[t], re.at[t], cpeer)
+
+        def ein(t):
+            return remote(fin.at[t, 1 - c], fin.at[t, 1 - c], se.at[t], re.at[t], cpeer)
+
+        def store(t):
+            return pltpu.make_async_copy(fin.at[t], out.at[t], wo.at[t])
+
+        def stage_c(t):
+            first = 0
+            for src, (base, count) in zip(srcs, plan):
+
+                @pl.when((t >= first) & (t < first + count))
+                def _(src=src, skip=base - first):
+                    at = (t + skip) * TILE
+                    pltpu.make_async_copy(src.at[:, :, rows(at + c * HALF, HALF), :], own.at[t], lo.at[t]).start()
+                    remote(src.at[:, :, rows(at + (1 - c) * HALF, HALF), :], gc.at[t], sc.at[t], rc.at[t], cpeer).start()
+
+                first += count
+
+        def stage_x(t):
+            pltpu.make_async_copy(own.at[t], own.at[t], lo.at[t]).wait()
+            cwait(t).wait_recv()
+            own[t] = own[t] + gc[t]
+            xcopy(t).start()
+
+        def stage_y(t):
+            xcopy(t).wait_recv()
+            own[t, :, :, quarter(a), :] = own[t, :, :, quarter(a), :] + gx[t]
+            ycopy(t).start()
+
+        def stage_z(t):
+            ycopy(t).wait_recv()
+            own[t, :, i2, main, :] = own[t, :, i2, main, :] + gy[t]
+            for d in range(1, n1):
+                zcopy(t, lax.rem(i1 + d, n1)).start()
+
         def stage_f(t):
-            total=own[t,fs,main,:].astype(jnp.float32)
-            for d in range(1,n1):
-                j=lax.rem(i1+n1-d,n1)
-                zin(t,j).wait_recv()
-                total=total+gz[t,j].astype(jnp.float32)
-            own[t,fs,main,:]=total.astype(jnp.bfloat16)
+            total = own[t, i1, i2, main, :].astype(jnp.float32)
+            for d in range(1, n1):
+                j = lax.rem(i1 + n1 - d, n1)
+                zin(t, j).wait_recv()
+                total = total + gz[t, j].astype(jnp.float32)
+            own[t, i1, i2, main, :] = total.astype(jnp.bfloat16)
             fcopy(t).start()
+
         def stage_e(t):
             fcopy(t).wait_recv()
-            fin[t,c,quarter(a),:]=own[t,fs,quarter(a),:]
-            fin[t,c,quarter(1-a),:]=gf[t,rows((1-a)*QB,QA),:]
-            fin[t,c,middle,:]=own[t,fs,middle,:]+gf[t,rows(a*QA,QB),:]
+            fin[t, c, quarter(a), :] = own[t, i1, i2, quarter(a), :]
+            fin[t, c, quarter(1 - a), :] = gf[t, rows((1 - a) * QB, QA), :]
+            fin[t, c, middle, :] = own[t, i1, i2, middle, :] + gf[t, rows(a * QA, QB), :]
             ecopy(t).start()
+
         def stage_o(t):
             ein(t).wait_recv()
             ecopy(t).wait_send()
             store(t).start()
-        at(0,stage_c); at(lag,stage_x); at(2*lag,stage_y); at(3*lag,stage_z)
-        at_tile(3*lag+1,stage_f); at_tile(4*lag+1,stage_e); at_tile(5*lag+1,stage_o)
-        return carry
-    lax.fori_loop(0,items+5*lag+1,tick,0)
-    def finish(m,carry):
-        t,j=of(m)
-        for i in range(2):
-            remote(own.at[t,j*2+i],gc.at[t,j*2+i],sc.at[t,j*2+i],rc.at[t,j*2+i],cpeer).wait_send(); xcopy(t,j*2+i).wait_send()
-        ycopy(t,j).wait_send()
-        @pl.when(j!=i1)
-        def _(): zcopy(t,j).wait_send()
-        return carry
-    lax.fori_loop(0,items,finish,0)
-    def finish_tile(t,carry):
-        fcopy(t).wait_send(); store(t).wait()
-        return carry
-    lax.fori_loop(0,tiles,finish_tile,0)
-
-def scatter(sources, collective_id, lag=3):
-    n=lax.axis_size("fsdp"); n1=n//2
-    counts=tuple(x.shape[1]//TILE for x in sources)
-    tiles=sum(counts); w=sources[0].shape[2]
-    dma=pltpu.SemaphoreType.DMA
-    bf=jnp.bfloat16
-    out=pl.pallas_call(
-        partial(scatter_kernel,n1,counts,lag),
-        out_shape=jax.ShapeDtypeStruct((tiles,2,HALF,w),bf),
-        in_specs=[pl.BlockSpec(memory_space=pl.ANY)]*len(sources),
-        out_specs=pl.BlockSpec(memory_space=pl.ANY),
-        scratch_shapes=[pltpu.VMEM((tiles,n,HALF,w),bf),pltpu.VMEM((tiles,n,HALF,w),bf),pltpu.VMEM((tiles,n,QA,w),bf),
-            pltpu.VMEM((tiles,n1,QA+QB,w),bf),pltpu.VMEM((tiles,n1,QA+QB,w),bf),pltpu.VMEM((tiles,QA+QB,w),bf),pltpu.VMEM((tiles,2,HALF,w),bf)]
-            +[dma((tiles,n))]*5+[dma((tiles,n1))]*4+[dma((tiles,))]*5,
-        compiler_params=pltpu.CompilerParams(collective_id=collective_id,has_side_effects=True,vmem_limit_bytes=60<<20),
-        name="scatter_grads",
-    )(*sources)
-    out=out.reshape(tiles*TILE,w)
-    return out
+
+        stages = (stage_c, stage_x, stage_y, stage_z, stage_f, stage_e, stage_o)
+
+        def tick(tau):
+            for place_of, stage in enumerate(stages):
+                t = tau - place_of * lag
+
+                @pl.when((t >= 0) & (t < tiles))
+                def _(stage=stage, t=t):
+                    stage(t)
+
+        def finish():
+            def tile(t, carry):
+                cwait(t).wait_send()
+                xcopy(t).wait_send()
+                ycopy(t).wait_send()
+                for d in range(1, n1):
+                    zcopy(t, lax.rem(i1 + d, n1)).wait_send()
+                fcopy(t).wait_send()
+                store(t).wait()
+                return carry
+
+            lax.fori_loop(0, tiles, tile, 0)
+
+        self.tick = tick
+        self.total = tiles + (len(stages) - 1) * lag
+        self.finish = finish
+
+
+def scatter_plan(sources):
+    return tuple((first, count) for _, first, count in sources)
+
+
+def scatter_scratch(n, tiles):
+    n1 = n // 2
+    dma = pltpu.SemaphoreType.DMA
+    v = lambda *shape: pltpu.VMEM((tiles,) + shape + (WIDE,), jnp.bfloat16)
+    one = dma((tiles,))
+    return [
+        v(n1, 2, HALF), v(n1, 2, HALF), v(n1, 2, QA), v(n1, QA + QB), v(n1, QA + QB), v(QA + QB), v(2, HALF),
+        one, one, one, one, one, one, one, dma((tiles, n1)), dma((tiles, n1)), one, one, one, one, one,
+    ]
+
+
+def riding_kernel(kernel, counts, plan, lag, n1, sites, *refs):
+    n_in, n_out, n_scratch = counts
+    k = len(plan)
+    ins, refs = refs[:n_in], refs[n_in:]
+    srcs, refs = refs[:k], refs[k:]
+    outs, refs = refs[:n_out], refs[n_out:]
+    share, refs = refs[0], refs[1:]
+    scratch, refs = refs[:n_scratch], refs[n_scratch:]
+    engine = ScatterEngine(n1, plan, lag, srcs, share, *refs)
+    beats = Beats(engine.tick, engine.total, sites)
+    kernel(beats, *ins, *outs, *scratch)
+    beats.rest()
+    engine.finish()
+
+
+def call(kernel, args, in_specs, out_specs, out_shape, scratch, name, ride=None, collective_id=None, sites=1, lag=2):
+    if not ride:
+        return pl.pallas_call(
+            partial(kernel, Beats()),
+            in_specs=in_specs,
+            out_specs=out_specs,
+            out_shape=out_shape,
+            scratch_shapes=scratch,
+            compiler_params=pltpu.CompilerParams(vmem_limit_bytes=60 << 20),
+            name=name,
+        )(*args)
+    n = lax.axis_size("fsdp")
+    tiles = sum(count for _, _, count in ride)
+    counts = (len(args), len(out_shape), len(scratch))
+    *outs, share = pl.pallas_call(
+        partial(riding_kernel, kernel, counts, scatter_plan(ride), lag, n // 2, sites),
+        in_specs=in_specs + [ANY_SPEC] * len(ride),
+        out_specs=out_specs + [ANY_SPEC],
+        out_shape=out_shape + [sds((tiles, 2, HALF, WIDE), BF16)],
+        scratch_shapes=scratch + scatter_scratch(n, tiles),
+        compiler_params=pltpu.CompilerParams(collective_id=collective_id, has_side_effects=True, vmem_limit_bytes=61 << 20),
+        name=name + "_and_scatter",
+    )(*args, *[grads.reshape(n // 2, 2, -1, WIDE) for grads, _, _ in ride])
+    return outs, share.reshape(tiles * TILE, WIDE)
+
+
+def idle_kernel(beats):
+    pass
+
+
+def scatter(ride, collective_id):
+    return call(idle_kernel, [], [], [], [], [], "idle", ride, collective_id)[1]
 
 
 def pooled(parts):
@@ -916,7 +1020,7 @@
     mover.finish()
 
 
-def ffn_bwd(rows, v_ref, gain, w_in, w_out, h, loads, g_ref, gb, normed, dact, act, dh, dn, dw_in, dw_out, mover, grads, at_in, at_out):
+def ffn_bwd(rows, v_ref, gain, w_in, w_out, h, loads, g_ref, gb, normed, dact, act, dh, dn, dw_in, dw_out, mover, grads, at_in, at_out, beats):
     def prepare(rr, i, c):
         normed[rr, :] = (ln_parts(v_ref[rr, :].astype(jnp.float32))[0] * gain).astype(jnp.bfloat16)
         gb[rr, :] = (0.5 * g_ref[rr, :]).astype(jnp.bfloat16)
@@ -927,6 +1031,7 @@
     for b in range(h.shape[0]):
         cols = slice(b * WIDE, (b + 1) * WIDE)
         dact[...] = nt(gb[...], w_out[0][cols, :])
+        beats.run(1)
         loads[b].wait()
 
         def slope(rr, i, c):
@@ -937,12 +1042,16 @@
             return c
 
         row_loop(rows, slope)
+        beats.run(1)
         dw_out[cols, :] = tn(act[...], gb[...]).astype(jnp.bfloat16)
+        beats.run(1)
         dw_in[:, cols] = tn(normed[...], dh[:, cols]).astype(jnp.bfloat16)
+        beats.run(1)
     mover.put_weight(dw_out, grads, at_out)
     mover.put_weight(dw_in, grads, at_in)
     w_in[1].wait()
     dn[...] = nt(dh[...], w_in[0][...])
+    beats.run(2)
 
     def back(rr, i, total):
         dv, dg = ln_back(v_ref[rr, :].astype(jnp.float32), gain, dn[rr, :])
@@ -956,7 +1065,7 @@
     return jnp.sum(folded, 0, keepdims=True)
 
 
-def back_one_kernel(table, grad_ref, y4_ref, y3_ref, d_ref, pooled_ref, small, whole, h_hbm, g_out, db_out, grads, sums, gain_out,
+def back_one_kernel(table, beats, grad_ref, y4_ref, y3_ref, d_ref, pooled_ref, small, whole, h_hbm, g_out, db_out, grads, sums, gain_out,
                     w_pout, w_sin, w_sout, g, gb, normed, dact, act, dh, dn, dw_in, dw_out, dw_pout, h, db, sems):
     rows, width = g.shape
     mover = Mover(sems)
@@ -965,6 +1074,7 @@
     loads = [mover.load(h_hbm.at[b], h.at[b]) for b in range(h.shape[0])]
     sin = mover.load_weight(whole, table["s_in"], w_sin, False)
     wo = mover.load_weight(whole, table["p_out"], w_pout, False)
+    beats.run(5)
 
     def first(rr, i, total):
         dv, dg = ln_back(y4_ref[rr, :], gains[4:5], grad_ref[rr, :])
@@ -973,7 +1083,7 @@
 
     gain4 = down(row_loop(rows, first, jnp.zeros((8, width), jnp.float32)))
     gain3 = down(ffn_bwd(rows, y3_ref, gains[3:4], (w_sin, sin), (w_sout, sout), h, loads, g, gb, normed, dact, act, dh, dn,
-                         dw_in, dw_out, mover, grads, table["s_in"], table["s_out"]))
+                         dw_in, dw_out, mover, grads, table["s_in"], table["s_out"], beats))
     mover.put(g, g_out)
     gain_out[...] = jnp.concatenate([gain3, gain4, jnp.zeros((6, width), jnp.float32)], 0)
     mean = read_rows(pooled_ref, 0, width)
@@ -986,6 +1096,7 @@
     row_loop(rows, cast)
     wo.wait()
     dact[...] = nt(gb[...], w_pout[...])
+    beats.run(1)
 
     def bn(rr, i, totals):
         z = (d_ref[rr, :] - mean) * istd
@@ -998,6 +1109,7 @@
 
     zero = jnp.zeros((8, width), jnp.float32)
     one, two = row_loop(rows, bn, (zero, zero))
+    beats.run(2)
     mover.put(db, db_out)
     write_rows(sums, 0, down(one))
     write_rows(sums, 4, down(two))
@@ -1007,7 +1119,7 @@
     mover.finish()
 
 
-def back_two_kernel(utts, table, start, end, t_ref, x_ref, y1_ref, y2_ref, r_ref, t_in, c_ref, d_ref, db_ref, g_in, pooled_ref, sums_ref, late_ref, small, whole, h_hbm,
+def back_two_kernel(utts, table, start, end, beats, t_ref, x_ref, y1_ref, y2_ref, r_ref, t_in, c_ref, d_ref, db_ref, g_in, pooled_ref, sums_ref, late_ref, small, whole, h_hbm,
                     g_out, grads,
                     w_pin, w_proj, w_joint, w_fin, w_fout, g, gb, normed, dact, act, dh, dn, dw_pin, dw_proj, dw_joint, dw_in, dw_out, h, gp, dd, dr, dt, sm, sems):
     rows, width = g.shape
@@ -1029,7 +1141,9 @@
     ntaps = taps.shape[0]
     span = frames + 16
     per = frames // CHUNK_ROWS
+    beats.run(5)
     fill_gated(utts, frames, t_ref, r_ref, gp)
+    beats.run(1)
     for u in range(utts):
         dd[u * span : u * span + 8, :] = jnp.zeros((8, width), jnp.float32)
         dd[u * span + 8 + frames : (u + 1) * span, :] = jnp.zeros((8, width), jnp.float32)
@@ -1057,12 +1171,15 @@
 
     zero = jnp.zeros((8, width), jnp.float32)
     tap_grads = [down(x) for x in row_loop(rows, conv, (zero,) * ntaps)]
+    beats.run(2)
     for b in range(2):
         cols = slice(b * width, (b + 1) * width)
         dw_pin[:, cols] = tn(normed[...], dr[:, cols]).astype(jnp.bfloat16)
     mover.put_weight(dw_pin, grads, table["p_in"] - start)
+    beats.run(2)
     wi.wait()
     dn[...] = nt(dr[...], w_pin[...])
+    beats.run(1)
 
     def back_conv(rr, i, total):
         dv, dg = ln_back(y2_ref[rr, :], gains[2:3], dn[rr, :])
@@ -1075,13 +1192,16 @@
     gain2 = down(row_loop(rows, back_conv, zero))
     dw_proj[...] = tn(c_ref[...], gb[...]).astype(jnp.bfloat16)
     mover.put_weight(dw_proj, grads, table["w_proj"] - start)
+    beats.run(1)
     wp.wait()
     act[...] = nt(gb[...], w_proj[...]).astype(jnp.bfloat16)
     pairs = width // 128
     side = lax.broadcasted_iota(jnp.int32, (frames, 128), 1) < 64
     key_at = lax.broadcasted_iota(jnp.int32, (frames, 1), 0)
+    hook = beats.loop(utts * pairs)
 
     def pair_step(m, carry):
+        hook(m)
         u = m // pairs
         base = lax.rem(m, pairs) * 128
         rr = pl.ds(pl.multiple_of(u * frames, frames), frames)
@@ -1110,8 +1230,10 @@
         cols = slice(b * width, (b + 1) * width)
         dw_joint[:, cols] = tn(normed[...], dt[:, cols]).astype(jnp.bfloat16)
     mover.put_weight(dw_joint, grads, table["w_joint"] - start)
+    beats.run(2)
     wj.wait()
     dn[...] = nt(dt[...], w_joint[...])
+    beats.run(1)
 
     def back_attend(rr, i, total):
         dv, dg = ln_back(y1_ref[rr, :], gains[1:2], dn[rr, :])
@@ -1120,7 +1242,7 @@
 
     gain1 = down(row_loop(rows, back_attend, zero))
     gain0 = down(ffn_bwd(rows, x_ref, gains[0:1], (w_fin, fin), (w_fout, fout), h, loads, g, gb, normed, dact, act, dh, dn,
-                         dw_in, dw_out, mover, grads, table["f_in"] - start, table["f_out"] - start))
+                         dw_in, dw_out, mover, grads, table["f_in"] - start, table["f_out"] - start, beats))
     mover.put(g, g_out)
     packed = jnp.concatenate([gain0, gain1, gain2, late_ref[0:2, :]] + tap_grads + [jnp.zeros((2, width), jnp.float32)], 0)
     n = grads.shape[0]
@@ -1186,27 +1308,30 @@
     return -(-count // TILE) * TILE
 
 
-def back_one(grad, y4, y3, d, pooled, small, whole, h, ff):
+def back_one(grad, y4, y3, d, pooled, small, whole, h, ff, ride=None, collective_id=None):
     rows, width = grad.shape
     n = whole.shape[0]
     table, _ = offsets(n, width, ff)
     nb = ff // WIDE
     v = pltpu.VMEM
-    return pl.pallas_call(
+    return call(
         partial(back_one_kernel, table),
-        in_specs=[VMEM_SPEC] * 6 + [ANY_SPEC] * 2,
-        out_specs=[ANY_SPEC] * 3 + [VMEM_SPEC] * 2,
-        out_shape=[sds((rows, width)), sds((rows, width)), sds((n, tiled(table["p_in"]), WIDE), BF16), sds((16, 128)), sds((8, width))],
-        scratch_shapes=[v((width, width), BF16), v((width, ff), BF16), v((ff, width), BF16), v((rows, width), F32),
-                        v((rows, width), BF16), v((rows, width), BF16), v((rows, width), F32), v((rows, width), BF16),
-                        v((rows, ff), BF16), v((rows, width), F32), v((width, ff), BF16), v((ff, width), BF16),
-                        v((width, width), BF16), v((nb, rows, WIDE), F32), v((rows, width), F32), pltpu.SemaphoreType.DMA((16,))],
-        compiler_params=pltpu.CompilerParams(vmem_limit_bytes=56 << 20),
-        name="back_part_one",
-    )(grad, y4, y3, d, pooled, small, whole, h)
-
-
-def back_two(t_len, x, y1, y2, r, t, c, d, db, g, pooled, sums, late, small, whole, h, ff):
+        (grad, y4, y3, d, pooled, small, whole, h),
+        [VMEM_SPEC] * 6 + [ANY_SPEC] * 2,
+        [ANY_SPEC] * 3 + [VMEM_SPEC] * 2,
+        [sds((rows, width)), sds((rows, width)), sds((n, tiled(table["p_in"]), WIDE), BF16), sds((16, 128)), sds((8, width))],
+        [v((width, width), BF16), v((width, ff), BF16), v((ff, width), BF16), v((rows, width), F32),
+         v((rows, width), BF16), v((rows, width), BF16), v((rows, width), F32), v((rows, width), BF16),
+         v((rows, ff), BF16), v((rows, width), F32), v((width, ff), BF16), v((ff, width), BF16),
+         v((width, width), BF16), v((nb, rows, WIDE), F32), v((rows, width), F32), pltpu.SemaphoreType.DMA((16,))],
+        "back_part_one",
+        ride,
+        collective_id,
+        28,
+    )
+
+
+def back_two(t_len, x, y1, y2, r, t, c, d, db, g, pooled, sums, late, small, whole, h, ff, ride=None, collective_id=None):
     rows, width = d.shape
     utts = t_len.shape[0]
     n = whole.shape[0]
@@ -1215,20 +1340,23 @@
     nb = ff // WIDE
     v = pltpu.VMEM
     pad_rows = utts * (rows // utts + 16)
-    return pl.pallas_call(
+    return call(
         partial(back_two_kernel, utts, table, start, end),
-        in_specs=[SMEM_SPEC] + [VMEM_SPEC] * 13 + [ANY_SPEC] * 2,
-        out_specs=[ANY_SPEC] * 2,
-        out_shape=[sds((rows, width)), sds((n, tiled(end - start + 16), WIDE), BF16)],
-        scratch_shapes=[v((width, 2 * width), BF16), v((width, width), BF16), v((width, 3 * width), BF16), v((width, ff), BF16),
-                        v((ff, width), BF16), v((rows, width), F32), v((rows, width), BF16), v((rows, width), BF16),
-                        v((rows, width), F32), v((rows, width), BF16), v((rows, ff), BF16), v((rows, width), F32),
-                        v((width, 2 * width), BF16), v((width, width), BF16), v((width, 3 * width), BF16), v((width, ff), BF16),
-                        v((ff, width), BF16), v((nb, rows, WIDE), F32), v((pad_rows, width), F32), v((pad_rows, width), F32),
-                        v((rows, 2 * width), BF16), v((rows, 3 * width), BF16), v((n, 16, WIDE), BF16), pltpu.SemaphoreType.DMA((20,))],
-        compiler_params=pltpu.CompilerParams(vmem_limit_bytes=60 << 20),
-        name="back_part_two",
-    )(t_len, x, y1, y2, r, t, c, d, db, g, pooled, sums, late, small, whole, h)
+        (t_len, x, y1, y2, r, t, c, d, db, g, pooled, sums, late, small, whole, h),
+        [SMEM_SPEC] + [VMEM_SPEC] * 13 + [ANY_SPEC] * 2,
+        [ANY_SPEC] * 2,
+        [sds((rows, width)), sds((n, tiled(end - start + 16), WIDE), BF16)],
+        [v((width, 2 * width), BF16), v((width, width), BF16), v((width, 3 * width), BF16), v((width, ff), BF16),
+         v((ff, width), BF16), v((rows, width), F32), v((rows, width), BF16), v((rows, width), BF16),
+         v((rows, width), F32), v((rows, width), BF16), v((rows, ff), BF16), v((rows, width), F32),
+         v((width, 2 * width), BF16), v((width, width), BF16), v((width, 3 * width), BF16), v((width, ff), BF16),
+         v((ff, width), BF16), v((nb, rows, WIDE), F32), v((pad_rows, width), F32), v((pad_rows, width), F32),
+         v((rows, 2 * width), BF16), v((rows, 3 * width), BF16), v((n, 16, WIDE), BF16), pltpu.SemaphoreType.DMA((20,))],
+        "back_part_two",
+        ride,
+        collective_id,
+        44,
+    )
 
 
 def lift(rows):
@@ -1290,7 +1418,27 @@
     )(*arrays)
 
 
-def unpack_kernel(layers, table, end, dims, share, gains, f_in, f_out, w_joint, w_proj, p_in, taps, p_out, s_in, s_out, enc, pred, tok, dur):
+class Joined:
+    def __init__(self, parts, ends):
+        self.parts = parts
+        self.ends = ends
+
+    def __getitem__(self, key):
+        rows_of, cols = key
+        got = []
+        first = 0
+        for part, last in zip(self.parts, self.ends):
+            lo, hi = max(rows_of.start, first), min(rows_of.stop, last)
+            if lo < hi:
+                got.append(part[lo - first : hi - first, cols])
+            first = last
+        return got[0] if len(got) == 1 else jnp.concatenate(got, 0)
+
+
+def unpack_kernel(layers, table, end, dims, ends, *refs):
+    parts, refs = refs[: len(ends)], refs[len(ends) :]
+    gains, f_in, f_out, w_joint, w_proj, p_in, taps, p_out, s_in, s_out, enc, pred, tok, dur = refs
+    share = Joined(parts, ends)
     outs = {"f_in": f_in, "f_out": f_out, "w_joint": w_joint, "w_proj": w_proj, "p_in": p_in, "p_out": p_out, "s_in": s_in, "s_out": s_out}
     starts, width, joint = dims
     shard = gains.shape[2]
@@ -1320,15 +1468,18 @@
     dur[...] = share[at : at + tall, 256:384].astype(jnp.float32)[:, : dur.shape[1]]
 
 
-def unpack(layers, table, end, dims, share, like):
+def unpack(layers, table, end, dims, shares, like):
+    ends = []
+    for share in shares:
+        ends.append(share.shape[0] + (ends[-1] if ends else 0))
     return pl.pallas_call(
-        partial(unpack_kernel, layers, table, end, dims),
-        in_specs=[VMEM_SPEC],
+        partial(unpack_kernel, layers, table, end, dims, tuple(ends)),
+        in_specs=[VMEM_SPEC] * len(shares),
         out_specs=[VMEM_SPEC] * len(like),
         out_shape=[sds(x.shape) for x in like],
         compiler_params=pltpu.CompilerParams(vmem_limit_bytes=48 << 20),
         name="unpack_grads",
-    )(share)
+    )(*shares)
 
 
 def cut(whole, sizes, offset=0):
@@ -1486,30 +1637,44 @@
     grad_w_pred = contract_rows(
         pred_low, grad_pred_rows.reshape(utts * slots, joint).astype(jnp.bfloat16)
     )
-    sources = [pack_joint_grads(grad_w_enc, grad_w_pred, grad_tok, grad_dur_w, n)]
+    def whole_of(source):
+        return (source, 0, source.shape[1] // TILE)
+
+    joint_grads = pack_joint_grads(grad_w_enc, grad_w_pred, grad_tok, grad_dur_w, n)
+    waiting = [whole_of(joint_grads)]
+    shares = []
+    starts = [None] * layers + [0]
+    at = joint_grads.shape[1]
     bn_grads = [None] * layers
     for layer in reversed(range(layers)):
         x0, y1, h1, y2, qkv, ctx, gates, depthwise, pooled, y3, h2, y4 = records[layer]
-        g3, db, grads_one, sums, late_gains = back_one(grad, y4, y3, depthwise, pooled, smalls[layer], wholes[layer], h2, ff)
+        args = (grad, y4, y3, depthwise, pooled, smalls[layer], wholes[layer], h2, ff)
+        if layer == layers - 1:
+            outs = back_one(*args)
+        else:
+            source, first, count = waiting.pop()
+            early = min(count, -(-count * 3 // 5))
+            outs, share = back_one(*args, [(source, first, early)], 16 + layer)
+            shares.append(share)
+            if early < count:
+                waiting.append((source, first + early, count - early))
+        g3, db, grads_one, sums, late_gains = outs
         sums = exchange(sums, "sum", 12 + layer)
-        grad, grads_two = back_two(
-            frame_lengths, x0, y1, y2, gates, qkv, ctx, depthwise, db, g3, pooled, sums, late_gains, smalls[layer], wholes[layer], h1, ff
-        )
-        sources += [grads_one, grads_two]
+        waiting.append(whole_of(grads_one))
+        args = (frame_lengths, x0, y1, y2, gates, qkv, ctx, depthwise, db, g3, pooled, sums, late_gains)
+        (grad, grads_two), share = back_two(*args, smalls[layer], wholes[layer], h1, ff, waiting, 20 + layer)
+        shares.append(share)
+        waiting = [whole_of(grads_two)]
+        starts[layer] = (at, at + grads_one.shape[1])
+        at += grads_one.shape[1] + grads_two.shape[1]
         bn_grads[layer] = (sums[4:8].reshape(width), sums[0:4].reshape(width))
-    share = scatter(sources, 4)
-    starts = [None] * layers + [0]
-    at = sources[0].shape[1]
-    for place, layer in enumerate(reversed(range(layers))):
-        one, two = sources[1 + 2 * place], sources[2 + 2 * place]
-        starts[layer] = (at, at + one.shape[1])
-        at += one.shape[1] + two.shape[1]
+    shares.append(scatter(waiting, 4))
     grads = unpack(
         layers,
         table,
         end,
         (starts, width, joint),
-        share,
+        shares,
         [norm_gains, first_in, first_out, attend_joint, attend_out, point_in, depth_taps, point_out, second_in, second_out,
          enc_weight, pred_weight, token_weight, duration_weight],
     )
@@ -1527,7 +1692,6 @@
 
 
 def solution(mesh):
-    set_tile(mesh.shape["fsdp"])
     placed = (
         P(("dp", "fsdp"), None, None),
         P(("dp", "fsdp")),

time: 728 us -> 707 us (0.971)
  Pallas kernels: 661 us -> 639 us
    pallas_call x8, Pallas kernels: 414 us -> 391 us  [the longest x4 229 us: call(): pl.pallas_call(partial(riding_kernel, kernel, counts, scatter_plan(ride),...]
    unnamed x74 -> x81, local copies, waits for them, and re-layouts: 25.1 us -> 26.6 us
where the time goes in v4:
time: 707 us; the launch traced here: 696 us
  Pallas kernels  639 us (90%)
  local copies, waits for them, and re-layouts  44.2 us (6%)
    pallas_call x4, Pallas kernels, call(): pl.pallas_call(partial(riding_kernel, kernel, counts, scatter_plan(ride),...  229 us
    pallas_call x2, Pallas kernels, gather(): pl.pallas_call(partial(gather_kernel, n1, tiles, lag, part), out_shape=ja...  139 us
    pallas_call x1, Pallas kernels, joint_backward(): pl.pallas_call(partial(joint_bwd_kernel, groups, durs), grid=(utts * grou...  59.2 us
    pallas_call x2, Pallas kernels, part_one(): pl.pallas_call(partial(part_one_kernel, utts, table), in_specs=[SMEM_SPEC...  46.8 us
    pallas_call x4, Pallas kernels, exchange(): pl.pallas_call(partial(exchange_kernel, kind, groups, n), out_shape=jax.S...  44.3 us
    pallas_call x1, Pallas kernels, lattice(): pl.pallas_call(partial(lattice_kernel, slots), out_shape=(jax.ShapeDtypeS...  37.7 us
    pallas_call x1, Pallas kernels, joint_forward(): pl.pallas_call(partial(joint_fwd_kernel, groups, durs), grid=(utts * grou...  36.4 us
    unnamed x81, local copies, waits for them, and re-layouts  26.6 us

profile of v4, /device:TPU:0, one launch (start us, length us, event | category | flops | bytes accessed | tf_op | source)
XLA Modules:
  0.0 696.3 jit_solution(15803972317483178585)
XLA Ops:
  0.7 0.7 concatenate.18.labels_ref
  1.3 0.7 copy.49.refs_8_
  2.0 0.7 copy.50.refs_9_
  2.7 0.8 copy.51.refs_15_
  3.5 1.0 copy-done.7
  4.6 1.0 copy-done.8
  5.6 1.0 copy-done.9
  6.6 1.0 copy-done.10
  7.7 1.0 copy-done.12
  8.7 0.9 copy-done.13
  9.6 0.9 copy-done.14
  10.5 0.9 copy-done.15
  11.5 0.9 copy-done.16
  12.4 0.9 copy-done.17
  13.3 0.9 copy-done.18
  14.1 0.7 copy-done.21
  14.8 0.7 copy-done.22
  15.5 1.5 pack_weights.1
  17.0 1.2 copy-done.3
  18.1 76.7 %gather_weights.2.whole.refs_14_ = bf16[8,1920,512]{2,1,0:T(8,128)(2,1)} custom-call(bf16[1920,512]{1,0:T(8,128)(2,1)} %get-tuple-element.83.src), custom_call_target="tpu_custom_call" | custom-call | tf_op jit(solution)/shard_map/gather_weights/pallas_call | solution.py:423
  94.9 1.0 slice.69
  96.1 62.5 %gather_weights.3.whole.refs_6_.refs_14_ = bf16[8,1536,512]{2,1,0:T(8,128)(2,1)} custom-call(bf16[1536,512]{1,0:T(8,128)(2,1)} %copy-done.3), custom_call_target="tpu_custom_call" | custom-call | tf_op jit(solution)/shard_map/gather_weights/pallas_call | solution.py:423
  158.6 0.8 convert_bitcast_fusion.1
  159.4 0.7 reshape.139.small.refs_5_.refs_13_
  160.1 23.2 %layer_part_one.2 = (f32[512,512]{1,0:T(8,128)}, f32[4,512,512]{2,1,0:T(8,128)}, f32[512,512]{1,0:T(8,128)}, bf16[512,1536]{1,0:T(8,128)(2,1)}, bf16[512,512]{1,...) custom-call(s32[2]{0:T(128)} %refs_0_.5, bf16[512,512]{1,0:T(8,128)(2,1)} %bitcast.67, ...), custom_call_target="tpu_custom_call" | custom-call | tf_op jit(solution)/shard_map/layer_part_one/pallas_call | solution.py:1273
  183.3 11.4 %exchange_pool.2.pooled_ref.refs_4_.refs_10_ = f32[16,128]{1,0:T(8,128)} custom-call(f32[16,128]{1,0:T(8,128)} %get-tuple-element.87.x_ref), custom_call_target="tpu_custom_call" | custom-call | tf_op jit(solution)/shard_map/exchange_pool/pallas_call | solution.py:714
  194.7 11.0 %layer_part_two.2 = (f32[512,512]{1,0:T(8,128)}, f32[4,512,512]{2,1,0:T(8,128)}, f32[512,512]{1,0:T(8,128)}, f32[512,512]{1,0:T(8,128)}) custom-call(f32[512,512]{1,0:T(8,128)} %get-tuple-element.85.d_ref.refs_3_.refs_7_, f32[512,512]{1,0:T(8,128)} %get-tuple-element.86.y2_ref.refs_3_, f32[16,128]{1,0:T(8,128)} %exchange_pool.2.pooled_ref.refs_4_.refs_10_, ...), custom_call_target="tpu_custom_call" | custom-call | tf_op jit(solution)/shard_map/layer_part_two/pallas_call | solution.py:1294
  205.7 0.8 convert_bitcast_fusion
  206.5 0.7 reshape.141.small.refs_13_
  207.2 23.6 %layer_part_one.3 = (f32[512,512]{1,0:T(8,128)}, f32[4,512,512]{2,1,0:T(8,128)}, f32[512,512]{1,0:T(8,128)}, bf16[512,1536]{1,0:T(8,128)(2,1)}, bf16[512,512]{1,...) custom-call(s32[2]{0:T(128)} %refs_0_.5, ...), custom_call_target="tpu_custom_call" | custom-call | tf_op jit(solution)/shard_map/layer_part_one/pallas_call | solution.py:1273
  230.8 10.9 %exchange_pool.3.pooled_ref.refs_10_ = f32[16,128]{1,0:T(8,128)} custom-call(f32[16,128]{1,0:T(8,128)} %get-tuple-element.91.x_ref), custom_call_target="tpu_custom_call" | custom-call | tf_op jit(solution)/shard_map/exchange_pool/pallas_call | solution.py:714
  241.7 11.0 %layer_part_two.3 = (f32[512,512]{1,0:T(8,128)}, f32[4,512,512]{2,1,0:T(8,128)}, f32[512,512]{1,0:T(8,128)}, f32[512,512]{1,0:T(8,128)}) custom-call(f32[512,512]{1,0:T(8,128)} %get-tuple-element.89.d_ref.refs_7_, f32[512,512]{1,0:T(8,128)} %get-tuple-element.90.y2_ref.refs_3_, f32[16,128]{1,0:T(8,128)} %exchange_pool.3.pooled_ref.refs_10_, ...), custom_call_target="tpu_custom_call" | custom-call | tf_op jit(solution)/shard_map/layer_part_two/pallas_call | solution.py:1294
  252.8 1.8 fusion.10.enc_ref
  254.6 1.5 fusion.15
  257.3 2.3 copy.55
  259.6 3.9 pad.9.pred_ref
  263.5 1.3 slice-done.2
  264.8 1.3 copy.56
  266.5 1.9 pad_maximum_fusion
  268.3 2.6 copy.57.wt_ref
  271.0 36.4 %joint_forward.1 = (f32[8,64,256]{2,1,0:T(8,128)S(1)}, bf16[10,5,1024,256]{3,2,1,0:T(8,128)(2,1)}) custom-call(s32[2,25]{1,0:T(2,128)S(1)} %concatenate.18.labels_ref, f32[640,512]{1,0:T(8,128)S(1)} %fusion.10.enc_ref, f32[10,640,8]{2,1,0:T(8,128)} %pad.9.pred_ref, bf16[1152,640]{1,0:T(8,128)(2,1)S(1)} %copy.57.wt_ref), custom_call_target="tpu_custom_call" | custom-call | tf_op jit(solution)/shard_map/joint_forward/pallas_call | solution.py:211
  307.4 37.7 %lattice.1 = (f32[7,64,256]{2,1,0:T(8,128)S(1)}, f32[8,128]{1,0:T(8,128)S(1)}) custom-call(f32[7,64,256]{2,1,0:T(8,128)S(1)} %slice.76.feats_ref, s32[2]{0:T(128)S(1)} %copy-done.19, s32[2]{0:T(128)S(1)} %copy-done.23), custom_call_target="tpu_custom_call" | custom-call | tf_op jit(solution)/shard_map/lattice/pallas_call | solution.py:149
  345.1 0.8 copy-done.11
  346.5 59.2 %joint_backward.1 = (f32[640,512]{1,0:T(8,128)}, f32[10,640,8]{2,1,0:T(8,128)}, bf16[640,1024]{1,0:T(8,128)(2,1)}, bf16[640,128]{1,0:T(8,128)(2,1)}) custom-call(s32[2,25]{1,0:T(2,128)} %copy-done.20, f32[640,512]{1,0:T(8,128)} %copy-done, f32[10,640,8]{2,1,0:T(8,128)} %pad.9.pred_ref, bf16[640,1152]{1,0:T(8,128)(2,1)} %get-tuple-element.186.w_ref, ...), custom_call_target="tpu_custom_call" | custom-call | tf_op jit(solution)/shard_map/joint_backward/pallas_call | solution.py:284
  405.7 3.0 fusion.7.grad_ref
  408.7 19.4 %back_part_one.1 = (f32[512,512]{1,0:T(8,128)}, f32[512,512]{1,0:T(8,128)}, bf16[8,576,512]{2,1,0:T(8,128)(2,1)}, f32[16,128]{1,0:T(8,128)}, f32[8,512]{1,0:T(8,128)}) custom-call(f32[512,512]{1,0:T(8,128)} %fusion.7.grad_ref, f32[512,512]{1,0:T(8,128)} %get-tuple-element.106.y4_ref, f32[512,512]{1,0:T(8,128)} %get-tuple-element.107.y3_ref, ...), custom_call_target="tpu_custom_call" | custom-call | tf_op jit(solution)/shard_map/back_part_one/pallas_call | solution.py:626
  428.1 11.0 %exchange_sum.2.refs_11_ = f32[16,128]{1,0:T(8,128)} custom-call(f32[16,128]{1,0:T(8,128)} %get-tuple-element.111.x_ref), custom_call_target="tpu_custom_call" | custom-call | tf_op jit(solution)/shard_map/exchange_sum/pallas_call | solution.py:714
  439.7 0.8 slice_dynamic-update-slice_fusion.3
  440.5 0.6 copy-done.29
  441.5 0.8 copy.58
  442.8 1.0 slice_dynamic-update-slice_fusion.2
  443.7 0.9 slice_dynamic-update-slice_fusion.1
  444.7 0.9 slice_dynamic-update-slice_fusion
  445.7 1.0 fusion.5
  446.6 65.0 %back_part_two_and_scatter.2 = (f32[512,512]{1,0:T(8,128)}, bf16[8,960,512]{2,1,0:T(8,128)(2,1)}, bf16[10,2,48,512]{3,2,1,0:T(8,128)(2,1)}) custom-call(s32[2]{0:T(128)} %refs_0_.5, f32[512,512]{1,0:T(8,128)} %get-tuple-element.88.x_ref.refs_1_, f32[512,512]{1,0:T(8,128)} %get-tuple-element.99.refs_2_, f32[512,512]{1,0:T(8,128)} %get-tuple-element.90.y2_ref.refs_3_, ...), custom_call_target="tpu_custom_call" | custom-call | tf_op jit(solution)/shard_map/back_part_two_and_scatter/pallas_call | solution.py:638
  511.6 46.3 %back_part_one_and_scatter.1 = (f32[512,512]{1,0:T(8,128)}, f32[512,512]{1,0:T(8,128)}, bf16[8,576,512]{2,1,0:T(8,128)(2,1)}, f32[16,128]{1,0:T(8,128)}, f32[8,5...) custom-call(f32[512,512]{1,0:T(8,128)} %get-tuple-element.118.refs_0_, f32[512,512]{1,0:T(8,128)} %get-tuple-element.119.refs_1_, ...), custom_call_target="tpu_custom_call" | custom-call | tf_op jit(solution)/shard_map/back_part_one_and_scatter/pallas_call | solution.py:638
  558.0 11.1 %exchange_sum.3.refs_11_ = f32[16,128]{1,0:T(8,128)} custom-call(f32[16,128]{1,0:T(8,128)} %get-tuple-element.125.x_ref), custom_call_target="tpu_custom_call" | custom-call | tf_op jit(solution)/shard_map/exchange_sum/pallas_call | solution.py:714
  569.1 64.2 %back_part_two_and_scatter.3 = (f32[512,512]{1,0:T(8,128)}, bf16[8,960,512]{2,1,0:T(8,128)(2,1)}, bf16[10,2,48,512]{3,2,1,0:T(8,128)(2,1)}) custom-call(s32[2]{0:T(128)} %refs_0_.5, bf16[512,512]{1,0:T(8,128)(2,1)} %bitcast.68, f32[512,512]{1,0:T(8,128)} %get-tuple-element.95.refs_2_, f32[512,512]{1,0:T(8,128)} %get-tuple-element.86.y2_ref.refs_3_, ...), custom_call_target="tpu_custom_call" | custom-call | tf_op jit(solution)/shard_map/back_part_two_and_scatter/pallas_call | solution.py:638
  633.3 53.7 %idle_and_scatter.1 = bf16[10,2,48,512]{3,2,1,0:T(8,128)(2,1)} custom-call(bf16[4,2,960,512]{3,2,1,0:T(8,128)(2,1)} %bitcast.54), custom_call_target="tpu_custom_call" | custom-call | tf_op jit(solution)/shard_map/idle_and_scatter/pallas_call | solution.py:638
  687.1 1.2 copy-done.1
  688.3 3.1 unpack_grads.1
  692.5 0.7 fusion.12
  693.2 0.7 copy.61
  693.9 2.3 copy.68
  (80 shorter events, 5.1 us)
Async XLA Ops:
  1.3 269.6 %copy-start.20 = (s32[2,25]{1,0:T(2,128)}, s32[2,25]{1,0:T(2,128)S(1)}, u32[]{:S(2)}) copy-start(s32[2,25]{1,0:T(2,128)S(1)} %concatenate.18.labels_ref) | copy-start | bytes 604
  3.5 1.0 copy-start.7
  4.6 1.0 copy-start.8
  5.6 1.0 copy-start.9
  6.6 1.0 copy-start.10
  7.7 1.0 copy-start.12
  8.7 0.9 copy-start.13
  9.6 0.9 copy-start.14
  10.5 0.9 copy-start.15
  11.5 0.9 copy-start.16
  12.4 0.9 copy-start.17
  13.3 0.9 copy-start.18
  14.1 0.7 copy-start.21
  14.8 0.7 copy-start.22
  17.0 1.2 copy-start.3
  94.9 1.1 slice-start
  96.1 156.7 %copy-start.24 = (bf16[8,64,640]{2,1,0:T(8,128)(2,1)}, bf16[8,64,640]{2,1,0:T(8,128)(2,1)S(1)}, u32[]{:S(2)}) copy-start(bf16[8,64,640]{2,1,0:T(8,128)(2,1)S(1)} %pad_maximum_fusion.2) | copy-start | bytes 1966084
  254.6 16.4 %copy-start = (f32[640,512]{1,0:T(8,128)}, f32[640,512]{1,0:T(8,128)S(1)}, u32[]{:S(2)}) copy-start(f32[640,512]{1,0:T(8,128)S(1)} %fusion.10.enc_ref) | copy-start | bytes 3932164
  254.6 1.7 slice-start.1
  256.1 0.9 copy-start.31
  263.5 1.3 slice-start.2
  270.9 36.4 %copy-start.19 = (s32[2]{0:T(128)S(1)}, s32[2]{0:T(128)}, u32[]{:S(2)}) copy-start(s32[2]{0:T(128)} %refs_0_.5) | copy-start | bytes 28
  270.9 36.4 %copy-start.23 = (s32[2]{0:T(128)S(1)}, s32[2]{0:T(128)}, u32[]{:S(2)}) copy-start(s32[2]{0:T(128)} %ulen_ref.1) | copy-start | bytes 28
  307.3 39.2 %copy-start.2 = (f32[8,64,256]{2,1,0:T(8,128)}, f32[8,64,256]{2,1,0:T(8,128)S(1)}, u32[]{:S(2)}) copy-start(f32[8,64,256]{2,1,0:T(8,128)S(1)} %get-tuple-element.93.feats_ref) | copy-start | bytes 1572868
  345.1 0.8 copy-start.11
  346.5 59.2 %copy-start.25 = (bf16[8,64,640]{2,1,0:T(8,128)(2,1)S(1)}, bf16[8,64,640]{2,1,0:T(8,128)(2,1)}, u32[]{:S(2)}) copy-start(bf16[8,64,640]{2,1,0:T(8,128)(2,1)} %copy-done.24) | copy-start | bytes 1966084
  408.7 30.4 %copy-start.26 = (f32[640,512]{1,0:T(8,128)S(1)}, f32[640,512]{1,0:T(8,128)}, u32[]{:S(2)}) copy-start(f32[640,512]{1,0:T(8,128)} %get-tuple-element.105) | copy-start | bytes 3932164
  408.7 30.4 %copy-start.27 = (f32[512,512]{1,0:T(8,128)S(1)}, f32[512,512]{1,0:T(8,128)}, u32[]{:S(2)}) copy-start(f32[512,512]{1,0:T(8,128)} %get-tuple-element.92) | copy-start | bytes 3145732
  439.1 2.1 copy-start.29
  442.3 1.4 copy-start.28
  443.7 1.9 copy-start.30
  633.3 53.8 %copy-start.4 = (bf16[10,2,48,512]{3,2,1,0:T(8,128)(2,1)S(1)}, bf16[10,2,48,512]{3,2,1,0:T(8,128)(2,1)}, u32[]{:S(2)}) copy-start(bf16[10,2,48,512]{3,2,1,0:T(8,128)(2,1)} %get-tuple-element.130) | copy-start | bytes 2949124
  633.3 53.8 %copy-start.5 = (bf16[10,2,48,512]{3,2,1,0:T(8,128)(2,1)S(1)}, bf16[10,2,48,512]{3,2,1,0:T(8,128)(2,1)}, u32[]{:S(2)}) copy-start(bf16[10,2,48,512]{3,2,1,0:T(8,128)(2,1)} %get-tuple-element.132) | copy-start | bytes 2949124
  633.3 53.8 %copy-start.6 = (bf16[6,2,48,512]{3,2,1,0:T(8,128)(2,1)S(1)}, bf16[6,2,48,512]{3,2,1,0:T(8,128)(2,1)}, u32[]{:S(2)}) copy-start(bf16[6,2,48,512]{3,2,1,0:T(8,128)(2,1)} %get-tuple-element.131) | copy-start | bytes 1769476
  687.1 1.2 copy-start.1
  688.3 4.3 copy-start.33
  688.3 4.3 copy-start.32

commit v5 on v4

--- a/solution.py
+++ b/solution.py
@@ -73,44 +73,50 @@
     first = jnp.where((lax.broadcasted_iota(jnp.int32, (1, 128), 1) % 32 == 0)
                       & (lax.broadcasted_iota(jnp.int32, (1, 128), 1) < 32 * utts), 0.0, NEG)
 
-    def lse(terms):
-        tops = list(terms)
-        while len(tops) > 1:
-            tops = [jnp.maximum(tops[i], tops[i + 1]) if i + 1 < len(tops) else tops[i] for i in range(0, len(tops), 2)]
-        top = tops[0]
-        parts = [jnp.exp(x - top) for x in terms]
-        while len(parts) > 1:
-            parts = [parts[i] + parts[i + 1] if i + 1 < len(parts) else parts[i] for i in range(0, len(parts), 2)]
-        return jnp.maximum(top + jnp.log(parts[0]), NEG)
-
     a_ref[pl.ds(pad, 1), :] = first
     last = diags
 
+    def tree(parts, op):
+        while len(parts) > 1:
+            parts = [op(parts[i], parts[i + 1]) if i + 1 < len(parts) else parts[i] for i in range(0, len(parts), 2)]
+        return parts[0]
+
+    def older(hist, rolled, edge_s, edge_l):
+        terms = [hist[e - 2] + edge_s(e) for e in range(2, reach + 1)]
+        terms += [rolled[e - 1] + edge_l(e) for e in range(1, reach + 1)]
+        top = tree(terms, jnp.maximum)
+        return top, tree([jnp.exp(x - top) for x in terms], jnp.add)
+
+    def newest(old, one, two):
+        top = jnp.maximum(jnp.maximum(one, two), old[0])
+        total = (jnp.exp(one - top) + jnp.exp(two - top)) + old[1] * jnp.exp(old[0] - top)
+        return jnp.maximum(top + jnp.log(total), NEG)
+
     def step(i, carry):
-        ha, hra, hb, hrb = carry
+        ha, hra, olda, hb, hrb, oldb = carry
         row = pad + i
-        terms = [ha[e - 1] + s_ref[e - 1, pl.ds(row - e, 1), :] for e in range(1, reach + 1)]
-        terms += [hra[e] + ls_ref[e, pl.ds(row - e - 1, 1), :] for e in range(reach + 1)]
-        a = lse(terms[::-1])
+        rowb = pad + last - i
+        nexta = older(ha, hra, lambda e: s_ref[e - 1, pl.ds(row + 1 - e, 1), :], lambda e: ls_ref[e, pl.ds(row - e, 1), :])
+        nextb = older(hb, hrb, lambda e: s_ref[e - 1, pl.ds(rowb - 1, 1), :], lambda e: l_ref[e, pl.ds(rowb - 1, 1), :])
+        a = newest(olda, ha[0] + s_ref[0, pl.ds(row - 1, 1), :], hra[0] + ls_ref[0, pl.ds(row - 1, 1), :])
+        b = newest(oldb, hb[0] + s_ref[0, pl.ds(rowb, 1), :], hrb[0] + l_ref[0, pl.ds(rowb, 1), :])
+        b = jnp.maximum(b, init_ref[pl.ds(rowb, 1), :])
         a_ref[pl.ds(row, 1), :] = a
+        b_ref[pl.ds(rowb, 1), :] = b
         ra = pltpu.roll(a, 1, 1)
-        rowb = pad + last - i
-        terms = [hb[e - 1] + s_ref[e - 1, pl.ds(rowb, 1), :] for e in range(1, reach + 1)]
-        terms += [hrb[e] + l_ref[e, pl.ds(rowb, 1), :] for e in range(reach + 1)]
-        b = jnp.maximum(lse(terms[::-1]), init_ref[pl.ds(rowb, 1), :])
-        b_ref[pl.ds(rowb, 1), :] = b
         rb = pltpu.roll(b, 127, 1)
-        return ((a,) + ha[:-1], (ra,) + hra[:-1], (b,) + hb[:-1], (rb,) + hrb[:-1])
+        return ((a,) + ha[:-1], (ra,) + hra[:-1], nexta, (b,) + hb[:-1], (rb,) + hrb[:-1], nextb)
 
     b0 = init_ref[pl.ds(pad + last, 1), :]
     b_ref[pl.ds(pad + last, 1), :] = b0
     none = a_ref[pl.ds(0, 1), :]
     first = a_ref[pl.ds(pad, 1), :]
-    ha = (first,) + (none,) * (reach - 1)
-    hra = (pltpu.roll(first, 1, 1),) + (none,) * reach
-    hb = (b0,) + (none,) * (reach - 1)
-    hrb = (pltpu.roll(b0, 127, 1),) + (none,) * reach
-    lax.fori_loop(1, last + 1, step, (ha, hra, hb, hrb))
+    ha = (first,) + (none,) * (reach - 2)
+    hra = (pltpu.roll(first, 1, 1),) + (none,) * (reach - 1)
+    hb = (b0,) + (none,) * (reach - 2)
+    hrb = (pltpu.roll(b0, 127, 1),) + (none,) * (reach - 1)
+    empty = (none, none - none)
+    lax.fori_loop(1, last + 1, step, (ha, hra, empty, hb, hrb, empty), unroll=4)
 
     zrow = b_ref[pl.ds(pad, 1), :]
     lane1 = lax.broadcasted_iota(jnp.int32, (1, 128), 1)
@@ -330,113 +336,13 @@
 def rows(base, size):
     return pl.ds(pl.multiple_of(base,16),size)
 
-def gather_kernel(n1, tiles, lag, part, src, out, own_sem, sz, rz, sy, ry, sx, rx, sc, rc):
-    dp,fs,a,c,i1,i2=place()
-    greet(n1,dp,fs,a,c,i1,i2)
-    ypeer=(dp,i1*2+1-i2); xpeer=((1-a)*2+c,fs); cpeer=(a*2+1-c,fs)
-    items=n1*tiles
-    half_rows=3*part
-    def main(t): return rows((2*t+c)*half_rows+a*part,2*part)
-    def quarter(t,aa): return rows((2*t+c)*half_rows+aa*2*part,part)
-    def half(t,cc): return rows((2*t+cc)*half_rows,half_rows)
-    def of(m): return m//n1, m%n1, lax.rem(i1+n1-m%n1,n1)
-    def zcopy(t,d):
-        j=lax.rem(i1+d,n1)
-        return remote(src.at[main(t),:],out.at[fs,main(t),:],sz.at[t,d],rz.at[t,i1],(dp,j*2+i2))
-    def zin(t,j):
-        return remote(src.at[main(t),:],out.at[j*2+i2,main(t),:],sz.at[t,0],rz.at[t,j],ypeer)
-    def ycopy(t,j):
-        s=j*2+i2
-        return remote(out.at[s,main(t),:],out.at[s,main(t),:],sy.at[t,j],ry.at[t,j],ypeer)
-    def ycopy_own(t):
-        return remote(src.at[main(t),:],out.at[fs,main(t),:],sy.at[t,i1],ry.at[t,i1],ypeer)
-    def yin(t,j):
-        s=j*2+1-i2
-        return remote(src.at[main(t),:],out.at[s,main(t),:],sy.at[t,j],ry.at[t,j],ypeer)
-    def xcopy(t,s):
-        return remote(out.at[s,quarter(t,a),:],out.at[s,quarter(t,a),:],sx.at[t,s],rx.at[t,s],xpeer)
-    def xin(t,s):
-        return remote(src.at[quarter(t,a),:],out.at[s,quarter(t,1-a),:],sx.at[t,s],rx.at[t,s],xpeer)
-    def ccopy(t,s):
-        return remote(out.at[s,half(t,c),:],out.at[s,half(t,c),:],sc.at[t,s],rc.at[t,s],cpeer)
-    def cin(t,s):
-        return remote(src.at[half(t,c),:],out.at[s,half(t,1-c),:],sc.at[t,s],rc.at[t,s],cpeer)
-    local=pltpu.make_async_copy(src,out.at[fs],own_sem)
-    local.start()
-
-    def tick(tau,carry):
-        @pl.when(tau<items)
-        def _():
-            t,d,j=of(tau)
-            @pl.when(d>0)
-            def _(): zcopy(t,d).start()
-            @pl.when(d==0)
-            def _(): ycopy_own(t).start()
-        m1=tau-lag
-        @pl.when((m1>=0)&(m1<items))
-        def _():
-            t,d,j=of(m1)
-            @pl.when(d>0)
-            def _():
-                zin(t,j).wait_recv()
-                ycopy(t,j).start()
-                xcopy(t,j*2+i2).start()
-        m2=tau-2*lag
-        @pl.when((m2>=0)&(m2<items))
-        def _():
-            t,d,j=of(m2)
-            yin(t,j).wait_recv()
-            xcopy(t,j*2+1-i2).start()
-        m3=tau-3*lag
-        @pl.when((m3>=0)&(m3<items))
-        def _():
-            t,d,j=of(m3)
-            @pl.when(d>0)
-            def _():
-                xin(t,j*2+i2).wait_recv()
-                ccopy(t,j*2+i2).start()
-            xin(t,j*2+1-i2).wait_recv()
-            ccopy(t,j*2+1-i2).start()
-        return carry
-    lax.fori_loop(0,items+3*lag,tick,0)
-    local.wait()
-    def finish(m,carry):
-        t,d,j=of(m)
-        @pl.when(d>0)
-        def _():
-            cin(t,j*2+i2).wait_recv()
-            zcopy(t,d).wait_send()
-            xcopy(t,j*2+i2).wait_send()
-            ccopy(t,j*2+i2).wait_send()
-        cin(t,j*2+1-i2).wait_recv()
-        ycopy(t,j).wait_send()
-        xcopy(t,j*2+1-i2).wait_send()
-        ccopy(t,j*2+1-i2).wait_send()
-        return carry
-    lax.fori_loop(0,items,finish,0)
-
-def gather(packed, collective_id, lag=4):
-    n=lax.axis_size("fsdp"); n1=n//2
-    part=32 if packed.shape[0]%192==0 else 16
-    tiles=packed.shape[0]//(6*part)
-    dma=pltpu.SemaphoreType.DMA
-    return pl.pallas_call(
-        partial(gather_kernel,n1,tiles,lag,part),
-        out_shape=jax.ShapeDtypeStruct((n,)+packed.shape,packed.dtype),
-        in_specs=[pl.BlockSpec(memory_space=pl.ANY)],
-        out_specs=pl.BlockSpec(memory_space=pl.ANY),
-        scratch_shapes=[dma]+[dma((tiles,n1))]*4+[dma((tiles,n))]*4,
-        compiler_params=pltpu.CompilerParams(collective_id=collective_id,has_side_effects=True),
-        name="gather_weights",
-    )(packed)
-
 class Beats:
-    def __init__(self, tick=None, total=0, sites=1):
+    def __init__(self, tick=None, total=0, sites=None):
         self.tick = tick
         self.total = total
         self.at = 0
         self.credit = 0.0
-        self.scale = total / sites
+        self.scale = total / sites if sites else 1.0
 
     def grant(self, count):
         self.credit += count * self.scale
@@ -453,10 +359,11 @@
 
         lax.fori_loop(low, high, step, 0)
 
-    def loop(self, count):
+    def loop(self, sites, count=None):
         if self.tick is None:
             return lambda i: None
-        first, steps = self.grant(count)
+        first, steps = self.grant(sites)
+        count = count or sites
         return lambda i: self.span(first + i * steps // count, first + (i + 1) * steps // count)
 
     def run(self, count):
@@ -466,10 +373,13 @@
         if steps:
             self.span(first, first + steps)
 
+    def until(self, step):
+        if self.at < step:
+            self.span(self.at, step)
+            self.at = step
+
     def rest(self):
-        if self.at < self.total:
-            self.span(self.at, self.total)
-            self.at = self.total
+        self.until(self.total)
 
 
 class ScatterEngine:
@@ -621,7 +531,7 @@
     engine.finish()
 
 
-def call(kernel, args, in_specs, out_specs, out_shape, scratch, name, ride=None, collective_id=None, sites=1, lag=2):
+def call(kernel, args, in_specs, out_specs, out_shape, scratch, name, ride=None, collective_id=None, sites=None, lag=2):
     if not ride:
         return pl.pallas_call(
             partial(kernel, Beats()),
@@ -771,9 +681,9 @@
 
 
 class Mover:
-    def __init__(self, sems):
+    def __init__(self, sems, used=0):
         self.sems = sems
-        self.used = 0
+        self.used = used
         self.pending = []
 
     def take(self):
@@ -790,15 +700,16 @@
         cp.start()
         self.pending.append(cp)
 
-    def load_weight(self, whole, at, dst, tall):
-        n = whole.shape[0]
+    def load_weight(self, whole, at, dst):
+        flat = len(whole.shape) == 3
+        n = whole.shape[0] if flat else 2 * whole.shape[0]
         height = dst.shape[0] // n
         sem = self.take()
 
         def one(s, carry):
             for b in range(dst.shape[1] // WIDE):
                 pltpu.make_async_copy(
-                    whole.at[s, pl.ds(at + b * height, height), :],
+                    (whole.at[s] if flat else whole.at[s // 2, s % 2]).at[pl.ds(at + b * height, height), :],
                     dst.at[pl.ds(pl.multiple_of(s * height, 16), height), pl.ds(b * WIDE, WIDE)],
                     sem,
                 ).start()
@@ -827,6 +738,7 @@
     def finish(self):
         for cp in self.pending:
             cp.wait()
+        self.pending = []
 
 
 def valid_rows_of(t_ref, frames, i):
@@ -843,114 +755,6 @@
 
 def read_rows(ref, base, width):
     return jnp.concatenate([ref[base + i : base + i + 1, :] for i in range(width // 128)], 1)
-
-
-def ffn_fwd(rows, x_ref, gain, w_in, w_out, normed, h, act, y, mover, h_out):
-    def prepare(r, i, c):
-        normed[r, :] = (ln_parts(x_ref[r, :].astype(jnp.float32))[0] * gain).astype(jnp.bfloat16)
-        return c
-
-    row_loop(rows, prepare)
-    w_in[1].wait()
-    for b in range(h.shape[0]):
-        h[b] = nn(normed[...], w_in[0][:, b * WIDE : (b + 1) * WIDE])
-        mover.put(h.at[b], h_out.at[b])
-
-        def swish(r, i, c):
-            v = h[b, r, :]
-            act[r, b * WIDE : (b + 1) * WIDE] = (v * jax.nn.sigmoid(v)).astype(jnp.bfloat16)
-            return c
-
-        row_loop(rows, swish)
-    w_out[1].wait()
-    y[...] = x_ref[...].astype(jnp.float32) + 0.5 * nn(act[...], w_out[0][...])
-
-
-def part_one_kernel(utts, table, t_ref, x_ref, small, whole, y1_out, h_out, y2_out, t_out, c_out, r_out, d_out, stats,
-                    w_fin, w_fout, w_joint, w_proj, w_pin, y1, y2, normed, h, act, tq, ctx, r, gp, d, sems):
-    rows, width = y1.shape
-    frames = rows // utts
-    mover = Mover(sems)
-    gains = small[...]
-    fin = mover.load_weight(whole, table["f_in"], w_fin, False)
-    fout = mover.load_weight(whole, table["f_out"], w_fout, True)
-    wj = mover.load_weight(whole, table["w_joint"], w_joint, False)
-    wp = mover.load_weight(whole, table["w_proj"], w_proj, False)
-    wi = mover.load_weight(whole, table["p_in"], w_pin, False)
-    ffn_fwd(rows, x_ref, gains[0:1], (w_fin, fin), (w_fout, fout), normed, h, act, y1, mover, h_out)
-    mover.put(y1, y1_out)
-
-    def prepare(rr, i, c):
-        normed[rr, :] = (ln_parts(y1[rr, :])[0] * gains[1:2]).astype(jnp.bfloat16)
-        return c
-
-    row_loop(rows, prepare)
-    wj.wait()
-    for b in range(3):
-        tq[:, b * width : (b + 1) * width] = nn(normed[...], w_joint[:, b * width : (b + 1) * width]).astype(jnp.bfloat16)
-    mover.put(tq, t_out)
-    pairs = width // 128
-    side = lax.broadcasted_iota(jnp.int32, (frames, 128), 1) < 64
-    key_at = lax.broadcasted_iota(jnp.int32, (1, frames), 1)
-
-    def pair_step(m, carry):
-        u = m // pairs
-        base = lax.rem(m, pairs) * 128
-        rr = pl.ds(pl.multiple_of(u * frames, frames), frames)
-        bias = jnp.where(key_at < t_ref[u], 0.0, MASKED)
-        q = tq[rr, pl.ds(pl.multiple_of(base, 128), 128)]
-        k = tq[rr, pl.ds(pl.multiple_of(base + width, 128), 128)]
-        v = tq[rr, pl.ds(pl.multiple_of(base + 2 * width, 128), 128)]
-        got = []
-        for half in range(2):
-            mine = side if half == 0 else ~side
-            s = nt(jnp.where(mine, q, jnp.zeros_like(q)), k) * 0.125 + bias
-            p = jnp.exp(s - jnp.max(s, -1, keepdims=True))
-            p = p * (1.0 / jnp.sum(p, -1, keepdims=True))
-            got.append(nn(p.astype(jnp.bfloat16), v))
-        ctx[rr, pl.ds(pl.multiple_of(base, 128), 128)] = jnp.where(side, got[0], got[1]).astype(jnp.bfloat16)
-        return carry
-
-    lax.fori_loop(0, utts * pairs, pair_step, 0)
-    mover.put(ctx, c_out)
-    wp.wait()
-    y2[...] = y1[...] + nn(ctx[...], w_proj[...])
-    mover.put(y2, y2_out)
-
-    def prepare_conv(rr, i, c):
-        normed[rr, :] = (ln_parts(y2[rr, :])[0] * gains[2:3]).astype(jnp.bfloat16)
-        return c
-
-    row_loop(rows, prepare_conv)
-    wi.wait()
-    for b in range(2):
-        r[:, b * width : (b + 1) * width] = nn(normed[...], w_pin[:, b * width : (b + 1) * width])
-    mover.put(r, r_out)
-    fill_gated(utts, frames, t_ref, r, gp)
-    taps = gains[5:14]
-
-    def conv(rr, i, total):
-        d_chunk = spread(gp, utts, frames, i, taps)
-        d[rr, :] = d_chunk
-        return total + fold8(d_chunk * valid_rows_of(t_ref, frames, i), jnp.add)
-
-    total = row_loop(rows, conv, jnp.zeros((8, width), jnp.float32))
-    mover.put(d, d_out)
-    count = t_ref[0]
-    for u in range(1, utts):
-        count = count + t_ref[u]
-    count = count.astype(jnp.float32)
-    mean = jnp.sum(total, 0, keepdims=True) / count
-
-    def deviate(rr, i, total):
-        gap = (d[rr, :] - mean) * valid_rows_of(t_ref, frames, i)
-        return total + fold8(gap * gap, jnp.add)
-
-    dev = jnp.sum(row_loop(rows, deviate, jnp.zeros((8, width), jnp.float32)), 0, keepdims=True)
-    write_rows(stats, 0, mean)
-    write_rows(stats, 4, dev)
-    stats[8:16, :] = jnp.full((8, 128), count, jnp.float32)
-    mover.finish()
 
 
 def fill_gated(utts, frames, t_ref, r, gp):
@@ -985,39 +789,6 @@
         term = win[shift : shift + CHUNK_ROWS] * taps[j : j + 1]
         total = term if total is None else total + term
     return total
-
-
-def part_two_kernel(table, d_ref, y2_ref, pooled_ref, small, whole, y3_out, h_out, y4_out, x_out,
-                    w_pout, w_sin, w_sout, act_b, y3, normed, h, act, y4, x, sems):
-    rows, width = y3.shape
-    mover = Mover(sems)
-    gains = small[...]
-    wo = mover.load_weight(whole, table["p_out"], w_pout, False)
-    sin = mover.load_weight(whole, table["s_in"], w_sin, False)
-    sout = mover.load_weight(whole, table["s_out"], w_sout, True)
-    mean = read_rows(pooled_ref, 0, width)
-    count = pooled_ref[8:9, 0:1]
-    istd = lax.rsqrt(read_rows(pooled_ref, 4, width) / count + EPS)
-
-    def bn(rr, i, c):
-        b = (d_ref[rr, :] - mean) * istd * gains[14:15] + gains[15:16]
-        act_b[rr, :] = (b * jax.nn.sigmoid(b)).astype(jnp.bfloat16)
-        return c
-
-    row_loop(rows, bn)
-    wo.wait()
-    y3[...] = y2_ref[...] + nn(act_b[...], w_pout[...])
-    mover.put(y3, y3_out)
-    ffn_fwd(rows, y3, gains[3:4], (w_sin, sin), (w_sout, sout), normed, h, act, y4, mover, h_out)
-    mover.put(y4, y4_out)
-
-    def last(rr, i, c):
-        x[rr, :] = ln_parts(y4[rr, :])[0] * gains[4:5]
-        return c
-
-    row_loop(rows, last)
-    mover.put(x, x_out)
-    mover.finish()
 
 
 def ffn_bwd(rows, v_ref, gain, w_in, w_out, h, loads, g_ref, gb, normed, dact, act, dh, dn, dw_in, dw_out, mover, grads, at_in, at_out, beats):
@@ -1065,15 +836,15 @@
     return jnp.sum(folded, 0, keepdims=True)
 
 
-def back_one_kernel(table, beats, grad_ref, y4_ref, y3_ref, d_ref, pooled_ref, small, whole, h_hbm, g_out, db_out, grads, sums, gain_out,
+def back_one_kernel(table, held, beats, grad_ref, y4_ref, y3_ref, d_ref, pooled_ref, small, whole, h_hbm, g_out, db_out, grads, sums, gain_out,
                     w_pout, w_sin, w_sout, g, gb, normed, dact, act, dh, dn, dw_in, dw_out, dw_pout, h, db, sems):
     rows, width = g.shape
     mover = Mover(sems)
     gains = small[...]
-    sout = mover.load_weight(whole, table["s_out"], w_sout, True)
+    sout = mover.load_weight(whole, held["s_out"], w_sout)
     loads = [mover.load(h_hbm.at[b], h.at[b]) for b in range(h.shape[0])]
-    sin = mover.load_weight(whole, table["s_in"], w_sin, False)
-    wo = mover.load_weight(whole, table["p_out"], w_pout, False)
+    sin = mover.load_weight(whole, held["s_in"], w_sin)
+    wo = mover.load_weight(whole, held["p_out"], w_pout)
     beats.run(5)
 
     def first(rr, i, total):
@@ -1119,19 +890,19 @@
     mover.finish()
 
 
-def back_two_kernel(utts, table, start, end, beats, t_ref, x_ref, y1_ref, y2_ref, r_ref, t_in, c_ref, d_ref, db_ref, g_in, pooled_ref, sums_ref, late_ref, small, whole, h_hbm,
+def back_two_kernel(utts, table, held, start, end, beats, t_ref, x_ref, y1_ref, y2_ref, r_ref, t_in, c_ref, d_ref, db_ref, g_in, pooled_ref, sums_ref, late_ref, small, whole, h_hbm,
                     g_out, grads,
                     w_pin, w_proj, w_joint, w_fin, w_fout, g, gb, normed, dact, act, dh, dn, dw_pin, dw_proj, dw_joint, dw_in, dw_out, h, gp, dd, dr, dt, sm, sems):
     rows, width = g.shape
     frames = rows // utts
     mover = Mover(sems)
     gains = small[...]
-    wi = mover.load_weight(whole, table["p_in"], w_pin, False)
-    wp = mover.load_weight(whole, table["w_proj"], w_proj, False)
-    wj = mover.load_weight(whole, table["w_joint"], w_joint, False)
-    fout = mover.load_weight(whole, table["f_out"], w_fout, True)
+    wi = mover.load_weight(whole, held["p_in"], w_pin)
+    wp = mover.load_weight(whole, held["w_proj"], w_proj)
+    wj = mover.load_weight(whole, held["w_joint"], w_joint)
+    fout = mover.load_weight(whole, held["f_out"], w_fout)
     loads = [mover.load(h_hbm.at[b], h.at[b]) for b in range(h.shape[0])]
-    fin = mover.load_weight(whole, table["f_in"], w_fin, False)
+    fin = mover.load_weight(whole, held["f_in"], w_fin)
     mean = read_rows(pooled_ref, 0, width)
     count = pooled_ref[8:9, 0:1]
     istd = lax.rsqrt(read_rows(pooled_ref, 4, width) / count + EPS)
@@ -1264,58 +1035,18 @@
     return jax.ShapeDtypeStruct(shape, dtype)
 
 
-def part_one(t_len, x, small, whole, ff):
-    rows, width = x.shape
-    utts = t_len.shape[0]
-    table, _ = offsets(whole.shape[0], width, ff)
-    nb = ff // WIDE
-    v = pltpu.VMEM
-    return pl.pallas_call(
-        partial(part_one_kernel, utts, table),
-        in_specs=[SMEM_SPEC, VMEM_SPEC, VMEM_SPEC, ANY_SPEC],
-        out_specs=[ANY_SPEC] * 7 + [VMEM_SPEC],
-        out_shape=[sds((rows, width)), sds((nb, rows, WIDE)), sds((rows, width)), sds((rows, 3 * width), BF16),
-                   sds((rows, width), BF16), sds((rows, 2 * width)), sds((rows, width)), sds((16, 128))],
-        scratch_shapes=[v((width, ff), BF16), v((ff, width), BF16), v((width, 3 * width), BF16), v((width, width), BF16),
-                        v((width, 2 * width), BF16), v((rows, width), F32), v((rows, width), F32), v((rows, width), BF16),
-                        v((nb, rows, WIDE), F32), v((rows, ff), BF16), v((rows, 3 * width), BF16), v((rows, width), BF16),
-                        v((rows, 2 * width), F32), v((utts * (rows // utts + 16), width), F32), v((rows, width), F32),
-                        pltpu.SemaphoreType.DMA((24,))],
-        compiler_params=pltpu.CompilerParams(vmem_limit_bytes=56 << 20),
-        name="layer_part_one",
-    )(t_len, x, small, whole)
-
-
-def part_two(d, y2, pooled, small, whole, ff):
-    rows, width = d.shape
-    table, _ = offsets(whole.shape[0], width, ff)
-    nb = ff // WIDE
-    v = pltpu.VMEM
-    return pl.pallas_call(
-        partial(part_two_kernel, table),
-        in_specs=[VMEM_SPEC] * 4 + [ANY_SPEC],
-        out_specs=[ANY_SPEC] * 4,
-        out_shape=[sds((rows, width)), sds((nb, rows, WIDE)), sds((rows, width)), sds((rows, width))],
-        scratch_shapes=[v((width, width), BF16), v((width, ff), BF16), v((ff, width), BF16), v((rows, width), BF16),
-                        v((rows, width), F32), v((rows, width), BF16), v((nb, rows, WIDE), F32), v((rows, ff), BF16),
-                        v((rows, width), F32), v((rows, width), F32), pltpu.SemaphoreType.DMA((16,))],
-        compiler_params=pltpu.CompilerParams(vmem_limit_bytes=56 << 20),
-        name="layer_part_two",
-    )(d, y2, pooled, small, whole)
-
-
 def tiled(count):
     return -(-count // TILE) * TILE
 
 
-def back_one(grad, y4, y3, d, pooled, small, whole, h, ff, ride=None, collective_id=None):
+def back_one(grad, y4, y3, d, pooled, small, whole, h, ff, held, ride=None, collective_id=None):
     rows, width = grad.shape
     n = whole.shape[0]
     table, _ = offsets(n, width, ff)
     nb = ff // WIDE
     v = pltpu.VMEM
     return call(
-        partial(back_one_kernel, table),
+        partial(back_one_kernel, table, held),
         (grad, y4, y3, d, pooled, small, whole, h),
         [VMEM_SPEC] * 6 + [ANY_SPEC] * 2,
         [ANY_SPEC] * 3 + [VMEM_SPEC] * 2,
@@ -1331,7 +1062,7 @@
     )
 
 
-def back_two(t_len, x, y1, y2, r, t, c, d, db, g, pooled, sums, late, small, whole, h, ff, ride=None, collective_id=None):
+def back_two(t_len, x, y1, y2, r, t, c, d, db, g, pooled, sums, late, small, whole, h, ff, held, ride=None, collective_id=None):
     rows, width = d.shape
     utts = t_len.shape[0]
     n = whole.shape[0]
@@ -1341,7 +1072,7 @@
     v = pltpu.VMEM
     pad_rows = utts * (rows // utts + 16)
     return call(
-        partial(back_two_kernel, utts, table, start, end),
+        partial(back_two_kernel, utts, table, held, start, end),
         (t_len, x, y1, y2, r, t, c, d, db, g, pooled, sums, late, small, whole, h),
         [SMEM_SPEC] + [VMEM_SPEC] * 13 + [ANY_SPEC] * 2,
         [ANY_SPEC] * 2,
@@ -1359,37 +1090,186 @@
     )
 
 
-def lift(rows):
-    return -(-rows // 16) * 16
-
-
-def joint_sizes(w_enc, w_pred, w_tok):
-    low, tall = lift(w_enc.shape[0]), lift(w_pred.shape[0])
-    return [low, tall, tall * (w_tok.shape[1] // WIDE), tall]
-
-
-def pack_kernel(layers, table, end, *refs):
-    names = PLACE + ("gains", "taps", "bn_gain", "bn_bias", "enc", "pred", "tok", "dur")
-    src = dict(zip(names, refs))
-    outs = refs[len(names) :]
+FIRST = ("small", "f_in", "f_out", "w_joint", "w_proj", "p_in", "p_out", "s_in", "s_out")
+
+
+def gathered_rows(n, width, ff, layers):
+    low = width // n
+    tall = ff // n
+    sizes = {
+        "f_in": low * (ff // WIDE), "f_out": tall, "small": 16, "w_joint": 3 * low, "w_proj": low,
+        "p_in": 2 * low, "p_out": low, "s_in": low * (ff // WIDE), "s_out": tall,
+    }
+    tables = []
+    at = 0
     for layer in range(layers):
-        out = outs[layer]
-        for name in PLACE:
+        table = {}
+        for name in FIRST:
+            table[name] = (at, at + sizes[name])
+            at += sizes[name]
+        tables.append(table)
+    return tables, at
+
+
+class GatherEngine:
+    def __init__(self, n1, tiles, lag, packed, out, so, sz, rz, sy, ry, sx, rx, sc, rc):
+        dp, fs, a, c, i1, i2 = place()
+        ypeer = (dp, i1 * 2 + 1 - i2)
+        xpeer = ((1 - a) * 2 + c, fs)
+        cpeer = (a * 2 + 1 - c, fs)
+
+        def main(t):
+            return rows(t * TILE + c * HALF + a * QA, QA + QB)
+
+        def quarter(t, aa):
+            return rows(t * TILE + c * HALF + aa * (QA + QB), QA)
+
+        def half(t, cc):
+            return rows(t * TILE + cc * HALF, HALF)
+
+        def local(t):
+            return pltpu.make_async_copy(packed.at[main(t), :], out.at[i1, i2, main(t), :], so.at[t])
+
+        def zcopy(t, j):
+            return remote(packed.at[main(t), :], out.at[i1, i2, main(t), :], sz.at[t, j], rz.at[t, i1], (dp, j * 2 + i2))
+
+        def zin(t, j):
+            return remote(packed.at[main(t), :], out.at[j, i2, main(t), :], sz.at[t, j], rz.at[t, j], ypeer)
+
+        def ycopy(t):
+            return remote(out.at[:, i2, main(t), :], out.at[:, i2, main(t), :], sy.at[t], ry.at[t], ypeer)
+
+        def yin(t):
+            return remote(out.at[:, i2, main(t), :], out.at[:, 1 - i2, main(t), :], sy.at[t], ry.at[t], ypeer)
+
+        def xcopy(t):
+            return remote(out.at[:, :, quarter(t, a), :], out.at[:, :, quarter(t, a), :], sx.at[t], rx.at[t], xpeer)
+
+        def xin(t):
+            return remote(out.at[:, :, quarter(t, a), :], out.at[:, :, quarter(t, 1 - a), :], sx.at[t], rx.at[t], xpeer)
+
+        def ccopy(t):
+            return remote(out.at[:, :, half(t, c), :], out.at[:, :, half(t, c), :], sc.at[t], rc.at[t], cpeer)
+
+        def cin(t):
+            return remote(out.at[:, :, half(t, c), :], out.at[:, :, half(t, 1 - c), :], sc.at[t], rc.at[t], cpeer)
+
+        def stage_z(t):
+            for d in range(1, n1):
+                zcopy(t, lax.rem(i1 + d, n1)).start()
+            local(t).start()
+
+        def stage_y(t):
+            local(t).wait()
+            for d in range(1, n1):
+                zin(t, lax.rem(i1 + n1 - d, n1)).wait_recv()
+            ycopy(t).start()
+
+        def stage_x(t):
+            yin(t).wait_recv()
+            xcopy(t).start()
+
+        def stage_c(t):
+            xin(t).wait_recv()
+            ccopy(t).start()
+
+        def stage_o(t):
+            cin(t).wait_recv()
+
+        stages = (stage_z, stage_y, stage_x, stage_c, stage_o)
+
+        def tick(tau):
+            for place_of, stage in enumerate(stages):
+                t = tau - place_of * lag
+
+                @pl.when((t >= 0) & (t < tiles))
+                def _(stage=stage, t=t):
+                    stage(t)
+
+        def finish():
+            def tile(t, carry):
+                for d in range(1, n1):
+                    zcopy(t, lax.rem(i1 + d, n1)).wait_send()
+                ycopy(t).wait_send()
+                xcopy(t).wait_send()
+                ccopy(t).wait_send()
+                return carry
+
+            lax.fori_loop(0, tiles, tile, 0)
+
+        self.tick = tick
+        self.total = tiles + (len(stages) - 1) * lag
+        self.after = lambda end: -(-end // TILE) + (len(stages) - 1) * lag
+        self.finish = finish
+
+
+class Exchange:
+    def __init__(self, groups, n, near, far, s1, r1, s2, r2):
+        self.groups, self.n = groups, n
+        self.near, self.far = near, far
+        self.sems = (s1, r1, s2, r2)
+
+    def merge(self, ref, members):
+        mean, dev, count = pooled([ref[i] for i in range(members)])
+        return jnp.concatenate([mean, dev, jnp.broadcast_to(count, (8, 128))], 0)
+
+    def run(self, x, beats):
+        dp = lax.axis_index("dp")
+        fs = lax.axis_index("fsdp")
+        near, far, groups, n = self.near, self.far, self.groups, self.n
+        s1, r1, s2, r2 = self.sems
+        near[dp] = x
+        sent = []
+        for d in range(1, groups):
+            cp = remote(near.at[dp], near.at[dp], s1.at[d], r1.at[dp], (lax.rem(dp + d, groups), fs))
+            cp.start()
+            sent.append(cp)
+        beats.run(1)
+        for d in range(1, groups):
+            other = lax.rem(dp + d, groups)
+            remote(near.at[dp], near.at[other], s1.at[d], r1.at[other], (other, fs)).wait_recv()
+        far[fs] = self.merge(near, groups)
+        for d in range(1, n):
+            cp = remote(far.at[fs], far.at[fs], s2.at[d], r2.at[fs], (dp, lax.rem(fs + d, n)))
+            cp.start()
+            sent.append(cp)
+        beats.run(1)
+        for d in range(1, n):
+            other = lax.rem(fs + d, n)
+            remote(far.at[fs], far.at[other], s2.at[d], r2.at[other], (dp, other)).wait_recv()
+        for cp in sent:
+            cp.wait_send()
+        return self.merge(far, n)
+
+
+def meet(groups, n):
+    dp = lax.axis_index("dp")
+    fs = lax.axis_index("fsdp")
+    barrier = pltpu.get_barrier_semaphore()
+    for d in range(1, groups):
+        pl.semaphore_signal(barrier, inc=1, device_id=(lax.rem(dp + d, groups), fs), device_id_type=MESH)
+    for d in range(1, n):
+        pl.semaphore_signal(barrier, inc=1, device_id=(dp, lax.rem(fs + d, n)), device_id_type=MESH)
+    return lambda: pl.semaphore_wait(barrier, groups + n - 2)
+
+
+def pack_into(out, src, tables, joint_at, layers):
+    for layer in range(layers):
+        for name in FIRST:
+            base, stop = tables[layer][name]
+            if name == "small":
+                small = [src["gains"][layer], src["taps"][layer], src["bn_gain"][layer : layer + 1, :], src["bn_bias"][layer : layer + 1, :]]
+                small = jnp.concatenate([x.astype(jnp.float32) for x in small], 0)
+                small = jnp.concatenate([small, jnp.zeros((16, WIDE - small.shape[1]), jnp.float32)], 1)
+                out[base:stop, :] = small.astype(jnp.bfloat16)
+                continue
             ref = src[name]
             height = ref.shape[1]
             for b in range(ref.shape[2] // WIDE):
-                at = table[name] + b * height
-                out[at : at + height, :] = ref[layer, :, b * WIDE : (b + 1) * WIDE]
-        small = [src["gains"][layer], src["taps"][layer], src["bn_gain"][layer : layer + 1, :], src["bn_bias"][layer : layer + 1, :]]
-        small = jnp.concatenate([x.astype(jnp.float32) for x in small], 0)
-        small = jnp.concatenate([small, jnp.zeros((16, WIDE - small.shape[1]), jnp.float32)], 1)
-        out[end : end + 16, :] = small.astype(jnp.bfloat16)
-        if out.shape[0] > end + 16:
-            out[end + 16 :, :] = jnp.zeros((out.shape[0] - end - 16, WIDE), jnp.bfloat16)
-    out = outs[layers - 1]
+                out[base + b * height : base + (b + 1) * height, :] = ref[layer, :, b * WIDE : (b + 1) * WIDE]
     enc, pred, tok, dur = src["enc"], src["pred"], src["tok"], src["dur"]
     low, tall = enc.shape[0], pred.shape[0]
-    at = end + 16
+    at = joint_at
     out[at : at + low, :] = enc[:, :WIDE]
     at += lift(low)
     out[at : at + tall, :] = pred[:, :WIDE]
@@ -1403,19 +1283,259 @@
     out[at : at + tall, 256:384] = jnp.concatenate([dur, jnp.zeros((tall, 128 - dur.shape[1]), jnp.float32)], 1).astype(jnp.bfloat16)
 
 
-def pack(layers, table, end, extra, arrays):
-    shapes = []
+def ffn_fwd(rows, x_ref, gain, weights, names, normed, h, act, y, mover, h_out, beats):
+    w_in = weights[names[0]]
+
+    def prepare(r, i, c):
+        normed[r, :] = (ln_parts(x_ref[r, :].astype(jnp.float32))[0] * gain).astype(jnp.bfloat16)
+        return c
+
+    row_loop(rows, prepare)
+    w_in[1].wait()
+    for b in range(h.shape[0]):
+        h[b] = nn(normed[...], w_in[0][:, b * WIDE : (b + 1) * WIDE])
+        mover.put(h.at[b], h_out.at[b])
+
+        def swish(r, i, c):
+            v = h[b, r, :]
+            act[r, b * WIDE : (b + 1) * WIDE] = (v * jax.nn.sigmoid(v)).astype(jnp.bfloat16)
+            return c
+
+        row_loop(rows, swish)
+        beats.run(1)
+    w_out = weights[names[1]]
+    w_out[1].wait()
+    y[...] = x_ref[...].astype(jnp.float32) + 0.5 * nn(act[...], w_out[0][...])
+    beats.run(1)
+
+
+def part_one(utts, beats, mover, t_ref, x_ref, gains, weights, outs, scratch):
+    y1_out, h_out, y2_out, t_out, c_out, r_out, d_out = outs
+    y1, y2, normed, h, act, tq, ctx, r, gp, d = scratch
+    rows, width = y1.shape
+    frames = rows // utts
+    ffn_fwd(rows, x_ref, gains[0:1], weights, ("f_in", "f_out"), normed, h, act, y1, mover, h_out, beats)
+    mover.put(y1, y1_out)
+
+    def prepare(rr, i, c):
+        normed[rr, :] = (ln_parts(y1[rr, :])[0] * gains[1:2]).astype(jnp.bfloat16)
+        return c
+
+    row_loop(rows, prepare)
+    w_joint = weights["w_joint"][0]
+    weights["w_joint"][1].wait()
+    for b in range(3):
+        tq[:, b * width : (b + 1) * width] = nn(normed[...], w_joint[:, b * width : (b + 1) * width]).astype(jnp.bfloat16)
+    mover.put(tq, t_out)
+    beats.run(1)
+    pairs = width // 128
+    side = lax.broadcasted_iota(jnp.int32, (frames, 128), 1) < 64
+    key_at = lax.broadcasted_iota(jnp.int32, (1, frames), 1)
+    hook = beats.loop(3, utts * pairs)
+
+    def pair_step(m, carry):
+        hook(m)
+        u = m // pairs
+        base = lax.rem(m, pairs) * 128
+        rr = pl.ds(pl.multiple_of(u * frames, frames), frames)
+        bias = jnp.where(key_at < t_ref[u], 0.0, MASKED)
+        q = tq[rr, pl.ds(pl.multiple_of(base, 128), 128)]
+        k = tq[rr, pl.ds(pl.multiple_of(base + width, 128), 128)]
+        v = tq[rr, pl.ds(pl.multiple_of(base + 2 * width, 128), 128)]
+        got = []
+        for half in range(2):
+            mine = side if half == 0 else ~side
+            s = nt(jnp.where(mine, q, jnp.zeros_like(q)), k) * 0.125 + bias
+            p = jnp.exp(s - jnp.max(s, -1, keepdims=True))
+            p = p * (1.0 / jnp.sum(p, -1, keepdims=True))
+            got.append(nn(p.astype(jnp.bfloat16), v))
+        ctx[rr, pl.ds(pl.multiple_of(base, 128), 128)] = jnp.where(side, got[0], got[1]).astype(jnp.bfloat16)
+        return carry
+
+    lax.fori_loop(0, utts * pairs, pair_step, 0)
+    mover.put(ctx, c_out)
+    weights["w_proj"][1].wait()
+    y2[...] = y1[...] + nn(ctx[...], weights["w_proj"][0][...])
+    mover.put(y2, y2_out)
+
+    def prepare_conv(rr, i, c):
+        normed[rr, :] = (ln_parts(y2[rr, :])[0] * gains[2:3]).astype(jnp.bfloat16)
+        return c
+
+    row_loop(rows, prepare_conv)
+    w_pin = weights["p_in"][0]
+    weights["p_in"][1].wait()
+    for b in range(2):
+        r[:, b * width : (b + 1) * width] = nn(normed[...], w_pin[:, b * width : (b + 1) * width])
+    mover.put(r, r_out)
+    beats.run(1)
+    fill_gated(utts, frames, t_ref, r, gp)
+    taps = gains[5:14]
+
+    def conv(rr, i, total):
+        d_chunk = spread(gp, utts, frames, i, taps)
+        d[rr, :] = d_chunk
+        return total + fold8(d_chunk * valid_rows_of(t_ref, frames, i), jnp.add)
+
+    total = row_loop(rows, conv, jnp.zeros((8, width), jnp.float32))
+    mover.put(d, d_out)
+    beats.run(1)
+    count = t_ref[0]
+    for u in range(1, utts):
+        count = count + t_ref[u]
+    count = count.astype(jnp.float32)
+    mean = jnp.sum(total, 0, keepdims=True) / count
+
+    def deviate(rr, i, total):
+        gap = (d[rr, :] - mean) * valid_rows_of(t_ref, frames, i)
+        return total + fold8(gap * gap, jnp.add)
+
+    dev = jnp.sum(row_loop(rows, deviate, jnp.zeros((8, width), jnp.float32)), 0, keepdims=True)
+    cut4 = lambda v: [v[:, i * 128 : (i + 1) * 128] for i in range(width // 128)]
+    return jnp.concatenate(cut4(mean) + cut4(dev) + [jnp.full((8, 128), count, jnp.float32)], 0)
+
+
+def part_two(beats, mover, pooled_ref, gains, weights, outs, scratch):
+    y3_out, h_out, y4_out, x_out = outs
+    d, y2, y3, normed, h, act, y4, x = scratch
+    rows, width = y3.shape
+    mean = read_rows(pooled_ref, 0, width)
+    count = pooled_ref[8:9, 0:1]
+    istd = lax.rsqrt(read_rows(pooled_ref, 4, width) / count + EPS)
+
+    def bn(rr, i, c):
+        b = (d[rr, :] - mean) * istd * gains[14:15] + gains[15:16]
+        normed[rr, :] = (b * jax.nn.sigmoid(b)).astype(jnp.bfloat16)
+        return c
+
+    row_loop(rows, bn)
+    weights["p_out"][1].wait()
+    y3[...] = y2[...] + nn(normed[...], weights["p_out"][0][...])
+    mover.put(y3, y3_out)
+    ffn_fwd(rows, y3, gains[3:4], weights, ("s_in", "s_out"), normed, h, act, y4, mover, h_out, beats)
+    mover.put(y4, y4_out)
+
+    def last(rr, i, c):
+        x[rr, :] = ln_parts(y4[rr, :])[0] * gains[4:5]
+        return c
+
+    row_loop(rows, last)
+    mover.put(x, x_out)
+
+
+def forward_kernel(utts, layers, n1, groups, tables, joint_at, tiles, lag, t_ref, frames_ref, *refs):
+    n = 2 * n1
+    names = PLACE + ("gains", "taps", "bn_gain", "bn_bias", "enc", "pred", "tok", "dur")
+    src = dict(zip(names, refs))
+    refs = refs[len(names) :]
+    whole, refs = refs[0], refs[1:]
+    layer_outs = []
     for layer in range(layers):
-        count = end + 16 + (extra if layer == layers - 1 else 0)
-        shapes.append(sds((tiled(count), WIDE), BF16))
-    return pl.pallas_call(
-        partial(pack_kernel, layers, table, end),
-        in_specs=[VMEM_SPEC] * len(arrays),
-        out_specs=[VMEM_SPEC] * layers,
-        out_shape=shapes,
-        compiler_params=pltpu.CompilerParams(vmem_limit_bytes=48 << 20),
-        name="pack_weights",
-    )(*arrays)
+        layer_outs.append((refs[0:7], refs[7:11], refs[11], refs[12]))
+        refs = refs[13:]
+    buffers, refs = refs[:8], refs[8:]
+    packed, smalls, y1, y2, normed, h, act, tq, ctx, r, gp, d, y3, y4, x, sems = refs[:16]
+    refs = refs[16:]
+    entered = meet(groups, n)
+    pack_into(packed, src, tables, joint_at, layers)
+    entered()
+    engine = GatherEngine(n1, tiles, lag, packed, whole, *refs[:9])
+    refs = refs[9:]
+    beats = Beats(engine.tick, engine.total)
+    held = dict(zip(("f_in", "f_out", "w_joint", "w_proj", "p_in", "p_out", "s_in", "s_out"), buffers))
+    used = 0
+    for layer in range(layers):
+        table = tables[layer]
+        mover = Mover(sems, used)
+
+        def load(name):
+            beats.until(engine.after(table[name][1]))
+            return held[name], mover.load_weight(whole, table[name][0], held[name])
+
+        weights = {"f_in": load("f_in")}
+        small = mover.load(whole.at[:, :, pl.ds(table["small"][0], 16), :], smalls)
+        small.wait()
+        gains = None
+        for s in range(n):
+            part = smalls[s // 2, s % 2].astype(jnp.float32)
+            part = part if s == 0 else pltpu.roll(part, s * (WIDE // n), 1)
+            gains = part if gains is None else gains + part
+        layer_outs[layer][3][...] = gains
+        weights = Late(weights, load)
+        first, second, pooled_out, _ = layer_outs[layer]
+        source = frames_ref if layer == 0 else x
+        stats = part_one(utts, beats, mover, t_ref, source, gains, weights, first, (y1, y2, normed, h, act, tq, ctx, r, gp, d))
+        exchange = Exchange(groups, n, *refs[:6])
+        refs = refs[6:]
+        for name in ("p_out", "s_in", "s_out"):
+            weights.fetch(name)
+        pooled_out[...] = exchange.run(stats, beats)
+        mover.finish()
+        part_two(beats, mover, pooled_out, gains, weights, second, (d, y2, y3, normed, h, act, y4, x))
+        mover.finish()
+        used = mover.used
+    beats.rest()
+    engine.finish()
+
+
+class Late:
+    def __init__(self, got, load):
+        self.got = got
+        self.load = load
+
+    def fetch(self, name):
+        if name not in self.got:
+            self.got[name] = self.load(name)
+
+    def __getitem__(self, name):
+        self.fetch(name)
+        return self.got[name]
+
+
+def forward(t_len, frames_in, arrays, layers, ff, sizes, collective_id, lag=2):
+    rows, width = frames_in.shape
+    utts = t_len.shape[0]
+    n = lax.axis_size("fsdp")
+    groups = lax.axis_size("dp")
+    n1 = n // 2
+    tables, joint_at = gathered_rows(n, width, ff, layers)
+    total = tiled(joint_at + sum(sizes))
+    tiles = total // TILE
+    nb = ff // WIDE
+    v = pltpu.VMEM
+    dma = pltpu.SemaphoreType.DMA
+    big = sds((rows, width))
+    one = [big, sds((nb, rows, WIDE)), big, sds((rows, 3 * width), BF16), sds((rows, width), BF16), sds((rows, 2 * width)), big]
+    two = [big, sds((nb, rows, WIDE)), big, big]
+    pad_rows = utts * (rows // utts + 16)
+    outs = pl.pallas_call(
+        partial(forward_kernel, utts, layers, n1, groups, tables, joint_at, tiles, lag),
+        in_specs=[SMEM_SPEC] + [VMEM_SPEC] * (1 + len(arrays)),
+        out_specs=[ANY_SPEC] + ([ANY_SPEC] * 11 + [VMEM_SPEC] * 2) * layers,
+        out_shape=[sds((n1, 2, total, WIDE), BF16)] + (one + two + [sds((16, 128)), sds((16, width))]) * layers,
+        scratch_shapes=[
+            v((width, ff), BF16), v((ff, width), BF16), v((width, 3 * width), BF16), v((width, width), BF16), v((width, 2 * width), BF16),
+            v((width, width), BF16), v((width, ff), BF16), v((ff, width), BF16),
+            v((total, WIDE), BF16), v((n1, 2, 16, WIDE), BF16), v((rows, width), F32), v((rows, width), F32), v((rows, width), BF16),
+            v((nb, rows, WIDE), F32), v((rows, ff), BF16), v((rows, 3 * width), BF16), v((rows, width), BF16), v((rows, 2 * width), F32),
+            v((pad_rows, width), F32), v((rows, width), F32), v((rows, width), F32), v((rows, width), F32), v((rows, width), F32), dma((80,)),
+            dma((tiles,)), dma((tiles, n1)), dma((tiles, n1)), dma((tiles,)), dma((tiles,)), dma((tiles,)), dma((tiles,)), dma((tiles,)), dma((tiles,)),
+        ]
+        + [v((groups, 16, 128), F32), v((n, 16, 128), F32), dma((groups,)), dma((groups,)), dma((n,)), dma((n,))] * layers,
+        compiler_params=pltpu.CompilerParams(collective_id=collective_id, has_side_effects=True, vmem_limit_bytes=61 << 20),
+        name="gather_and_forward",
+    )(t_len, frames_in, *arrays)
+    whole = outs[0].reshape(n, total, WIDE)
+    return whole, [outs[1 + 13 * layer : 14 + 13 * layer] for layer in range(layers)], tables, joint_at
+
+
+def lift(rows):
+    return -(-rows // 16) * 16
+
+
+def joint_sizes(w_enc, w_pred, w_tok):
+    low, tall = lift(w_enc.shape[0]), lift(w_pred.shape[0])
+    return [low, tall, tall * (w_tok.shape[1] // WIDE), tall]
 
 
 class Joined:
@@ -1494,6 +1614,102 @@
     n, height, _ = part.shape
     blocks = cols // WIDE
     return jnp.swapaxes(part.reshape(n, blocks, height // blocks, WIDE)[:, :, :rows], 1, 2).reshape(-1, cols)
+
+
+def joint_inputs_kernel(base, x_ref, pred_ref, whole, low_ref, enc_t, pred_t, w_t, w_enc, w_pred, w_cat, sems):
+    n = whole.shape[0]
+    joint = w_enc.shape[1]
+    low, tall = w_enc.shape[0] // n, w_pred.shape[0] // n
+    vocab = w_cat.shape[1] - 128
+    first = base + low + tall
+    rest = first + tall * (vocab // WIDE)
+
+    def spread(at, height, dst, cols, lanes, sem):
+        def one(s, carry):
+            pltpu.make_async_copy(
+                whole.at[s, pl.ds(at, height), lanes], dst.at[pl.ds(pl.multiple_of(s * height, 16), height), cols], sem
+            ).start()
+            return carry
+
+        lax.fori_loop(0, n, one, 0)
+
+    every = pl.ds(0, WIDE)
+    spread(base, low, w_enc, every, every, sems.at[0])
+    spread(rest, low, w_enc, pl.ds(WIDE, 128), pl.ds(0, 128), sems.at[0])
+    spread(base + low, tall, w_pred, every, every, sems.at[1])
+    spread(rest, tall, w_pred, pl.ds(WIDE, 128), pl.ds(128, 128), sems.at[1])
+    for b in range(vocab // WIDE):
+        spread(first + b * tall, tall, w_cat, pl.ds(b * WIDE, WIDE), every, sems.at[2])
+    spread(rest, tall, w_cat, pl.ds(vocab, 128), pl.ds(256, 128), sems.at[2])
+    low_ref[...] = x_ref[...].astype(jnp.bfloat16)
+    pltpu.make_async_copy(w_enc, w_enc, sems.at[0]).wait()
+    enc_t[...] = nn(low_ref[...], w_enc[...]).T
+    pltpu.make_async_copy(w_pred, w_pred, sems.at[1]).wait()
+    pred = nn(pred_ref[...], w_pred[...])
+    for g in range(pred_t.shape[0]):
+        pred_t[g] = pred[g * 8 : (g + 1) * 8, :].T
+    pltpu.make_async_copy(w_cat, w_cat, sems.at[2]).wait()
+    w_t[...] = w_cat[...].T
+
+
+def joint_inputs(x, pred_low, whole, base, joint, vocab):
+    rows, width = x.shape
+    groups = pred_low.shape[0] // 8
+    return pl.pallas_call(
+        partial(joint_inputs_kernel, base),
+        in_specs=[VMEM_SPEC, VMEM_SPEC, ANY_SPEC],
+        out_specs=[VMEM_SPEC] * 7,
+        out_shape=[sds((rows, width), BF16), sds((joint, rows)), sds((groups, joint, 8)), sds((vocab + 128, joint), BF16),
+                   sds((width, joint), BF16), sds((joint, joint), BF16), sds((joint, vocab + 128), BF16)],
+        scratch_shapes=[pltpu.SemaphoreType.DMA((3,))],
+        compiler_params=pltpu.CompilerParams(vmem_limit_bytes=48 << 20),
+        name="joint_inputs",
+    )(x, pred_low, whole)
+
+
+def joint_outputs_kernel(genc_t, gpred_t, gtok, gdur, low_ref, pred_ref, w_enc, gx, pack, g_low, gp):
+    n = pack.shape[0]
+    joint = w_enc.shape[1]
+    low, tall = w_enc.shape[0] // n, joint // n
+    g_low[...] = genc_t[...].T.astype(jnp.bfloat16)
+    gx[...] = nt(g_low[...], w_enc[...])
+    g_enc = tn(low_ref[...], g_low[...]).astype(jnp.bfloat16)
+    real = lax.broadcasted_iota(jnp.int32, (8, joint), 0) < GROUP
+    for g in range(gpred_t.shape[0]):
+        gp[g * 8 : (g + 1) * 8, :] = jnp.where(real, gpred_t[g].T, 0.0)
+    g_pred = tn(pred_ref[...], gp[...].astype(jnp.bfloat16)).astype(jnp.bfloat16)
+    blocks = gtok.shape[1] // WIDE
+    rest = low + tall * (1 + blocks)
+    for s in range(n):
+        mine = slice(s * tall, (s + 1) * tall)
+        pack[s, 0:low, :] = g_enc[s * low : (s + 1) * low, :WIDE]
+        pack[s, low : low + tall, :] = g_pred[mine, :WIDE]
+        for b in range(blocks):
+            at = low + tall * (1 + b)
+            pack[s, at : at + tall, :] = gtok[mine, b * WIDE : (b + 1) * WIDE]
+        pack[s, rest : rest + low, 0:128] = g_enc[s * low : (s + 1) * low, WIDE:]
+        if tall > low:
+            pack[s, rest + low : rest + tall, 0:128] = jnp.zeros((tall - low, 128), jnp.bfloat16)
+        pack[s, rest : rest + tall, 128:256] = g_pred[mine, WIDE:]
+        pack[s, rest : rest + tall, 256:384] = gdur[mine, :]
+        pack[s, rest : rest + tall, 384:] = jnp.zeros((tall, WIDE - 384), jnp.bfloat16)
+        if pack.shape[1] > rest + tall:
+            pack[s, rest + tall :, :] = jnp.zeros((pack.shape[1] - rest - tall, WIDE), jnp.bfloat16)
+
+
+def joint_outputs(genc_t, gpred_t, gtok, gdur, low, pred_low, w_enc, n):
+    rows, width = low.shape
+    joint = w_enc.shape[1]
+    count = width // n + (joint // n) * (2 + gtok.shape[1] // WIDE)
+    return pl.pallas_call(
+        joint_outputs_kernel,
+        in_specs=[VMEM_SPEC] * 7,
+        out_specs=[VMEM_SPEC] * 2,
+        out_shape=[sds((rows, width)), sds((n, tiled(count), WIDE), BF16)],
+        scratch_shapes=[pltpu.VMEM((rows, joint), BF16), pltpu.VMEM((pred_low.shape[0], joint), F32)],
+        compiler_params=pltpu.CompilerParams(vmem_limit_bytes=48 << 20),
+        name="joint_outputs",
+    )(genc_t, gpred_t, gtok, gdur, low, pred_low, w_enc)
 
 
 def unpack_joint(whole, first, sizes, w_enc, w_pred, vocab):
@@ -1584,71 +1800,59 @@
     shard = width // n
     sizes = joint_sizes(enc_weight, pred_weight, token_weight)
     vocab = token_weight.shape[1]
-    packs = pack(
-        layers,
-        table,
-        end,
-        sum(sizes),
-        [mats[name] for name in PLACE]
-        + [norm_gains, depth_taps, batch_gain, batch_bias, enc_weight, pred_weight, token_weight, duration_weight],
-    )
-    wholes = []
-    smalls = []
-    for layer in range(layers):
-        whole = gather(packs[layer], 1 + layer)
-        small = whole[:, end : end + 16, :shard].astype(jnp.float32)
-        wholes.append(whole)
-        smalls.append(jnp.swapaxes(small, 0, 1).reshape(16, width))
+    arrays = [mats[name] for name in PLACE]
+    arrays += [norm_gains, depth_taps, batch_gain, batch_bias, enc_weight, pred_weight, token_weight, duration_weight]
     resid = frames_in.reshape(rows, width)
-    records = []
-    for layer in range(layers):
-        y1, h1, y2, qkv, ctx, gates, depthwise, stats = part_one(frame_lengths, resid, smalls[layer], wholes[layer], ff)
-        pooled = exchange(stats, "pool", 8 + layer)
-        y3, h2, y4, result = part_two(depthwise, y2, pooled, smalls[layer], wholes[layer], ff)
-        records.append((resid, y1, h1, y2, qkv, ctx, gates, depthwise, pooled, y3, h2, y4))
-        resid = result
-    w_enc, w_pred, w_tok, w_dur = unpack_joint(wholes[-1], end + 16, sizes, enc_weight, pred_weight, vocab)
-    joint = w_enc.shape[1]
-    vocab = w_tok.shape[1]
-    out_low = resid.astype(jnp.bfloat16)
-    enc = matmul(out_low, w_enc)
-    pred_low = pred_states.reshape(utts * slots, joint)
-    pred = matmul(pred_low, w_pred).reshape(utts, slots, joint)
+    whole, records, tables, joint_at = forward(frame_lengths, resid, arrays, layers, ff, sizes, 1)
+    held = [{name: spot[0] for name, spot in t.items()} for t in tables]
+    starts_of = [resid] + [record[10] for record in records]
+    resid = starts_of[-1]
+    joint = enc_weight.shape[1]
     groups = slots // GROUP
     durs = duration_weight.shape[1]
-    pred_t = jnp.pad(
-        jnp.swapaxes(pred.reshape(utts * groups, GROUP, joint), 1, 2),
-        ((0, 0), (0, 0), (0, 8 - GROUP)),
-    )
-    w_cat = jnp.concatenate([w_tok, w_dur], 1)
-    enc_t = enc.T
+    aligned = joint % (16 * n) == 0 and width % (16 * n) == 0
+    pred_low = pred_states.reshape(utts * groups, GROUP, joint)
+    pred_low = jnp.pad(pred_low, ((0, 0), (0, 8 - GROUP), (0, 0))).reshape(-1, joint)
+    if aligned:
+        out_low, enc_t, pred_t, w_cat_t, w_enc, _, w_cat = joint_inputs(resid, pred_low, whole, joint_at, joint, vocab)
+    else:
+        w_enc, w_pred, w_tok, w_dur = unpack_joint(whole, joint_at, sizes, enc_weight, pred_weight, vocab)
+        out_low = resid.astype(jnp.bfloat16)
+        enc_t = matmul(out_low, w_enc).T
+        pred_t = jnp.swapaxes(matmul(pred_low, w_pred).reshape(utts * groups, 8, joint), 1, 2)
+        w_cat = jnp.concatenate([w_tok, w_dur], 1)
+        w_cat_t = w_cat.T
     labels_ext = jnp.concatenate([label_ids, jnp.zeros((utts, 1), jnp.int32)], 1)
-    feats, expd = joint_forward(enc_t, pred_t, labels_ext, w_cat.T, vocab, durs, frames)
+    feats, expd = joint_forward(enc_t, pred_t, labels_ext, w_cat_t, vocab, durs, frames)
     lat_grads, scores = lattice(feats[: 2 + durs], frame_lengths, label_lengths, slots)
     log_prob = scores[:utts, 0]
     utt_loss = -log_prob / frame_lengths.astype(jnp.float32)
     grad_enc_t, grad_pred_t, grad_tok, grad_dur_w = joint_backward(
         enc_t, pred_t, labels_ext, w_cat, feats, lat_grads, expd, vocab, durs, frames
     )
-    grad_pred_rows = jnp.swapaxes(grad_pred_t[:, :, :GROUP], 1, 2)
-    grad_enc_low = grad_enc_t.T.astype(jnp.bfloat16)
-    grad_w_enc = contract_rows(out_low, grad_enc_low)
-    grad = contract_cols(grad_enc_low, w_enc)
-    grad_w_pred = contract_rows(
-        pred_low, grad_pred_rows.reshape(utts * slots, joint).astype(jnp.bfloat16)
-    )
+    if aligned:
+        grad, joint_grads = joint_outputs(grad_enc_t, grad_pred_t, grad_tok, grad_dur_w, out_low, pred_low, w_enc, n)
+    else:
+        grad_pred_rows = jnp.swapaxes(grad_pred_t[:, :, :GROUP], 1, 2)
+        grad_pred_rows = jnp.pad(grad_pred_rows, ((0, 0), (0, 8 - GROUP), (0, 0))).reshape(-1, joint)
+        grad_enc_low = grad_enc_t.T.astype(jnp.bfloat16)
+        grad = contract_cols(grad_enc_low, w_enc)
+        grad_w_enc = contract_rows(out_low, grad_enc_low)
+        grad_w_pred = contract_rows(pred_low, grad_pred_rows.astype(jnp.bfloat16))
+        joint_grads = pack_joint_grads(grad_w_enc, grad_w_pred, grad_tok, grad_dur_w, n)
+
     def whole_of(source):
         return (source, 0, source.shape[1] // TILE)
 
-    joint_grads = pack_joint_grads(grad_w_enc, grad_w_pred, grad_tok, grad_dur_w, n)
     waiting = [whole_of(joint_grads)]
     shares = []
     starts = [None] * layers + [0]
     at = joint_grads.shape[1]
     bn_grads = [None] * layers
     for layer in reversed(range(layers)):
-        x0, y1, h1, y2, qkv, ctx, gates, depthwise, pooled, y3, h2, y4 = records[layer]
-        args = (grad, y4, y3, depthwise, pooled, smalls[layer], wholes[layer], h2, ff)
+        x0 = starts_of[layer]
+        y1, h1, y2, qkv, ctx, gates, depthwise, y3, h2, y4, result, pooled, small = records[layer]
+        args = (grad, y4, y3, depthwise, pooled, small, whole, h2, ff, held[layer])
         if layer == layers - 1:
             outs = back_one(*args)
         else:
@@ -1662,7 +1866,7 @@
         sums = exchange(sums, "sum", 12 + layer)
         waiting.append(whole_of(grads_one))
         args = (frame_lengths, x0, y1, y2, gates, qkv, ctx, depthwise, db, g3, pooled, sums, late_gains)
-        (grad, grads_two), share = back_two(*args, smalls[layer], wholes[layer], h1, ff, waiting, 20 + layer)
+        (grad, grads_two), share = back_two(*args, small, whole, h1, ff, held[layer], waiting, 20 + layer)
         shares.append(share)
         waiting = [whole_of(grads_two)]
         starts[layer] = (at, at + grads_one.shape[1])

time: 707 us -> 608 us (0.86)
  Pallas kernels: 639 us -> 578 us
  local copies, waits for them, and re-layouts: 44.2 us -> 16.6 us
    pallas_call x7 -> x3, Pallas kernels: 210 us -> 177 us  [the longest x1 167 us: forward(): pl.pallas_call(partial(forward_kernel, utts, layers, n1, groups, tables,...]
    pallas_call x4 -> x2, Pallas kernels: 44.3 us -> 23.3 us  [exchange(): pl.pallas_call(partial(exchange_kernel, kind, groups, n), out_shape=jax.S...]
    unnamed x81 -> x44, local copies, waits for them, and re-layouts: 26.6 us -> 15.8 us
where the time goes in v5:
time: 608 us; the launch traced here: 597 us
  Pallas kernels  578 us (95%)
  local copies, waits for them, and re-layouts  16.6 us (3%)
    pallas_call x4, Pallas kernels, call(): pl.pallas_call(partial(riding_kernel, kernel, counts, scatter_plan(ride),...  227 us
    pallas_call x1, Pallas kernels, forward(): pl.pallas_call(partial(forward_kernel, utts, layers, n1, groups, tables,...  167 us
    pallas_call x1, Pallas kernels, joint_backward(): pl.pallas_call(partial(joint_bwd_kernel, groups, durs), grid=(utts * grou...  59.1 us
    pallas_call x1, Pallas kernels, lattice(): pl.pallas_call(partial(lattice_kernel, slots), out_shape=(jax.ShapeDtypeS...  35.1 us
    pallas_call x1, Pallas kernels, joint_forward(): pl.pallas_call(partial(joint_fwd_kernel, groups, durs), grid=(utts * grou...  34.8 us
    pallas_call x2, Pallas kernels, exchange(): pl.pallas_call(partial(exchange_kernel, kind, groups, n), out_shape=jax.S...  23.3 us
    pallas_call x1, Pallas kernels, call(): pl.pallas_call(partial(kernel, Beats()), in_specs=in_specs, out_specs=out...  19.2 us
    unnamed x44, local copies, waits for them, and re-layouts  15.8 us

profile of v5, /device:TPU:0, one launch (start us, length us, event | category | flops | bytes accessed | tf_op | source)
XLA Modules:
  0.0 597.5 jit_solution(10842258229883035397)
XLA Ops:
  0.7 0.0 copy-start.15
  0.7 0.7 concatenate.3.labels_ref
  1.4 0.0 copy-start.12
  1.4 1.3 copy.45.refs_8_
  2.6 1.3 copy.46.refs_9_
  3.9 1.4 copy.47.refs_15_
  5.3 166.6 %gather_and_forward.1 = (bf16[4,2,3360,512]{3,2,1,0:T(8,128)(2,1)}, f32[512,512]{1,0:T(8,128)}, f32[4,512,512]{2,1,0:T(8,128)}, f32[512,512]{1,0:T(8,128)}, bf16...) custom-call(s32[2]{0:T(128)} %refs_0_.5, ...), custom_call_target="tpu_custom_call" | custom-call | tf_op jit(solution)/shard_map/gather_and_forward/pallas_call | solution.py:1511
  171.9 0.0 copy-done.15
  172.0 0.0 copy-start.5
  172.0 1.2 copy-done.5
  173.2 5.5 joint_inputs.1
  178.7 0.0 copy-start
  178.7 0.0 copy-done.12
  178.8 0.0 copy-start.13
  178.8 0.0 copy-start.14
  178.8 34.8 %joint_forward.1 = (f32[8,64,256]{2,1,0:T(8,128)S(1)}, bf16[10,5,1024,256]{3,2,1,0:T(8,128)(2,1)}) custom-call(s32[2,25]{1,0:T(2,128)S(1)} %concatenate.3.labels_ref, f32[640,512]{1,0:T(8,128)S(1)} %get-tuple-element.94.enc_ref, f32[10,640,8]{2,1,0:T(8,128)} %get-tuple-element.95.pred_ref, bf16[1152,640]{1,0:T(8,128)(2,1)S(1)} %get-tuple-element.96.wt_ref), custom_call_target="tpu_custom_call" | custom-call | tf_op jit(solution)/shard_map/joint_forward/pallas_call | solution.py:217
  213.6 0.0 copy-start.2
  213.6 0.0 copy-done
  213.7 0.0 copy-done.13
  213.7 0.0 copy-done.14
  213.7 35.1 %lattice.1 = (f32[7,64,256]{2,1,0:T(8,128)S(1)}, f32[8,128]{1,0:T(8,128)S(1)}) custom-call(f32[7,64,256]{2,1,0:T(8,128)S(1)} %slice.18.feats_ref, s32[2]{0:T(128)S(1)} %copy-done.13, s32[2]{0:T(128)S(1)} %copy-done.14), custom_call_target="tpu_custom_call" | custom-call | tf_op jit(solution)/shard_map/lattice/pallas_call | solution.py:155
  248.8 0.0 copy-start.10
  248.8 0.8 copy-done.10
  249.5 0.1 negate_reduce_fusion
  249.7 0.5 convert_divide_fusion
  250.2 0.0 copy-done.2
  250.2 59.1 %joint_backward.1 = (f32[640,512]{1,0:T(8,128)}, f32[10,640,8]{2,1,0:T(8,128)}, bf16[640,1024]{1,0:T(8,128)(2,1)}, bf16[640,128]{1,0:T(8,128)(2,1)}) custom-call(s32[2,25]{1,0:T(2,128)} %copy-done.12, f32[640,512]{1,0:T(8,128)} %copy-done, f32[10,640,8]{2,1,0:T(8,128)} %get-tuple-element.95.pred_ref, bf16[640,1152]{1,0:T(8,128)(2,1)} %get-tuple-element.112.w_ref, ...), custom_call_target="tpu_custom_call" | custom-call | tf_op jit(solution)/shard_map/joint_backward/pallas_call | solution.py:290
  309.3 0.0 copy-start.3
  309.3 1.3 copy-done.3
  310.7 0.0 copy-start.4
  310.7 1.3 copy-done.4
  312.0 0.0 copy-start.11
  312.0 0.9 copy-done.11
  312.9 5.0 joint_outputs.1
  317.9 0.0 copy-start.6
  317.9 1.0 copy-done.6
  318.8 19.2 %back_part_one.1 = (f32[512,512]{1,0:T(8,128)}, f32[512,512]{1,0:T(8,128)}, bf16[8,576,512]{2,1,0:T(8,128)(2,1)}, f32[16,128]{1,0:T(8,128)}, f32[8,512]{1,0:T(8,128)}) custom-call(f32[512,512]{1,0:T(8,128)} %copy-done.6, f32[512,512]{1,0:T(8,128)} %get-tuple-element.122.y4_ref, f32[512,512]{1,0:T(8,128)} %get-tuple-element.123.y3_ref, ...), custom_call_target="tpu_custom_call" | custom-call | tf_op jit(solution)/shard_map/back_part_one/pallas_call | solution.py:536
  338.0 11.4 %exchange_sum.2.refs_11_ = f32[16,128]{1,0:T(8,128)} custom-call(f32[16,128]{1,0:T(8,128)} %get-tuple-element.129.x_ref), custom_call_target="tpu_custom_call" | custom-call | tf_op jit(solution)/shard_map/exchange_sum/pallas_call | solution.py:624
  349.5 63.5 %back_part_two_and_scatter.2 = (f32[512,512]{1,0:T(8,128)}, bf16[8,960,512]{2,1,0:T(8,128)(2,1)}, bf16[10,2,48,512]{3,2,1,0:T(8,128)(2,1)}) custom-call(s32[2]{0:T(128)} %refs_0_.5, f32[512,512]{1,0:T(8,128)} %get-tuple-element.105.refs_1_, f32[512,512]{1,0:T(8,128)} %get-tuple-element.106.refs_2_, f32[512,512]{1,0:T(8,128)} %get-tuple-element.107.refs_3_, ...), custom_call_target="tpu_custom_call" | custom-call | tf_op jit(solution)/shard_map/back_part_two_and_scatter/pallas_call | solution.py:548
  413.0 45.2 %back_part_one_and_scatter.1 = (f32[512,512]{1,0:T(8,128)}, f32[512,512]{1,0:T(8,128)}, bf16[8,576,512]{2,1,0:T(8,128)(2,1)}, f32[16,128]{1,0:T(8,128)}, f32[8,5...) custom-call(f32[512,512]{1,0:T(8,128)} %get-tuple-element.134.refs_0_, f32[512,512]{1,0:T(8,128)} %get-tuple-element.135.refs_1_, ...), custom_call_target="tpu_custom_call" | custom-call | tf_op jit(solution)/shard_map/back_part_one_and_scatter/pallas_call | solution.py:548
  458.3 11.9 %exchange_sum.3.refs_11_ = f32[16,128]{1,0:T(8,128)} custom-call(f32[16,128]{1,0:T(8,128)} %get-tuple-element.143.x_ref), custom_call_target="tpu_custom_call" | custom-call | tf_op jit(solution)/shard_map/exchange_sum/pallas_call | solution.py:624
  470.1 64.3 %back_part_two_and_scatter.3 = (f32[512,512]{1,0:T(8,128)}, bf16[8,960,512]{2,1,0:T(8,128)(2,1)}, bf16[10,2,48,512]{3,2,1,0:T(8,128)(2,1)}) custom-call(s32[2]{0:T(128)} %refs_0_.5, bf16[512,512]{1,0:T(8,128)(2,1)} %bitcast.34, f32[512,512]{1,0:T(8,128)} %get-tuple-element.99.refs_2_, f32[512,512]{1,0:T(8,128)} %get-tuple-element.100.refs_3_, ...), custom_call_target="tpu_custom_call" | custom-call | tf_op jit(solution)/shard_map/back_part_two_and_scatter/pallas_call | solution.py:548
  534.4 0.0 copy-start.7
  534.4 0.0 copy-start.8
  534.4 0.0 copy-start.9
  534.4 53.5 %idle_and_scatter.1 = bf16[10,2,48,512]{3,2,1,0:T(8,128)(2,1)} custom-call(bf16[4,2,960,512]{3,2,1,0:T(8,128)(2,1)} %bitcast.29), custom_call_target="tpu_custom_call" | custom-call | tf_op jit(solution)/shard_map/idle_and_scatter/pallas_call | solution.py:548
  587.9 0.0 copy-done.7
  587.9 0.0 copy-done.8
  587.9 0.0 copy-done.9
  588.0 0.0 copy-start.1
  588.0 1.2 copy-done.1
  589.2 0.0 copy-start.17
  589.2 0.0 copy-start.16
  589.2 3.1 unpack_grads.1
  592.2 0.6 copy.49
  592.8 0.6 copy.50
  593.4 0.0 copy-done.17
  593.4 0.0 copy-done.16
  593.4 0.7 fusion
  594.1 0.7 copy.51
  594.8 2.3 copy.53
  (6 shorter events, 0.1 us)
Async XLA Ops:
  0.7 171.2 %copy-start.15 = (bf16[2,25,640]{2,0,1:T(2,128)(2,1)S(1)}, bf16[2,25,640]{2,0,1:T(2,128)(2,1)}, u32[]{:S(2)}) copy-start(bf16[2,25,640]{2,0,1:T(2,128)(2,1)} %param.25) | copy-start | bytes 192004
  1.4 177.4 %copy-start.12 = (s32[2,25]{1,0:T(2,128)}, s32[2,25]{1,0:T(2,128)S(1)}, u32[]{:S(2)}) copy-start(s32[2,25]{1,0:T(2,128)S(1)} %concatenate.3.labels_ref) | copy-start | bytes 604
  172.0 1.2 copy-start.5
  178.7 34.9 %copy-start = (f32[640,512]{1,0:T(8,128)}, f32[640,512]{1,0:T(8,128)S(1)}, u32[]{:S(2)}) copy-start(f32[640,512]{1,0:T(8,128)S(1)} %get-tuple-element.94.enc_ref) | copy-start | bytes 3932164
  178.8 34.9 %copy-start.13 = (s32[2]{0:T(128)S(1)}, s32[2]{0:T(128)}, u32[]{:S(2)}) copy-start(s32[2]{0:T(128)} %refs_0_.5) | copy-start | bytes 28
  178.8 34.9 %copy-start.14 = (s32[2]{0:T(128)S(1)}, s32[2]{0:T(128)}, u32[]{:S(2)}) copy-start(s32[2]{0:T(128)} %ulen_ref.1) | copy-start | bytes 28
  213.6 36.6 %copy-start.2 = (f32[8,64,256]{2,1,0:T(8,128)}, f32[8,64,256]{2,1,0:T(8,128)S(1)}, u32[]{:S(2)}) copy-start(f32[8,64,256]{2,1,0:T(8,128)S(1)} %get-tuple-element.97.feats_ref) | copy-start | bytes 1572868
  248.8 0.8 copy-start.10
  309.3 1.3 copy-start.3
  310.7 1.3 copy-start.4
  312.0 0.9 copy-start.11
  317.9 1.0 copy-start.6
  534.4 53.5 %copy-start.7 = (bf16[10,2,48,512]{3,2,1,0:T(8,128)(2,1)S(1)}, bf16[10,2,48,512]{3,2,1,0:T(8,128)(2,1)}, u32[]{:S(2)}) copy-start(bf16[10,2,48,512]{3,2,1,0:T(8,128)(2,1)} %get-tuple-element.148) | copy-start | bytes 2949124
  534.4 53.5 %copy-start.8 = (bf16[10,2,48,512]{3,2,1,0:T(8,128)(2,1)S(1)}, bf16[10,2,48,512]{3,2,1,0:T(8,128)(2,1)}, u32[]{:S(2)}) copy-start(bf16[10,2,48,512]{3,2,1,0:T(8,128)(2,1)} %get-tuple-element.150) | copy-start | bytes 2949124
  534.4 53.5 %copy-start.9 = (bf16[6,2,48,512]{3,2,1,0:T(8,128)(2,1)S(1)}, bf16[6,2,48,512]{3,2,1,0:T(8,128)(2,1)}, u32[]{:S(2)}) copy-start(bf16[6,2,48,512]{3,2,1,0:T(8,128)(2,1)} %get-tuple-element.149) | copy-start | bytes 1769476
  588.0 1.2 copy-start.1
  589.2 4.3 copy-start.17
  589.2 4.3 copy-start.16

commit v6 on v5

--- a/solution.py
+++ b/solution.py
@@ -230,7 +230,7 @@
         name="joint_forward",
     )(labels,enc_t,pred_t,w_t)
 
-def joint_bwd_kernel(groups, durs, labels_ref, enc_ref, pred_ref, w_ref, feats_ref, grads_ref, p_ref, genc_ref, gpred_ref, gtok_ref, gdur_ref, h_ref, d_ref, acc_ref):
+def joint_bwd_kernel(groups, durs, labels_ref, enc_ref, pred_ref, w_ref, feats_ref, grads_ref, p_ref, genc_ref, gpred_ref, gtok_ref, gdur_ref, h_ref, d_ref, acc_ref, th_ref):
     step=pl.program_id(0)
     vocab=p_ref.shape[2]
     frames=p_ref.shape[3]
@@ -249,6 +249,7 @@
         cols=slice(j*frames,(j+1)*frames)
         th=jnp.tanh(enc_ref[...]+pred_ref[0,:,j:j+1])
         h_ref[:,cols]=th.astype(jnp.bfloat16)
+        th_ref[...]=th
         gb=grads_ref[0,pl.ds(row,1),:]
         gl=grads_ref[1,pl.ds(row,1),:]
         scale=-(gb+gl)*feats_ref[2+durs,pl.ds(row,1),:]
@@ -271,12 +272,11 @@
         d_ref[vocab:vocab+16,cols]=dd.astype(jnp.bfloat16)
         d_ref[vocab+16:,cols]=jnp.zeros((d_ref.shape[0]-vocab-16,frames),jnp.bfloat16)
         dh=nn(w_ref[...],d_ref[:,cols])
-        th=jnp.tanh(enc_ref[...]+pred_ref[0,:,j:j+1])
+        th=th_ref[...]
         dp=dh*(1.0-th*th)
         genc_ref[...]+=dp
         gpred_ref[0,:,j:j+1]=jnp.sum(dp,1,keepdims=True)
-    for c in range(0,d_ref.shape[0],384):
-        acc_ref[:,c:c+384]+=nt(h_ref[...],d_ref[c:c+384,:])
+    acc_ref[...]+=nt(h_ref[...],d_ref[...])
     @pl.when(step==pl.num_programs(0)-1)
     def _():
         gtok_ref[...]=acc_ref[:,:vocab].astype(jnp.bfloat16)
@@ -305,7 +305,7 @@
             jax.ShapeDtypeStruct((joint,128),jnp.bfloat16)],
         scratch_shapes=[pltpu.VMEM((joint,GROUP*frames),jnp.bfloat16),
             pltpu.VMEM((vocab+128,GROUP*frames),jnp.bfloat16),
-            pltpu.VMEM((joint,vocab+128),jnp.float32)],
+            pltpu.VMEM((joint,vocab+128),jnp.float32),pltpu.VMEM((joint,frames),jnp.float32)],
         compiler_params=pltpu.CompilerParams(vmem_limit_bytes=56<<20),
         name="joint_backward",
     )(labels,enc_t,pred_t,w,feats,grads,p)
@@ -385,7 +385,6 @@
 class ScatterEngine:
     def __init__(self, n1, plan, lag, srcs, out, own, gc, gx, gy, gz, gf, fin, lo, sc, rc, sx, rx, sy, ry, sz, rz, sf, rf, se, re, wo):
         dp, fs, a, c, i1, i2 = place()
-        greet(n1, dp, fs, a, c, i1, i2)
         ypeer = (dp, i1 * 2 + 1 - i2)
         xpeer = ((1 - a) * 2 + c, fs)
         cpeer = (a * 2 + 1 - c, fs)
@@ -397,31 +396,32 @@
             return rows(aa * (QA + QB), QA)
 
         def cwait(t):
-            return remote(own.at[t], gc.at[t], sc.at[t], rc.at[t], cpeer)
+            return remote(own.at[t], gc.at[t], sc.at[0], rc.at[t], cpeer)
 
         def xcopy(t):
-            return remote(own.at[t, :, :, quarter(1 - a), :], gx.at[t], sx.at[t], rx.at[t], xpeer)
+            return remote(own.at[t, :, :, quarter(1 - a), :], gx.at[t], sx.at[0], rx.at[t], xpeer)
 
         def ycopy(t):
-            return remote(own.at[t, :, 1 - i2, main, :], gy.at[t], sy.at[t], ry.at[t], ypeer)
+            return remote(own.at[t, :, 1 - i2, main, :], gy.at[t], sy.at[0], ry.at[t], ypeer)
 
         def zcopy(t, j):
-            return remote(own.at[t, j, i2, main, :], gz.at[t, i1], sz.at[t, j], rz.at[t, i1], (dp, j * 2 + i2))
-
-        def zin(t, j):
-            return remote(own.at[t, i1, i2, main, :], gz.at[t, j], sz.at[t, j], rz.at[t, j], ypeer)
+            return remote(own.at[t, j, i2, main, :], gz.at[t, i1], sz.at[0], rz.at[t], (dp, j * 2 + i2))
+
+        def zin(t):
+            arrived = gz.at[t, pl.ds(0, n1 - 1)]
+            return remote(arrived, arrived, sz.at[0], rz.at[t], ypeer)
 
         def fcopy(t):
-            return remote(own.at[t, i1, i2, main, :], gf.at[t], sf.at[t], rf.at[t], xpeer)
+            return remote(own.at[t, i1, i2, main, :], gf.at[t], sf.at[0], rf.at[t], xpeer)
 
         def ecopy(t):
-            return remote(fin.at[t, c], fin.at[t, c], se.at[t], re.at[t], cpeer)
+            return remote(fin.at[t, c], fin.at[t, c], se.at[0], re.at[t], cpeer)
 
         def ein(t):
-            return remote(fin.at[t, 1 - c], fin.at[t, 1 - c], se.at[t], re.at[t], cpeer)
+            return remote(fin.at[t, 1 - c], fin.at[t, 1 - c], se.at[0], re.at[t], cpeer)
 
         def store(t):
-            return pltpu.make_async_copy(fin.at[t], out.at[t], wo.at[t])
+            return pltpu.make_async_copy(fin.at[t], out.at[t], wo.at[0])
 
         def stage_c(t):
             first = 0
@@ -431,7 +431,7 @@
                 def _(src=src, skip=base - first):
                     at = (t + skip) * TILE
                     pltpu.make_async_copy(src.at[:, :, rows(at + c * HALF, HALF), :], own.at[t], lo.at[t]).start()
-                    remote(src.at[:, :, rows(at + (1 - c) * HALF, HALF), :], gc.at[t], sc.at[t], rc.at[t], cpeer).start()
+                    remote(src.at[:, :, rows(at + (1 - c) * HALF, HALF), :], gc.at[t], sc.at[0], rc.at[t], cpeer).start()
 
                 first += count
 
@@ -454,9 +454,9 @@
 
         def stage_f(t):
             total = own[t, i1, i2, main, :].astype(jnp.float32)
+            zin(t).wait_recv()
             for d in range(1, n1):
                 j = lax.rem(i1 + n1 - d, n1)
-                zin(t, j).wait_recv()
                 total = total + gz[t, j].astype(jnp.float32)
             own[t, i1, i2, main, :] = total.astype(jnp.bfloat16)
             fcopy(t).start()
@@ -470,7 +470,6 @@
 
         def stage_o(t):
             ein(t).wait_recv()
-            ecopy(t).wait_send()
             store(t).start()
 
         stages = (stage_c, stage_x, stage_y, stage_z, stage_f, stage_e, stage_o)
@@ -484,17 +483,11 @@
                     stage(t)
 
         def finish():
-            def tile(t, carry):
-                cwait(t).wait_send()
-                xcopy(t).wait_send()
-                ycopy(t).wait_send()
-                for d in range(1, n1):
-                    zcopy(t, lax.rem(i1 + d, n1)).wait_send()
-                fcopy(t).wait_send()
-                store(t).wait()
-                return carry
-
-            lax.fori_loop(0, tiles, tile, 0)
+            for sent, sem in (
+                (own, sc), (gx, sx), (gy, sy), (gz.at[:, pl.ds(0, n1 - 1)], sz), (gf, sf), (fin.at[:, 0], se),
+            ):
+                remote(sent, sent, sem.at[0], rc.at[0], cpeer).wait_send()
+            pltpu.make_async_copy(fin, fin, wo.at[0]).wait()
 
         self.tick = tick
         self.total = tiles + (len(stages) - 1) * lag
@@ -509,14 +502,15 @@
     n1 = n // 2
     dma = pltpu.SemaphoreType.DMA
     v = lambda *shape: pltpu.VMEM((tiles,) + shape + (WIDE,), jnp.bfloat16)
-    one = dma((tiles,))
+    one = dma((1,))
+    each = dma((tiles,))
     return [
         v(n1, 2, HALF), v(n1, 2, HALF), v(n1, 2, QA), v(n1, QA + QB), v(n1, QA + QB), v(QA + QB), v(2, HALF),
-        one, one, one, one, one, one, one, dma((tiles, n1)), dma((tiles, n1)), one, one, one, one, one,
+        each, one, each, one, each, one, each, one, each, one, each, one, each, one,
     ]
 
 
-def riding_kernel(kernel, counts, plan, lag, n1, sites, *refs):
+def riding_kernel(kernel, counts, plan, lag, n1, sites, groups, *refs):
     n_in, n_out, n_scratch = counts
     k = len(plan)
     ins, refs = refs[:n_in], refs[n_in:]
@@ -524,6 +518,10 @@
     outs, refs = refs[:n_out], refs[n_out:]
     share, refs = refs[0], refs[1:]
     scratch, refs = refs[:n_scratch], refs[n_scratch:]
+    if groups:
+        meet(groups, 2 * n1)()
+    else:
+        greet(n1, *place())
     engine = ScatterEngine(n1, plan, lag, srcs, share, *refs)
     beats = Beats(engine.tick, engine.total, sites)
     kernel(beats, *ins, *outs, *scratch)
@@ -531,7 +529,7 @@
     engine.finish()
 
 
-def call(kernel, args, in_specs, out_specs, out_shape, scratch, name, ride=None, collective_id=None, sites=None, lag=2):
+def call(kernel, args, in_specs, out_specs, out_shape, scratch, name, ride=None, collective_id=None, sites=None, groups=0, lag=2):
     if not ride:
         return pl.pallas_call(
             partial(kernel, Beats()),
@@ -546,7 +544,7 @@
     tiles = sum(count for _, _, count in ride)
     counts = (len(args), len(out_shape), len(scratch))
     *outs, share = pl.pallas_call(
-        partial(riding_kernel, kernel, counts, scatter_plan(ride), lag, n // 2, sites),
+        partial(riding_kernel, kernel, counts, scatter_plan(ride), lag, n // 2, sites, groups),
         in_specs=in_specs + [ANY_SPEC] * len(ride),
         out_specs=out_specs + [ANY_SPEC],
         out_shape=out_shape + [sds((tiles, 2, HALF, WIDE), BF16)],
@@ -574,66 +572,6 @@
         gap = x[0:4] - mean
         dev = dev + (x[4:8] + gap * gap * n)
     return mean, dev, count
-
-
-def exchange_kernel(kind, groups, n, x_ref, out_ref, near, far, s1, r1, s2, r2):
-    dp = lax.axis_index("dp")
-    fs = lax.axis_index("fsdp")
-    barrier = pltpu.get_barrier_semaphore()
-    for d in range(1, groups):
-        pl.semaphore_signal(barrier, inc=1, device_id=(lax.rem(dp + d, groups), fs), device_id_type=MESH)
-    for d in range(1, n):
-        pl.semaphore_signal(barrier, inc=1, device_id=(dp, lax.rem(fs + d, n)), device_id_type=MESH)
-    pl.semaphore_wait(barrier, groups + n - 2)
-
-    def merge(ref, members):
-        if kind == "sum":
-            total = ref[0]
-            for i in range(1, members):
-                total = total + ref[i]
-            return total
-        mean, dev, count = pooled([ref[i] for i in range(members)])
-        return jnp.concatenate([mean, dev, jnp.broadcast_to(count, (8, 128))], 0)
-
-    near[dp] = x_ref[...]
-    first = []
-    for d in range(1, groups):
-        cp = remote(near.at[dp], near.at[dp], s1.at[d], r1.at[dp], (lax.rem(dp + d, groups), fs))
-        cp.start()
-        first.append(cp)
-    for d in range(1, groups):
-        other = lax.rem(dp + d, groups)
-        remote(near.at[dp], near.at[other], s1.at[d], r1.at[other], (other, fs)).wait_recv()
-    far[fs] = merge(near, groups)
-    for d in range(1, n):
-        cp = remote(far.at[fs], far.at[fs], s2.at[d], r2.at[fs], (dp, lax.rem(fs + d, n)))
-        cp.start()
-        first.append(cp)
-    for d in range(1, n):
-        other = lax.rem(fs + d, n)
-        remote(far.at[fs], far.at[other], s2.at[d], r2.at[other], (dp, other)).wait_recv()
-    out_ref[...] = merge(far, n)
-    for cp in first:
-        cp.wait_send()
-
-
-def exchange(x, kind, collective_id):
-    n = lax.axis_size("fsdp")
-    groups = lax.axis_size("dp")
-    dma = pltpu.SemaphoreType.DMA
-    return pl.pallas_call(
-        partial(exchange_kernel, kind, groups, n),
-        out_shape=jax.ShapeDtypeStruct(x.shape, x.dtype),
-        in_specs=[pl.BlockSpec(memory_space=pltpu.VMEM)],
-        out_specs=pl.BlockSpec(memory_space=pltpu.VMEM),
-        scratch_shapes=[
-            pltpu.VMEM((groups,) + x.shape, x.dtype),
-            pltpu.VMEM((n,) + x.shape, x.dtype),
-            dma((groups,)), dma((groups,)), dma((n,)), dma((n,)),
-        ],
-        compiler_params=pltpu.CompilerParams(collective_id=collective_id, has_side_effects=True),
-        name="exchange_" + kind,
-    )(x)
 
 
 CHUNK_ROWS = 64
@@ -890,9 +828,9 @@
     mover.finish()
 
 
-def back_two_kernel(utts, table, held, start, end, beats, t_ref, x_ref, y1_ref, y2_ref, r_ref, t_in, c_ref, d_ref, db_ref, g_in, pooled_ref, sums_ref, late_ref, small, whole, h_hbm,
-                    g_out, grads,
-                    w_pin, w_proj, w_joint, w_fin, w_fout, g, gb, normed, dact, act, dh, dn, dw_pin, dw_proj, dw_joint, dw_in, dw_out, h, gp, dd, dr, dt, sm, sems):
+def back_two_kernel(utts, table, held, start, end, beats, t_ref, x_ref, y1_ref, y2_ref, r_ref, t_in, c_ref, d_ref, db_ref, g_in, pooled_ref, local_ref, late_ref, small, whole, h_hbm,
+                    g_out, grads, sums_ref,
+                    w_pin, w_proj, w_joint, w_fin, w_fout, g, gb, normed, dact, act, dh, dn, dw_pin, dw_proj, dw_joint, dw_in, dw_out, h, gp, dd, dr, dt, sm, sems, *meeting):
     rows, width = g.shape
     frames = rows // utts
     mover = Mover(sems)
@@ -906,18 +844,23 @@
     mean = read_rows(pooled_ref, 0, width)
     count = pooled_ref[8:9, 0:1]
     istd = lax.rsqrt(read_rows(pooled_ref, 4, width) / count + EPS)
-    bias_sum = read_rows(sums_ref, 0, width)
-    gain_sum = read_rows(sums_ref, 4, width)
     taps = gains[5:14]
     ntaps = taps.shape[0]
     span = frames + 16
     per = frames // CHUNK_ROWS
     beats.run(5)
+    exchange = Exchange("sum", meeting[0].shape[0], meeting[1].shape[0], *meeting)
+    exchange.begin(local_ref[...])
     fill_gated(utts, frames, t_ref, r_ref, gp)
+    exchange.middle()
     beats.run(1)
     for u in range(utts):
         dd[u * span : u * span + 8, :] = jnp.zeros((8, width), jnp.float32)
         dd[u * span + 8 + frames : (u + 1) * span, :] = jnp.zeros((8, width), jnp.float32)
+
+    sums_ref[...] = exchange.end()
+    bias_sum = read_rows(sums_ref, 0, width)
+    gain_sum = read_rows(sums_ref, 4, width)
 
     def bn(rr, i, c):
         z = (d_ref[rr, :] - mean) * istd
@@ -1070,23 +1013,27 @@
     start = table["p_in"]
     nb = ff // WIDE
     v = pltpu.VMEM
+    dma = pltpu.SemaphoreType.DMA
+    groups = lax.axis_size("dp")
     pad_rows = utts * (rows // utts + 16)
     return call(
         partial(back_two_kernel, utts, table, held, start, end),
         (t_len, x, y1, y2, r, t, c, d, db, g, pooled, sums, late, small, whole, h),
         [SMEM_SPEC] + [VMEM_SPEC] * 13 + [ANY_SPEC] * 2,
-        [ANY_SPEC] * 2,
-        [sds((rows, width)), sds((n, tiled(end - start + 16), WIDE), BF16)],
+        [ANY_SPEC] * 2 + [VMEM_SPEC],
+        [sds((rows, width)), sds((n, tiled(end - start + 16), WIDE), BF16), sds((16, 128))],
         [v((width, 2 * width), BF16), v((width, width), BF16), v((width, 3 * width), BF16), v((width, ff), BF16),
          v((ff, width), BF16), v((rows, width), F32), v((rows, width), BF16), v((rows, width), BF16),
          v((rows, width), F32), v((rows, width), BF16), v((rows, ff), BF16), v((rows, width), F32),
          v((width, 2 * width), BF16), v((width, width), BF16), v((width, 3 * width), BF16), v((width, ff), BF16),
          v((ff, width), BF16), v((nb, rows, WIDE), F32), v((pad_rows, width), F32), v((pad_rows, width), F32),
-         v((rows, 2 * width), BF16), v((rows, 3 * width), BF16), v((n, 16, WIDE), BF16), pltpu.SemaphoreType.DMA((20,))],
+         v((rows, 2 * width), BF16), v((rows, 3 * width), BF16), v((n, 16, WIDE), BF16), pltpu.SemaphoreType.DMA((20,)),
+         v((groups, 16, 128), F32), v((n, 16, 128), F32), dma((groups,)), dma((groups,)), dma((n,)), dma((n,))],
         "back_part_two",
         ride,
         collective_id,
         44,
+        groups,
     )
 
 
@@ -1131,28 +1078,29 @@
             return pltpu.make_async_copy(packed.at[main(t), :], out.at[i1, i2, main(t), :], so.at[t])
 
         def zcopy(t, j):
-            return remote(packed.at[main(t), :], out.at[i1, i2, main(t), :], sz.at[t, j], rz.at[t, i1], (dp, j * 2 + i2))
-
-        def zin(t, j):
-            return remote(packed.at[main(t), :], out.at[j, i2, main(t), :], sz.at[t, j], rz.at[t, j], ypeer)
+            return remote(packed.at[main(t), :], out.at[i1, i2, main(t), :], sz.at[0], rz.at[t], (dp, j * 2 + i2))
+
+        def zin(t):
+            arrived = out.at[pl.ds(0, n1 - 1), i2, main(t), :]
+            return remote(arrived, arrived, sz.at[0], rz.at[t], ypeer)
 
         def ycopy(t):
-            return remote(out.at[:, i2, main(t), :], out.at[:, i2, main(t), :], sy.at[t], ry.at[t], ypeer)
+            return remote(out.at[:, i2, main(t), :], out.at[:, i2, main(t), :], sy.at[0], ry.at[t], ypeer)
 
         def yin(t):
-            return remote(out.at[:, i2, main(t), :], out.at[:, 1 - i2, main(t), :], sy.at[t], ry.at[t], ypeer)
+            return remote(out.at[:, i2, main(t), :], out.at[:, 1 - i2, main(t), :], sy.at[0], ry.at[t], ypeer)
 
         def xcopy(t):
-            return remote(out.at[:, :, quarter(t, a), :], out.at[:, :, quarter(t, a), :], sx.at[t], rx.at[t], xpeer)
+            return remote(out.at[:, :, quarter(t, a), :], out.at[:, :, quarter(t, a), :], sx.at[0], rx.at[t], xpeer)
 
         def xin(t):
-            return remote(out.at[:, :, quarter(t, a), :], out.at[:, :, quarter(t, 1 - a), :], sx.at[t], rx.at[t], xpeer)
+            return remote(out.at[:, :, quarter(t, a), :], out.at[:, :, quarter(t, 1 - a), :], sx.at[0], rx.at[t], xpeer)
 
         def ccopy(t):
-            return remote(out.at[:, :, half(t, c), :], out.at[:, :, half(t, c), :], sc.at[t], rc.at[t], cpeer)
+            return remote(out.at[:, :, half(t, c), :], out.at[:, :, half(t, c), :], sc.at[0], rc.at[t], cpeer)
 
         def cin(t):
-            return remote(out.at[:, :, half(t, c), :], out.at[:, :, half(t, 1 - c), :], sc.at[t], rc.at[t], cpeer)
+            return remote(out.at[:, :, half(t, c), :], out.at[:, :, half(t, 1 - c), :], sc.at[0], rc.at[t], cpeer)
 
         def stage_z(t):
             for d in range(1, n1):
@@ -1161,8 +1109,7 @@
 
         def stage_y(t):
             local(t).wait()
-            for d in range(1, n1):
-                zin(t, lax.rem(i1 + n1 - d, n1)).wait_recv()
+            zin(t).wait_recv()
             ycopy(t).start()
 
         def stage_x(t):
@@ -1187,15 +1134,15 @@
                     stage(t)
 
         def finish():
-            def tile(t, carry):
-                for d in range(1, n1):
-                    zcopy(t, lax.rem(i1 + d, n1)).wait_send()
-                ycopy(t).wait_send()
-                xcopy(t).wait_send()
-                ccopy(t).wait_send()
-                return carry
-
-            lax.fori_loop(0, tiles, tile, 0)
+            every = pl.ds(0, n1)
+            for peer, sem, far, near, height in (
+                (ypeer, sz, pl.ds(0, n1 - 1), 0, QA + QB),
+                (ypeer, sy, every, 0, QA + QB),
+                (xpeer, sx, every, pl.ds(0, 2), QA),
+                (cpeer, sc, every, pl.ds(0, 2), HALF),
+            ):
+                sent = out.at[far, near, pl.ds(0, tiles * height), :]
+                remote(sent, sent, sem.at[0], rc.at[0], peer).wait_send()
 
         self.tick = tick
         self.total = tiles + (len(stages) - 1) * lag
@@ -1204,27 +1151,38 @@
 
 
 class Exchange:
-    def __init__(self, groups, n, near, far, s1, r1, s2, r2):
+    def __init__(self, kind, groups, n, near, far, s1, r1, s2, r2):
+        self.kind = kind
         self.groups, self.n = groups, n
         self.near, self.far = near, far
         self.sems = (s1, r1, s2, r2)
+        self.sent = []
 
     def merge(self, ref, members):
+        if self.kind == "sum":
+            total = ref[0]
+            for i in range(1, members):
+                total = total + ref[i]
+            return total
         mean, dev, count = pooled([ref[i] for i in range(members)])
         return jnp.concatenate([mean, dev, jnp.broadcast_to(count, (8, 128))], 0)
 
-    def run(self, x, beats):
+    def begin(self, x):
+        dp = lax.axis_index("dp")
+        fs = lax.axis_index("fsdp")
+        near, groups = self.near, self.groups
+        s1, r1, s2, r2 = self.sems
+        near[dp] = x
+        for d in range(1, groups):
+            cp = remote(near.at[dp], near.at[dp], s1.at[d], r1.at[dp], (lax.rem(dp + d, groups), fs))
+            cp.start()
+            self.sent.append(cp)
+
+    def middle(self):
         dp = lax.axis_index("dp")
         fs = lax.axis_index("fsdp")
         near, far, groups, n = self.near, self.far, self.groups, self.n
         s1, r1, s2, r2 = self.sems
-        near[dp] = x
-        sent = []
-        for d in range(1, groups):
-            cp = remote(near.at[dp], near.at[dp], s1.at[d], r1.at[dp], (lax.rem(dp + d, groups), fs))
-            cp.start()
-            sent.append(cp)
-        beats.run(1)
         for d in range(1, groups):
             other = lax.rem(dp + d, groups)
             remote(near.at[dp], near.at[other], s1.at[d], r1.at[other], (other, fs)).wait_recv()
@@ -1232,12 +1190,17 @@
         for d in range(1, n):
             cp = remote(far.at[fs], far.at[fs], s2.at[d], r2.at[fs], (dp, lax.rem(fs + d, n)))
             cp.start()
-            sent.append(cp)
-        beats.run(1)
+            self.sent.append(cp)
+
+    def end(self):
+        dp = lax.axis_index("dp")
+        fs = lax.axis_index("fsdp")
+        far, n = self.far, self.n
+        s1, r1, s2, r2 = self.sems
         for d in range(1, n):
             other = lax.rem(fs + d, n)
             remote(far.at[fs], far.at[other], s2.at[d], r2.at[other], (dp, other)).wait_recv()
-        for cp in sent:
+        for cp in self.sent:
             cp.wait_send()
         return self.merge(far, n)
 
@@ -1465,12 +1428,15 @@
         first, second, pooled_out, _ = layer_outs[layer]
         source = frames_ref if layer == 0 else x
         stats = part_one(utts, beats, mover, t_ref, source, gains, weights, first, (y1, y2, normed, h, act, tq, ctx, r, gp, d))
-        exchange = Exchange(groups, n, *refs[:6])
+        exchange = Exchange("pool", groups, n, *refs[:6])
+        exchange.begin(stats)
         refs = refs[6:]
         for name in ("p_out", "s_in", "s_out"):
             weights.fetch(name)
-        pooled_out[...] = exchange.run(stats, beats)
+        exchange.middle()
+        beats.run(1)
         mover.finish()
+        pooled_out[...] = exchange.end()
         part_two(beats, mover, pooled_out, gains, weights, second, (d, y2, y3, normed, h, act, y4, x))
         mover.finish()
         used = mover.used
@@ -1519,7 +1485,7 @@
             v((total, WIDE), BF16), v((n1, 2, 16, WIDE), BF16), v((rows, width), F32), v((rows, width), F32), v((rows, width), BF16),
             v((nb, rows, WIDE), F32), v((rows, ff), BF16), v((rows, 3 * width), BF16), v((rows, width), BF16), v((rows, 2 * width), F32),
             v((pad_rows, width), F32), v((rows, width), F32), v((rows, width), F32), v((rows, width), F32), v((rows, width), F32), dma((80,)),
-            dma((tiles,)), dma((tiles, n1)), dma((tiles, n1)), dma((tiles,)), dma((tiles,)), dma((tiles,)), dma((tiles,)), dma((tiles,)), dma((tiles,)),
+            dma((tiles,)), dma((1,)), dma((tiles,)), dma((1,)), dma((tiles,)), dma((1,)), dma((tiles,)), dma((1,)), dma((tiles,)),
         ]
         + [v((groups, 16, 128), F32), v((n, 16, 128), F32), dma((groups,)), dma((groups,)), dma((n,)), dma((n,))] * layers,
         compiler_params=pltpu.CompilerParams(collective_id=collective_id, has_side_effects=True, vmem_limit_bytes=61 << 20),
@@ -1853,22 +1819,15 @@
         x0 = starts_of[layer]
         y1, h1, y2, qkv, ctx, gates, depthwise, y3, h2, y4, result, pooled, small = records[layer]
         args = (grad, y4, y3, depthwise, pooled, small, whole, h2, ff, held[layer])
+        g3, db, grads_one, sums, late_gains = back_one(*args)
         if layer == layers - 1:
-            outs = back_one(*args)
+            ride, later = waiting + [whole_of(grads_one)], []
         else:
-            source, first, count = waiting.pop()
-            early = min(count, -(-count * 3 // 5))
-            outs, share = back_one(*args, [(source, first, early)], 16 + layer)
-            shares.append(share)
-            if early < count:
-                waiting.append((source, first + early, count - early))
-        g3, db, grads_one, sums, late_gains = outs
-        sums = exchange(sums, "sum", 12 + layer)
-        waiting.append(whole_of(grads_one))
+            ride, later = waiting, [whole_of(grads_one)]
         args = (frame_lengths, x0, y1, y2, gates, qkv, ctx, depthwise, db, g3, pooled, sums, late_gains)
-        (grad, grads_two), share = back_two(*args, small, whole, h1, ff, held[layer], waiting, 20 + layer)
+        (grad, grads_two, sums), share = back_two(*args, small, whole, h1, ff, held[layer], ride, 20 + layer)
         shares.append(share)
-        waiting = [whole_of(grads_two)]
+        waiting = later + [whole_of(grads_two)]
         starts[layer] = (at, at + grads_one.shape[1])
         at += grads_one.shape[1] + grads_two.shape[1]
         bn_grads[layer] = (sums[4:8].reshape(width), sums[0:4].reshape(width))

time: 608 us -> 571 us (0.939)
  Pallas kernels: 578 us -> 543 us
    pallas_call x2 -> x0, Pallas kernels: 23.3 us -> none  [exchange(): pl.pallas_call(partial(exchange_kernel, kind, groups, n), out_shape=jax.S...]
    pallas_call x4 -> x3, Pallas kernels: 227 us -> 207 us  [call(): pl.pallas_call(partial(riding_kernel, kernel, counts, scatter_plan(ride),...]
    pallas_call x1 -> x2, Pallas kernels: 19.2 us -> 38.2 us  [call(): pl.pallas_call(partial(kernel, Beats()), in_specs=in_specs, out_specs=out...]
    pallas_call x1, Pallas kernels: 167 us -> 160 us  [forward(): pl.pallas_call(partial(forward_kernel, utts, layers, n1, groups, tables,...]
where the time goes in v6:
time: 571 us; the launch traced here: 561 us
  Pallas kernels  543 us (95%)
  local copies, waits for them, and re-layouts  15.5 us (3%)
    pallas_call x3, Pallas kernels, call(): pl.pallas_call(partial(riding_kernel, kernel, counts, scatter_plan(ride),...  207 us
    pallas_call x1, Pallas kernels, forward(): pl.pallas_call(partial(forward_kernel, utts, layers, n1, groups, tables,...  160 us
    pallas_call x1, Pallas kernels, joint_backward(): pl.pallas_call(partial(joint_bwd_kernel, groups, durs), grid=(utts * grou...  54.4 us
    pallas_call x2, Pallas kernels, call(): pl.pallas_call(partial(kernel, Beats()), in_specs=in_specs, out_specs=out...  38.2 us
    pallas_call x1, Pallas kernels, lattice(): pl.pallas_call(partial(lattice_kernel, slots), out_shape=(jax.ShapeDtypeS...  35.1 us
    pallas_call x1, Pallas kernels, joint_forward(): pl.pallas_call(partial(joint_fwd_kernel, groups, durs), grid=(utts * grou...  33.9 us
    unnamed x44, local copies, waits for them, and re-layouts  14.7 us

profile of v6, /device:TPU:0, one launch (start us, length us, event | category | flops | bytes accessed | tf_op | source)
XLA Modules:
  0.0 560.8 jit_solution(5729312134596514444)
XLA Ops:
  0.7 0.0 copy-start.15
  0.7 0.7 concatenate.3.labels_ref
  1.4 0.0 copy-start.11
  1.4 1.3 copy.45.refs_8_
  2.6 1.3 copy.46.refs_9_
  3.9 1.4 copy.47.refs_15_
  5.3 160.0 %gather_and_forward.1 = (bf16[4,2,3360,512]{3,2,1,0:T(8,128)(2,1)}, f32[512,512]{1,0:T(8,128)}, f32[4,512,512]{2,1,0:T(8,128)}, f32[512,512]{1,0:T(8,128)}, bf16...) custom-call(s32[2]{0:T(128)} %refs_0_.5, ...), custom_call_target="tpu_custom_call" | custom-call | tf_op jit(solution)/shard_map/gather_and_forward/pallas_call | solution.py:1477
  165.3 0.0 copy-done.15
  165.4 0.0 copy-start.5
  165.4 1.2 copy-done.5
  166.6 5.5 joint_inputs.1
  172.1 0.0 copy-start.1
  172.1 0.0 copy-done.11
  172.2 0.0 copy-start.12
  172.2 0.0 copy-start.13
  172.2 33.9 %joint_forward.1 = (f32[8,64,256]{2,1,0:T(8,128)S(1)}, bf16[10,5,1024,256]{3,2,1,0:T(8,128)(2,1)}) custom-call(s32[2,25]{1,0:T(2,128)S(1)} %concatenate.3.labels_ref, f32[640,512]{1,0:T(8,128)S(1)} %get-tuple-element.95.enc_ref, f32[10,640,8]{2,1,0:T(8,128)} %get-tuple-element.96.pred_ref, bf16[1152,640]{1,0:T(8,128)(2,1)S(1)} %get-tuple-element.97.wt_ref), custom_call_target="tpu_custom_call" | custom-call | tf_op jit(solution)/shard_map/joint_forward/pallas_call | solution.py:217
  206.1 0.0 copy-start.2
  206.2 0.0 copy-done.1
  206.2 0.0 copy-done.12
  206.2 0.0 copy-done.13
  206.2 35.1 %lattice.1 = (f32[7,64,256]{2,1,0:T(8,128)S(1)}, f32[8,128]{1,0:T(8,128)S(1)}) custom-call(f32[7,64,256]{2,1,0:T(8,128)S(1)} %slice.18.feats_ref, s32[2]{0:T(128)S(1)} %copy-done.12, s32[2]{0:T(128)S(1)} %copy-done.13), custom_call_target="tpu_custom_call" | custom-call | tf_op jit(solution)/shard_map/lattice/pallas_call | solution.py:155
  241.3 0.0 copy-start.9
  241.3 0.8 copy-done.9
  242.1 0.1 negate_reduce_fusion
  242.2 0.5 convert_divide_fusion
  242.7 0.0 copy-done.2
  242.7 54.4 %joint_backward.1 = (f32[640,512]{1,0:T(8,128)}, f32[10,640,8]{2,1,0:T(8,128)}, bf16[640,1024]{1,0:T(8,128)(2,1)}, bf16[640,128]{1,0:T(8,128)(2,1)}) custom-call(s32[2,25]{1,0:T(2,128)} %copy-done.11, f32[640,512]{1,0:T(8,128)} %copy-done.1, f32[10,640,8]{2,1,0:T(8,128)} %get-tuple-element.96.pred_ref, bf16[640,1152]{1,0:T(8,128)(2,1)} %get-tuple-element.113.w_ref, ...), custom_call_target="tpu_custom_call" | custom-call | tf_op jit(solution)/shard_map/joint_backward/pallas_call | solution.py:290
  297.1 0.0 copy-start.3
  297.1 1.3 copy-done.3
  298.4 0.0 copy-start.4
  298.4 1.3 copy-done.4
  299.7 0.0 copy-start.10
  299.7 0.9 copy-done.10
  300.6 5.0 joint_outputs.1
  305.6 0.0 copy-start.6
  305.6 1.0 copy-done.6
  306.6 19.2 %back_part_one.2 = (f32[512,512]{1,0:T(8,128)}, f32[512,512]{1,0:T(8,128)}, bf16[8,576,512]{2,1,0:T(8,128)(2,1)}, f32[16,128]{1,0:T(8,128)}, f32[8,512]{1,0:T(8,128)}) custom-call(f32[512,512]{1,0:T(8,128)} %copy-done.6, f32[512,512]{1,0:T(8,128)} %get-tuple-element.123.y4_ref, f32[512,512]{1,0:T(8,128)} %get-tuple-element.124.y3_ref, ...), custom_call_target="tpu_custom_call" | custom-call | tf_op jit(solution)/shard_map/back_part_one/pallas_call | solution.py:534
  325.8 66.9 %back_part_two_and_scatter.2 = (f32[512,512]{1,0:T(8,128)}, bf16[8,960,512]{2,1,0:T(8,128)(2,1)}, f32[16,128]{1,0:T(8,128)}, bf16[10,2,48,512]{3,2,1,0:T(8,128)(2,1)}) custom-call(s32[2]{0:T(128)} %refs_0_.5, f32[512,512]{1,0:T(8,128)} %get-tuple-element.106.refs_1_, f32[512,512]{1,0:T(8,128)} %get-tuple-element.107.refs_2_, ...), custom_call_target="tpu_custom_call" | custom-call | tf_op jit(solution)/shard_map/back_part_two_and_scatter/pallas_call | solution.py:546
  392.7 19.0 %back_part_one.3 = (f32[512,512]{1,0:T(8,128)}, f32[512,512]{1,0:T(8,128)}, bf16[8,576,512]{2,1,0:T(8,128)(2,1)}, f32[16,128]{1,0:T(8,128)}, f32[8,512]{1,0:T(8,128)}) custom-call(f32[512,512]{1,0:T(8,128)} %get-tuple-element.135.grad_ref, f32[512,512]{1,0:T(8,128)} %get-tuple-element.136.y4_ref, f32[512,512]{1,0:T(8,128)} %get-tuple-element.137.y3_ref, ...), custom_call_target="tpu_custom_call" | custom-call | tf_op jit(solution)/shard_map/back_part_one/pallas_call | solution.py:534
  411.7 68.4 %back_part_two_and_scatter.3 = (f32[512,512]{1,0:T(8,128)}, bf16[8,960,512]{2,1,0:T(8,128)(2,1)}, f32[16,128]{1,0:T(8,128)}, bf16[10,2,48,512]{3,2,1,0:T(8,128)(2,1)}) custom-call(s32[2]{0:T(128)} %refs_0_.5, bf16[512,512]{1,0:T(8,128)(2,1)} %bitcast.31, f32[512,512]{1,0:T(8,128)} %get-tuple-element.100.refs_2_, f32[512,512]{1,0:T(8,128)} %get-tuple-element.101.refs_3_, ...), custom_call_target="tpu_custom_call" | custom-call | tf_op jit(solution)/shard_map/back_part_two_and_scatter/pallas_call | solution.py:546
  480.0 0.0 copy-start.7
  480.1 0.0 copy-start.8
  480.1 72.2 %idle_and_scatter.1 = bf16[16,2,48,512]{3,2,1,0:T(8,128)(2,1)} custom-call(bf16[4,2,576,512]{3,2,1,0:T(8,128)(2,1)} %bitcast.28, bf16[4,2,960,512]{3,2,1,0:T(8,128)(2,1)} %bitcast.26), custom_call_target="tpu_custom_call" | custom-call | tf_op jit(solution)/shard_map/idle_and_scatter/pallas_call | solution.py:546
  552.3 0.0 copy-done.7
  552.3 0.0 copy-done.8
  552.3 0.0 copy-start
  552.3 1.4 copy-done
  553.7 0.0 copy-start.17
  553.7 0.0 copy-start.16
  553.8 0.0 copy-start.14
  553.8 3.1 unpack_grads.1
  556.8 0.6 copy.49
  557.4 0.6 copy.50
  558.0 0.0 copy-done.17
  558.0 0.0 copy-done.16
  558.0 0.7 fusion
  558.7 0.7 copy.51
  559.3 0.0 copy-done.14
  559.4 1.0 copy.53
  (6 shorter events, 0.1 us)
Async XLA Ops:
  0.7 164.6 %copy-start.15 = (bf16[2,25,640]{2,0,1:T(2,128)(2,1)S(1)}, bf16[2,25,640]{2,0,1:T(2,128)(2,1)}, u32[]{:S(2)}) copy-start(bf16[2,25,640]{2,0,1:T(2,128)(2,1)} %param.25) | copy-start | bytes 192004
  1.4 170.8 %copy-start.11 = (s32[2,25]{1,0:T(2,128)}, s32[2,25]{1,0:T(2,128)S(1)}, u32[]{:S(2)}) copy-start(s32[2,25]{1,0:T(2,128)S(1)} %concatenate.3.labels_ref) | copy-start | bytes 604
  165.4 1.2 copy-start.5
  172.1 34.0 %copy-start.1 = (f32[640,512]{1,0:T(8,128)}, f32[640,512]{1,0:T(8,128)S(1)}, u32[]{:S(2)}) copy-start(f32[640,512]{1,0:T(8,128)S(1)} %get-tuple-element.95.enc_ref) | copy-start | bytes 3932164
  172.2 34.0 %copy-start.12 = (s32[2]{0:T(128)S(1)}, s32[2]{0:T(128)}, u32[]{:S(2)}) copy-start(s32[2]{0:T(128)} %refs_0_.5) | copy-start | bytes 28
  172.2 34.0 %copy-start.13 = (s32[2]{0:T(128)S(1)}, s32[2]{0:T(128)}, u32[]{:S(2)}) copy-start(s32[2]{0:T(128)} %ulen_ref.1) | copy-start | bytes 28
  206.1 36.6 %copy-start.2 = (f32[8,64,256]{2,1,0:T(8,128)}, f32[8,64,256]{2,1,0:T(8,128)S(1)}, u32[]{:S(2)}) copy-start(f32[8,64,256]{2,1,0:T(8,128)S(1)} %get-tuple-element.98.feats_ref) | copy-start | bytes 1572868
  241.3 0.8 copy-start.9
  297.1 1.3 copy-start.3
  298.4 1.3 copy-start.4
  299.7 0.9 copy-start.10
  305.6 1.0 copy-start.6
  480.0 72.3 %copy-start.7 = (bf16[10,2,48,512]{3,2,1,0:T(8,128)(2,1)S(1)}, bf16[10,2,48,512]{3,2,1,0:T(8,128)(2,1)}, u32[]{:S(2)}) copy-start(bf16[10,2,48,512]{3,2,1,0:T(8,128)(2,1)} %get-tuple-element.148) | copy-start | bytes 2949124
  480.1 72.3 %copy-start.8 = (bf16[10,2,48,512]{3,2,1,0:T(8,128)(2,1)S(1)}, bf16[10,2,48,512]{3,2,1,0:T(8,128)(2,1)}, u32[]{:S(2)}) copy-start(bf16[10,2,48,512]{3,2,1,0:T(8,128)(2,1)} %get-tuple-element.149) | copy-start | bytes 2949124
  552.3 1.4 copy-start
  553.7 4.3 copy-start.17
  553.7 4.3 copy-start.16
  553.8 5.6 copy-start.14

commit v7 on v6

--- a/solution.py
+++ b/solution.py
@@ -574,7 +574,8 @@
     return mean, dev, count
 
 
-CHUNK_ROWS = 64
+CHUNK_ROWS = 128
+PAIRS_AT_ONCE = 4
 WIDE = 512
 PLACE = ("p_out", "s_in", "s_out", "p_in", "w_proj", "w_joint", "f_in", "f_out")
 
@@ -587,7 +588,7 @@
     def step(i, carry):
         return body(pl.ds(pl.multiple_of(i * CHUNK_ROWS, CHUNK_ROWS), CHUNK_ROWS), i, carry)
 
-    return lax.fori_loop(0, count // CHUNK_ROWS, step, init)
+    return lax.fori_loop(0, count // CHUNK_ROWS, step, init, unroll=count // CHUNK_ROWS)
 
 
 def ln_parts(v):
@@ -830,7 +831,7 @@
 
 def back_two_kernel(utts, table, held, start, end, beats, t_ref, x_ref, y1_ref, y2_ref, r_ref, t_in, c_ref, d_ref, db_ref, g_in, pooled_ref, local_ref, late_ref, small, whole, h_hbm,
                     g_out, grads, sums_ref,
-                    w_pin, w_proj, w_joint, w_fin, w_fout, g, gb, normed, dact, act, dh, dn, dw_pin, dw_proj, dw_joint, dw_in, dw_out, h, gp, dd, dr, dt, sm, sems, *meeting):
+                    w_pin, w_proj, w_joint, w_fin, w_fout, g, gb, normed, dact, act, dh, dn, dw_pin, dw_proj, dw_joint, dw_in, dw_out, h, gp, dd, sm, sems, *meeting):
     rows, width = g.shape
     frames = rows // utts
     mover = Mover(sems)
@@ -848,6 +849,8 @@
     ntaps = taps.shape[0]
     span = frames + 16
     per = frames // CHUNK_ROWS
+    dr = dh.at[:, pl.ds(0, 2 * width)]
+    dt = dh.at[:, pl.ds(0, 3 * width)]
     beats.run(5)
     exchange = Exchange("sum", meeting[0].shape[0], meeting[1].shape[0], *meeting)
     exchange.begin(local_ref[...])
@@ -912,10 +915,10 @@
     pairs = width // 128
     side = lax.broadcasted_iota(jnp.int32, (frames, 128), 1) < 64
     key_at = lax.broadcasted_iota(jnp.int32, (frames, 1), 0)
-    hook = beats.loop(utts * pairs)
+    turns = utts * pairs // PAIRS_AT_ONCE
+    hook = beats.loop(utts * pairs, turns)
 
     def pair_step(m, carry):
-        hook(m)
         u = m // pairs
         base = lax.rem(m, pairs) * 128
         rr = pl.ds(pl.multiple_of(u * frames, frames), frames)
@@ -939,7 +942,13 @@
             dt[rr, at[b]] = jnp.where(side, got[0][b], got[1][b]).astype(jnp.bfloat16)
         return carry
 
-    lax.fori_loop(0, utts * pairs, pair_step, 0)
+    def pair_turn(m, carry):
+        hook(m)
+        for i in range(PAIRS_AT_ONCE):
+            carry = pair_step(m * PAIRS_AT_ONCE + i, carry)
+        return carry
+
+    lax.fori_loop(0, turns, pair_turn, 0)
     for b in range(3):
         cols = slice(b * width, (b + 1) * width)
         dw_joint[:, cols] = tn(normed[...], dt[:, cols]).astype(jnp.bfloat16)
@@ -1027,7 +1036,7 @@
          v((rows, width), F32), v((rows, width), BF16), v((rows, ff), BF16), v((rows, width), F32),
          v((width, 2 * width), BF16), v((width, width), BF16), v((width, 3 * width), BF16), v((width, ff), BF16),
          v((ff, width), BF16), v((nb, rows, WIDE), F32), v((pad_rows, width), F32), v((pad_rows, width), F32),
-         v((rows, 2 * width), BF16), v((rows, 3 * width), BF16), v((n, 16, WIDE), BF16), pltpu.SemaphoreType.DMA((20,)),
+         v((n, 16, WIDE), BF16), pltpu.SemaphoreType.DMA((20,)),
          v((groups, 16, 128), F32), v((n, 16, 128), F32), dma((groups,)), dma((groups,)), dma((n,)), dma((n,))],
         "back_part_two",
         ride,
@@ -1294,10 +1303,10 @@
     pairs = width // 128
     side = lax.broadcasted_iota(jnp.int32, (frames, 128), 1) < 64
     key_at = lax.broadcasted_iota(jnp.int32, (1, frames), 1)
-    hook = beats.loop(3, utts * pairs)
+    turns = utts * pairs // PAIRS_AT_ONCE
+    hook = beats.loop(3, turns)
 
     def pair_step(m, carry):
-        hook(m)
         u = m // pairs
         base = lax.rem(m, pairs) * 128
         rr = pl.ds(pl.multiple_of(u * frames, frames), frames)
@@ -1315,7 +1324,13 @@
         ctx[rr, pl.ds(pl.multiple_of(base, 128), 128)] = jnp.where(side, got[0], got[1]).astype(jnp.bfloat16)
         return carry
 
-    lax.fori_loop(0, utts * pairs, pair_step, 0)
+    def pair_turn(m, carry):
+        hook(m)
+        for i in range(PAIRS_AT_ONCE):
+            carry = pair_step(m * PAIRS_AT_ONCE + i, carry)
+        return carry
+
+    lax.fori_loop(0, turns, pair_turn, 0)
     mover.put(ctx, c_out)
     weights["w_proj"][1].wait()
     y2[...] = y1[...] + nn(ctx[...], weights["w_proj"][0][...])

time: 571 us -> 544 us (0.953)
  Pallas kernels: 543 us -> 516 us
    pallas_call x2, Pallas kernels: 38.2 us -> 25.9 us  [call(): pl.pallas_call(partial(kernel, Beats()), in_specs=in_specs, out_specs=out...]
    pallas_call x1, Pallas kernels: 160 us -> 149 us  [forward(): pl.pallas_call(partial(forward_kernel, utts, layers, n1, groups, tables,...]
where the time goes in v7:
time: 544 us; the launch traced here: 534 us
  Pallas kernels  516 us (95%)
  local copies, waits for them, and re-layouts  15.5 us (3%)
    pallas_call x3, Pallas kernels, call(): pl.pallas_call(partial(riding_kernel, kernel, counts, scatter_plan(ride),...  204 us
    pallas_call x1, Pallas kernels, forward(): pl.pallas_call(partial(forward_kernel, utts, layers, n1, groups, tables,...  149 us
    pallas_call x1, Pallas kernels, joint_backward(): pl.pallas_call(partial(joint_bwd_kernel, groups, durs), grid=(utts * grou...  54.4 us
    pallas_call x1, Pallas kernels, lattice(): pl.pallas_call(partial(lattice_kernel, slots), out_shape=(jax.ShapeDtypeS...  34.9 us
    pallas_call x1, Pallas kernels, joint_forward(): pl.pallas_call(partial(joint_fwd_kernel, groups, durs), grid=(utts * grou...  33.9 us
    pallas_call x2, Pallas kernels, call(): pl.pallas_call(partial(kernel, Beats()), in_specs=in_specs, out_specs=out...  25.9 us
    unnamed x44, local copies, waits for them, and re-layouts  14.7 us

profile of v7, /device:TPU:0, one launch (start us, length us, event | category | flops | bytes accessed | tf_op | source)
XLA Modules:
  0.0 533.6 jit_solution(12223057038799585963)
XLA Ops:
  0.7 0.0 copy-start.15
  0.7 0.7 concatenate.3.labels_ref
  1.4 0.0 copy-start.11
  1.4 1.3 copy.45.refs_8_
  2.6 1.3 copy.46.refs_9_
  3.9 1.4 copy.47.refs_15_
  5.3 148.7 %gather_and_forward.1 = (bf16[4,2,3360,512]{3,2,1,0:T(8,128)(2,1)}, f32[512,512]{1,0:T(8,128)}, f32[4,512,512]{2,1,0:T(8,128)}, f32[512,512]{1,0:T(8,128)}, bf16...) custom-call(s32[2]{0:T(128)} %refs_0_.5, ...), custom_call_target="tpu_custom_call" | custom-call | tf_op jit(solution)/shard_map/gather_and_forward/pallas_call | solution.py:1492
  154.0 0.0 copy-done.15
  154.1 0.0 copy-start.5
  154.1 1.2 copy-done.5
  155.4 5.5 %joint_inputs.1 = (bf16[512,512]{1,0:T(8,128)(2,1)S(1)}, f32[640,512]{1,0:T(8,128)S(1)}, f32[10,640,8]{2,1,0:T(8,128)}, bf16[1152,640]{1,0:T(8,128)(2,1)S(1)}, b...) custom-call(f32[512,512]{1,0:T(8,128)S(1)} %copy-done.5, ...), custom_call_target="tpu_custom_call" | custom-call | tf_op jit(solution)/shard_map/joint_inputs/pallas_call | solution.py:1639
  160.9 0.0 copy-start.1
  160.9 0.0 copy-done.11
  160.9 0.0 copy-start.12
  160.9 0.0 copy-start.13
  160.9 33.9 %joint_forward.1 = (f32[8,64,256]{2,1,0:T(8,128)S(1)}, bf16[10,5,1024,256]{3,2,1,0:T(8,128)(2,1)}) custom-call(s32[2,25]{1,0:T(2,128)S(1)} %concatenate.3.labels_ref, f32[640,512]{1,0:T(8,128)S(1)} %get-tuple-element.95.enc_ref, f32[10,640,8]{2,1,0:T(8,128)} %get-tuple-element.96.pred_ref, bf16[1152,640]{1,0:T(8,128)(2,1)S(1)} %get-tuple-element.97.wt_ref), custom_call_target="tpu_custom_call" | custom-call | tf_op jit(solution)/shard_map/joint_forward/pallas_call | solution.py:217
  194.8 0.0 copy-start.2
  194.9 0.0 copy-done.1
  194.9 0.0 copy-done.12
  194.9 0.0 copy-done.13
  194.9 34.9 %lattice.1 = (f32[7,64,256]{2,1,0:T(8,128)S(1)}, f32[8,128]{1,0:T(8,128)S(1)}) custom-call(f32[7,64,256]{2,1,0:T(8,128)S(1)} %slice.18.feats_ref, s32[2]{0:T(128)S(1)} %copy-done.12, s32[2]{0:T(128)S(1)} %copy-done.13), custom_call_target="tpu_custom_call" | custom-call | tf_op jit(solution)/shard_map/lattice/pallas_call | solution.py:155
  229.9 0.0 copy-start.9
  229.9 0.8 copy-done.9
  230.6 0.1 negate_reduce_fusion
  230.7 0.5 convert_divide_fusion
  231.3 0.0 copy-done.2
  231.3 54.4 %joint_backward.1 = (f32[640,512]{1,0:T(8,128)}, f32[10,640,8]{2,1,0:T(8,128)}, bf16[640,1024]{1,0:T(8,128)(2,1)}, bf16[640,128]{1,0:T(8,128)(2,1)}) custom-call(s32[2,25]{1,0:T(2,128)} %copy-done.11, f32[640,512]{1,0:T(8,128)} %copy-done.1, f32[10,640,8]{2,1,0:T(8,128)} %get-tuple-element.96.pred_ref, bf16[640,1152]{1,0:T(8,128)(2,1)} %get-tuple-element.113.w_ref, ...), custom_call_target="tpu_custom_call" | custom-call | tf_op jit(solution)/shard_map/joint_backward/pallas_call | solution.py:290
  285.7 0.0 copy-start.3
  285.7 1.3 copy-done.3
  287.0 0.0 copy-start.4
  287.0 1.3 copy-done.4
  288.3 0.0 copy-start.10
  288.3 0.9 copy-done.10
  289.2 5.0 joint_outputs.1
  294.2 0.0 copy-start.6
  294.2 1.0 copy-done.6
  295.2 13.0 %back_part_one.2 = (f32[512,512]{1,0:T(8,128)}, f32[512,512]{1,0:T(8,128)}, bf16[8,576,512]{2,1,0:T(8,128)(2,1)}, f32[16,128]{1,0:T(8,128)}, f32[8,512]{1,0:T(8,128)}) custom-call(f32[512,512]{1,0:T(8,128)} %copy-done.6, f32[512,512]{1,0:T(8,128)} %get-tuple-element.123.y4_ref, f32[512,512]{1,0:T(8,128)} %get-tuple-element.124.y3_ref, ...), custom_call_target="tpu_custom_call" | custom-call | tf_op jit(solution)/shard_map/back_part_one/pallas_call | solution.py:534
  308.1 65.2 %back_part_two_and_scatter.2 = (f32[512,512]{1,0:T(8,128)}, bf16[8,960,512]{2,1,0:T(8,128)(2,1)}, f32[16,128]{1,0:T(8,128)}, bf16[10,2,48,512]{3,2,1,0:T(8,128)(2,1)}) custom-call(s32[2]{0:T(128)} %refs_0_.5, f32[512,512]{1,0:T(8,128)} %get-tuple-element.106.refs_1_, f32[512,512]{1,0:T(8,128)} %get-tuple-element.107.refs_2_, ...), custom_call_target="tpu_custom_call" | custom-call | tf_op jit(solution)/shard_map/back_part_two_and_scatter/pallas_call | solution.py:546
  373.3 12.9 %back_part_one.3 = (f32[512,512]{1,0:T(8,128)}, f32[512,512]{1,0:T(8,128)}, bf16[8,576,512]{2,1,0:T(8,128)(2,1)}, f32[16,128]{1,0:T(8,128)}, f32[8,512]{1,0:T(8,128)}) custom-call(f32[512,512]{1,0:T(8,128)} %get-tuple-element.135.grad_ref, f32[512,512]{1,0:T(8,128)} %get-tuple-element.136.y4_ref, f32[512,512]{1,0:T(8,128)} %get-tuple-element.137.y3_ref, ...), custom_call_target="tpu_custom_call" | custom-call | tf_op jit(solution)/shard_map/back_part_one/pallas_call | solution.py:534
  386.2 66.9 %back_part_two_and_scatter.3 = (f32[512,512]{1,0:T(8,128)}, bf16[8,960,512]{2,1,0:T(8,128)(2,1)}, f32[16,128]{1,0:T(8,128)}, bf16[10,2,48,512]{3,2,1,0:T(8,128)(2,1)}) custom-call(s32[2]{0:T(128)} %refs_0_.5, bf16[512,512]{1,0:T(8,128)(2,1)} %bitcast.31, f32[512,512]{1,0:T(8,128)} %get-tuple-element.100.refs_2_, f32[512,512]{1,0:T(8,128)} %get-tuple-element.101.refs_3_, ...), custom_call_target="tpu_custom_call" | custom-call | tf_op jit(solution)/shard_map/back_part_two_and_scatter/pallas_call | solution.py:546
  453.1 0.0 copy-start.7
  453.2 0.0 copy-start.8
  453.2 72.2 %idle_and_scatter.1 = bf16[16,2,48,512]{3,2,1,0:T(8,128)(2,1)} custom-call(bf16[4,2,576,512]{3,2,1,0:T(8,128)(2,1)} %bitcast.28, bf16[4,2,960,512]{3,2,1,0:T(8,128)(2,1)} %bitcast.26), custom_call_target="tpu_custom_call" | custom-call | tf_op jit(solution)/shard_map/idle_and_scatter/pallas_call | solution.py:546
  525.4 0.0 copy-done.7
  525.4 0.0 copy-done.8
  525.4 0.0 copy-start
  525.4 1.4 copy-done
  526.8 0.0 copy-start.17
  526.8 0.0 copy-start.16
  526.8 0.0 copy-start.14
  526.8 3.1 unpack_grads.1
  529.9 0.6 copy.49
  530.5 0.6 copy.50
  531.1 0.0 copy-done.17
  531.1 0.0 copy-done.16
  531.1 0.7 fusion
  531.7 0.7 copy.51
  532.4 0.0 copy-done.14
  532.4 1.0 copy.53
  (6 shorter events, 0.1 us)
Async XLA Ops:
  0.7 153.4 %copy-start.15 = (bf16[2,25,640]{2,0,1:T(2,128)(2,1)S(1)}, bf16[2,25,640]{2,0,1:T(2,128)(2,1)}, u32[]{:S(2)}) copy-start(bf16[2,25,640]{2,0,1:T(2,128)(2,1)} %param.25) | copy-start | bytes 192004
  1.4 159.5 %copy-start.11 = (s32[2,25]{1,0:T(2,128)}, s32[2,25]{1,0:T(2,128)S(1)}, u32[]{:S(2)}) copy-start(s32[2,25]{1,0:T(2,128)S(1)} %concatenate.3.labels_ref) | copy-start | bytes 604
  154.1 1.2 copy-start.5
  160.9 34.0 %copy-start.1 = (f32[640,512]{1,0:T(8,128)}, f32[640,512]{1,0:T(8,128)S(1)}, u32[]{:S(2)}) copy-start(f32[640,512]{1,0:T(8,128)S(1)} %get-tuple-element.95.enc_ref) | copy-start | bytes 3932164
  160.9 34.0 %copy-start.12 = (s32[2]{0:T(128)S(1)}, s32[2]{0:T(128)}, u32[]{:S(2)}) copy-start(s32[2]{0:T(128)} %refs_0_.5) | copy-start | bytes 28
  160.9 34.0 %copy-start.13 = (s32[2]{0:T(128)S(1)}, s32[2]{0:T(128)}, u32[]{:S(2)}) copy-start(s32[2]{0:T(128)} %ulen_ref.1) | copy-start | bytes 28
  194.8 36.4 %copy-start.2 = (f32[8,64,256]{2,1,0:T(8,128)}, f32[8,64,256]{2,1,0:T(8,128)S(1)}, u32[]{:S(2)}) copy-start(f32[8,64,256]{2,1,0:T(8,128)S(1)} %get-tuple-element.98.feats_ref) | copy-start | bytes 1572868
  229.9 0.8 copy-start.9
  285.7 1.3 copy-start.3
  287.0 1.3 copy-start.4
  288.3 0.9 copy-start.10
  294.2 1.0 copy-start.6
  453.1 72.2 %copy-start.7 = (bf16[10,2,48,512]{3,2,1,0:T(8,128)(2,1)S(1)}, bf16[10,2,48,512]{3,2,1,0:T(8,128)(2,1)}, u32[]{:S(2)}) copy-start(bf16[10,2,48,512]{3,2,1,0:T(8,128)(2,1)} %get-tuple-element.148) | copy-start | bytes 2949124
  453.2 72.2 %copy-start.8 = (bf16[10,2,48,512]{3,2,1,0:T(8,128)(2,1)S(1)}, bf16[10,2,48,512]{3,2,1,0:T(8,128)(2,1)}, u32[]{:S(2)}) copy-start(bf16[10,2,48,512]{3,2,1,0:T(8,128)(2,1)} %get-tuple-element.149) | copy-start | bytes 2949124
  525.4 1.4 copy-start
  526.8 4.3 copy-start.17
  526.8 4.3 copy-start.16
  526.8 5.6 %copy-start.14 = (f32[512,512]{1,0:T(8,128)S(1)}, f32[512,512]{1,0:T(8,128)}, u32[]{:S(2)}) copy-start(f32[512,512]{1,0:T(8,128)} %get-tuple-element.147) | copy-start | bytes 3145732
